TPU v7x, 32 devices: a whole 2x2x4 slice. The times are simulated.
32 devices in a mesh: ctx: 8 (over z, core), fsdp: 4 (over y, x).
Axes of the slice: x: 2, y: 2, z: 4, core: 2. Of those that a mesh axis runs over, the one named last changes fastest.
Arguments:
- tokens: bfloat16 [4, 2048, 2048], P('fsdp', 'ctx'), may hold values from -6 to 6
- block_place: int32 [128], replicated, may hold values from 0 to 127, as said below
- seq_lengths: int32 [4, 4], P('fsdp'), may hold values from 1 to 1024, 2048 in all within a row
- norm_gain: bfloat16 [2048], P('fsdp'), may hold values from 0.5 to 1.5
- norm_bias: bfloat16 [2048], P('fsdp'), may hold values from -3 to 3
- qkv_weight: bfloat16 [2048, 6144], P('fsdp'), may hold values from -0.125 to 0.125
- qkv_bias: bfloat16 [6144], P('fsdp'), may hold values from -3 to 3
- out_weight: bfloat16 [2048, 2048], P('fsdp'), may hold values from -0.5 to 0.5
- out_bias: bfloat16 [2048], P('fsdp'), may hold values from -3 to 3
- up_weight: bfloat16 [2048, 8192], P('fsdp'), may hold values from -0.125 to 0.125
- up_bias: bfloat16 [8192], P('fsdp'), may hold values from -3 to 3
- down_weight: bfloat16 [8192, 2048], P('fsdp'), may hold values from -0.0625 to 0.0625
- down_bias: bfloat16 [2048], P('fsdp'), may hold values from -3 to 3
- out_grad: bfloat16 [4, 2048, 2048], P('fsdp', 'ctx'), may hold values from -6 to 6
Outputs:
- layer_output: bfloat16 [4, 2048, 2048], P('fsdp', 'ctx')
- input_grad: bfloat16 [4, 2048, 2048], P('fsdp', 'ctx')
- norm_gain_grad: float32 [2048], P('fsdp')
- norm_bias_grad: float32 [2048], P('fsdp')
- qkv_weight_grad: float32 [2048, 6144], P('fsdp')
- qkv_bias_grad: float32 [6144], P('fsdp')
- out_weight_grad: float32 [2048, 2048], P('fsdp')
- out_bias_grad: float32 [2048], P('fsdp')
- up_weight_grad: float32 [2048, 8192], P('fsdp')
- up_bias_grad: float32 [8192], P('fsdp')
- down_weight_grad: float32 [8192, 2048], P('fsdp')
- down_bias_grad: float32 [2048], P('fsdp')
Inputs may be any that keep to these rules, and one draw needn't show every extreme that they name: `block_place`: A permutation of the group's blocks. For each device d of ctx, its entries d * 16 to (d + 1) * 16 - 1 hold exactly 2 places of each remainder modulo 8. `seq_lengths`: each row sums to 2048.
All inputs are finite; a program needn't handle non-finite values.
Results may differ from a plain program's by a relative error of at most 0.017.
Values may be sent and summed in bfloat16 or wider, within the bound.
No kernel may reach another device: no remote copies, remote signals or barrier semaphores. Data moves between devices by JAX's collectives and lax.ppermute only.
A program may use at most 704 MiB of HBM per device.

v0:
```python
import jax
import jax.numpy as jnp
from jax import lax
from jax.sharding import PartitionSpec as P

HEAD_DIM = 64
ROT = 32
BLK = 16


def from_behind(shard, axis, by):
    devices = lax.axis_size(axis)
    return lax.ppermute(shard, axis, [(i, (i + by) % devices) for i in range(devices)])


def dealt_places(block_place, cycle_size, owner):
    places = block_place.reshape(cycle_size, -1)
    per_dev = places.shape[1]
    repeat = per_dev // cycle_size
    matches = places % cycle_size == owner
    rank_in = jnp.cumsum(matches.astype(jnp.int32), axis=1) - 1
    slot_ids = jnp.arange(repeat, dtype=jnp.int32)
    picked = matches[:, None, :] & (rank_in[:, None, :] == slot_ids[None, :, None])
    return jnp.sum(jnp.where(picked, places[:, None, :], 0), axis=2).reshape(-1)


def arrival_slots(block_place, cycle_size, owner):
    places = block_place.reshape(cycle_size, -1)
    own_places = lax.dynamic_index_in_dim(places, owner, 0, keepdims=False)
    per_dev = own_places.shape[0]
    repeat = per_dev // cycle_size
    residue = own_places % cycle_size
    item_order = jnp.arange(per_dev, dtype=jnp.int32)
    earlier = (residue[:, None] == residue[None, :]) & (item_order[None, :] < item_order[:, None])
    rank_in = jnp.sum(earlier.astype(jnp.int32), axis=1)
    slot_of = residue * repeat + rank_in
    arrival_of = jnp.sum(
        jnp.where(slot_of[None, :] == item_order[:, None], item_order[None, :], 0), axis=1
    )
    return (slot_of, arrival_of)


def layout(block_place, lengths, owner, cycle_size, tok_rows, block_rows):
    places = dealt_places(block_place, cycle_size, owner)
    row_index = jnp.arange(tok_rows, dtype=jnp.int32)
    position = (
        jnp.repeat(places, block_rows, total_repeat_length=tok_rows) * block_rows
        + row_index % block_rows
    )
    seq_ends = jnp.cumsum(lengths)
    seq_starts = seq_ends - lengths
    segment = jnp.sum((position[:, None] >= seq_ends[None, :]).astype(jnp.int32), axis=1)
    which = segment[:, None] == jnp.arange(lengths.shape[0], dtype=jnp.int32)[None, :]
    seq_begin = jnp.sum(jnp.where(which, seq_starts[None, :], 0), axis=1)
    return (position, segment, position - seq_begin)


def rotate(values, within, direction):
    half_rot = ROT // 2
    frequency = 10000.0 ** (-jnp.arange(half_rot, dtype=jnp.float32) * 2.0 / ROT)
    angles = within.astype(jnp.float32)[:, None] * frequency[None, :]
    cosine = jnp.cos(angles)[:, None, :]
    sine_part = direction * jnp.sin(angles)[:, None, :]
    first_half = values[..., :half_rot]
    second_half = values[..., half_rot:ROT]
    return jnp.concatenate(
        [
            first_half * cosine - second_half * sine_part,
            second_half * cosine + first_half * sine_part,
            values[..., ROT:],
        ],
        axis=-1,
    )


def transposed_dot(left_rows, right_rows):
    return lax.dot_general(
        left_rows, right_rows, (((1,), (1,)), ((), ())), preferred_element_type=jnp.float32
    )


def term_maker(left_rows, right_rows):
    return lax.dot_general(
        left_rows, right_rows, (((0,), (0,)), ((), ())), preferred_element_type=jnp.float32
    )


def shards(
    tokens,
    block_place,
    seq_lengths,
    norm_gain,
    norm_bias,
    qkv_weight,
    qkv_bias,
    out_weight,
    out_bias,
    up_weight,
    up_bias,
    down_weight,
    down_bias,
    out_grad,
):
    cycle_size = lax.axis_size("ctx")
    own_index = lax.axis_index("ctx")
    shard_count = lax.axis_size("fsdp")
    shard_index = lax.axis_index("fsdp")
    arrival = tokens[0]
    tok_rows, model_width = arrival.shape
    per_dev = tok_rows // BLK
    slot_of, arrival_of = arrival_slots(block_place, cycle_size, own_index)

    def to_slots(rows_in):
        return rows_in.reshape(per_dev, BLK, model_width)[arrival_of].reshape(tok_rows, model_width)

    def from_slots(rows_in):
        return rows_in.reshape(per_dev, BLK, model_width)[slot_of].reshape(tok_rows, model_width)

    dealt_tokens, grad_rows = (
        lax.all_to_all(to_slots(arrival), "ctx", split_axis=0, concat_axis=0, tiled=True),
        lax.all_to_all(to_slots(out_grad[0]), "ctx", split_axis=0, concat_axis=0, tiled=True),
    )
    inputs = dealt_tokens.astype(jnp.float32)
    lengths = seq_lengths[0]
    head_count = model_width // HEAD_DIM
    score_scale = HEAD_DIM ** (-0.5)
    head_shape = (tok_rows, head_count, HEAD_DIM)
    position, segment, within = layout(block_place, lengths, own_index, cycle_size, tok_rows, BLK)
    gathered = (
        lax.all_gather(norm_gain, "fsdp", axis=0, tiled=True),
        lax.all_gather(norm_bias, "fsdp", axis=0, tiled=True),
        lax.all_gather(qkv_weight, "fsdp", axis=0, tiled=True),
        lax.all_gather(qkv_bias, "fsdp", axis=0, tiled=True),
        lax.all_gather(out_weight, "fsdp", axis=0, tiled=True),
        lax.all_gather(out_bias, "fsdp", axis=0, tiled=True),
        lax.all_gather(up_weight, "fsdp", axis=0, tiled=True),
        lax.all_gather(up_bias, "fsdp", axis=0, tiled=True),
        lax.all_gather(down_weight, "fsdp", axis=0, tiled=True),
        lax.all_gather(down_bias, "fsdp", axis=0, tiled=True),
    )
    (
        gain_all,
        shift_all,
        qkv_all,
        qkv_bias_all,
        out_all,
        out_bias_all,
        up_all,
        up_bias_all,
        down_all,
        down_bias_all,
    ) = gathered
    row_mean = jnp.mean(inputs, axis=1, keepdims=True)
    centred = inputs - row_mean
    inv_std = lax.rsqrt(jnp.mean(centred * centred, axis=1, keepdims=True) + 1e-05)
    scaled = centred * inv_std
    normed = (scaled * gain_all.astype(jnp.float32) + shift_all.astype(jnp.float32)).astype(
        jnp.bfloat16
    )
    projected = jnp.dot(normed, qkv_all, preferred_element_type=jnp.float32) + qkv_bias_all.astype(
        jnp.float32
    )
    queries = rotate(projected[:, :model_width].reshape(head_shape), within, 1.0).astype(
        jnp.bfloat16
    )
    key_rows = rotate(
        projected[:, model_width : 2 * model_width].reshape(head_shape), within, 1.0
    ).astype(jnp.bfloat16)
    value_rows = projected[:, 2 * model_width :].reshape(head_shape).astype(jnp.bfloat16)
    hidden = jnp.dot(normed, up_all, preferred_element_type=jnp.float32) + up_bias_all.astype(
        jnp.float32
    )
    active = jax.nn.gelu(hidden, approximate=True).astype(jnp.bfloat16)

    def visible_for(source):
        key_pos, key_seg, unused = layout(block_place, lengths, source, cycle_size, tok_rows, BLK)
        return ((segment[:, None] == key_seg[None, :]) & (key_pos[None, :] <= position[:, None]))[
            None
        ]

    def forward_block(softmax_state, key_part, value_part, source):
        row_top, row_total, summed = softmax_state
        visible = visible_for(source)
        scores = (
            jnp.einsum("qhd,khd->hqk", queries, key_part, preferred_element_type=jnp.float32)
            * score_scale
        )
        scores = jnp.where(visible, scores, -1e30)
        new_top = jnp.maximum(row_top, jnp.max(scores, axis=2))
        weights = jnp.where(visible, jnp.exp(scores - new_top[:, :, None]), 0.0)
        factor = jnp.exp(row_top - new_top)
        row_total = row_total * factor + jnp.sum(weights, axis=2)
        summed = summed * jnp.transpose(factor)[:, :, None] + jnp.einsum(
            "hqk,khd->qhd",
            weights.astype(jnp.bfloat16),
            value_part,
            preferred_element_type=jnp.float32,
        )
        return (new_top, row_total, summed)

    init_state = (
        jnp.full((head_count, tok_rows), -1e30, jnp.float32),
        jnp.zeros((head_count, tok_rows), jnp.float32),
        jnp.zeros(head_shape, jnp.float32),
    )
    softmax_state = forward_block(init_state, key_rows, value_rows, own_index)

    def forward_step(cycle_step, loop_carry):
        key_part, value_part, softmax_state = loop_carry
        key_part, value_part = from_behind((key_part, value_part), "ctx", 1)
        source = (own_index - cycle_step) % cycle_size
        return (key_part, value_part, forward_block(softmax_state, key_part, value_part, source))

    unused_keys, unused_values, softmax_state = lax.fori_loop(
        1, cycle_size, forward_step, (key_rows, value_rows, softmax_state)
    )
    row_top, row_total, summed = softmax_state
    attended = summed / jnp.transpose(row_total)[:, :, None]
    log_total = row_top + jnp.log(row_total)
    attended_low = attended.astype(jnp.bfloat16).reshape(tok_rows, model_width)
    output = (
        inputs
        + jnp.dot(attended_low, out_all, preferred_element_type=jnp.float32)
        + out_bias_all.astype(jnp.float32)
    )
    output = (
        output
        + jnp.dot(active, down_all, preferred_element_type=jnp.float32)
        + down_bias_all.astype(jnp.float32)
    )
    grad_float = grad_rows.astype(jnp.float32)
    grad_att = transposed_dot(grad_rows, out_all).astype(jnp.bfloat16).reshape(head_shape)
    grad_active = transposed_dot(grad_rows, down_all)
    unused_out, gelu_back = jax.vjp(lambda inner: jax.nn.gelu(inner, approximate=True), hidden)
    grad_hidden = gelu_back(grad_active)[0].astype(jnp.bfloat16)
    delta_rows = jnp.transpose(jnp.sum(grad_att.astype(jnp.float32) * attended, axis=2))

    def backward_block(key_part, value_part, source):
        visible = visible_for(source)
        scores = (
            jnp.einsum("qhd,khd->hqk", queries, key_part, preferred_element_type=jnp.float32)
            * score_scale
        )
        scores = jnp.where(visible, scores, -1e30)
        weights = jnp.where(visible, jnp.exp(scores - log_total[:, :, None]), 0.0)
        grad_weights = jnp.einsum(
            "qhd,khd->hqk", grad_att, value_part, preferred_element_type=jnp.float32
        )
        grad_scores = (weights * (grad_weights - delta_rows[:, :, None])).astype(jnp.bfloat16)
        part_q = (
            jnp.einsum("hqk,khd->qhd", grad_scores, key_part, preferred_element_type=jnp.float32)
            * score_scale
        )
        part_k = (
            jnp.einsum("hqk,qhd->khd", grad_scores, queries, preferred_element_type=jnp.float32)
            * score_scale
        )
        part_v = jnp.einsum(
            "hqk,qhd->khd",
            weights.astype(jnp.bfloat16),
            grad_att,
            preferred_element_type=jnp.float32,
        )
        return (part_q, part_k, part_v)

    grad_q, grad_k, grad_v = backward_block(key_rows, value_rows, own_index)

    def backward_step(cycle_step, loop_carry):
        key_part, value_part, grad_k, grad_v, grad_q = loop_carry
        key_part, value_part = from_behind((key_part, value_part), "ctx", 1)
        grad_k, grad_v = (
            from_behind(grad_k.astype(jnp.bfloat16), "ctx", 1).astype(grad_k.dtype),
            from_behind(grad_v.astype(jnp.bfloat16), "ctx", 1).astype(grad_v.dtype),
        )
        source = (own_index - cycle_step) % cycle_size
        part_q, part_k, part_v = backward_block(key_part, value_part, source)
        return (key_part, value_part, grad_k + part_k, grad_v + part_v, grad_q + part_q)

    unused_keys, unused_values, grad_k, grad_v, grad_q = lax.fori_loop(
        1, cycle_size, backward_step, (key_rows, value_rows, grad_k, grad_v, grad_q)
    )
    grad_k, grad_v = (
        from_behind(grad_k.astype(jnp.bfloat16), "ctx", 1).astype(grad_k.dtype),
        from_behind(grad_v.astype(jnp.bfloat16), "ctx", 1).astype(grad_v.dtype),
    )
    grad_query = rotate(grad_q, within, -1.0).reshape(tok_rows, model_width)
    grad_key = rotate(grad_k, within, -1.0).reshape(tok_rows, model_width)
    grad_mixed = jnp.concatenate(
        [grad_query, grad_key, grad_v.reshape(tok_rows, model_width)], axis=1
    ).astype(jnp.bfloat16)
    grad_normed = transposed_dot(grad_mixed, qkv_all) + transposed_dot(grad_hidden, up_all)
    grad_scaled = grad_normed * gain_all.astype(jnp.float32)
    grad_input = inv_std * (
        grad_scaled
        - jnp.mean(grad_scaled, axis=1, keepdims=True)
        - scaled * jnp.mean(grad_scaled * scaled, axis=1, keepdims=True)
    )
    input_grad = (grad_float + grad_input).astype(jnp.bfloat16)
    home_out, home_grad = (
        lax.all_to_all(output.astype(jnp.bfloat16), "ctx", split_axis=0, concat_axis=0, tiled=True),
        lax.all_to_all(input_grad, "ctx", split_axis=0, concat_axis=0, tiled=True),
    )
    gain_term = jnp.sum(grad_normed * scaled, axis=0)
    shift_term = jnp.sum(grad_normed, axis=0)
    qkv_bias_term = jnp.sum(grad_mixed.astype(jnp.float32), axis=0)
    bias_term = jnp.sum(grad_float, axis=0)
    up_bias_term = jnp.sum(grad_hidden.astype(jnp.float32), axis=0)
    grad_joined = jnp.concatenate([grad_mixed, grad_hidden], axis=1)
    last_left = jnp.concatenate(
        [
            attended_low.reshape(tok_rows, shard_count, -1),
            active.reshape(tok_rows, shard_count, -1),
        ],
        axis=2,
    )
    last_rows = last_left.shape[2] * shard_count
    last_flat = last_left.reshape(tok_rows, last_rows)
    in_shard = lax.psum_scatter(
        term_maker(normed, grad_joined).astype(jnp.bfloat16),
        "fsdp",
        scatter_dimension=0,
        tiled=True,
    )
    last_shard = lax.psum_scatter(
        term_maker(last_flat, grad_rows).astype(jnp.bfloat16),
        "fsdp",
        scatter_dimension=0,
        tiled=True,
    )
    in_total, last_total = (
        lax.psum(in_shard, "ctx").astype(jnp.float32),
        lax.psum(last_shard, "ctx").astype(jnp.float32),
    )
    whole_sums = lax.psum(
        (gain_term, shift_term, qkv_bias_term, bias_term, up_bias_term), ("ctx", "fsdp")
    )

    def own_part(vector):
        piece_len = vector.shape[0] // shard_count
        return lax.dynamic_slice_in_dim(vector, shard_index * piece_len, piece_len)

    gain_total, shift_total, qkv_bias_total, bias_total, up_bias_total = [
        own_part(item) for item in whole_sums
    ]
    out_rows = model_width // shard_count
    qkv_columns = 3 * model_width
    return (
        from_slots(home_out)[None],
        from_slots(home_grad)[None],
        gain_total,
        shift_total,
        in_total[:, :qkv_columns],
        qkv_bias_total,
        last_total[:out_rows],
        bias_total,
        in_total[:, qkv_columns:],
        up_bias_total,
        last_total[out_rows:],
        bias_total,
    )


def solution(mesh):
    in_specs = (
        P("fsdp", "ctx", None),
        P(),
        P("fsdp", None),
        P("fsdp"),
        P("fsdp"),
        P("fsdp", None),
        P("fsdp"),
        P("fsdp", None),
        P("fsdp"),
        P("fsdp", None),
        P("fsdp"),
        P("fsdp", None),
        P("fsdp"),
        P("fsdp", "ctx", None),
    )
    out_specs = (
        P("fsdp", "ctx", None),
        P("fsdp", "ctx", None),
        P("fsdp"),
        P("fsdp"),
        P("fsdp", None),
        P("fsdp"),
        P("fsdp", None),
        P("fsdp"),
        P("fsdp", None),
        P("fsdp"),
        P("fsdp", None),
        P("fsdp"),
    )
    return jax.shard_map(shards, mesh=mesh, in_specs=in_specs, out_specs=out_specs, check_vma=False)
```

profile of v0, /device:TPU:0, one launch (start us, length us, event | category | flops | bytes accessed | tf_op | source)
XLA Modules:
  0.0 2713.1 jit_solution(3946526973941653070)
XLA Ops:
  12.1 6.3 all-to-all-start
  19.9 8.1 all-gather.1
  28.0 8.1 all-gather
  36.1 7.4 all_gather.37
  44.1 8.1 all-gather.2
  54.6 10.3 fusion.71
  72.4 24.3 all-to-all-done.2
  100.5 6.7 convolution_convert_fusion.2
  109.8 220.4 %all-gather.10.cloned.1.call-done = bf16[2048,6144]{1,0:T(8,128)(2,1)} async-done(((bf16[512,6144]{1,0:T(8,128)(2,1)}), bf16[2048,6144]{1,0:T(8,128)(2,1)}) %all-gather.10.cloned.1.call-update) | async-done | bytes 25165840 | tf_op jit(solution)/shard_map/all_gather | solution.py:132
  330.1 11.6 convolution_add_fusion.1
  365.8 5.3 bitcast_add_fusion.4
  371.1 258.3 %while.59 = (s32[]{:T(128)}, bf16[256,32,64]{0,2,1:T(8,128)(2,1)}, bf16[256,32,64]{0,2,1:T(8,128)(2,1)}, f32[32,256]{1,0:T(8,128)S(1)}, f32[32,256]{1,0:T(8,128)...) while((s32[]{:T(128)}, bf16[256,32,64]{0,2,1:T(8,128)(2,1)}, ...), condition=%wide.region_18.20_spmd, body=%wide.region_12.19_spmd.sunk | while | flops 565423104 | bytes 62683964 | solution.py:214
  376.6 10.7 fusion.175
  388.9 10.2 collective-permute-done
  411.7 10.7 fusion.175
  424.0 11.9 collective-permute-done
  448.6 10.8 fusion.175
  460.9 11.8 collective-permute-done
  485.4 10.7 fusion.175
  497.7 11.9 collective-permute-done
  522.3 10.7 fusion.175
  534.5 11.9 collective-permute-done
  559.1 10.7 fusion.175
  571.4 11.9 collective-permute-done
  596.0 10.7 fusion.175
  608.2 11.9 collective-permute-done
  634.3 23.0 fusion.103
  657.4 270.9 %all-gather.14.cloned.1.call-done = bf16[2048,8192]{1,0:T(8,128)(2,1)} async-done(((bf16[512,8192]{1,0:T(8,128)(2,1)}), bf16[2048,8192]{1,0:T(8,128)(2,1)}) %all-gather.14.cloned.1.call-update) | async-done | bytes 33554448 | tf_op jit(solution)/shard_map/all_gather | solution.py:136
  928.2 26.3 convert_reduce_fusion.2
  954.6 7.9 reshape.1092
  970.7 19.4 convolution_convert_fusion.1
  991.3 7.6 multiply_convert_fusion.1
  1003.5 6.6 fusion.61
  1010.1 480.2 %while.60 = (s32[]{:T(128)}, bf16[256,32,64]{0,2,1:T(8,128)(2,1)}, bf16[256,32,64]{0,2,1:T(8,128)(2,1)}, bf16[256,32,64]{0,2,1:T(8,128)(2,1)}, bf16[256,32,64]{0...) while((s32[]{:T(128)}, bf16[256,32,64]{0,2,1:T(8,128)(2,1)}, ...), condition=%wide.region_24.26_spmd, body=%wide.region_20.25_spmd.sunk | while | flops 1372277760 | bytes 95730528 | solution.py:279
  1014.7 10.1 fusion.192
  1025.0 35.1 %collective-permute-done.2 = bf16[256,32,64]{0,2,1:T(8,128)(2,1)S(1)} collective-permute-done((bf16[256,32,64]{0,2,1:T(8,128)(2,1)}, bf16[256,32,64]{0,2,1:T(8,128)(2,1)S(1)}, u32[]{:S(2)}, u32[]{:S(2)}) %collective-permute-start.2) | collective-permute-done | bytes 1048608 | tf_op jit(solution)/shard_map/while/body/eval_jaxpr/ppermute | solution.py:13
  1081.6 10.1 fusion.192
  1092.0 36.9 %collective-permute-done.2 = bf16[256,32,64]{0,2,1:T(8,128)(2,1)S(1)} collective-permute-done((bf16[256,32,64]{0,2,1:T(8,128)(2,1)}, bf16[256,32,64]{0,2,1:T(8,128)(2,1)S(1)}, u32[]{:S(2)}, u32[]{:S(2)}) %collective-permute-start.2) | collective-permute-done | bytes 1048608 | tf_op jit(solution)/shard_map/while/body/eval_jaxpr/ppermute | solution.py:13
  1149.0 10.1 fusion.192
  1159.4 38.2 %collective-permute-done.2 = bf16[256,32,64]{0,2,1:T(8,128)(2,1)S(1)} collective-permute-done((bf16[256,32,64]{0,2,1:T(8,128)(2,1)}, bf16[256,32,64]{0,2,1:T(8,128)(2,1)S(1)}, u32[]{:S(2)}, u32[]{:S(2)}) %collective-permute-start.2) | collective-permute-done | bytes 1048608 | tf_op jit(solution)/shard_map/while/body/eval_jaxpr/ppermute | solution.py:13
  1217.6 10.1 fusion.192
  1227.9 38.2 %collective-permute-done.2 = bf16[256,32,64]{0,2,1:T(8,128)(2,1)S(1)} collective-permute-done((bf16[256,32,64]{0,2,1:T(8,128)(2,1)}, bf16[256,32,64]{0,2,1:T(8,128)(2,1)S(1)}, u32[]{:S(2)}, u32[]{:S(2)}) %collective-permute-start.2) | collective-permute-done | bytes 1048608 | tf_op jit(solution)/shard_map/while/body/eval_jaxpr/ppermute | solution.py:13
  1286.2 10.1 fusion.192
  1296.6 38.2 %collective-permute-done.2 = bf16[256,32,64]{0,2,1:T(8,128)(2,1)S(1)} collective-permute-done((bf16[256,32,64]{0,2,1:T(8,128)(2,1)}, bf16[256,32,64]{0,2,1:T(8,128)(2,1)S(1)}, u32[]{:S(2)}, u32[]{:S(2)}) %collective-permute-start.2) | collective-permute-done | bytes 1048608 | tf_op jit(solution)/shard_map/while/body/eval_jaxpr/ppermute | solution.py:13
  1354.8 10.1 fusion.192
  1365.1 38.2 %collective-permute-done.2 = bf16[256,32,64]{0,2,1:T(8,128)(2,1)S(1)} collective-permute-done((bf16[256,32,64]{0,2,1:T(8,128)(2,1)}, bf16[256,32,64]{0,2,1:T(8,128)(2,1)S(1)}, u32[]{:S(2)}, u32[]{:S(2)}) %collective-permute-start.2) | collective-permute-done | bytes 1048608 | tf_op jit(solution)/shard_map/while/body/eval_jaxpr/ppermute | solution.py:13
  1423.3 10.1 fusion.192
  1433.6 38.2 %collective-permute-done.2 = bf16[256,32,64]{0,2,1:T(8,128)(2,1)S(1)} collective-permute-done((bf16[256,32,64]{0,2,1:T(8,128)(2,1)}, bf16[256,32,64]{0,2,1:T(8,128)(2,1)S(1)}, u32[]{:S(2)}, u32[]{:S(2)}) %collective-permute-start.2) | collective-permute-done | bytes 1048608 | tf_op jit(solution)/shard_map/while/body/eval_jaxpr/ppermute | solution.py:13
  1492.9 13.7 collective-permute-done.6
  1512.2 5.8 collective-permute-done.7
  1520.3 30.3 %convolution_convert_fusion = bf16[2048,14336]{1,0:T(8,128)(2,1)} fusion(bf16[256,2048]{1,0:T(8,128)(2,1)S(1)} %copy-done.18, bf16[256,8192]{1,0:T(8,128)(2,1)} %get-tuple-element.1325, bf16[256,2048]{1,0:T(8,128)(2,1)} %copy.94, bf16[256,2048]{1,0:T(8,128)(2,1)} %copy.93, bf16[256,2048]{1,0:T(8,128)(2,1)} %copy.92), kind=kOutput, calls=%fused_computation.93 | convolution fusion | flops 15091105792 | bytes 67108864 | tf_op jit(solution)/shard_map/dot_general | solution.py:83
  1555.2 17.6 fusion.104
  1572.8 15.0 multiply_reduce_fusion
  1588.0 451.8 %reduce-scatter.5.cloned.1.call-done = bf16[512,14336]{1,0:T(8,128)(2,1)} async-done(((bf16[2048,14336]{1,0:T(8,128)(2,1)}), bf16[512,14336]{1,0:T(8,128)(2,1)}) %reduce-scatter.5.cloned.1.call-update) | async-done | bytes 14680080 | tf_op jit(solution)/shard_map/reduce_scatter | solution.py:318
  2040.5 7.9 all-gather.4
  2048.4 7.5 all-gather.3
  2055.9 5.9 fusion.56
  2061.8 16.6 fusion.57
  2086.6 23.9 all-to-all-done.1
  2114.8 58.6 %all-reduce.6.cloned.1.call-done = (f32[2048]{0:T(1024)}, f32[2048]{0:T(1024)}, f32[6144]{0:T(1024)}, f32[2048]{0:T(1024)}, f32[8192]{0:T(1024)}) async-done(((f32[2048]{0:T(1024)}, f32[2048]{0:T(1024)}, f32[6144]{0:T(1024)}, f32[2048]{0:T(1024)}, f32[8192]{0:T(1024)}), (f32[2048]{0:T(1024)}, f32[2048]{0:T(1024)}, f32[6144]{0:T(1024)}, f32[2048]{0:T(1024)}, f32[8192]{0:T(1024)})) %all-reduce.6.cloned.1.call-update) | async-done | bytes 81936 | tf_op jit(solution)/shard_map/psum | solution.py:334
  2182.6 486.0 %all-reduce.8.cloned.1.call-done = (bf16[512,14336]{1,0:T(8,128)(2,1)}, bf16[2560,2048]{1,0:T(8,128)(2,1)}) async-done(((bf16[512,14336]{1,0:T(8,128)(2,1)}, bf16[2560,2048]{1,0:T(8,128)(2,1)}), (bf16[512,14336]{1,0:T(8,128)(2,1)}, bf16[2560,2048]{1,0:T(8,128)(2,1)})) %all-reduce.8.cloned.1.call-update) | async-done | bytes 25165840 | tf_op jit(solution)/shard_map/psum | solution.py:331
  2672.8 11.7 slice.322
  2684.4 9.2 slice.319
  2693.6 11.8 slice.321
  (685 shorter events, 354.5 us)
Async XLA Ops:
  7.2 93.3 %all-gather.12.cloned.1.call-start = ((), (), s32[]{:S(2)}) async-start(), calls=%async_computation.7 | async-start | bytes 10485760 | tf_op jit(solution)/shard_map/all_gather | solution.py:134
  7.9 322.2 %all-gather.10.cloned.1.call-start = ((), (), s32[]{:S(2)}) async-start(), calls=%async_computation.6 | async-start | bytes 31457280 | tf_op jit(solution)/shard_map/all_gather | solution.py:132
  8.7 625.6 %all-gather.16.cloned.1.call-start = ((), (), s32[]{:S(2)}) async-start(), calls=%async_computation.9 | async-start | bytes 41943040 | tf_op jit(solution)/shard_map/all_gather | solution.py:138
  9.5 42.8 %copy-start.34 = (bf16[1,256,2048]{2,1,0:T(8,128)(2,1)S(1)}, bf16[1,256,2048]{2,1,0:T(8,128)(2,1)}, u32[]{:S(2)}) copy-start(bf16[1,256,2048]{2,1,0:T(8,128)(2,1)} %param.43) | copy-start | bytes 3145732
  9.5 918.8 %all-gather.14.cloned.1.call-start = ((), (), s32[]{:S(2)}) async-start(), calls=%async_computation.8 | async-start | bytes 41943040 | tf_op jit(solution)/shard_map/all_gather | solution.py:136
  10.1 44.5 %copy-start.41 = (s32[2,128]{1,0:T(2,128)S(1)}, s32[2,128]{1,0:T(2,128)}, u32[]{:S(2)}) copy-start(s32[2,128]{1,0:T(2,128)} %constant.750.clone.1) | copy-start | bytes 3076
  12.1 52.9 %all-to-all-start = ((bf16[8,32,2048]{2,1,0:T(8,128)(2,1)}), bf16[8,32,2048]{2,1,0:T(8,128)(2,1)S(1)}, u32[]{:S(2)}, u32[]{:S(2)}) async-start(bf16[8,32,2048]{2,1,0:T(8,128)(2,1)} %bitcast.48), calls=%async_computation | async-start | bytes 2097152 | tf_op jit(solution)/shard_map/all_to_all | solution.py:120
  36.1 71.2 %copy-start.44 = (f32[4,1,512]{2,1,0:T(1,128)}, f32[4,1,512]{2,1,0:T(1,128)S(1)}, u32[]{:S(2)}) copy-start(f32[4,1,512]{2,1,0:T(1,128)S(1)} %convert_element_type.336) | copy-start | bytes 24580
  65.1 42.2 %copy-start.5 = (bf16[8,32,2048]{2,1,0:T(8,128)(2,1)}, bf16[8,32,2048]{2,1,0:T(8,128)(2,1)S(1)}, u32[]{:S(2)}) copy-start(bf16[8,32,2048]{2,1,0:T(8,128)(2,1)S(1)} %all-to-all-done) | copy-start | bytes 3145732
  65.1 31.7 %all-to-all-start.2 = ((bf16[8,32,2048]{2,1,0:T(8,128)(2,1)}), bf16[8,32,2048]{2,1,0:T(8,128)(2,1)S(1)}, u32[]{:S(2)}, u32[]{:S(2)}) async-start(bf16[8,32,2048]{2,1,0:T(8,128)(2,1)} %bitcast.90), calls=%async_computation.2 | async-start | bytes 2097152 | tf_op jit(solution)/shard_map/all_to_all | solution.py:121
  70.2 1517.8 %reduce-scatter.7.cloned.1.call-start = ((), (), s32[]{:S(2)}) async-start(), calls=%async_computation.11 | async-start | bytes 52428800
  71.0 285.7 %copy-start.39 = (f32[256,16]{0,1:T(8,128)}, f32[256,16]{0,1:T(8,128)S(1)}, u32[]{:S(2)}) copy-start(f32[256,16]{0,1:T(8,128)S(1)} %get-tuple-element.1383) | copy-start | bytes 49156
  72.4 257.7 %copy-start.17 = (bf16[256,2048]{1,0:T(8,128)(2,1)}, bf16[256,2048]{1,0:T(8,128)(2,1)S(1)}, u32[]{:S(2)}) copy-start(bf16[256,2048]{1,0:T(8,128)(2,1)S(1)} %add_convert_fusion.1) | copy-start | bytes 3145732
  371.5 32.1 %collective-permute-start.1 = (bf16[256,32,64]{0,2,1:T(8,128)(2,1)}, bf16[256,32,64]{0,2,1:T(8,128)(2,1)S(1)}, u32[]{:S(2)}, u32[]{:S(2)}) collective-permute-start(bf16[256,32,64]{0,2,1:T(8,128)(2,1)} %get-tuple-element.1681), channel_id=1, source_target_pairs={{0,4},{4,8},{8,12},{12,16},{16,20},{20,24},{24,28},{28,0},{1,5},{5... | collective-permute-start | bytes 3145736 | tf_op jit(solution)/shard_map/while/body/eval_jaxpr/ppermute | solution.py:13
  371.7 27.4 %collective-permute-start = (bf16[256,32,64]{0,2,1:T(8,128)(2,1)}, bf16[256,32,64]{0,2,1:T(8,128)(2,1)S(1)}, u32[]{:S(2)}, u32[]{:S(2)}) collective-permute-start(bf16[256,32,64]{0,2,1:T(8,128)(2,1)} %get-tuple-element.1680), channel_id=1, source_target_pairs={{0,4},{4,8},{8,12},{12,16},{16,20},{20,24},{24,28},{28,0},{1,5},{5... | collective-permute-start | bytes 3145736 | tf_op jit(solution)/shard_map/while/body/eval_jaxpr/ppermute | solution.py:13
  408.4 32.1 %collective-permute-start.1 = (bf16[256,32,64]{0,2,1:T(8,128)(2,1)}, bf16[256,32,64]{0,2,1:T(8,128)(2,1)S(1)}, u32[]{:S(2)}, u32[]{:S(2)}) collective-permute-start(bf16[256,32,64]{0,2,1:T(8,128)(2,1)} %get-tuple-element.1681), channel_id=1, source_target_pairs={{0,4},{4,8},{8,12},{12,16},{16,20},{20,24},{24,28},{28,0},{1,5},{5... | collective-permute-start | bytes 3145736 | tf_op jit(solution)/shard_map/while/body/eval_jaxpr/ppermute | solution.py:13
  408.4 27.5 %collective-permute-start = (bf16[256,32,64]{0,2,1:T(8,128)(2,1)}, bf16[256,32,64]{0,2,1:T(8,128)(2,1)S(1)}, u32[]{:S(2)}, u32[]{:S(2)}) collective-permute-start(bf16[256,32,64]{0,2,1:T(8,128)(2,1)} %get-tuple-element.1680), channel_id=1, source_target_pairs={{0,4},{4,8},{8,12},{12,16},{16,20},{20,24},{24,28},{28,0},{1,5},{5... | collective-permute-start | bytes 3145736 | tf_op jit(solution)/shard_map/while/body/eval_jaxpr/ppermute | solution.py:13
  445.2 32.1 %collective-permute-start.1 = (bf16[256,32,64]{0,2,1:T(8,128)(2,1)}, bf16[256,32,64]{0,2,1:T(8,128)(2,1)S(1)}, u32[]{:S(2)}, u32[]{:S(2)}) collective-permute-start(bf16[256,32,64]{0,2,1:T(8,128)(2,1)} %get-tuple-element.1681), channel_id=1, source_target_pairs={{0,4},{4,8},{8,12},{12,16},{16,20},{20,24},{24,28},{28,0},{1,5},{5... | collective-permute-start | bytes 3145736 | tf_op jit(solution)/shard_map/while/body/eval_jaxpr/ppermute | solution.py:13
  445.3 27.5 %collective-permute-start = (bf16[256,32,64]{0,2,1:T(8,128)(2,1)}, bf16[256,32,64]{0,2,1:T(8,128)(2,1)S(1)}, u32[]{:S(2)}, u32[]{:S(2)}) collective-permute-start(bf16[256,32,64]{0,2,1:T(8,128)(2,1)} %get-tuple-element.1680), channel_id=1, source_target_pairs={{0,4},{4,8},{8,12},{12,16},{16,20},{20,24},{24,28},{28,0},{1,5},{5... | collective-permute-start | bytes 3145736 | tf_op jit(solution)/shard_map/while/body/eval_jaxpr/ppermute | solution.py:13
  482.1 32.1 %collective-permute-start.1 = (bf16[256,32,64]{0,2,1:T(8,128)(2,1)}, bf16[256,32,64]{0,2,1:T(8,128)(2,1)S(1)}, u32[]{:S(2)}, u32[]{:S(2)}) collective-permute-start(bf16[256,32,64]{0,2,1:T(8,128)(2,1)} %get-tuple-element.1681), channel_id=1, source_target_pairs={{0,4},{4,8},{8,12},{12,16},{16,20},{20,24},{24,28},{28,0},{1,5},{5... | collective-permute-start | bytes 3145736 | tf_op jit(solution)/shard_map/while/body/eval_jaxpr/ppermute | solution.py:13
  482.1 27.5 %collective-permute-start = (bf16[256,32,64]{0,2,1:T(8,128)(2,1)}, bf16[256,32,64]{0,2,1:T(8,128)(2,1)S(1)}, u32[]{:S(2)}, u32[]{:S(2)}) collective-permute-start(bf16[256,32,64]{0,2,1:T(8,128)(2,1)} %get-tuple-element.1680), channel_id=1, source_target_pairs={{0,4},{4,8},{8,12},{12,16},{16,20},{20,24},{24,28},{28,0},{1,5},{5... | collective-permute-start | bytes 3145736 | tf_op jit(solution)/shard_map/while/body/eval_jaxpr/ppermute | solution.py:13
  518.9 32.1 %collective-permute-start.1 = (bf16[256,32,64]{0,2,1:T(8,128)(2,1)}, bf16[256,32,64]{0,2,1:T(8,128)(2,1)S(1)}, u32[]{:S(2)}, u32[]{:S(2)}) collective-permute-start(bf16[256,32,64]{0,2,1:T(8,128)(2,1)} %get-tuple-element.1681), channel_id=1, source_target_pairs={{0,4},{4,8},{8,12},{12,16},{16,20},{20,24},{24,28},{28,0},{1,5},{5... | collective-permute-start | bytes 3145736 | tf_op jit(solution)/shard_map/while/body/eval_jaxpr/ppermute | solution.py:13
  519.0 27.5 %collective-permute-start = (bf16[256,32,64]{0,2,1:T(8,128)(2,1)}, bf16[256,32,64]{0,2,1:T(8,128)(2,1)S(1)}, u32[]{:S(2)}, u32[]{:S(2)}) collective-permute-start(bf16[256,32,64]{0,2,1:T(8,128)(2,1)} %get-tuple-element.1680), channel_id=1, source_target_pairs={{0,4},{4,8},{8,12},{12,16},{16,20},{20,24},{24,28},{28,0},{1,5},{5... | collective-permute-start | bytes 3145736 | tf_op jit(solution)/shard_map/while/body/eval_jaxpr/ppermute | solution.py:13
  555.8 32.1 %collective-permute-start.1 = (bf16[256,32,64]{0,2,1:T(8,128)(2,1)}, bf16[256,32,64]{0,2,1:T(8,128)(2,1)S(1)}, u32[]{:S(2)}, u32[]{:S(2)}) collective-permute-start(bf16[256,32,64]{0,2,1:T(8,128)(2,1)} %get-tuple-element.1681), channel_id=1, source_target_pairs={{0,4},{4,8},{8,12},{12,16},{16,20},{20,24},{24,28},{28,0},{1,5},{5... | collective-permute-start | bytes 3145736 | tf_op jit(solution)/shard_map/while/body/eval_jaxpr/ppermute | solution.py:13
  555.8 27.5 %collective-permute-start = (bf16[256,32,64]{0,2,1:T(8,128)(2,1)}, bf16[256,32,64]{0,2,1:T(8,128)(2,1)S(1)}, u32[]{:S(2)}, u32[]{:S(2)}) collective-permute-start(bf16[256,32,64]{0,2,1:T(8,128)(2,1)} %get-tuple-element.1680), channel_id=1, source_target_pairs={{0,4},{4,8},{8,12},{12,16},{16,20},{20,24},{24,28},{28,0},{1,5},{5... | collective-permute-start | bytes 3145736 | tf_op jit(solution)/shard_map/while/body/eval_jaxpr/ppermute | solution.py:13
  592.6 32.1 %collective-permute-start.1 = (bf16[256,32,64]{0,2,1:T(8,128)(2,1)}, bf16[256,32,64]{0,2,1:T(8,128)(2,1)S(1)}, u32[]{:S(2)}, u32[]{:S(2)}) collective-permute-start(bf16[256,32,64]{0,2,1:T(8,128)(2,1)} %get-tuple-element.1681), channel_id=1, source_target_pairs={{0,4},{4,8},{8,12},{12,16},{16,20},{20,24},{24,28},{28,0},{1,5},{5... | collective-permute-start | bytes 3145736 | tf_op jit(solution)/shard_map/while/body/eval_jaxpr/ppermute | solution.py:13
  592.7 27.5 %collective-permute-start = (bf16[256,32,64]{0,2,1:T(8,128)(2,1)}, bf16[256,32,64]{0,2,1:T(8,128)(2,1)S(1)}, u32[]{:S(2)}, u32[]{:S(2)}) collective-permute-start(bf16[256,32,64]{0,2,1:T(8,128)(2,1)} %get-tuple-element.1680), channel_id=1, source_target_pairs={{0,4},{4,8},{8,12},{12,16},{16,20},{20,24},{24,28},{28,0},{1,5},{5... | collective-permute-start | bytes 3145736 | tf_op jit(solution)/shard_map/while/body/eval_jaxpr/ppermute | solution.py:13
  990.1 1049.7 %reduce-scatter.5.cloned.1.call-start = ((), (), s32[]{:S(2)}) async-start(), calls=%async_computation.10 | async-start | bytes 73400320 | tf_op jit(solution)/shard_map/reduce_scatter | solution.py:318
  1010.2 51.3 %collective-permute-start.5 = (bf16[256,32,64]{0,2,1:T(8,128)(2,1)}, bf16[256,32,64]{0,2,1:T(8,128)(2,1)}, u32[]{:S(2)}, u32[]{:S(2)}) collective-permute-start(bf16[256,32,64]{0,2,1:T(8,128)(2,1)} %get-tuple-element.1740), channel_id=1, source_target_pairs={{0,4},{4,8},{8,12},{12,16},{16,20},{20,24},{24,28},{28,0},{1,5},{5... | collective-permute-start | bytes 3145736 | tf_op jit(solution)/shard_map/while/body/eval_jaxpr/ppermute | solution.py:13
  1010.2 64.1 %collective-permute-start.4 = (bf16[256,32,64]{0,2,1:T(8,128)(2,1)}, bf16[256,32,64]{0,2,1:T(8,128)(2,1)S(1)}, u32[]{:S(2)}, u32[]{:S(2)}) collective-permute-start(bf16[256,32,64]{0,2,1:T(8,128)(2,1)} %get-tuple-element.1739), channel_id=1, source_target_pairs={{0,4},{4,8},{8,12},{12,16},{16,20},{20,24},{24,28},{28,0},{1,5},{5... | collective-permute-start | bytes 3145736 | tf_op jit(solution)/shard_map/while/body/eval_jaxpr/ppermute | solution.py:13
  1011.8 55.0 %collective-permute-start.3 = (bf16[256,32,64]{0,2,1:T(8,128)(2,1)}, bf16[256,32,64]{0,2,1:T(8,128)(2,1)}, u32[]{:S(2)}, u32[]{:S(2)}) collective-permute-start(bf16[256,32,64]{0,2,1:T(8,128)(2,1)} %get-tuple-element.1738), channel_id=1, source_target_pairs={{0,4},{4,8},{8,12},{12,16},{16,20},{20,24},{24,28},{28,0},{1,5},{5... | collective-permute-start | bytes 3145736 | tf_op jit(solution)/shard_map/while/body/eval_jaxpr/ppermute | solution.py:13
  1011.9 48.3 %collective-permute-start.2 = (bf16[256,32,64]{0,2,1:T(8,128)(2,1)}, bf16[256,32,64]{0,2,1:T(8,128)(2,1)S(1)}, u32[]{:S(2)}, u32[]{:S(2)}) collective-permute-start(bf16[256,32,64]{0,2,1:T(8,128)(2,1)} %get-tuple-element.1737), channel_id=1, source_target_pairs={{0,4},{4,8},{8,12},{12,16},{16,20},{20,24},{24,28},{28,0},{1,5},{5... | collective-permute-start | bytes 3145736 | tf_op jit(solution)/shard_map/while/body/eval_jaxpr/ppermute | solution.py:13
  1078.9 51.2 %collective-permute-start.5 = (bf16[256,32,64]{0,2,1:T(8,128)(2,1)}, bf16[256,32,64]{0,2,1:T(8,128)(2,1)}, u32[]{:S(2)}, u32[]{:S(2)}) collective-permute-start(bf16[256,32,64]{0,2,1:T(8,128)(2,1)} %get-tuple-element.1740), channel_id=1, source_target_pairs={{0,4},{4,8},{8,12},{12,16},{16,20},{20,24},{24,28},{28,0},{1,5},{5... | collective-permute-start | bytes 3145736 | tf_op jit(solution)/shard_map/while/body/eval_jaxpr/ppermute | solution.py:13
  1078.9 64.1 %collective-permute-start.4 = (bf16[256,32,64]{0,2,1:T(8,128)(2,1)}, bf16[256,32,64]{0,2,1:T(8,128)(2,1)S(1)}, u32[]{:S(2)}, u32[]{:S(2)}) collective-permute-start(bf16[256,32,64]{0,2,1:T(8,128)(2,1)} %get-tuple-element.1739), channel_id=1, source_target_pairs={{0,4},{4,8},{8,12},{12,16},{16,20},{20,24},{24,28},{28,0},{1,5},{5... | collective-permute-start | bytes 3145736 | tf_op jit(solution)/shard_map/while/body/eval_jaxpr/ppermute | solution.py:13
  1078.9 56.8 %collective-permute-start.3 = (bf16[256,32,64]{0,2,1:T(8,128)(2,1)}, bf16[256,32,64]{0,2,1:T(8,128)(2,1)}, u32[]{:S(2)}, u32[]{:S(2)}) collective-permute-start(bf16[256,32,64]{0,2,1:T(8,128)(2,1)} %get-tuple-element.1738), channel_id=1, source_target_pairs={{0,4},{4,8},{8,12},{12,16},{16,20},{20,24},{24,28},{28,0},{1,5},{5... | collective-permute-start | bytes 3145736 | tf_op jit(solution)/shard_map/while/body/eval_jaxpr/ppermute | solution.py:13
  1079.0 49.9 %collective-permute-start.2 = (bf16[256,32,64]{0,2,1:T(8,128)(2,1)}, bf16[256,32,64]{0,2,1:T(8,128)(2,1)S(1)}, u32[]{:S(2)}, u32[]{:S(2)}) collective-permute-start(bf16[256,32,64]{0,2,1:T(8,128)(2,1)} %get-tuple-element.1737), channel_id=1, source_target_pairs={{0,4},{4,8},{8,12},{12,16},{16,20},{20,24},{24,28},{28,0},{1,5},{5... | collective-permute-start | bytes 3145736 | tf_op jit(solution)/shard_map/while/body/eval_jaxpr/ppermute | solution.py:13
  1147.6 51.2 %collective-permute-start.5 = (bf16[256,32,64]{0,2,1:T(8,128)(2,1)}, bf16[256,32,64]{0,2,1:T(8,128)(2,1)}, u32[]{:S(2)}, u32[]{:S(2)}) collective-permute-start(bf16[256,32,64]{0,2,1:T(8,128)(2,1)} %get-tuple-element.1740), channel_id=1, source_target_pairs={{0,4},{4,8},{8,12},{12,16},{16,20},{20,24},{24,28},{28,0},{1,5},{5... | collective-permute-start | bytes 3145736 | tf_op jit(solution)/shard_map/while/body/eval_jaxpr/ppermute | solution.py:13
  1147.6 64.0 %collective-permute-start.4 = (bf16[256,32,64]{0,2,1:T(8,128)(2,1)}, bf16[256,32,64]{0,2,1:T(8,128)(2,1)S(1)}, u32[]{:S(2)}, u32[]{:S(2)}) collective-permute-start(bf16[256,32,64]{0,2,1:T(8,128)(2,1)} %get-tuple-element.1739), channel_id=1, source_target_pairs={{0,4},{4,8},{8,12},{12,16},{16,20},{20,24},{24,28},{28,0},{1,5},{5... | collective-permute-start | bytes 3145736 | tf_op jit(solution)/shard_map/while/body/eval_jaxpr/ppermute | solution.py:13
  1147.6 56.6 %collective-permute-start.3 = (bf16[256,32,64]{0,2,1:T(8,128)(2,1)}, bf16[256,32,64]{0,2,1:T(8,128)(2,1)}, u32[]{:S(2)}, u32[]{:S(2)}) collective-permute-start(bf16[256,32,64]{0,2,1:T(8,128)(2,1)} %get-tuple-element.1738), channel_id=1, source_target_pairs={{0,4},{4,8},{8,12},{12,16},{16,20},{20,24},{24,28},{28,0},{1,5},{5... | collective-permute-start | bytes 3145736 | tf_op jit(solution)/shard_map/while/body/eval_jaxpr/ppermute | solution.py:13
  1147.6 49.9 %collective-permute-start.2 = (bf16[256,32,64]{0,2,1:T(8,128)(2,1)}, bf16[256,32,64]{0,2,1:T(8,128)(2,1)S(1)}, u32[]{:S(2)}, u32[]{:S(2)}) collective-permute-start(bf16[256,32,64]{0,2,1:T(8,128)(2,1)} %get-tuple-element.1737), channel_id=1, source_target_pairs={{0,4},{4,8},{8,12},{12,16},{16,20},{20,24},{24,28},{28,0},{1,5},{5... | collective-permute-start | bytes 3145736 | tf_op jit(solution)/shard_map/while/body/eval_jaxpr/ppermute | solution.py:13
  1216.2 51.2 %collective-permute-start.5 = (bf16[256,32,64]{0,2,1:T(8,128)(2,1)}, bf16[256,32,64]{0,2,1:T(8,128)(2,1)}, u32[]{:S(2)}, u32[]{:S(2)}) collective-permute-start(bf16[256,32,64]{0,2,1:T(8,128)(2,1)} %get-tuple-element.1740), channel_id=1, source_target_pairs={{0,4},{4,8},{8,12},{12,16},{16,20},{20,24},{24,28},{28,0},{1,5},{5... | collective-permute-start | bytes 3145736 | tf_op jit(solution)/shard_map/while/body/eval_jaxpr/ppermute | solution.py:13
  1216.2 64.1 %collective-permute-start.4 = (bf16[256,32,64]{0,2,1:T(8,128)(2,1)}, bf16[256,32,64]{0,2,1:T(8,128)(2,1)S(1)}, u32[]{:S(2)}, u32[]{:S(2)}) collective-permute-start(bf16[256,32,64]{0,2,1:T(8,128)(2,1)} %get-tuple-element.1739), channel_id=1, source_target_pairs={{0,4},{4,8},{8,12},{12,16},{16,20},{20,24},{24,28},{28,0},{1,5},{5... | collective-permute-start | bytes 3145736 | tf_op jit(solution)/shard_map/while/body/eval_jaxpr/ppermute | solution.py:13
  1216.2 56.6 %collective-permute-start.3 = (bf16[256,32,64]{0,2,1:T(8,128)(2,1)}, bf16[256,32,64]{0,2,1:T(8,128)(2,1)}, u32[]{:S(2)}, u32[]{:S(2)}) collective-permute-start(bf16[256,32,64]{0,2,1:T(8,128)(2,1)} %get-tuple-element.1738), channel_id=1, source_target_pairs={{0,4},{4,8},{8,12},{12,16},{16,20},{20,24},{24,28},{28,0},{1,5},{5... | collective-permute-start | bytes 3145736 | tf_op jit(solution)/shard_map/while/body/eval_jaxpr/ppermute | solution.py:13
  1216.2 49.9 %collective-permute-start.2 = (bf16[256,32,64]{0,2,1:T(8,128)(2,1)}, bf16[256,32,64]{0,2,1:T(8,128)(2,1)S(1)}, u32[]{:S(2)}, u32[]{:S(2)}) collective-permute-start(bf16[256,32,64]{0,2,1:T(8,128)(2,1)} %get-tuple-element.1737), channel_id=1, source_target_pairs={{0,4},{4,8},{8,12},{12,16},{16,20},{20,24},{24,28},{28,0},{1,5},{5... | collective-permute-start | bytes 3145736 | tf_op jit(solution)/shard_map/while/body/eval_jaxpr/ppermute | solution.py:13
  1284.8 51.2 %collective-permute-start.5 = (bf16[256,32,64]{0,2,1:T(8,128)(2,1)}, bf16[256,32,64]{0,2,1:T(8,128)(2,1)}, u32[]{:S(2)}, u32[]{:S(2)}) collective-permute-start(bf16[256,32,64]{0,2,1:T(8,128)(2,1)} %get-tuple-element.1740), channel_id=1, source_target_pairs={{0,4},{4,8},{8,12},{12,16},{16,20},{20,24},{24,28},{28,0},{1,5},{5... | collective-permute-start | bytes 3145736 | tf_op jit(solution)/shard_map/while/body/eval_jaxpr/ppermute | solution.py:13
  1284.8 64.0 %collective-permute-start.4 = (bf16[256,32,64]{0,2,1:T(8,128)(2,1)}, bf16[256,32,64]{0,2,1:T(8,128)(2,1)S(1)}, u32[]{:S(2)}, u32[]{:S(2)}) collective-permute-start(bf16[256,32,64]{0,2,1:T(8,128)(2,1)} %get-tuple-element.1739), channel_id=1, source_target_pairs={{0,4},{4,8},{8,12},{12,16},{16,20},{20,24},{24,28},{28,0},{1,5},{5... | collective-permute-start | bytes 3145736 | tf_op jit(solution)/shard_map/while/body/eval_jaxpr/ppermute | solution.py:13
  1284.8 56.6 %collective-permute-start.3 = (bf16[256,32,64]{0,2,1:T(8,128)(2,1)}, bf16[256,32,64]{0,2,1:T(8,128)(2,1)}, u32[]{:S(2)}, u32[]{:S(2)}) collective-permute-start(bf16[256,32,64]{0,2,1:T(8,128)(2,1)} %get-tuple-element.1738), channel_id=1, source_target_pairs={{0,4},{4,8},{8,12},{12,16},{16,20},{20,24},{24,28},{28,0},{1,5},{5... | collective-permute-start | bytes 3145736 | tf_op jit(solution)/shard_map/while/body/eval_jaxpr/ppermute | solution.py:13
  1284.9 49.9 %collective-permute-start.2 = (bf16[256,32,64]{0,2,1:T(8,128)(2,1)}, bf16[256,32,64]{0,2,1:T(8,128)(2,1)S(1)}, u32[]{:S(2)}, u32[]{:S(2)}) collective-permute-start(bf16[256,32,64]{0,2,1:T(8,128)(2,1)} %get-tuple-element.1737), channel_id=1, source_target_pairs={{0,4},{4,8},{8,12},{12,16},{16,20},{20,24},{24,28},{28,0},{1,5},{5... | collective-permute-start | bytes 3145736 | tf_op jit(solution)/shard_map/while/body/eval_jaxpr/ppermute | solution.py:13
  1353.3 51.2 %collective-permute-start.5 = (bf16[256,32,64]{0,2,1:T(8,128)(2,1)}, bf16[256,32,64]{0,2,1:T(8,128)(2,1)}, u32[]{:S(2)}, u32[]{:S(2)}) collective-permute-start(bf16[256,32,64]{0,2,1:T(8,128)(2,1)} %get-tuple-element.1740), channel_id=1, source_target_pairs={{0,4},{4,8},{8,12},{12,16},{16,20},{20,24},{24,28},{28,0},{1,5},{5... | collective-permute-start | bytes 3145736 | tf_op jit(solution)/shard_map/while/body/eval_jaxpr/ppermute | solution.py:13
  1353.3 64.0 %collective-permute-start.4 = (bf16[256,32,64]{0,2,1:T(8,128)(2,1)}, bf16[256,32,64]{0,2,1:T(8,128)(2,1)S(1)}, u32[]{:S(2)}, u32[]{:S(2)}) collective-permute-start(bf16[256,32,64]{0,2,1:T(8,128)(2,1)} %get-tuple-element.1739), channel_id=1, source_target_pairs={{0,4},{4,8},{8,12},{12,16},{16,20},{20,24},{24,28},{28,0},{1,5},{5... | collective-permute-start | bytes 3145736 | tf_op jit(solution)/shard_map/while/body/eval_jaxpr/ppermute | solution.py:13
  1353.3 56.6 %collective-permute-start.3 = (bf16[256,32,64]{0,2,1:T(8,128)(2,1)}, bf16[256,32,64]{0,2,1:T(8,128)(2,1)}, u32[]{:S(2)}, u32[]{:S(2)}) collective-permute-start(bf16[256,32,64]{0,2,1:T(8,128)(2,1)} %get-tuple-element.1738), channel_id=1, source_target_pairs={{0,4},{4,8},{8,12},{12,16},{16,20},{20,24},{24,28},{28,0},{1,5},{5... | collective-permute-start | bytes 3145736 | tf_op jit(solution)/shard_map/while/body/eval_jaxpr/ppermute | solution.py:13
  1353.4 49.9 %collective-permute-start.2 = (bf16[256,32,64]{0,2,1:T(8,128)(2,1)}, bf16[256,32,64]{0,2,1:T(8,128)(2,1)S(1)}, u32[]{:S(2)}, u32[]{:S(2)}) collective-permute-start(bf16[256,32,64]{0,2,1:T(8,128)(2,1)} %get-tuple-element.1737), channel_id=1, source_target_pairs={{0,4},{4,8},{8,12},{12,16},{16,20},{20,24},{24,28},{28,0},{1,5},{5... | collective-permute-start | bytes 3145736 | tf_op jit(solution)/shard_map/while/body/eval_jaxpr/ppermute | solution.py:13
  1421.8 51.2 %collective-permute-start.5 = (bf16[256,32,64]{0,2,1:T(8,128)(2,1)}, bf16[256,32,64]{0,2,1:T(8,128)(2,1)}, u32[]{:S(2)}, u32[]{:S(2)}) collective-permute-start(bf16[256,32,64]{0,2,1:T(8,128)(2,1)} %get-tuple-element.1740), channel_id=1, source_target_pairs={{0,4},{4,8},{8,12},{12,16},{16,20},{20,24},{24,28},{28,0},{1,5},{5... | collective-permute-start | bytes 3145736 | tf_op jit(solution)/shard_map/while/body/eval_jaxpr/ppermute | solution.py:13
  1421.8 64.0 %collective-permute-start.4 = (bf16[256,32,64]{0,2,1:T(8,128)(2,1)}, bf16[256,32,64]{0,2,1:T(8,128)(2,1)S(1)}, u32[]{:S(2)}, u32[]{:S(2)}) collective-permute-start(bf16[256,32,64]{0,2,1:T(8,128)(2,1)} %get-tuple-element.1739), channel_id=1, source_target_pairs={{0,4},{4,8},{8,12},{12,16},{16,20},{20,24},{24,28},{28,0},{1,5},{5... | collective-permute-start | bytes 3145736 | tf_op jit(solution)/shard_map/while/body/eval_jaxpr/ppermute | solution.py:13
  1421.8 56.6 %collective-permute-start.3 = (bf16[256,32,64]{0,2,1:T(8,128)(2,1)}, bf16[256,32,64]{0,2,1:T(8,128)(2,1)}, u32[]{:S(2)}, u32[]{:S(2)}) collective-permute-start(bf16[256,32,64]{0,2,1:T(8,128)(2,1)} %get-tuple-element.1738), channel_id=1, source_target_pairs={{0,4},{4,8},{8,12},{12,16},{16,20},{20,24},{24,28},{28,0},{1,5},{5... | collective-permute-start | bytes 3145736 | tf_op jit(solution)/shard_map/while/body/eval_jaxpr/ppermute | solution.py:13
  1421.9 49.9 %collective-permute-start.2 = (bf16[256,32,64]{0,2,1:T(8,128)(2,1)}, bf16[256,32,64]{0,2,1:T(8,128)(2,1)S(1)}, u32[]{:S(2)}, u32[]{:S(2)}) collective-permute-start(bf16[256,32,64]{0,2,1:T(8,128)(2,1)} %get-tuple-element.1737), channel_id=1, source_target_pairs={{0,4},{4,8},{8,12},{12,16},{16,20},{20,24},{24,28},{28,0},{1,5},{5... | collective-permute-start | bytes 3145736 | tf_op jit(solution)/shard_map/while/body/eval_jaxpr/ppermute | solution.py:13
  1490.4 16.3 collective-permute-start.6
  1490.4 27.6 %collective-permute-start.7 = (bf16[256,32,64]{0,2,1:T(8,128)(2,1)}, bf16[256,32,64]{0,2,1:T(8,128)(2,1)}, u32[]{:S(2)}, u32[]{:S(2)}) collective-permute-start(bf16[256,32,64]{0,2,1:T(8,128)(2,1)} %get-tuple-element.1854), channel_id=1, source_target_pairs={{0,4},{4,8},{8,12},{12,16},{16,20},{20,24},{24,28},{28,0},{1,5},{5... | collective-permute-start | bytes 3145736 | tf_op jit(solution)/shard_map/ppermute | solution.py:13
  1510.8 41.7 %copy-start.12 = (bf16[256,32,64]{0,2,1:T(8,128)(2,1)}, bf16[256,32,64]{0,2,1:T(8,128)(2,1)S(1)}, u32[]{:S(2)}) copy-start(bf16[256,32,64]{0,2,1:T(8,128)(2,1)S(1)} %pad_maximum_fusion.5) | copy-start | bytes 3145732
  1550.6 622.8 %all-reduce.6.cloned.1.call-start = ((), (), s32[]{:S(2)}) async-start(), calls=%async_computation.12 | async-start | bytes 163840 | tf_op jit(solution)/shard_map/psum | solution.py:334
  1587.9 1080.7 %all-reduce.8.cloned.1.call-start = ((), (), s32[]{:S(2)}) async-start(), calls=%async_computation.13 | async-start | bytes 50331648 | tf_op jit(solution)/shard_map/psum | solution.py:331
  2078.4 32.1 %all-to-all-start.1 = ((bf16[8,32,2048]{2,1,0:T(8,128)(2,1)}), bf16[8,32,2048]{2,1,0:T(8,128)(2,1)S(1)}, u32[]{:S(2)}, u32[]{:S(2)}) async-start(bf16[8,32,2048]{2,1,0:T(8,128)(2,1)} %bitcast.328), calls=%async_computation.1 | async-start | bytes 2097152 | tf_op jit(solution)/shard_map/all_to_all | solution.py:300
  2110.5 70.6 %all-to-all-start.3 = ((bf16[8,32,2048]{2,1,0:T(8,128)(2,1)}), bf16[8,32,2048]{2,1,0:T(8,128)(2,1)S(1)}, u32[]{:S(2)}, u32[]{:S(2)}) async-start(bf16[8,32,2048]{2,1,0:T(8,128)(2,1)} %bitcast.323), calls=%async_computation.3 | async-start | bytes 2097152 | tf_op jit(solution)/shard_map/all_to_all | solution.py:301
  2175.4 530.0 %copy-start.54 = (f32[512]{0:T(512)}, f32[512]{0:T(512)S(1)}, u32[]{:S(2)}) copy-start(f32[512]{0:T(512)S(1)} %dynamic_slice.23) | copy-start | bytes 6148
  (110 other events, 679.1 us)
Sparse Core Ops, SparseCore 0:
  9.9 90.6 all-gather.11
  102.4 227.6 all-gather.9
  332.0 297.2 all-gather.15
  630.9 297.2 all-gather.13
  990.2 356.3 reduce-scatter.6
  1550.7 489.0 reduce-scatter.4
  2047.3 125.9 all-reduce.5
  2176.0 492.6 all-reduce.7
where the time goes:
time: 2720 us; the launch traced here: 2710 us
  waiting for transfers between devices  1910 us (70%)
  matrix products  323 us (12%)
  other arithmetic  225 us (8%)
  local copies, waits for them, and re-layouts  167 us (6%)
  blocking collectives  47 us (2%)
  starting transfers between devices  28.2 us (1%)
    psum x1, waiting for transfers between devices, shards(): lax.psum(in_shard, 'ctx').astype(jnp.float32)  486 us
    reduce_scatter x1, waiting for transfers between devices, shards(): lax.psum_scatter(term_maker(normed, grad_joined).astype(jnp.bfloat16), 'f...  452 us
    ppermute x44, waiting for transfers between devices, from_behind(): lax.ppermute(shard, axis, [(i, (i + by) % devices) for i in range(devices)])  364 us
    all_gather x1, waiting for transfers between devices, shards(): lax.all_gather(up_weight, 'fsdp', axis=0, tiled=True)  271 us
    all_gather x1, waiting for transfers between devices, shards(): lax.all_gather(qkv_weight, 'fsdp', axis=0, tiled=True)  220 us
    add x15, other arithmetic, layout(): jnp.repeat(places, block_rows, total_repeat_length=tok_rows) * block_rows  156 us
    dot_general x4, matrix products, transposed_dot(): lax.dot_general(left_rows, right_rows, (((1,), (1,)), ((), ())), preferre...  62.4 us
    psum x1, waiting for transfers between devices, shards(): lax.psum((gain_term, shift_term, qkv_bias_term, bias_term, up_bias_term),...  58.6 us
  transfers between devices with their start and end apart: 56, of which 24 were waited for; matrix products, arithmetic and copies ran while one was open for 22% of the time, Pallas kernels for 0%

commit v1 on v0

v1 whole, which is shorter than its diff:
```python
import functools

import jax
import jax.numpy as jnp
from jax import lax
from jax.experimental import pallas as pl
from jax.experimental.pallas import tpu as pltpu
from jax.sharding import PartitionSpec as P

HEAD_DIM = 64
ROT = 32
BLK = 16
TILE = 256
LANES = 128
F32 = jnp.float32
BF16 = jnp.bfloat16


def dot_nn(left, right):
    return lax.dot_general(left, right, (((1,), (0,)), ((), ())), preferred_element_type=F32)


def dot_nt(left, right):
    return lax.dot_general(left, right, (((1,), (1,)), ((), ())), preferred_element_type=F32)


def dot_tn(left, right):
    return lax.dot_general(left, right, (((0,), (0,)), ((), ())), preferred_element_type=F32)


def swap(value, axis, mask):
    devices = lax.axis_size(axis)
    return lax.ppermute(value, axis, [(i, i ^ mask) for i in range(devices)])


def bits_of(axis):
    return range(lax.axis_size(axis).bit_length() - 1)


def gather_rows(own, order):
    index = lax.axis_index("fsdp")
    count = lax.axis_size("fsdp")
    rows = own.shape[0]
    whole = lax.dynamic_update_slice_in_dim(
        jnp.zeros((count * rows, own.shape[1]), own.dtype), own, index * rows, 0
    )
    held = [(index, own)]
    for bit in order:
        arrived = [(where ^ (1 << bit), swap(piece, "fsdp", 1 << bit)) for where, piece in held]
        for where, piece in arrived:
            whole = lax.dynamic_update_slice_in_dim(whole, piece, where * rows, 0)
        held = held + arrived
    return whole


def scatter_sum(parts, order):
    index = lax.axis_index("fsdp")
    bits = len(order)
    left = list(range(bits))[::-1]
    held = parts.reshape((2,) * bits + parts.shape[1:])
    for bit in order:
        axis = left.index(bit)
        mine = (index >> bit) & 1
        send = lax.dynamic_index_in_dim(held, 1 - mine, axis, keepdims=False)
        keep = lax.dynamic_index_in_dim(held, mine, axis, keepdims=False)
        got = swap(send, "fsdp", 1 << bit)
        held = (keep.astype(F32) + got.astype(F32)).astype(BF16)
        left.pop(axis)
    return held


def line_sum(parts):
    index = lax.axis_index("ctx")
    count = lax.axis_size("ctx")
    line = count // 2
    core, place = index % 2, index // 2
    pairs = parts.reshape((line, 2, parts.shape[0] // count) + parts.shape[1:])
    other = lax.dynamic_index_in_dim(pairs, 1 - core, 1, keepdims=False)
    mine = lax.dynamic_index_in_dim(pairs, core, 1, keepdims=False)
    held = (mine.astype(F32) + swap(other, "ctx", 1).astype(F32)).astype(BF16)

    def block(target):
        return lax.dynamic_index_in_dim(
            held, jnp.clip(target, 0, line - 1), 0, keepdims=False
        ).astype(F32)

    ups = downs = None
    for step in range(line - 1):
        far = line - 1 - step
        up = block(place + far)
        down = block(place - far)
        if step:
            up, down = up + ups, down + downs
        ups = lax.ppermute(
            up.astype(BF16), "ctx", [(i, i + 2) for i in range(count - 2) if i // 2 + far < line]
        ).astype(F32)
        downs = lax.ppermute(
            down.astype(BF16), "ctx", [(i, i - 2) for i in range(2, count) if i // 2 - far >= 0]
        ).astype(F32)
    total = block(place)
    return total + ups + downs if line > 1 else total


def sum_everywhere(vector):
    for axis in ("ctx", "fsdp"):
        for bit in bits_of(axis):
            vector = vector + swap(vector, axis, 1 << bit)
    return vector


def turn(values, cosine, sine):
    lane = lax.broadcasted_iota(jnp.int32, values.shape, 1) % HEAD_DIM
    half = ROT // 2
    partner = jnp.where(
        lane < half, pltpu.roll(values, LANES - half, 1), pltpu.roll(values, half, 1)
    )
    return values * cosine + partner * sine


def attention_kernel(
    place_ref, ends_ref, cos_ref, sin_ref, lin_hbm, grad_hbm, att_hbm, mixed_hbm,
    lin, grad, rows, keys_t, values_t, grad_t, grad_k, grad_v, weights, grad_w, att, mixed, sems,
):
    tokens, width = grad.shape
    tile = TILE
    tiles = tokens // tile
    blocks = tokens // BLK
    sequences = ends_ref.shape[0]
    pairs = width // LANES

    @pl.loop(0, blocks)
    def _(block):
        source = pl.ds(pl.multiple_of(block * BLK, BLK), BLK)
        target = pl.ds(pl.multiple_of(place_ref[block] * BLK, BLK), BLK)
        pltpu.make_async_copy(lin_hbm.at[source], lin.at[target], sems.at[0]).start()
        pltpu.make_async_copy(grad_hbm.at[source], grad.at[target], sems.at[1]).start()

    grad_k[...] = jnp.zeros_like(grad_k)
    grad_v[...] = jnp.zeros_like(grad_v)
    pltpu.make_async_copy(lin_hbm, lin, sems.at[0]).wait()
    pltpu.make_async_copy(grad_hbm, grad, sems.at[1]).wait()

    @pl.loop(0, tiles)
    def _(step):
        part = pl.ds(pl.multiple_of(step * tile, tile), tile)
        cosine, sine = cos_ref[part, :], sin_ref[part, :]
        for pair in range(pairs):
            lanes = slice(pair * LANES, (pair + 1) * LANES)
            key_lanes = slice(width + pair * LANES, width + (pair + 1) * LANES)
            value_lanes = slice(2 * width + pair * LANES, 2 * width + (pair + 1) * LANES)
            query = turn(lin[part, lanes], cosine, sine) * HEAD_DIM ** (-0.5)
            rows[part, lanes] = query.astype(BF16)
            key = turn(lin[part, key_lanes], cosine, sine).astype(BF16)
            rows[part, key_lanes] = key
            keys_t[lanes, part] = key.T
            value = lin[part, value_lanes].astype(BF16)
            rows[part, value_lanes] = value
            values_t[lanes, part] = value.T
            grad_t[lanes, part] = grad[part, lanes].T

    def first_half(values):
        lane = lax.broadcasted_iota(jnp.int32, values.shape, 1)
        return lane < HEAD_DIM

    for pair in range(pairs):
        lanes = slice(pair * LANES, (pair + 1) * LANES)
        key_lanes = slice(width + pair * LANES, width + (pair + 1) * LANES)
        value_lanes = slice(2 * width + pair * LANES, 2 * width + (pair + 1) * LANES)
        head_rows = [
            slice(pair * LANES + head * HEAD_DIM, pair * LANES + (head + 1) * HEAD_DIM)
            for head in range(2)
        ]

        @pl.loop(0, tiles)
        def _(step):
            top = step * tile
            part = pl.ds(pl.multiple_of(top, tile), tile)
            column = top + lax.broadcasted_iota(jnp.int32, (1, tile), 1)
            begin = jnp.zeros((1, tile), jnp.int32)
            first = jnp.int32(0)
            for sequence in range(sequences):
                end = ends_ref[sequence]
                begin = jnp.where(column >= end, jnp.maximum(begin, end), begin)
                first = jnp.where(top >= end, jnp.maximum(first, end), first)
            low = first // tile
            query = rows[part, lanes]
            back = grad[part, lanes]
            half = first_half(query)
            zero = jnp.zeros_like(query)
            queries = [jnp.where(half, query, zero), jnp.where(half, zero, query)]
            backs = [jnp.where(half, back, zero), jnp.where(half, zero, back)]

            def score(index, tops):
                there = pl.ds(pl.multiple_of(index * tile, tile), tile)
                row = index * tile + lax.broadcasted_iota(jnp.int32, (tile, tile), 0)
                visible = (row <= column) & (row >= begin)
                key = rows[there, key_lanes]
                result = []
                for head in range(2):
                    scores = jnp.where(visible, dot_nt(key, queries[head]), -1e30)
                    weights[head, there, :] = scores
                    result.append(
                        jnp.maximum(tops[head], jnp.max(scores, axis=0, keepdims=True))
                    )
                return tuple(result)

            tops = lax.fori_loop(
                low, step + 1, score, (jnp.full((1, tile), -1e30, F32),) * 2
            )

            def combine(index, state):
                there = pl.ds(pl.multiple_of(index * tile, tile), tile)
                value = rows[there, value_lanes]
                result = []
                for head in range(2):
                    total, summed = state[head]
                    weight = jnp.exp(weights[head, there, :] - tops[head])
                    weights[head, there, :] = weight
                    grad_w[head, there, :] = dot_nt(value, backs[head])
                    total = total + jnp.sum(weight, axis=0, keepdims=True)
                    summed = summed + dot_nn(
                        values_t[head_rows[head], there], weight.astype(BF16)
                    )
                    result.append((total, summed))
                return tuple(result)

            state = lax.fori_loop(
                low,
                step + 1,
                combine,
                ((jnp.zeros((1, tile), F32), jnp.zeros((HEAD_DIM, tile), F32)),) * 2,
            )
            inverse = [1.0 / total for total, summed in state]
            attended = [state[head][1] * inverse[head] for head in range(2)]
            delta = [
                jnp.sum(
                    attended[head] * grad_t[head_rows[head], part].astype(F32),
                    axis=0,
                    keepdims=True,
                )
                for head in range(2)
            ]
            att[part, lanes] = jnp.concatenate(attended, axis=0).T.astype(BF16)

            def back_step(index, sums):
                there = pl.ds(pl.multiple_of(index * tile, tile), tile)
                result = []
                add_k = add_v = None
                for head in range(2):
                    weight = weights[head, there, :] * inverse[head]
                    grad_s = (weight * (grad_w[head, there, :] - delta[head])).astype(BF16)
                    part_k = dot_nn(grad_s, queries[head])
                    part_v = dot_nn(weight.astype(BF16), backs[head])
                    add_k = part_k if head == 0 else add_k + part_k
                    add_v = part_v if head == 0 else add_v + part_v
                    result.append(sums[head] + dot_nn(keys_t[head_rows[head], there], grad_s))
                grad_k[there, lanes] += add_k
                grad_v[there, lanes] += add_v
                return tuple(result)

            sums = lax.fori_loop(
                low, step + 1, back_step, (jnp.zeros((HEAD_DIM, tile), F32),) * 2
            )
            grad_q = jnp.concatenate(sums, axis=0).T * HEAD_DIM ** (-0.5)
            mixed[part, lanes] = turn(grad_q, cos_ref[part, :], -sin_ref[part, :]).astype(BF16)

    @pl.loop(0, tiles)
    def _(step):
        part = pl.ds(pl.multiple_of(step * tile, tile), tile)
        cosine, sine = cos_ref[part, :], sin_ref[part, :]
        for pair in range(pairs):
            lanes = slice(pair * LANES, (pair + 1) * LANES)
            key_lanes = slice(width + pair * LANES, width + (pair + 1) * LANES)
            value_lanes = slice(2 * width + pair * LANES, 2 * width + (pair + 1) * LANES)
            mixed[part, key_lanes] = turn(grad_k[part, lanes], cosine, -sine).astype(BF16)
            mixed[part, value_lanes] = grad_v[part, lanes].astype(BF16)

    @pl.loop(0, blocks)
    def _(block):
        target = pl.ds(pl.multiple_of(block * BLK, BLK), BLK)
        source = pl.ds(pl.multiple_of(place_ref[block] * BLK, BLK), BLK)
        pltpu.make_async_copy(att.at[source], att_hbm.at[target], sems.at[0]).start()
        pltpu.make_async_copy(mixed.at[source], mixed_hbm.at[target], sems.at[1]).start()

    pltpu.make_async_copy(att, att_hbm, sems.at[0]).wait()
    pltpu.make_async_copy(mixed, mixed_hbm, sems.at[1]).wait()


def attention(block_place, lengths, linear, grad_att):
    tokens, width = grad_att.shape
    ends = jnp.cumsum(lengths).astype(jnp.int32)
    position = jnp.arange(tokens, dtype=jnp.int32)
    begin = jnp.max(jnp.where(position[:, None] >= ends[None, :], ends[None, :], 0), axis=1)
    within = (position - begin).astype(F32)
    half = ROT // 2
    frequency = 10000.0 ** (-jnp.arange(half, dtype=F32) * 2.0 / ROT)
    angles = within[:, None] * frequency[None, :]
    cosine, sine = jnp.cos(angles), jnp.sin(angles)
    ones = jnp.ones((tokens, HEAD_DIM - ROT), F32)
    cos_table = jnp.concatenate([cosine, cosine, ones] * 2, axis=1)
    sin_table = jnp.concatenate([-sine, sine, 0.0 * ones] * 2, axis=1)
    smem = pl.BlockSpec(memory_space=pltpu.SMEM)
    vmem = pl.BlockSpec(memory_space=pltpu.VMEM)
    anywhere = pl.BlockSpec(memory_space=pl.ANY)
    return pl.pallas_call(
        attention_kernel,
        out_shape=(
            jax.ShapeDtypeStruct((tokens, width), BF16),
            jax.ShapeDtypeStruct((tokens, 3 * width), BF16),
        ),
        in_specs=[smem, smem, vmem, vmem, anywhere, anywhere],
        out_specs=(anywhere, anywhere),
        scratch_shapes=[
            pltpu.VMEM((tokens, 3 * width), F32),
            pltpu.VMEM((tokens, width), BF16),
            pltpu.VMEM((tokens, 3 * width), BF16),
            pltpu.VMEM((width, tokens), BF16),
            pltpu.VMEM((width, tokens), BF16),
            pltpu.VMEM((width, tokens), BF16),
            pltpu.VMEM((tokens, width), F32),
            pltpu.VMEM((tokens, width), F32),
            pltpu.VMEM((2, tokens, TILE), F32),
            pltpu.VMEM((2, tokens, TILE), F32),
            pltpu.VMEM((tokens, width), BF16),
            pltpu.VMEM((tokens, 3 * width), BF16),
            pltpu.SemaphoreType.DMA((2,)),
        ],
        compiler_params=pltpu.CompilerParams(vmem_limit_bytes=56 << 20),
        cost_estimate=pl.CostEstimate(
            flops=30 * 10**9, bytes_accessed=15 * 10**6, transcendentals=0
        ),
    )(block_place, ends, cos_table, sin_table, linear, grad_att)


def shards(
    tokens,
    block_place,
    seq_lengths,
    norm_gain,
    norm_bias,
    qkv_weight,
    qkv_bias,
    out_weight,
    out_bias,
    up_weight,
    up_bias,
    down_weight,
    down_bias,
    out_grad,
):
    ctx_count, ctx_index = lax.axis_size("ctx"), lax.axis_index("ctx")
    shard_count, shard_index = lax.axis_size("fsdp"), lax.axis_index("fsdp")
    own_tokens, own_grad = tokens[0], out_grad[0]
    own_rows, model_width = own_tokens.shape
    hidden_width = up_weight.shape[1]
    heads = model_width // HEAD_DIM
    own_heads = heads // ctx_count
    shard_heads = heads // shard_count
    unit = hidden_width // shard_count // ctx_count
    own_width = own_heads * HEAD_DIM
    head_turns = ctx_count // shard_heads
    low_first = list(bits_of("fsdp"))
    high_first = low_first[::-1]

    def pick(value, axis):
        return lax.dynamic_index_in_dim(value, ctx_index, axis, keepdims=False)

    half_width = model_width // 2
    grad_rows = [
        lax.all_gather(piece, "ctx", axis=0, tiled=True)
        for piece in (own_grad[:, :half_width], own_grad[:, half_width:])
    ]

    vectors = (norm_gain, norm_bias, qkv_bias, out_bias, up_bias, down_bias)
    packed = lax.all_gather(jnp.concatenate(vectors), "fsdp", axis=0, tiled=False)
    cuts = [0]
    for vector in vectors:
        cuts.append(cuts[-1] + vector.shape[0])
    gain_all, shift_all, qkv_bias_all, out_bias_all, up_bias_all, down_bias_all = [
        packed[:, start:stop].reshape(-1).astype(F32) for start, stop in zip(cuts, cuts[1:])
    ]
    own_qkv_bias = pick(qkv_bias_all.reshape(3 * own_heads, ctx_count, HEAD_DIM), 1).reshape(-1)
    own_up_bias = pick(up_bias_all.reshape(shard_count, ctx_count, unit), 1).reshape(-1)

    inputs = own_tokens.astype(F32)
    row_mean = jnp.mean(inputs, axis=1, keepdims=True)
    centred = inputs - row_mean
    inv_std = lax.rsqrt(jnp.mean(centred * centred, axis=1, keepdims=True) + 1e-05)
    scaled = centred * inv_std
    own_normed = (scaled * gain_all + shift_all).astype(BF16)
    normed = lax.all_gather(own_normed, "ctx", axis=0, tiled=True)

    own_up = pick(up_weight.reshape(-1, shard_count, ctx_count, unit), 2)
    up_all = gather_rows(own_up.reshape(-1, shard_count * unit), low_first)
    own_down = pick(down_weight.reshape(ctx_count, unit, model_width), 0)
    down_all = gather_rows(own_down, high_first)
    own_qkv = pick(qkv_weight.reshape(-1, 3 * own_heads, ctx_count, HEAD_DIM), 2)
    qkv_all = gather_rows(own_qkv.reshape(-1, 3 * own_width), high_first)
    turn_index, head_slot = ctx_index // shard_heads, ctx_index % shard_heads
    own_out = lax.dynamic_index_in_dim(
        out_weight.reshape(shard_heads, HEAD_DIM, model_width), head_slot, 0, keepdims=False
    )
    out_all = gather_rows(own_out, low_first).reshape(
        own_heads, head_turns, HEAD_DIM, model_width
    )
    out_all = lax.dynamic_index_in_dim(out_all, turn_index, 1, keepdims=False).reshape(
        own_width, model_width
    )

    hidden = dot_nn(normed, up_all) + own_up_bias
    active = jax.nn.gelu(hidden, approximate=True).astype(BF16)
    linear = dot_nn(normed, qkv_all) + own_qkv_bias

    down_parts = [
        scatter_sum(
            dot_tn(active, piece).astype(BF16).reshape(shard_count, unit, half_width),
            order,
        )
        for piece, order in zip(grad_rows, (low_first, high_first))
    ]
    grad_active = dot_nt(grad_rows[0], down_all[:, :half_width]) + dot_nt(
        grad_rows[1], down_all[:, half_width:]
    )
    unused_out, gelu_back = jax.vjp(lambda inner: jax.nn.gelu(inner, approximate=True), hidden)
    grad_hidden = gelu_back(grad_active)[0].astype(BF16)
    up_part = scatter_sum(
        dot_tn(normed, grad_hidden).astype(BF16).reshape(shard_count, -1, shard_count * unit),
        low_first,
    )
    grad_att = (
        dot_nt(grad_rows[0], out_all[:, :half_width])
        + dot_nt(grad_rows[1], out_all[:, half_width:])
    ).astype(BF16)
    attended, grad_mixed = attention(block_place, seq_lengths[0], linear, grad_att)
    qkv_part = scatter_sum(
        dot_tn(normed, grad_mixed).astype(BF16).reshape(shard_count, -1, 3 * own_width),
        high_first,
    )
    out_terms = jnp.concatenate([dot_tn(attended, piece) for piece in grad_rows], axis=1)
    out_terms = out_terms.astype(BF16).reshape(own_heads, 1, HEAD_DIM, model_width)
    if head_turns > 1:
        out_terms = lax.dynamic_update_slice_in_dim(
            jnp.zeros((own_heads, head_turns, HEAD_DIM, model_width), BF16),
            out_terms,
            turn_index,
            1,
        )
    out_part = scatter_sum(out_terms.reshape(shard_count, HEAD_DIM, model_width), low_first)

    out_partial = (dot_nn(attended, out_all) + dot_nn(active, down_all)).astype(BF16)
    output = (inputs + line_sum(out_partial) + (out_bias_all + down_bias_all)).astype(BF16)
    norm_partial = (dot_nt(grad_mixed, qkv_all) + dot_nt(grad_hidden, up_all)).astype(BF16)
    grad_normed = line_sum(norm_partial)

    grad_float = own_grad.astype(F32)
    grad_scaled = grad_normed * gain_all
    grad_input = inv_std * (
        grad_scaled
        - jnp.mean(grad_scaled, axis=1, keepdims=True)
        - scaled * jnp.mean(grad_scaled * scaled, axis=1, keepdims=True)
    )
    input_grad = (grad_float + grad_input).astype(BF16)

    def spread(value, count):
        value = value.reshape(-1, 1, value.shape[0] // count)
        whole = jnp.zeros((count, ctx_count, value.shape[2]), F32)
        return lax.dynamic_update_slice_in_dim(whole, value, ctx_index, 1).reshape(-1)

    sums = (
        jnp.sum(grad_normed * scaled, axis=0),
        jnp.sum(grad_normed, axis=0),
        spread(jnp.sum(grad_mixed.astype(F32), axis=0), 3 * own_heads),
        jnp.sum(grad_float, axis=0),
        spread(jnp.sum(grad_hidden.astype(F32), axis=0), shard_count),
    )
    total = sum_everywhere(jnp.concatenate(sums))
    own_sums, start = [], 0
    for item in sums:
        size = item.shape[0] // shard_count
        own_sums.append(lax.dynamic_slice_in_dim(total, start + shard_index * size, size))
        start += item.shape[0]
    gain_total, shift_total, qkv_bias_total, bias_total, up_bias_total = own_sums

    down_total = [
        lax.all_gather(piece, "ctx", axis=0, tiled=True).astype(F32) for piece in down_parts
    ]
    up_total = lax.all_gather(up_part, "ctx", axis=0, tiled=False)
    qkv_total = lax.all_gather(qkv_part, "ctx", axis=0, tiled=False)
    out_total = lax.all_gather(out_part, "ctx", axis=0, tiled=False)

    def deal(value, size):
        rows = value.shape[1]
        value = value.reshape(ctx_count, rows, -1, size)
        return jnp.transpose(value, (1, 2, 0, 3)).reshape(rows, -1).astype(F32)

    out_total = lax.dynamic_index_in_dim(
        out_total.reshape(head_turns, shard_heads * HEAD_DIM, model_width),
        shard_index % head_turns,
        0,
        keepdims=False,
    )
    return (
        output[None],
        input_grad[None],
        gain_total,
        shift_total,
        deal(qkv_total, HEAD_DIM),
        qkv_bias_total,
        out_total.astype(F32),
        bias_total,
        deal(up_total, unit),
        up_bias_total,
        jnp.concatenate(down_total, axis=1),
        bias_total,
    )


def solution(mesh):
    in_specs = (
        P("fsdp", "ctx", None),
        P(),
        P("fsdp", None),
        P("fsdp"),
        P("fsdp"),
        P("fsdp", None),
        P("fsdp"),
        P("fsdp", None),
        P("fsdp"),
        P("fsdp", None),
        P("fsdp"),
        P("fsdp", None),
        P("fsdp"),
        P("fsdp", "ctx", None),
    )
    out_specs = (
        P("fsdp", "ctx", None),
        P("fsdp", "ctx", None),
        P("fsdp"),
        P("fsdp"),
        P("fsdp", None),
        P("fsdp"),
        P("fsdp", None),
        P("fsdp"),
        P("fsdp", None),
        P("fsdp"),
        P("fsdp", None),
        P("fsdp"),
    )
    return jax.shard_map(shards, mesh=mesh, in_specs=in_specs, out_specs=out_specs, check_vma=False)
```

time: 2720 us -> 987 us (0.36)
  waiting for transfers between devices: 1910 us -> 386 us
  matrix products: 323 us -> 155 us
  other arithmetic: 225 us -> 77.9 us
  Pallas kernels: 0 us -> 57 us
  starting transfers between devices: 28.2 us -> 84.4 us
  blocking collectives: 47 us -> 9.82 us
  local copies, waits for them, and re-layouts: 167 us -> 198 us
    psum x2 -> x0, waiting for transfers between devices: 545 us -> none  [the longest x1 486 us: shards(): lax.psum(in_shard, 'ctx').astype(jnp.float32)]
    reduce_scatter x1 -> x0, waiting for transfers between devices: 452 us -> none  [shards(): lax.psum_scatter(term_maker(normed, grad_joined).astype(jnp.bfloat16), 'f...]
    all_gather x4 -> x8, waiting for transfers between devices: 495 us -> 76.9 us  [the longest x1 76.9 us: shards(): normed = lax.all_gather(own_normed, 'ctx', axis=0, tiled=True)]
    dot_general x65 -> x16, matrix products: 323 us -> 155 us  [the longest x6 64 us: dot_nt(): lax.dot_general(left, right, (((1,), (1,)), ((), ())), preferred_element_...]
    add x23 -> x5, other arithmetic: 157 us -> 0.05 us  [sum_everywhere(): vector = vector + swap(vector, axis, 1 << bit)]
    ppermute x44 -> x41, starting transfers between devices: 8.11 us -> 83.5 us  [the longest x29 48.8 us: swap(): return lax.ppermute(value, axis, [(i, i ^ mask) for i in range(devices)])]
    unnamed x119 -> x81, local copies, waits for them, and re-layouts: 11.4 us -> 83.1 us
    pallas_call x0 -> x1, Pallas kernels: none -> 57 us  [attention(): pl.pallas_call(attention_kernel, out_shape=(jax.ShapeDtypeStruct((tokens,...]
  transfers between devices with their start and end apart: 56 -> 49, of which waited for: 24 -> 28; matrix products, arithmetic and copies ran while one was open for 22% -> 38% of each run, Pallas kernels for 0% -> 6%
where the time goes in v1:
time: 987 us; the launch traced here: 983 us
  waiting for transfers between devices  386 us (39%)
  local copies, waits for them, and re-layouts  198 us (20%)
  matrix products  155 us (16%)
  starting transfers between devices  84.4 us (9%)
  other arithmetic  77.9 us (8%)
  Pallas kernels  57 us (6%)
  between operations  15.2 us (2%)
    ppermute x29, waiting for transfers between devices, swap(): return lax.ppermute(value, axis, [(i, i ^ mask) for i in range(devices)])  171 us
    ppermute x6, waiting for transfers between devices, line_sum(): lax.ppermute(up.astype(BF16), 'ctx', [(i, i + 2) for i in range(count - 2...  121 us
    unnamed x81, local copies, waits for them, and re-layouts  83.1 us
    all_gather x1, waiting for transfers between devices, shards(): normed = lax.all_gather(own_normed, 'ctx', axis=0, tiled=True)  76.9 us
    dot_general x6, matrix products, dot_nt(): lax.dot_general(left, right, (((1,), (1,)), ((), ())), preferred_element_...  64 us
    pallas_call x1, Pallas kernels, attention(): pl.pallas_call(attention_kernel, out_shape=(jax.ShapeDtypeStruct((tokens,...  57 us
    dot_general x4, matrix products, dot_nn(): lax.dot_general(left, right, (((1,), (0,)), ((), ())), preferred_element_...  53 us
    convert_element_type x3, local copies, waits for them, and re-layouts, deal(): return jnp.transpose(value, (1, 2, 0, 3)).reshape(rows, -1).astype(F32)  49.6 us
  transfers between devices with their start and end apart: 49, of which 28 were waited for; matrix products, arithmetic and copies ran while one was open for 38% of the time, Pallas kernels for 6%

profile of v1, /device:TPU:0, one launch (start us, length us, event | category | flops | bytes accessed | tf_op | source)
XLA Modules:
  0.0 982.8 jit_solution(12097649879961535989)
XLA Ops:
  15.2 9.8 all-gather.4
  27.5 8.7 copy.101
  45.3 11.9 %copy.104 = bf16[512,8192]{0,1:T(8,128)(2,1)} copy(bf16[512,8192]{1,0:T(8,128)(2,1)} %param.23) | data formatting | bytes 16777216 | tf_op args[9]
  61.3 3.7 multiply_sine_fusion
  70.5 4.4 concatenate.27.cos_ref
  83.0 4.2 collective-permute-done.5
  92.2 9.7 collective-permute-done.2
  102.8 5.0 fusion.60
  107.9 5.3 fusion.23.grad_hbm
  113.2 76.9 %all-gather.14.cloned.1.call-done = bf16[2048,2048]{1,0:T(8,128)(2,1)} async-done(((bf16[256,2048]{1,0:T(8,128)(2,1)}), bf16[2048,2048]{1,0:T(8,128)(2,1)}) %all-gather.14.cloned.1.call-update) | async-done | bytes 8388624 | tf_op jit(solution)/shard_map/all_gather | solution.py:391
  190.1 11.9 %broadcast_add_fusion.lin_hbm = f32[2048,768]{1,0:T(8,128)} fusion(f32[768]{0:T(1024)S(1)} %add.362, bf16[2048,2048]{1,0:T(8,128)(2,1)} %all-gather.14.cloned.1.call-done, bf16[2048,768]{0,1:T(8,128)(2,1)} %constant_dynamic-update-slice_fusion.12), kind=kOutput, calls=%fused_computation.32 | convolution fusion | flops 6444023808 | bytes 17828864 | tf_op jit(solution)/shard_map/dot_general | solution.py:20
  202.0 57.0 %shard_map.229 = (bf16[2048,256]{1,0:T(8,128)(2,1)}, bf16[2048,768]{1,0:T(8,128)(2,1)}) custom-call(s32[128]{0:T(128)} %place_ref.1, s32[4]{0:T(128)} %bitcast.301, f32[2048,128]{1,0:T(8,128)} %concatenate.27.cos_ref, f32[2048,128]{1,0:T(8,128)} %concatenate.28.sin_ref, f32[2048,768]{1,0:T(8,128)} %broadcast_add_fusion.lin_hbm, ...), custom_call_target="tpu_custom_call" | custom-call | flops 30000001024 | bytes 15000000 | tf_op jit(solution)/shard_map/pallas_call | solution.py:305
  263.2 5.0 collective-permute-start.33
  275.4 5.2 collective-permute-done.33
  281.9 17.4 %collective-permute-done.8 = bf16[512,1024]{0,1:T(8,128)(2,1)S(1)} collective-permute-done((bf16[512,1024]{0,1:T(8,128)(2,1)}, bf16[512,1024]{0,1:T(8,128)(2,1)S(1)}, u32[]{:S(2)}, u32[]{:S(2)}) %collective-permute-start.8) | collective-permute-done | bytes 1048608 | tf_op jit(solution)/shard_map/ppermute | solution.py:33
  304.8 16.8 %multiply_convert_fusion = (bf16[2048,1024]{1,0:T(8,128)(2,1)S(1)}, f32[2048,1024]{1,0:T(8,128)}) fusion(f32[1024]{0:T(1024)S(1)} %bitcast.298, bf16[2048,2048]{1,0:T(8,128)(2,1)} %all-gather.14.cloned.1.call-done, bf16[2048,1024]{0,1:T(8,128)(2,1)} %constant_dynamic-update-slice_fusion.4), kind=kOutput, calls=%fused_computation.22 | convolution fusion | flops 8610906112 | bytes 25169920 | tf_op jit(solution)/shard_map/dot_general | solution.py:20
  321.7 4.8 convolution_convert_fusion.2
  326.8 23.9 %collective-permute-done.39 = bf16[2,256,1024]{2,1,0:T(8,128)(2,1)S(1)} collective-permute-done((bf16[2,256,1024]{2,1,0:T(8,128)(2,1)S(1)}, bf16[2,256,1024]{2,1,0:T(8,128)(2,1)S(1)}, u32[]{:S(2)}, u32[]{:S(2)}) %collective-permute-start.39) | collective-permute-done | bytes 1048608 | tf_op jit(solution)/shard_map/ppermute | solution.py:33
  351.8 11.3 %collective-permute-done.40 = bf16[256,1024]{1,0:T(8,128)(2,1)S(1)} collective-permute-done((bf16[256,1024]{1,0:T(8,128)(2,1)S(1)}, bf16[256,1024]{1,0:T(8,128)(2,1)S(1)}, u32[]{:S(2)}, u32[]{:S(2)}) %collective-permute-start.40) | collective-permute-done | bytes 524320 | tf_op jit(solution)/shard_map/ppermute | solution.py:33
  364.2 8.0 convolution_convert_fusion.3
  373.5 21.2 %collective-permute-done.37 = bf16[2,256,1024]{2,1,0:T(8,128)(2,1)S(1)} collective-permute-done((bf16[2,256,1024]{2,1,0:T(8,128)(2,1)S(1)}, bf16[2,256,1024]{2,1,0:T(8,128)(2,1)S(1)}, u32[]{:S(2)}, u32[]{:S(2)}) %collective-permute-start.37) | collective-permute-done | bytes 1048608 | tf_op jit(solution)/shard_map/ppermute | solution.py:33
  396.6 8.9 collective-permute-done.38
  413.8 9.4 convolution_convert_fusion.1
  426.9 11.6 %collective-permute-done.9 = bf16[256,2048]{1,0:T(8,128)(2,1)} collective-permute-done((bf16[256,2048]{1,0:T(8,128)(2,1)}, bf16[256,2048]{1,0:T(8,128)(2,1)}, u32[]{:S(2)}, u32[]{:S(2)}) %collective-permute-start.9) | collective-permute-done | bytes 1048608 | tf_op jit(solution)/shard_map/ppermute | solution.py:33
  442.6 9.0 collective-permute-done.10
  453.9 14.8 %collective-permute-done.11 = bf16[256,2048]{1,0:T(8,128)(2,1)S(1)} collective-permute-done((bf16[256,2048]{1,0:T(8,128)(2,1)}, bf16[256,2048]{1,0:T(8,128)(2,1)S(1)}, u32[]{:S(2)}, u32[]{:S(2)}) %collective-permute-start.11) | collective-permute-done | bytes 1048608 | tf_op jit(solution)/shard_map/ppermute | solution.py:33
  474.3 8.4 fusion.34
  482.7 4.3 collective-permute-done.32
  488.3 17.4 %convert_reduce_fusion = (f32[1024]{0:T(1024)S(1)}, bf16[2048,1024]{1,0:T(8,128)(2,1)S(1)}) fusion(f32[2048,1024]{1,0:T(8,128)} %get-tuple-element.109, f32[1024]{0:T(1024)S(1)} %bitcast.299, f32[1024,2048]{0,1:T(8,128)} %fusion.34, bf16[2048,1024]{1,0:T(8,128)(2,1)} %all-gather.16.cloned.1.call-done, bf16[1024,2048]{1,0:T(8,128)(2,1)} %constant_dynamic-update-slice_fusion), kind=kOutput, calls=%fused_computation.21 | convolution fusion | flops 4345297920 | bytes 27271168 | tf_op jit(solution)/shard_map/dot_general | solution.py:24
  505.7 11.6 %convolution_convert_fusion = bf16[2048,1024]{1,0:T(8,128)(2,1)S(1)} fusion(bf16[2048,2048]{1,0:T(8,128)(2,1)} %all-gather.14.cloned.1.call-done, bf16[2048,1024]{1,0:T(8,128)(2,1)S(1)} %get-tuple-element.111), kind=kOutput, calls=%fused_computation.28 | convolution fusion | flops 8592031744 | bytes 16777216 | tf_op jit(solution)/shard_map/dot_general | solution.py:28
  519.2 14.6 %fusion.70 = f32[2048,2048]{1,0:T(8,128)} fusion(bf16[2048,1024]{1,0:T(8,128)(2,1)S(1)} %get-tuple-element.111, bf16[2048,1024]{0,1:T(8,128)(2,1)} %constant_dynamic-update-slice_fusion.4), kind=kOutput, calls=%fused_computation.180 | convolution fusion | flops 8589934592 | bytes 25165824 | tf_op jit(solution)/shard_map/dot_general | solution.py:24
  533.8 13.4 %add_convert_fusion = bf16[2048,2048]{1,0:T(8,128)(2,1)} fusion(f32[2048,2048]{1,0:T(8,128)} %fusion.70, bf16[2048,768]{1,0:T(8,128)(2,1)S(1)} %copy-done.9, bf16[2048,768]{0,1:T(8,128)(2,1)} %constant_dynamic-update-slice_fusion.12), kind=kOutput, calls=%fused_computation | convolution fusion | flops 6450839552 | bytes 31457280 | tf_op jit(solution)/shard_map/dot_general | solution.py:24
  547.2 11.5 %collective-permute-done.35 = bf16[2,512,1024]{2,1,0:T(8,128)(2,1)S(1)} collective-permute-done((bf16[2,512,1024]{2,1,0:T(8,128)(2,1)S(1)}, bf16[2,512,1024]{2,1,0:T(8,128)(2,1)S(1)}, u32[]{:S(2)}, u32[]{:S(2)}) %collective-permute-start.35) | collective-permute-done | bytes 2097184 | tf_op jit(solution)/shard_map/ppermute | solution.py:33
  561.6 14.4 %fusion.69 = f32[2048,2048]{1,0:T(8,128)} fusion(bf16[2048,1024]{1,0:T(8,128)(2,1)S(1)} %copy-done.28, bf16[1024,2048]{1,0:T(8,128)(2,1)} %constant_dynamic-update-slice_fusion), kind=kOutput, calls=%fused_computation.179 | convolution fusion | flops 8589934592 | bytes 25165824 | tf_op jit(solution)/shard_map/dot_general | solution.py:20
  579.1 4.9 dynamic-slice_bitcast_fusion
  584.0 9.9 %add_convert_fusion.1 = bf16[2048,2048]{1,0:T(8,128)(2,1)S(1)} fusion(f32[2048,2048]{1,0:T(8,128)} %fusion.69, bf16[2048,256]{1,0:T(8,128)(2,1)S(1)} %copy-done.12, bf16[256,2048]{1,0:T(8,128)(2,1)} %constant_dynamic-update-slice_fusion.8), kind=kOutput, calls=%fused_computation.1 | convolution fusion | flops 2155872256 | bytes 27262976 | tf_op jit(solution)/shard_map/dot_general | solution.py:20
  599.1 5.6 fusion.7
  607.2 4.1 fusion.8
  618.5 33.8 %collective-permute-done.20 = bf16[256,2048]{1,0:T(8,128)(2,1)} collective-permute-done((bf16[256,2048]{1,0:T(8,128)(2,1)S(1)}, bf16[256,2048]{1,0:T(8,128)(2,1)}, u32[]{:S(2)}, u32[]{:S(2)}) %collective-permute-start.20) | collective-permute-done | bytes 1048608 | tf_op jit(solution)/shard_map/ppermute | solution.py:94
  655.1 5.5 collective-permute-start.21
  662.2 35.0 %collective-permute-done.13 = bf16[256,2048]{1,0:T(8,128)(2,1)} collective-permute-done((bf16[256,2048]{1,0:T(8,128)(2,1)}, bf16[256,2048]{1,0:T(8,128)(2,1)}, u32[]{:S(2)}, u32[]{:S(2)}) %collective-permute-start.13) | collective-permute-done | bytes 1048608 | tf_op jit(solution)/shard_map/ppermute | solution.py:94
  699.2 5.4 collective-permute-start.14
  704.6 18.1 %collective-permute-done.21 = bf16[256,2048]{1,0:T(8,128)(2,1)} collective-permute-done((bf16[256,2048]{1,0:T(8,128)(2,1)}, bf16[256,2048]{1,0:T(8,128)(2,1)}, u32[]{:S(2)}, u32[]{:S(2)}) %collective-permute-start.21) | collective-permute-done | bytes 1048608 | tf_op jit(solution)/shard_map/ppermute | solution.py:94
  722.8 4.4 fusion.43
  728.8 16.1 %collective-permute-done.14 = bf16[256,2048]{1,0:T(8,128)(2,1)} collective-permute-done((bf16[256,2048]{1,0:T(8,128)(2,1)S(1)}, bf16[256,2048]{1,0:T(8,128)(2,1)}, u32[]{:S(2)}, u32[]{:S(2)}) %collective-permute-start.14) | collective-permute-done | bytes 1048608 | tf_op jit(solution)/shard_map/ppermute | solution.py:94
  744.9 3.6 fusion.48
  749.3 6.2 collective-permute-start.22
  760.6 4.7 collective-permute-start.15
  770.5 7.8 collective-permute-done.22
  778.4 7.9 collective-permute-done.25
  789.5 10.2 %collective-permute-done.15 = bf16[256,2048]{1,0:T(8,128)(2,1)S(1)} collective-permute-done((bf16[256,2048]{1,0:T(8,128)(2,1)}, bf16[256,2048]{1,0:T(8,128)(2,1)S(1)}, u32[]{:S(2)}, u32[]{:S(2)}) %collective-permute-start.15) | collective-permute-done | bytes 1048608 | tf_op jit(solution)/shard_map/ppermute | solution.py:94
  799.8 8.0 collective-permute-done.18
  807.8 4.6 convert_reduce_fusion.2
  813.8 16.3 %collective-permute-start.27 = (f32[20480]{0:T(1024)S(1)}, f32[20480]{0:T(1024)S(1)}, u32[]{:S(2)}, u32[]{:S(2)}) collective-permute-start(f32[20480]{0:T(1024)S(1)} %add.412), channel_id=1, source_target_pairs={{0,8},{4,12},{8,0},{12,4},{16,24},{20,28},{24,16},{28,20},{1,9},{5... | collective-permute-start | bytes 245768 | tf_op jit(solution)/shard_map/ppermute | solution.py:33
  833.6 5.9 collective-permute-done.28
  845.8 4.1 convert_element_type.576
  851.9 11.7 %maximum_convert_fusion = f32[2048,2048]{1,0:T(8,128)} fusion(bf16[2048,1024]{1,0:T(8,128)(2,1)} %all-gather.22.cloned.1.call-done, bf16[2048,1024]{1,0:T(8,128)(2,1)} %all-gather.20.cloned.1.call-done), kind=kLoop, calls=%fused_computation.11 | loop fusion | flops 16777216 | bytes 25165824 | tf_op jit(solution)/shard_map/concatenate | solution.py:513
  863.7 9.3 convert_element_type.577
  873.0 21.9 %copy.134 = f32[96,8,8,512]{3,2,1,0:T(8,128)} copy(f32[96,8,8,512]{3,1,2,0:T(8,128)} %bitcast.259) | data formatting | bytes 25165824
  894.9 17.9 %copy.111 = f32[512,12,8,64]{0,3,2,1:T(8,128)} copy(f32[512,12,8,64]{0,2,3,1:T(8,128)} %bitcast.260) | data formatting | bytes 25165824 | tf_op jit(solution)/shard_map/convert_element_type | solution.py:494
  912.8 12.6 %copy.116 = f32[512,6144]{1,0:T(8,128)} copy(f32[512,6144]{0,1:T(8,128)} %bitcast.261) | data formatting | bytes 25165824
  925.5 16.5 %reshape.278 = f32[8,512,4,256]{3,2,1,0:T(4,128)} reshape(bf16[4096,1024]{1,0:T(8,128)(2,1)} %all-gather.28.cloned.1.call-done) | data formatting | bytes 25165824 | tf_op jit(solution)/shard_map/convert_element_type | solution.py:494
  941.9 15.2 %copy.114 = f32[8,512,4,256]{3,0,2,1:T(8,128)S(1)} copy(f32[8,512,4,256]{3,2,1,0:T(4,128)} %reshape.278) | data formatting | bytes 33554432 | tf_op jit(solution)/shard_map/convert_element_type | solution.py:494
  957.1 18.0 %copy.135 = f32[64,8,32,256]{3,1,2,0:T(8,128)} copy(f32[64,8,32,256]{3,2,1,0:T(8,128)S(1)} %bitcast.258) | data formatting | bytes 33554432
  (246 shorter events, 150.9 us)
Async XLA Ops:
  7.2 18.0 %copy-start.5 = (bf16[1,256,2048]{2,1,0:T(8,128)(2,1)S(1)}, bf16[1,256,2048]{2,1,0:T(8,128)(2,1)}, u32[]{:S(2)}) copy-start(bf16[1,256,2048]{2,1,0:T(8,128)(2,1)} %param.14) | copy-start | bytes 3145732
  7.2 95.7 %all-gather.18.cloned.1.call-start = ((), (), s32[]{:S(2)}) async-start(), calls=%async_computation.2 | async-start | bytes 4718592 | tf_op jit(solution)/shard_map/all_gather | solution.py:370
  9.6 98.3 %all-gather.16.cloned.1.call-start = ((), (), s32[]{:S(2)}) async-start(), calls=%async_computation.1 | async-start | bytes 4718592 | tf_op jit(solution)/shard_map/all_gather | solution.py:370
  10.3 179.7 %all-gather.14.cloned.1.call-start = ((), (), s32[]{:S(2)}) async-start(), calls=%async_computation | async-start | bytes 9437184 | tf_op jit(solution)/shard_map/all_gather | solution.py:391
  25.1 243.1 %copy-start.13 = (bf16[4,1,5632]{2,0,1:T(4,128)(2,1)}, bf16[4,1,5632]{2,0,1:T(4,128)(2,1)S(1)}, u32[]{:S(2)}) copy-start(bf16[4,1,5632]{2,0,1:T(4,128)(2,1)S(1)} %copy.138) | copy-start | bytes 135172
  25.1 11.1 %copy-start.14 = (f32[1,4,4,128]{3,1,2,0:T(4,128)}, f32[1,4,4,128]{3,1,2,0:T(4,128)S(1)}, u32[]{:S(2)}) copy-start(f32[1,4,4,128]{3,1,2,0:T(4,128)S(1)} %copy.129) | copy-start | bytes 24580
  27.3 818.6 %all-gather.26.cloned.1.call-start = ((), (), s32[]{:S(2)}) async-start(), calls=%async_computation.6 | async-start | bytes 2359296 | tf_op jit(solution)/shard_map/all_gather | solution.py:489
  38.3 40.1 %collective-permute-start = (bf16[512,768]{0,1:T(8,128)(2,1)}, bf16[512,768]{0,1:T(8,128)(2,1)}, u32[]{:S(2)}, u32[]{:S(2)}) collective-permute-start(bf16[512,768]{0,1:T(8,128)(2,1)} %bitcast.4), channel_id=1, source_target_pairs={{0,2},{1,3},{2,0},{3,1},{4,6},{5,7},{6,4},{7,5},{8,10},{9,11},{10,... | collective-permute-start | bytes 2359304 | tf_op jit(solution)/shard_map/ppermute | solution.py:33
  39.8 50.3 %collective-permute-start.1 = (bf16[512,768]{0,1:T(8,128)(2,1)}, bf16[512,768]{0,1:T(8,128)(2,1)}, u32[]{:S(2)}, u32[]{:S(2)}) collective-permute-start(bf16[512,768]{0,1:T(8,128)(2,1)} %bitcast.4), channel_id=1, source_target_pairs={{0,1},{1,0},{2,3},{3,2},{4,5},{5,4},{6,7},{7,6},{8,9},{9,8},{10,11... | collective-permute-start | bytes 2359304 | tf_op jit(solution)/shard_map/ppermute | solution.py:33
  43.2 17.8 %copy-start.26 = (s32[1,4]{1,0:T(1,128)S(1)}, s32[1,4]{1,0:T(1,128)}, u32[]{:S(2)}) copy-start(s32[1,4]{1,0:T(1,128)} %param.16) | copy-start | bytes 52
  43.2 34.7 %collective-permute-start.3 = (bf16[64,2048]{1,0:T(8,128)(2,1)}, bf16[64,2048]{1,0:T(8,128)(2,1)S(1)}, u32[]{:S(2)}, u32[]{:S(2)}) collective-permute-start(bf16[64,2048]{1,0:T(8,128)(2,1)} %get-tuple-element.82), channel_id=1, source_target_pairs={{0,1},{1,0},{2,3},{3,2},{4,5},{5,4},{6,7},{7,6},{8,9},{9,8},{10,11... | collective-permute-start | bytes 786440 | tf_op jit(solution)/shard_map/ppermute | solution.py:33
  44.7 35.9 %collective-permute-start.4 = (bf16[64,2048]{1,0:T(8,128)(2,1)}, bf16[64,2048]{1,0:T(8,128)(2,1)}, u32[]{:S(2)}, u32[]{:S(2)}) collective-permute-start(bf16[64,2048]{1,0:T(8,128)(2,1)} %get-tuple-element.82), channel_id=1, source_target_pairs={{0,2},{1,3},{2,0},{3,1},{4,6},{5,7},{6,4},{7,5},{8,10},{9,11},{10,... | collective-permute-start | bytes 786440 | tf_op jit(solution)/shard_map/ppermute | solution.py:33
  59.5 213.6 %collective-permute-start.6 = (bf16[512,1024]{0,1:T(8,128)(2,1)}, bf16[512,1024]{0,1:T(8,128)(2,1)}, u32[]{:S(2)}, u32[]{:S(2)}) collective-permute-start(bf16[512,1024]{0,1:T(8,128)(2,1)} %bitcast.10), channel_id=1, source_target_pairs={{0,1},{1,0},{2,3},{3,2},{4,5},{5,4},{6,7},{7,6},{8,9},{9,8},{10,11... | collective-permute-start | bytes 3145736 | tf_op jit(solution)/shard_map/ppermute | solution.py:33
  77.9 9.2 collective-permute-start.5
  78.4 23.4 %collective-permute-start.2 = (bf16[512,768]{0,1:T(8,128)(2,1)}, bf16[512,768]{0,1:T(8,128)(2,1)S(1)}, u32[]{:S(2)}, u32[]{:S(2)}) collective-permute-start(bf16[512,768]{0,1:T(8,128)(2,1)} %collective-permute-done), channel_id=1, source_target_pairs={{0,1},{1,0},{2,3},{3,2},{4,5},{5,4},{6,7},{7,6},{8,9},{9,8},{10,11... | collective-permute-start | bytes 2359304 | tf_op jit(solution)/shard_map/ppermute | solution.py:33
  80.7 200.2 %collective-permute-start.7 = (bf16[512,1024]{0,1:T(8,128)(2,1)}, bf16[512,1024]{0,1:T(8,128)(2,1)S(1)}, u32[]{:S(2)}, u32[]{:S(2)}) collective-permute-start(bf16[512,1024]{0,1:T(8,128)(2,1)} %bitcast.10), channel_id=1, source_target_pairs={{0,2},{1,3},{2,0},{3,1},{4,6},{5,7},{6,4},{7,5},{8,10},{9,11},{10,... | collective-permute-start | bytes 3145736 | tf_op jit(solution)/shard_map/ppermute | solution.py:33
  202.0 57.1 %copy-start.22 = (bf16[2048,1024]{1,0:T(8,128)(2,1)S(1)}, bf16[2048,1024]{1,0:T(8,128)(2,1)}, u32[]{:S(2)}) copy-start(bf16[2048,1024]{1,0:T(8,128)(2,1)} %all-gather.16.cloned.1.call-done) | copy-start | bytes 12582916
  263.2 17.4 %collective-permute-start.33 = (bf16[2,64,2048]{2,1,0:T(8,128)(2,1)S(1)}, bf16[2,64,2048]{2,1,0:T(8,128)(2,1)S(1)}, u32[]{:S(2)}, u32[]{:S(2)}) collective-permute-start(bf16[2,64,2048]{2,1,0:T(8,128)(2,1)S(1)} %fusion.57), channel_id=1, source_target_pairs={{0,1},{1,0},{2,3},{3,2},{4,5},{5,4},{6,7},{7,6},{8,9},{9,8},{10,11... | collective-permute-start | bytes 1572872 | tf_op jit(solution)/shard_map/ppermute | solution.py:33
  273.1 26.2 %collective-permute-start.8 = (bf16[512,1024]{0,1:T(8,128)(2,1)}, bf16[512,1024]{0,1:T(8,128)(2,1)S(1)}, u32[]{:S(2)}, u32[]{:S(2)}) collective-permute-start(bf16[512,1024]{0,1:T(8,128)(2,1)} %collective-permute-done.6), channel_id=1, source_target_pairs={{0,2},{1,3},{2,0},{3,1},{4,6},{5,7},{6,4},{7,5},{8,10},{9,11},{10,... | collective-permute-start | bytes 3145736 | tf_op jit(solution)/shard_map/ppermute | solution.py:33
  280.7 23.2 %collective-permute-start.34 = (bf16[64,2048]{1,0:T(8,128)(2,1)S(1)}, bf16[64,2048]{1,0:T(8,128)(2,1)S(1)}, u32[]{:S(2)}, u32[]{:S(2)}) collective-permute-start(bf16[64,2048]{1,0:T(8,128)(2,1)S(1)} %dynamic-slice_bitcast_fusion.14), channel_id=1, source_target_pairs={{0,2},{1,3},{2,0},{3,1},{4,6},{5,7},{6,4},{7,5},{8,10},{9,11},{10,... | collective-permute-start | bytes 786440 | tf_op jit(solution)/shard_map/ppermute | solution.py:33
  304.8 547.2 %all-gather.22.cloned.1.call-start = ((), (), s32[]{:S(2)}) async-start(), calls=%async_computation.4 | async-start | bytes 4718592 | tf_op jit(solution)/shard_map/all_gather | solution.py:485
  304.8 16.8 %copy-start.24 = (bf16[2048,1024]{1,0:T(8,128)(2,1)S(1)}, bf16[2048,1024]{1,0:T(8,128)(2,1)}, u32[]{:S(2)}) copy-start(bf16[2048,1024]{1,0:T(8,128)(2,1)} %all-gather.18.cloned.1.call-done) | copy-start | bytes 12582916
  326.5 24.1 %collective-permute-start.39 = (bf16[2,256,1024]{2,1,0:T(8,128)(2,1)S(1)}, bf16[2,256,1024]{2,1,0:T(8,128)(2,1)S(1)}, u32[]{:S(2)}, u32[]{:S(2)}) collective-permute-start(bf16[2,256,1024]{2,1,0:T(8,128)(2,1)S(1)} %dynamic-slice_bitcast_fusion.3), channel_id=1, source_target_pairs={{0,2},{1,3},{2,0},{3,1},{4,6},{5,7},{6,4},{7,5},{8,10},{9,11},{10,... | collective-permute-start | bytes 3145736 | tf_op jit(solution)/shard_map/ppermute | solution.py:33
  351.1 12.0 %collective-permute-start.40 = (bf16[256,1024]{1,0:T(8,128)(2,1)S(1)}, bf16[256,1024]{1,0:T(8,128)(2,1)S(1)}, u32[]{:S(2)}, u32[]{:S(2)}) collective-permute-start(bf16[256,1024]{1,0:T(8,128)(2,1)S(1)} %dynamic-slice_bitcast_fusion.12), channel_id=1, source_target_pairs={{0,1},{1,0},{2,3},{3,2},{4,5},{5,4},{6,7},{7,6},{8,9},{9,8},{10,11... | collective-permute-start | bytes 1572872 | tf_op jit(solution)/shard_map/ppermute | solution.py:33
  364.1 487.8 %all-gather.20.cloned.1.call-start = ((), (), s32[]{:S(2)}) async-start(), calls=%async_computation.3 | async-start | bytes 4718592 | tf_op jit(solution)/shard_map/all_gather | solution.py:485
  372.3 22.3 %collective-permute-start.37 = (bf16[2,256,1024]{2,1,0:T(8,128)(2,1)S(1)}, bf16[2,256,1024]{2,1,0:T(8,128)(2,1)S(1)}, u32[]{:S(2)}, u32[]{:S(2)}) collective-permute-start(bf16[2,256,1024]{2,1,0:T(8,128)(2,1)S(1)} %dynamic-slice_bitcast_fusion.4), channel_id=1, source_target_pairs={{0,1},{1,0},{2,3},{3,2},{4,5},{5,4},{6,7},{7,6},{8,9},{9,8},{10,11... | collective-permute-start | bytes 3145736 | tf_op jit(solution)/shard_map/ppermute | solution.py:33
  395.1 10.4 %collective-permute-start.38 = (bf16[256,1024]{1,0:T(8,128)(2,1)S(1)}, bf16[256,1024]{1,0:T(8,128)(2,1)S(1)}, u32[]{:S(2)}, u32[]{:S(2)}) collective-permute-start(bf16[256,1024]{1,0:T(8,128)(2,1)S(1)} %dynamic-slice_bitcast_fusion.13), channel_id=1, source_target_pairs={{0,2},{1,3},{2,0},{3,1},{4,6},{5,7},{6,4},{7,5},{8,10},{9,11},{10,... | collective-permute-start | bytes 1572872 | tf_op jit(solution)/shard_map/ppermute | solution.py:33
  406.5 457.1 %all-gather.24.cloned.1.call-start = ((), (), s32[]{:S(2)}) async-start(), calls=%async_computation.5 | async-start | bytes 7077888 | tf_op jit(solution)/shard_map/all_gather | solution.py:488
  412.1 26.4 %collective-permute-start.9 = (bf16[256,2048]{1,0:T(8,128)(2,1)}, bf16[256,2048]{1,0:T(8,128)(2,1)}, u32[]{:S(2)}, u32[]{:S(2)}) collective-permute-start(bf16[256,2048]{1,0:T(8,128)(2,1)} %get-tuple-element.84), channel_id=1, source_target_pairs={{0,2},{1,3},{2,0},{3,1},{4,6},{5,7},{6,4},{7,5},{8,10},{9,11},{10,... | collective-permute-start | bytes 3145736 | tf_op jit(solution)/shard_map/ppermute | solution.py:33
  425.0 45.4 %collective-permute-start.31 = (bf16[2,512,768]{1,2,0:T(8,128)(2,1)}, bf16[2,512,768]{1,2,0:T(8,128)(2,1)}, u32[]{:S(2)}, u32[]{:S(2)}) collective-permute-start(bf16[2,512,768]{1,2,0:T(8,128)(2,1)} %bitcast.281), channel_id=1, source_target_pairs={{0,2},{1,3},{2,0},{3,1},{4,6},{5,7},{6,4},{7,5},{8,10},{9,11},{10,... | collective-permute-start | bytes 4718600 | tf_op jit(solution)/shard_map/ppermute | solution.py:33
  425.2 26.4 %collective-permute-start.10 = (bf16[256,2048]{1,0:T(8,128)(2,1)}, bf16[256,2048]{1,0:T(8,128)(2,1)}, u32[]{:S(2)}, u32[]{:S(2)}) collective-permute-start(bf16[256,2048]{1,0:T(8,128)(2,1)} %get-tuple-element.84), channel_id=1, source_target_pairs={{0,1},{1,0},{2,3},{3,2},{4,5},{5,4},{6,7},{7,6},{8,9},{9,8},{10,11... | collective-permute-start | bytes 3145736 | tf_op jit(solution)/shard_map/ppermute | solution.py:33
  438.5 30.2 %collective-permute-start.11 = (bf16[256,2048]{1,0:T(8,128)(2,1)}, bf16[256,2048]{1,0:T(8,128)(2,1)S(1)}, u32[]{:S(2)}, u32[]{:S(2)}) collective-permute-start(bf16[256,2048]{1,0:T(8,128)(2,1)} %collective-permute-done.9), channel_id=1, source_target_pairs={{0,1},{1,0},{2,3},{3,2},{4,5},{5,4},{6,7},{7,6},{8,9},{9,8},{10,11... | collective-permute-start | bytes 3145736 | tf_op jit(solution)/shard_map/ppermute | solution.py:33
  472.5 14.4 %collective-permute-start.32 = (bf16[512,768]{0,1:T(8,128)(2,1)S(1)}, bf16[512,768]{0,1:T(8,128)(2,1)S(1)}, u32[]{:S(2)}, u32[]{:S(2)}) collective-permute-start(bf16[512,768]{0,1:T(8,128)(2,1)S(1)} %dynamic-slice_bitcast_fusion.11), channel_id=1, source_target_pairs={{0,1},{1,0},{2,3},{3,2},{4,5},{5,4},{6,7},{7,6},{8,9},{9,8},{10,11... | collective-permute-start | bytes 2359304 | tf_op jit(solution)/shard_map/ppermute | solution.py:33
  488.1 437.4 %all-gather.28.cloned.1.call-start = ((), (), s32[]{:S(2)}) async-start(), calls=%async_computation.7 | async-start | bytes 9437184 | tf_op jit(solution)/shard_map/all_gather | solution.py:487
  517.5 16.4 %copy-start.9 = (bf16[2048,768]{1,0:T(8,128)(2,1)S(1)}, bf16[2048,768]{1,0:T(8,128)(2,1)}, u32[]{:S(2)}) copy-start(bf16[2048,768]{1,0:T(8,128)(2,1)} %get-tuple-element.15) | copy-start | bytes 9437188
  517.5 41.3 %collective-permute-start.35 = (bf16[2,512,1024]{2,1,0:T(8,128)(2,1)S(1)}, bf16[2,512,1024]{2,1,0:T(8,128)(2,1)S(1)}, u32[]{:S(2)}, u32[]{:S(2)}) collective-permute-start(bf16[2,512,1024]{2,1,0:T(8,128)(2,1)S(1)} %dynamic-slice_bitcast_fusion.2), channel_id=1, source_target_pairs={{0,1},{1,0},{2,3},{3,2},{4,5},{5,4},{6,7},{7,6},{8,9},{9,8},{10,11... | collective-permute-start | bytes 6291464 | tf_op jit(solution)/shard_map/ppermute | solution.py:33
  547.2 14.4 %copy-start.28 = (bf16[2048,1024]{1,0:T(8,128)(2,1)S(1)}, bf16[2048,1024]{1,0:T(8,128)(2,1)}, u32[]{:S(2)}) copy-start(bf16[2048,1024]{1,0:T(8,128)(2,1)} %copy-done.27) | copy-start | bytes 12582916
  559.8 17.9 %collective-permute-start.36 = (bf16[512,1024]{1,0:T(8,128)(2,1)S(1)}, bf16[512,1024]{1,0:T(8,128)(2,1)S(1)}, u32[]{:S(2)}, u32[]{:S(2)}) collective-permute-start(bf16[512,1024]{1,0:T(8,128)(2,1)S(1)} %dynamic-slice_bitcast_fusion.5), channel_id=1, source_target_pairs={{0,2},{1,3},{2,0},{3,1},{4,6},{5,7},{6,4},{7,5},{8,10},{9,11},{10,... | collective-permute-start | bytes 3145736 | tf_op jit(solution)/shard_map/ppermute | solution.py:33
  584.0 15.0 %collective-permute-start.19 = (bf16[4,256,2048]{2,1,0:T(8,128)(2,1)}, bf16[4,256,2048]{2,1,0:T(8,128)(2,1)}, u32[]{:S(2)}, u32[]{:S(2)}) collective-permute-start(bf16[4,256,2048]{2,1,0:T(8,128)(2,1)} %dynamic-slice_bitcast_fusion), channel_id=1, source_target_pairs={{0,4},{4,0},{8,12},{12,8},{16,20},{20,16},{24,28},{28,24},{1,5},{5... | collective-permute-start | bytes 12582920 | tf_op jit(solution)/shard_map/ppermute | solution.py:33
  598.6 8.6 collective-permute-start.12
  605.0 47.3 %collective-permute-start.20 = (bf16[256,2048]{1,0:T(8,128)(2,1)S(1)}, bf16[256,2048]{1,0:T(8,128)(2,1)}, u32[]{:S(2)}, u32[]{:S(2)}) collective-permute-start(bf16[256,2048]{1,0:T(8,128)(2,1)S(1)} %get-tuple-element.87), channel_id=1, source_target_pairs={{0,8},{4,12},{1,9},{5,13},{2,10},{6,14},{3,11},{7,15}} | collective-permute-start | bytes 3145736 | tf_op jit(solution)/shard_map/ppermute | solution.py:94
  614.5 82.7 %collective-permute-start.13 = (bf16[256,2048]{1,0:T(8,128)(2,1)}, bf16[256,2048]{1,0:T(8,128)(2,1)}, u32[]{:S(2)}, u32[]{:S(2)}) collective-permute-start(bf16[256,2048]{1,0:T(8,128)(2,1)} %get-tuple-element.91), channel_id=1, source_target_pairs={{0,8},{4,12},{1,9},{5,13},{2,10},{6,14},{3,11},{7,15}} | collective-permute-start | bytes 3145736 | tf_op jit(solution)/shard_map/ppermute | solution.py:94
  616.8 87.8 %collective-permute-start.23 = (bf16[256,2048]{1,0:T(8,128)(2,1)S(1)}, bf16[256,2048]{1,0:T(8,128)(2,1)}, u32[]{:S(2)}, u32[]{:S(2)}) collective-permute-start(bf16[256,2048]{1,0:T(8,128)(2,1)S(1)} %get-tuple-element.88), channel_id=1, source_target_pairs={{24,16},{28,20},{25,17},{29,21},{26,18},{30,22},{27,19},{31,23}} | collective-permute-start | bytes 3145736 | tf_op jit(solution)/shard_map/ppermute | solution.py:97
  655.1 67.6 %collective-permute-start.21 = (bf16[256,2048]{1,0:T(8,128)(2,1)}, bf16[256,2048]{1,0:T(8,128)(2,1)}, u32[]{:S(2)}, u32[]{:S(2)}) collective-permute-start(bf16[256,2048]{1,0:T(8,128)(2,1)} %fusion.42), channel_id=1, source_target_pairs={{0,8},{4,12},{8,16},{12,20},{1,9},{5,13},{9,17},{13,21},{2,10},{6,... | collective-permute-start | bytes 3145736 | tf_op jit(solution)/shard_map/ppermute | solution.py:94
  660.6 68.2 %collective-permute-start.16 = (bf16[256,2048]{1,0:T(8,128)(2,1)S(1)}, bf16[256,2048]{1,0:T(8,128)(2,1)}, u32[]{:S(2)}, u32[]{:S(2)}) collective-permute-start(bf16[256,2048]{1,0:T(8,128)(2,1)S(1)} %get-tuple-element.92), channel_id=1, source_target_pairs={{24,16},{28,20},{25,17},{29,21},{26,18},{30,22},{27,19},{31,23}} | collective-permute-start | bytes 3145736 | tf_op jit(solution)/shard_map/ppermute | solution.py:97
  699.2 45.7 %collective-permute-start.14 = (bf16[256,2048]{1,0:T(8,128)(2,1)S(1)}, bf16[256,2048]{1,0:T(8,128)(2,1)}, u32[]{:S(2)}, u32[]{:S(2)}) collective-permute-start(bf16[256,2048]{1,0:T(8,128)(2,1)S(1)} %fusion.47), channel_id=1, source_target_pairs={{0,8},{4,12},{8,16},{12,20},{1,9},{5,13},{9,17},{13,21},{2,10},{6,... | collective-permute-start | bytes 3145736 | tf_op jit(solution)/shard_map/ppermute | solution.py:94
  704.6 40.3 %copy-start.3 = (bf16[4,256,2048]{2,1,0:T(8,128)(2,1)S(1)}, bf16[4,256,2048]{2,1,0:T(8,128)(2,1)}, u32[]{:S(2)}) copy-start(bf16[4,256,2048]{2,1,0:T(8,128)(2,1)} %copy-done.2) | copy-start | bytes 12582916
  727.1 28.4 %collective-permute-start.24 = (bf16[256,2048]{1,0:T(8,128)(2,1)}, bf16[256,2048]{1,0:T(8,128)(2,1)}, u32[]{:S(2)}, u32[]{:S(2)}) collective-permute-start(bf16[256,2048]{1,0:T(8,128)(2,1)} %get-tuple-element.86), channel_id=1, source_target_pairs={{16,8},{20,12},{24,16},{28,20},{17,9},{21,13},{25,17},{29,21},{18,... | collective-permute-start | bytes 3145736 | tf_op jit(solution)/shard_map/ppermute | solution.py:97
  748.5 16.8 %collective-permute-start.17 = (bf16[256,2048]{1,0:T(8,128)(2,1)}, bf16[256,2048]{1,0:T(8,128)(2,1)S(1)}, u32[]{:S(2)}, u32[]{:S(2)}) collective-permute-start(bf16[256,2048]{1,0:T(8,128)(2,1)} %get-tuple-element.90), channel_id=1, source_target_pairs={{16,8},{20,12},{24,16},{28,20},{17,9},{21,13},{25,17},{29,21},{18,... | collective-permute-start | bytes 3145736 | tf_op jit(solution)/shard_map/ppermute | solution.py:97
  749.3 37.0 %copy-start.6 = (bf16[1,256,2048]{2,1,0:T(8,128)(2,1)S(1)}, bf16[1,256,2048]{2,1,0:T(8,128)(2,1)}, u32[]{:S(2)}) copy-start(bf16[1,256,2048]{2,1,0:T(8,128)(2,1)} %param.14) | copy-start | bytes 3145732
  749.3 37.0 %copy-start.15 = (f32[1,4,4,128]{3,1,2,0:T(4,128)S(1)}, f32[1,4,4,128]{3,1,2,0:T(4,128)}, u32[]{:S(2)}) copy-start(f32[1,4,4,128]{3,1,2,0:T(4,128)} %copy-done.14) | copy-start | bytes 24580
  749.3 37.0 %copy-start.17 = (f32[256]{0:T(256)S(1)}, f32[256]{0:T(256)}, u32[]{:S(2)}) copy-start(f32[256]{0:T(256)} %copy-done.16) | copy-start | bytes 3076
  749.3 37.0 %copy-start.19 = (f32[256]{0:T(256)S(1)}, f32[256]{0:T(256)}, u32[]{:S(2)}) copy-start(f32[256]{0:T(256)} %copy-done.18) | copy-start | bytes 3076
  749.3 29.1 %collective-permute-start.22 = (bf16[256,2048]{1,0:T(8,128)(2,1)}, bf16[256,2048]{1,0:T(8,128)(2,1)}, u32[]{:S(2)}, u32[]{:S(2)}) collective-permute-start(bf16[256,2048]{1,0:T(8,128)(2,1)} %get-tuple-element.85), channel_id=1, source_target_pairs={{0,8},{4,12},{8,16},{12,20},{16,24},{20,28},{1,9},{5,13},{9,17},{1... | collective-permute-start | bytes 3145736 | tf_op jit(solution)/shard_map/ppermute | solution.py:94
  758.4 27.9 %collective-permute-start.25 = (bf16[256,2048]{1,0:T(8,128)(2,1)}, bf16[256,2048]{1,0:T(8,128)(2,1)}, u32[]{:S(2)}, u32[]{:S(2)}) collective-permute-start(bf16[256,2048]{1,0:T(8,128)(2,1)} %fusion.41), channel_id=1, source_target_pairs={{8,0},{12,4},{16,8},{20,12},{24,16},{28,20},{9,1},{13,5},{17,9},{2... | collective-permute-start | bytes 3145736 | tf_op jit(solution)/shard_map/ppermute | solution.py:97
  760.6 39.2 %collective-permute-start.15 = (bf16[256,2048]{1,0:T(8,128)(2,1)}, bf16[256,2048]{1,0:T(8,128)(2,1)S(1)}, u32[]{:S(2)}, u32[]{:S(2)}) collective-permute-start(bf16[256,2048]{1,0:T(8,128)(2,1)} %get-tuple-element.89), channel_id=1, source_target_pairs={{0,8},{4,12},{8,16},{12,20},{16,24},{20,28},{1,9},{5,13},{9,17},{1... | collective-permute-start | bytes 3145736 | tf_op jit(solution)/shard_map/ppermute | solution.py:94
  767.9 39.8 %copy-start.7 = (bf16[1,256,2048]{2,1,0:T(8,128)(2,1)S(1)}, bf16[1,256,2048]{2,1,0:T(8,128)(2,1)}, u32[]{:S(2)}) copy-start(bf16[1,256,2048]{2,1,0:T(8,128)(2,1)} %param.27) | copy-start | bytes 3145732
  767.9 39.8 %collective-permute-start.18 = (bf16[256,2048]{1,0:T(8,128)(2,1)}, bf16[256,2048]{1,0:T(8,128)(2,1)}, u32[]{:S(2)}, u32[]{:S(2)}) collective-permute-start(bf16[256,2048]{1,0:T(8,128)(2,1)} %fusion.46), channel_id=1, source_target_pairs={{8,0},{12,4},{16,8},{20,12},{24,16},{28,20},{9,1},{13,5},{17,9},{2... | collective-permute-start | bytes 3145736 | tf_op jit(solution)/shard_map/ppermute | solution.py:97
  812.4 1.3 collective-permute-start.26
  813.8 19.0 %collective-permute-start.27 = (f32[20480]{0:T(1024)S(1)}, f32[20480]{0:T(1024)S(1)}, u32[]{:S(2)}, u32[]{:S(2)}) collective-permute-start(f32[20480]{0:T(1024)S(1)} %add.412), channel_id=1, source_target_pairs={{0,8},{4,12},{8,0},{12,4},{16,24},{20,28},{24,16},{28,20},{1,9},{5... | collective-permute-start | bytes 245768 | tf_op jit(solution)/shard_map/ppermute | solution.py:33
  832.8 6.7 collective-permute-start.28
  839.5 4.5 collective-permute-start.29
  844.1 5.9 collective-permute-start.30
  851.9 123.2 %copy-start.20 = (f32[512]{0:T(512)}, f32[512]{0:T(512)S(1)}, u32[]{:S(2)}) copy-start(f32[512]{0:T(512)S(1)} %get-tuple-element.137) | copy-start | bytes 6148
  (14 other events, 84.0 us)
Sparse Core Ops, SparseCore 0:
  9.7 49.8 all-gather.17
  61.2 45.8 all-gather.15
  109.3 80.7 all-gather.13
  304.9 25.7 all-gather.25
  364.3 44.6 all-gather.21
  410.4 45.8 all-gather.19
  488.2 63.6 all-gather.23
  579.2 124.0 all-gather.27

commit v2 on v1

v2 whole, which is shorter than its diff:
```python
import functools

import jax
import jax.numpy as jnp
from jax import lax
from jax.experimental import pallas as pl
from jax.experimental.pallas import tpu as pltpu
from jax.sharding import PartitionSpec as P

HEAD_DIM = 64
ROT = 32
BLK = 16
TILE = 256
LANES = 128
F32 = jnp.float32
BF16 = jnp.bfloat16


def dot_nn(left, right):
    return lax.dot_general(left, right, (((1,), (0,)), ((), ())), preferred_element_type=F32)


def dot_nt(left, right):
    return lax.dot_general(left, right, (((1,), (1,)), ((), ())), preferred_element_type=F32)


def dot_tn(left, right):
    return lax.dot_general(left, right, (((0,), (0,)), ((), ())), preferred_element_type=F32)


def bits_of(axis):
    return range(lax.axis_size(axis).bit_length() - 1)


def swaps(axis, mask):
    return axis, [(i, i ^ mask) for i in range(lax.axis_size(axis))]


class Flow:
    def __init__(self, steps):
        self.steps = steps
        self.result = None
        self.moves = next(steps)

    def arrive(self, values):
        try:
            self.moves = self.steps.send(values)
        except StopIteration as stop:
            self.moves, self.result = [], stop.value


def beside(work, inputs, flows, late=(), early=()):
    starting = [*flows, *late]
    sends = [[value for value, _, _ in flow.moves] for flow in starting]
    inputs, sends = lax.optimization_barrier((inputs, sends))
    for flow, values in zip(starting, sends):
        flow.moving = [
            lax.ppermute(value, axis, pairs) for value, (_, axis, pairs) in zip(values, flow.moves)
        ]
    outputs = work(*inputs)
    ending = [*flows, *early]
    outputs, arrived = lax.optimization_barrier((outputs, [flow.moving for flow in ending]))
    for flow, values in zip(ending, arrived):
        flow.arrive(values)
    return outputs


def gather_steps(own, *orders):
    share = own.shape[0] // len(orders)
    held = [[(0, own[i * share : (i + 1) * share])] for i in range(len(orders))]
    for step in range(len(orders[0])):
        moves = [
            (piece, *swaps("fsdp", 1 << order[step]))
            for pieces, order in zip(held, orders)
            for _, piece in pieces
        ]
        arrived = iter((yield moves))
        for i, order in enumerate(orders):
            held[i] = held[i] + [(mask ^ (1 << order[step]), next(arrived)) for mask, _ in held[i]]
    return [
        (mask, i * share, piece) for i, pieces in enumerate(held) for mask, piece in pieces
    ]


def direct_steps(own):
    masks = range(1, lax.axis_size("fsdp"))
    arrived = yield [(own, *swaps("fsdp", mask)) for mask in masks]
    return [(0, 0, own)] + [(mask, 0, piece) for mask, piece in zip(masks, arrived)]


def scatter_steps(parts, *orders):
    index = lax.axis_index("fsdp")
    bits = len(orders[0])
    share = parts.shape[1] // len(orders)
    held = [
        parts[:, i * share : (i + 1) * share].reshape((2,) * bits + (share, parts.shape[2]))
        for i in range(len(orders))
    ]
    left = [list(range(bits))[::-1] for _ in orders]
    for step in range(bits):
        moves, keeps = [], []
        for i, order in enumerate(orders):
            axis = left[i].index(order[step])
            left[i].pop(axis)
            mine = (index >> order[step]) & 1
            send = lax.dynamic_index_in_dim(held[i], 1 - mine, axis, keepdims=False)
            keeps.append(lax.dynamic_index_in_dim(held[i], mine, axis, keepdims=False))
            moves.append((send, *swaps("fsdp", 1 << order[step])))
        arrived = yield moves
        held = [
            (keep.astype(F32) + got.astype(F32)).astype(BF16) for keep, got in zip(keeps, arrived)
        ]
    return jnp.concatenate(held, axis=0)


def line_steps(mine, other):
    count = lax.axis_size("ctx")
    line = count // 2
    place = lax.axis_index("ctx") // 2
    (got,) = yield [(other, *swaps("ctx", 1))]

    def block(target):
        target = jnp.clip(target, 0, line - 1)
        return sum(
            lax.dynamic_index_in_dim(half, target, 0, keepdims=False).astype(F32)
            for half in (mine, got)
        )

    for step in range(line - 1):
        far = line - 1 - step
        up = block(place + far)
        down = block(place - far)
        if step:
            up, down = up + ups.astype(F32), down + downs.astype(F32)
        ups, downs = yield [
            (up.astype(BF16), "ctx", [(i, i + 2) for i in range(count - 2) if i // 2 + far < line]),
            (down.astype(BF16), "ctx", [(i, i - 2) for i in range(2, count) if i // 2 - far >= 0]),
        ]
    return block(place) + ups.astype(F32) + downs.astype(F32)


def total_steps(vector):
    for axis in ("ctx", "fsdp"):
        for bit in bits_of(axis):
            (got,) = yield [(vector, *swaps(axis, 1 << bit))]
            vector = vector + got
    return vector


def turn(values, cosine, sine):
    lane = lax.broadcasted_iota(jnp.int32, values.shape, 1) % HEAD_DIM
    half = ROT // 2
    partner = jnp.where(
        lane < half, pltpu.roll(values, LANES - half, 1), pltpu.roll(values, half, 1)
    )
    return values * cosine + partner * sine


def first_half(shape):
    return lax.broadcasted_iota(jnp.int32, shape, 1) < HEAD_DIM


def visible_range(ends_ref, step, tile):
    top = step * tile
    column = top + lax.broadcasted_iota(jnp.int32, (1, tile), 1)
    begin = jnp.zeros((1, tile), jnp.int32)
    first = jnp.int32(0)
    for sequence in range(ends_ref.shape[0]):
        end = ends_ref[sequence]
        begin = jnp.where(column >= end, jnp.maximum(begin, end), begin)
        first = jnp.where(top >= end, jnp.maximum(first, end), first)
    return column, begin, first // tile


def each_head(values, axis=1):
    half = lax.broadcasted_iota(jnp.int32, values.shape, axis) < HEAD_DIM
    zero = jnp.zeros_like(values)
    return [jnp.where(half, values, zero), jnp.where(half, zero, values)]


def part_lanes(pair, which):
    start = (3 * pair + which) * LANES
    return slice(start, start + LANES)


def forward_kernel(
    place_ref, ends_ref, cos_ref, sin_ref, lin_hbm,
    att_hbm, rows, summed_ref, lse_ref, lin, values_t, att, sems,
):
    tokens = lin.shape[0]
    tile = TILE
    tiles = tokens // tile
    blocks = tokens // BLK
    pairs = lin.shape[1] // LANES // 3
    heads = 2 * pairs

    @pl.loop(0, blocks)
    def _(block):
        source = pl.ds(pl.multiple_of(block * BLK, BLK), BLK)
        target = pl.ds(pl.multiple_of(place_ref[block] * BLK, BLK), BLK)
        pltpu.make_async_copy(lin_hbm.at[source], lin.at[target], sems.at[0]).start()

    pltpu.make_async_copy(lin_hbm, lin, sems.at[0]).wait()

    @pl.loop(0, tiles)
    def _(step):
        part = pl.ds(pl.multiple_of(step * tile, tile), tile)
        cosine, sine = cos_ref[part, :], sin_ref[part, :]
        for pair in range(pairs):
            q, k, v = (part_lanes(pair, i) for i in range(3))
            query = turn(lin[part, q], cosine, sine) * HEAD_DIM ** (-0.5)
            rows[part, q] = query.astype(BF16)
            rows[part, k] = turn(lin[part, k], cosine, sine).astype(BF16)
            value = lin[part, v].astype(BF16)
            rows[part, v] = value
            values_t[pair * LANES : (pair + 1) * LANES, part] = value.T

    @pl.loop(0, tiles)
    def _(step):
        part = pl.ds(pl.multiple_of(step * tile, tile), tile)
        column, begin, low = visible_range(ends_ref, step, tile)
        queries = [item for pair in range(pairs) for item in each_head(rows[part, part_lanes(pair, 0)].T, 0)]
        summed_ref[:, part] = jnp.zeros((heads * HEAD_DIM, tile), F32)

        def combine(index, state):
            there = pl.ds(pl.multiple_of(index * tile, tile), tile)
            row = index * tile + lax.broadcasted_iota(jnp.int32, (tile, tile), 0)
            visible = (row <= column) & (row >= begin)
            result = []
            for head in range(heads):
                top, total = state[head]
                here = slice(head * HEAD_DIM, (head + 1) * HEAD_DIM)
                key = rows[there, part_lanes(head // 2, 1)]
                scores = jnp.where(visible, dot_nn(key, queries[head]), -1e30)
                new_top = jnp.maximum(top, jnp.max(scores, axis=0, keepdims=True))
                weight = jnp.exp(scores - new_top)
                factor = jnp.exp(top - new_top)
                total = total * factor + jnp.sum(weight, axis=0, keepdims=True)
                summed_ref[here, part] = summed_ref[here, part] * factor + dot_nn(
                    values_t[here, there], weight.astype(BF16)
                )
                result.append((new_top, total))
            return tuple(result)

        empty = (jnp.full((1, tile), -1e30, F32), jnp.zeros((1, tile), F32))
        state = lax.fori_loop(low, step + 1, combine, (empty,) * heads)
        for head in range(heads):
            top, total = state[head]
            here = slice(head * HEAD_DIM, (head + 1) * HEAD_DIM)
            summed_ref[here, part] = summed_ref[here, part] * (1.0 / total)
            lse_ref[head : head + 1, part] = top + jnp.log(total)
        for pair in range(pairs):
            lanes = slice(pair * LANES, (pair + 1) * LANES)
            att[part, lanes] = summed_ref[lanes, part].T.astype(BF16)

    @pl.loop(0, blocks)
    def _(block):
        target = pl.ds(pl.multiple_of(block * BLK, BLK), BLK)
        source = pl.ds(pl.multiple_of(place_ref[block] * BLK, BLK), BLK)
        pltpu.make_async_copy(att.at[source], att_hbm.at[target], sems.at[0]).start()

    pltpu.make_async_copy(att, att_hbm, sems.at[0]).wait()


def backward_kernel(
    place_ref, ends_ref, cos_ref, sin_ref, rows, summed_ref, lse_ref, grad_hbm,
    mixed_hbm, grad, grad_t, keys_t, grad_q, grad_k, grad_v, mixed, sems,
):
    tokens = grad.shape[0]
    tile = TILE
    tiles = tokens // tile
    blocks = tokens // BLK
    pairs = grad.shape[1] // LANES
    heads = 2 * pairs

    @pl.loop(0, blocks)
    def _(block):
        source = pl.ds(pl.multiple_of(block * BLK, BLK), BLK)
        target = pl.ds(pl.multiple_of(place_ref[block] * BLK, BLK), BLK)
        pltpu.make_async_copy(grad_hbm.at[source], grad.at[target], sems.at[0]).start()

    grad_k[...] = jnp.zeros_like(grad_k)
    grad_v[...] = jnp.zeros_like(grad_v)

    @pl.loop(0, tiles)
    def _(step):
        part = pl.ds(pl.multiple_of(step * tile, tile), tile)
        for pair in range(pairs):
            keys_t[pair * LANES : (pair + 1) * LANES, part] = rows[part, part_lanes(pair, 1)].T

    pltpu.make_async_copy(grad_hbm, grad, sems.at[0]).wait()

    @pl.loop(0, tiles)
    def _(step):
        part = pl.ds(pl.multiple_of(step * tile, tile), tile)
        column, begin, low = visible_range(ends_ref, step, tile)
        queries, backs, delta, lse, queries_t, backs_t = [], [], [], [], [], []
        for pair in range(pairs):
            lanes = slice(pair * LANES, (pair + 1) * LANES)
            queries += each_head(rows[part, part_lanes(pair, 0)])
            backs += each_head(grad[part, lanes])
            queries_t += each_head(rows[part, part_lanes(pair, 0)].T, 0)
            backs_t += each_head(grad[part, lanes].T, 0)
            grad_t[lanes, :] = grad[part, lanes].T.astype(F32)
        for head in range(heads):
            here = slice(head * HEAD_DIM, (head + 1) * HEAD_DIM)
            delta.append(jnp.sum(summed_ref[here, part] * grad_t[here, :], axis=0, keepdims=True))
            lse.append(lse_ref[head : head + 1, part])
        grad_q[...] = jnp.zeros_like(grad_q)

        def back_step(index, _):
            there = pl.ds(pl.multiple_of(index * tile, tile), tile)
            row = index * tile + lax.broadcasted_iota(jnp.int32, (tile, tile), 0)
            visible = (row <= column) & (row >= begin)
            for head in range(heads):
                pair = head // 2
                lanes = slice(pair * LANES, (pair + 1) * LANES)
                here = slice(head * HEAD_DIM, (head + 1) * HEAD_DIM)
                key, value = rows[there, part_lanes(pair, 1)], rows[there, part_lanes(pair, 2)]
                scores = jnp.where(visible, dot_nn(key, queries_t[head]), -1e30)
                weight = jnp.exp(scores - lse[head])
                grad_w = dot_nn(value, backs_t[head])
                grad_s = (weight * (grad_w - delta[head])).astype(BF16)
                part_k = dot_nn(grad_s, queries[head])
                part_v = dot_nn(weight.astype(BF16), backs[head])
                add_k = part_k if head % 2 == 0 else add_k + part_k
                add_v = part_v if head % 2 == 0 else add_v + part_v
                grad_q[here, :] += dot_nn(keys_t[here, there], grad_s)
                if head % 2:
                    grad_k[there, lanes] += add_k
                    grad_v[there, lanes] += add_v
            return 0

        lax.fori_loop(low, step + 1, back_step, 0)
        for pair in range(pairs):
            lanes = slice(pair * LANES, (pair + 1) * LANES)
            turned = turn(grad_q[lanes, :].T * HEAD_DIM ** (-0.5), cos_ref[part, :], -sin_ref[part, :])
            mixed[part, part_lanes(pair, 0)] = turned.astype(BF16)

    @pl.loop(0, tiles)
    def _(step):
        part = pl.ds(pl.multiple_of(step * tile, tile), tile)
        cosine, sine = cos_ref[part, :], sin_ref[part, :]
        for pair in range(pairs):
            lanes = slice(pair * LANES, (pair + 1) * LANES)
            mixed[part, part_lanes(pair, 1)] = turn(grad_k[part, lanes], cosine, -sine).astype(BF16)
            mixed[part, part_lanes(pair, 2)] = grad_v[part, lanes].astype(BF16)

    @pl.loop(0, blocks)
    def _(block):
        target = pl.ds(pl.multiple_of(block * BLK, BLK), BLK)
        source = pl.ds(pl.multiple_of(place_ref[block] * BLK, BLK), BLK)
        pltpu.make_async_copy(mixed.at[source], mixed_hbm.at[target], sems.at[0]).start()

    pltpu.make_async_copy(mixed, mixed_hbm, sems.at[0]).wait()


def turn_tables(ends, tokens):
    position = jnp.arange(tokens, dtype=jnp.int32)
    begin = jnp.max(jnp.where(position[:, None] >= ends[None, :], ends[None, :], 0), axis=1)
    within = (position - begin).astype(F32)
    half = ROT // 2
    frequency = 10000.0 ** (-jnp.arange(half, dtype=F32) * 2.0 / ROT)
    angles = within[:, None] * frequency[None, :]
    cosine, sine = jnp.cos(angles), jnp.sin(angles)
    ones = jnp.ones((tokens, HEAD_DIM - ROT), F32)
    cos_table = jnp.concatenate([cosine, cosine, ones] * 2, axis=1)
    sin_table = jnp.concatenate([-sine, sine, 0.0 * ones] * 2, axis=1)
    return cos_table, sin_table


SMEM = pl.BlockSpec(memory_space=pltpu.SMEM)
VMEM = pl.BlockSpec(memory_space=pltpu.VMEM)
ANYWHERE = pl.BlockSpec(memory_space=pl.ANY)


def attention_forward(block_place, ends, tables, linear):
    tokens, width3 = linear.shape
    width = width3 // 3
    return pl.pallas_call(
        forward_kernel,
        out_shape=(
            jax.ShapeDtypeStruct((tokens, width), BF16),
            jax.ShapeDtypeStruct((tokens, width3), BF16),
            jax.ShapeDtypeStruct((width, tokens), F32),
            jax.ShapeDtypeStruct((width // HEAD_DIM, tokens), F32),
        ),
        in_specs=[SMEM, SMEM, VMEM, VMEM, ANYWHERE],
        out_specs=(ANYWHERE, VMEM, VMEM, VMEM),
        scratch_shapes=[
            pltpu.VMEM((tokens, width3), F32),
            pltpu.VMEM((width, tokens), BF16),
            pltpu.VMEM((tokens, width), BF16),
            pltpu.SemaphoreType.DMA((1,)),
        ],
        compiler_params=pltpu.CompilerParams(vmem_limit_bytes=48 << 20),
        cost_estimate=pl.CostEstimate(
            flops=40 * 10**9, bytes_accessed=16 * 10**6, transcendentals=0
        ),
    )(block_place, ends, *tables, linear)


def attention_backward(block_place, ends, tables, kept, grad_att):
    tokens, width = grad_att.shape
    return pl.pallas_call(
        backward_kernel,
        out_shape=jax.ShapeDtypeStruct((tokens, 3 * width), BF16),
        in_specs=[SMEM, SMEM] + [VMEM] * 5 + [ANYWHERE],
        out_specs=ANYWHERE,
        scratch_shapes=[
            pltpu.VMEM((tokens, width), BF16),
            pltpu.VMEM((width, TILE), F32),
            pltpu.VMEM((width, tokens), BF16),
            pltpu.VMEM((width, TILE), F32),
            pltpu.VMEM((tokens, width), F32),
            pltpu.VMEM((tokens, width), F32),
            pltpu.VMEM((tokens, 3 * width), BF16),
            pltpu.SemaphoreType.DMA((1,)),
        ],
        compiler_params=pltpu.CompilerParams(vmem_limit_bytes=48 << 20),
        cost_estimate=pl.CostEstimate(
            flops=40 * 10**9, bytes_accessed=16 * 10**6, transcendentals=0
        ),
    )(block_place, ends, *tables, *kept, grad_att)

def row_call(kernel, where, rows, whole, assembled, outs, sums, flops, split=False):
    count = rows[0].shape[0]
    tiles = count // TILE
    shards = lax.axis_size("fsdp")
    pieces = [piece for _, group in assembled for _, _, piece in group]
    scratch = [
        pltpu.VMEM(
            (height * (shards if group[0][0] is not None else 1), group[0][2].shape[1]), BF16
        )
        for height, group in assembled
    ]

    def tile_of(step, at):
        return step % (tiles // 2) * 2 + (at[1] ^ (step // (tiles // 2))) if split else step

    def body(at, *refs):
        inputs = refs[: len(rows) + len(whole)]
        sources = refs[len(inputs) : len(inputs) + len(pieces)]
        targets = refs[len(inputs) + len(pieces) : -len(scratch) - 1]
        buffers, sems = refs[-len(scratch) - 1 : -1], refs[-1]

        @pl.when(pl.program_id(0) == 0)
        def _():
            copies = []
            for buffer, (height, group) in zip(buffers, assembled):
                for mask, start, piece in group:
                    first = start if mask is None else (at[0] ^ mask) * height + start
                    size = piece.shape[0]
                    target = buffer.at[pl.ds(pl.multiple_of(first, size), size)]
                    slot = len(copies)
                    copies.append(pltpu.make_async_copy(sources[slot], target, sems.at[slot]))
            for copy in copies:
                copy.start()
            for copy in copies:
                copy.wait()

        if not split:
            kernel(*inputs, *buffers, *targets)
            return
        mine, other, *rest = targets

        @pl.when(pl.program_id(0) < tiles // 2)
        def _():
            kernel(*inputs, *buffers, mine.at[0], *rest)

        @pl.when(pl.program_id(0) >= tiles // 2)
        def _():
            kernel(*inputs, *buffers, other.at[0], *rest)

    by_tile = lambda columns: pl.BlockSpec((TILE, columns), lambda i, at: (tile_of(i, at), 0))
    stay = lambda shape: pl.BlockSpec(shape, lambda i, at: (0, 0))
    moved = sum(item.size * item.dtype.itemsize for item in (*rows, *whole, *pieces))
    moved += sum(count * columns * jnp.dtype(kind).itemsize for columns, kind in outs)
    if split:
        ((columns, kind),) = outs
        half = tiles // 2
        out_shape = [jax.ShapeDtypeStruct((half, TILE, columns), kind)] * 2
        out_specs = [
            pl.BlockSpec((1, TILE, columns), lambda i, at: (jnp.minimum(i, half - 1), 0, 0)),
            pl.BlockSpec((1, TILE, columns), lambda i, at: (jnp.maximum(i - half, 0), 0, 0)),
        ]
    else:
        out_shape = [jax.ShapeDtypeStruct((count, columns), kind) for columns, kind in outs]
        out_specs = [by_tile(columns) for columns, _ in outs]
    return pl.pallas_call(
        body,
        out_shape=out_shape + [jax.ShapeDtypeStruct(shape, F32) for shape in sums],
        grid_spec=pltpu.PrefetchScalarGridSpec(
            num_scalar_prefetch=1,
            grid=(tiles,),
            in_specs=[by_tile(item.shape[1]) for item in rows]
            + [stay(item.shape) for item in whole]
            + [ANYWHERE] * len(pieces),
            out_specs=out_specs + [stay(shape) for shape in sums],
            scratch_shapes=[*scratch, pltpu.SemaphoreType.DMA((len(pieces),))],
        ),
        compiler_params=pltpu.CompilerParams(vmem_limit_bytes=56 << 20),
        cost_estimate=pl.CostEstimate(flops=flops, bytes_accessed=moved, transcendentals=0),
    )(where, *rows, *whole, *pieces)


def chunks_of(columns, size=256):
    return [slice(start, min(start + size, columns)) for start in range(0, columns, size)]


def standard(rows):
    values = rows.astype(F32)
    centred = values - jnp.mean(values, axis=1, keepdims=True)
    inv_std = lax.rsqrt(jnp.mean(centred * centred, axis=1, keepdims=True) + 1e-05)
    return centred * inv_std, inv_std


def enter_kernel(
    tokens, gain, shift, bias, inner, normed_out, slope_out, active_out, linear_out
):
    scaled, _ = standard(tokens[...])
    normed = (scaled * gain[...] + shift[...]).astype(BF16)
    normed_out[...] = normed
    units = active_out.shape[1]
    for part in chunks_of(units):
        hidden = dot_nn(normed, inner[:, part]) + bias[:, part]
        square = hidden * hidden
        bent = jnp.tanh(0.7978845608028654 * hidden * (1.0 + 0.044715 * square))
        active_out[:, part] = (0.5 * hidden * (1.0 + bent)).astype(BF16)
        slope = (1.0 - bent * bent) * (0.7978845608028654 * (1.0 + 0.134145 * square))
        slope_out[:, part] = 0.5 * (1.0 + bent + hidden * slope)
    for part in chunks_of(linear_out.shape[1]):
        there = slice(units + part.start, units + part.stop)
        linear_out[:, part] = dot_nn(normed, inner[:, there]) + bias[:, there]


def back_kernel(first, second, slope, down, out, hidden_out, att_out, hidden_sum):
    @pl.when(pl.program_id(0) == 0)
    def _():
        hidden_sum[...] = jnp.zeros_like(hidden_sum)

    left, right = first[...], second[...]
    middle = left.shape[1]

    def back(weights, part):
        return dot_nt(left, weights[part, :middle]) + dot_nt(right, weights[part, middle:])

    for part in chunks_of(down.shape[0]):
        grad = (back(down, part) * slope[:, part]).astype(BF16)
        hidden_out[:, part] = grad
        hidden_sum[:, part] += jnp.sum(grad.astype(F32), axis=0, keepdims=True)
    for part in chunks_of(out.shape[0]):
        att_out[:, part] = back(out, part).astype(BF16)


def leave_kernel(attended, active, out, down, result):
    left, right = attended[...], active[...]
    for part in chunks_of(out.shape[1], 512):
        result[:, part] = (dot_nn(left, out[:, part]) + dot_nn(right, down[:, part])).astype(BF16)


def norm_back_kernel(tokens, mixed, hidden, inner, result, gain_sum, shift_sum, mixed_sum):
    @pl.when(pl.program_id(0) == 0)
    def _():
        for total in (gain_sum, shift_sum, mixed_sum):
            total[...] = jnp.zeros_like(total)

    scaled, _ = standard(tokens[...])
    left, right = mixed[...], hidden[...]
    mixed_sum[...] += jnp.sum(left.astype(F32), axis=0, keepdims=True)
    units = right.shape[1]
    for part in chunks_of(inner.shape[0], 512):
        grad = dot_nt(left, inner[part, units:]) + dot_nt(right, inner[part, :units])
        result[:, part] = grad.astype(BF16)
        shift_sum[:, part] += jnp.sum(grad, axis=0, keepdims=True)
        gain_sum[:, part] += jnp.sum(grad * scaled[:, part], axis=0, keepdims=True)


def pick_kernel(plans, index_ref, *refs):
    *weights, target, tiles, sems = refs
    at = index_ref[0]
    count = plans[0][2]
    copies, late, slot, column = [], [], 0, 0
    for weight, (unit, order, _) in zip(weights, plans):
        if unit % LANES == 0:
            for place in order:
                first = pl.multiple_of((place * count + at) * unit, unit)
                copies.append(
                    (weight.at[:, pl.ds(first, unit)], target.at[:, column : column + unit])
                )
                column += unit
            continue
        for one, two in zip(order[::2], order[1::2]):
            for which, place in enumerate((one, two)):
                first = pl.multiple_of((place * count + at) // 2 * LANES, LANES)
                copies.append((weight.at[:, pl.ds(first, LANES)], tiles.at[slot, which]))
            late.append((slot, column))
            slot, column = slot + 1, column + LANES
    copies = [
        pltpu.make_async_copy(source, there, sems.at[i])
        for i, (source, there) in enumerate(copies)
    ]
    for copy in copies:
        copy.start()
    for copy in copies:
        copy.wait()
    for slot, column in late:
        first, second = tiles[slot, 0].astype(F32), tiles[slot, 1].astype(F32)
        odd = at % 2 == 1
        first = jnp.where(odd, pltpu.roll(first, HEAD_DIM, 1), first)
        second = jnp.where(odd, second, pltpu.roll(second, HEAD_DIM, 1))
        target[:, column : column + LANES] = jnp.where(
            first_half(first.shape), first, second
        ).astype(target.dtype)


def pick_columns(weights, units, orders, index, count):
    rows = weights[0].shape[0]
    width = sum(unit * len(order) for unit, order in zip(units, orders))
    narrow = [len(order) // 2 for unit, order in zip(units, orders) if unit % LANES]
    copies = sum(len(order) for order in orders)
    return pl.pallas_call(
        functools.partial(pick_kernel, [(unit, order, count) for unit, order in zip(units, orders)]),
        out_shape=jax.ShapeDtypeStruct((rows, width), weights[0].dtype),
        in_specs=[SMEM] + [ANYWHERE] * len(weights),
        out_specs=VMEM,
        scratch_shapes=[
            pltpu.VMEM((sum(narrow), 2, rows, LANES), weights[0].dtype),
            pltpu.SemaphoreType.DMA((copies,)),
        ],
        compiler_params=pltpu.CompilerParams(vmem_limit_bytes=32 << 20),
        cost_estimate=pl.CostEstimate(
            flops=0, bytes_accessed=4 * rows * width, transcendentals=0
        ),
    )(index.reshape(1), *weights)


def deal_kernel(unit, order, turn_ref, parts, target, *rest):
    count = parts.shape[0]
    for group, place in enumerate(order):
        if unit % LANES == 0:
            for owner in range(count):
                start = (place * count + owner) * unit
                target[:, start : start + unit] = parts[
                    owner, :, group * unit : (group + 1) * unit
                ].astype(F32)
            continue
        tile = slice(group // 2 * LANES, (group // 2 + 1) * LANES)
        for owner in range(0, count, 2):
            first = parts[owner, :, tile].astype(F32)
            second = parts[owner + 1, :, tile].astype(F32)
            if group % 2:
                first = pltpu.roll(first, HEAD_DIM, 1)
            else:
                second = pltpu.roll(second, HEAD_DIM, 1)
            start = (place * count + owner) * unit
            target[:, start : start + LANES] = jnp.where(
                first_half(first.shape), first, second
            )
    for out in rest:
        slots = out.shape[0] // HEAD_DIM
        for slot in range(slots):
            owner = slot if slots == count else turn_ref[0] * slots + slot
            out[slot * HEAD_DIM : (slot + 1) * HEAD_DIM, :] = parts[
                owner, :, len(order) * unit :
            ].astype(F32)


def deal_columns(parts, unit, order, turn_index, with_out=False):
    count, rows, columns = parts.shape
    width = len(order) * unit
    step = HEAD_DIM
    out_shape = [jax.ShapeDtypeStruct((rows, count * width), F32)]
    out_specs = [pl.BlockSpec((step, count * width), lambda i, at: (i, 0))]
    if with_out:
        out_shape.append(jax.ShapeDtypeStruct((rows, (columns - width) * (rows // step)), F32))
        out_specs.append(pl.BlockSpec((rows, columns - width), lambda i, at: (0, i)))
    return pl.pallas_call(
        functools.partial(deal_kernel, unit, order),
        out_shape=out_shape,
        grid_spec=pltpu.PrefetchScalarGridSpec(
            num_scalar_prefetch=1,
            grid=(rows // step,),
            in_specs=[pl.BlockSpec((count, step, columns), lambda i, at: (0, i, 0))],
            out_specs=out_specs,
        ),
        compiler_params=pltpu.CompilerParams(vmem_limit_bytes=32 << 20),
        cost_estimate=pl.CostEstimate(
            flops=0, bytes_accessed=6 * rows * count * columns, transcendentals=0
        ),
    )(turn_index.reshape(1), parts)


def join_kernel(turns, turn_ref, left, *refs):
    *pieces, target = refs
    width = left.shape[1]
    size = target.shape[1] - width
    target[:, :width] = left[...]
    keep = pl.program_id(0) % turns == turn_ref[0]
    for piece_index, piece in enumerate(pieces):
        for chunk in range(piece.shape[1] // size):
            value = piece[:, chunk * size : (chunk + 1) * size]
            if turns > 1:
                value = jnp.where(keep, value, jnp.zeros_like(value))
            row = (piece_index * (piece.shape[1] // size) + chunk) * HEAD_DIM
            target[row : row + HEAD_DIM, width:] = value


def join_terms(left, pieces, shards, turns, turn_index):
    rows = left.shape[0] // shards
    extra = sum(piece.shape[1] for piece in pieces) * HEAD_DIM // rows
    width = left.shape[1]
    return pl.pallas_call(
        functools.partial(join_kernel, turns),
        out_shape=jax.ShapeDtypeStruct((left.shape[0], width + extra), left.dtype),
        grid_spec=pltpu.PrefetchScalarGridSpec(
            num_scalar_prefetch=1,
            grid=(shards,),
            in_specs=[pl.BlockSpec((rows, width), lambda i, at: (i, 0))]
            + [
                pl.BlockSpec((HEAD_DIM, piece.shape[1]), lambda i, at: (i // turns, 0))
                for piece in pieces
            ],
            out_specs=pl.BlockSpec((rows, width + extra), lambda i, at: (i, 0)),
        ),
        cost_estimate=pl.CostEstimate(
            flops=0, bytes_accessed=4 * left.shape[0] * (width + extra), transcendentals=0
        ),
    )(turn_index.reshape(1), left, *pieces)


def side_kernel(*refs):
    *pieces, target = refs
    start = 0
    for piece in pieces:
        target[:, start : start + piece.shape[1]] = piece[...].astype(F32)
        start += piece.shape[1]


def side_by_side(*pieces):
    rows = pieces[0].shape[0]
    width = sum(piece.shape[1] for piece in pieces)
    return pl.pallas_call(
        side_kernel,
        out_shape=jax.ShapeDtypeStruct((rows, width), F32),
        grid=(rows // TILE,),
        in_specs=[pl.BlockSpec((TILE, piece.shape[1]), lambda i: (i, 0)) for piece in pieces],
        out_specs=pl.BlockSpec((TILE, width), lambda i: (i, 0)),
        cost_estimate=pl.CostEstimate(flops=0, bytes_accessed=6 * rows * width, transcendentals=0),
    )(*pieces)


def after(value, *others):
    return lax.optimization_barrier((value,) + others)[0]


def shards(
    tokens,
    block_place,
    seq_lengths,
    norm_gain,
    norm_bias,
    qkv_weight,
    qkv_bias,
    out_weight,
    out_bias,
    up_weight,
    up_bias,
    down_weight,
    down_bias,
    out_grad,
):
    ctx_count, ctx_index = lax.axis_size("ctx"), lax.axis_index("ctx")
    shard_count, shard_index = lax.axis_size("fsdp"), lax.axis_index("fsdp")
    own_tokens, own_grad = tokens[0], out_grad[0]
    own_rows, model_width = own_tokens.shape
    hidden_width = up_weight.shape[1]
    heads = model_width // HEAD_DIM
    own_heads = heads // ctx_count
    shard_heads = heads // shard_count
    unit = hidden_width // shard_count // ctx_count
    own_width = own_heads * HEAD_DIM
    head_turns = ctx_count // shard_heads
    low_first = list(bits_of("fsdp"))
    high_first = low_first[::-1]

    def pick(value, axis):
        return lax.dynamic_index_in_dim(value, ctx_index, axis, keepdims=False)

    half_width = model_width // 2
    pairs = own_heads // 2

    def section_order(slot):
        pair, rest = slot // 6, slot % 6
        return rest // 2 * own_heads + pair * 2 + rest % 2

    def by_ctx(value):
        return lax.all_gather(value, "ctx", axis=0, tiled=True)

    def as_row(value):
        return value.reshape(1, -1)

    token_count = ctx_count * own_rows
    units = shard_count * unit
    flops = 2 * token_count * model_width
    shard_rows = model_width // shard_count
    both = (low_first, high_first)
    qkv_order = [section_order(slot) for slot in range(3 * own_heads)]
    turn_index, head_slot = ctx_index // shard_heads, ctx_index % shard_heads
    where = jnp.stack([shard_index, ctx_index % 2]).astype(jnp.int32)

    all_tokens = by_ctx(own_tokens)
    own_inner = pick_columns(
        [up_weight, qkv_weight],
        [unit, HEAD_DIM],
        [list(range(shard_count)), qkv_order],
        ctx_index,
        ctx_count,
    )
    vectors = (norm_gain, norm_bias, qkv_bias, out_bias, up_bias, down_bias)
    inner_flow = Flow(gather_steps(own_inner, *both))
    vector_flow = Flow(direct_steps(jnp.concatenate(vectors).reshape(8, -1)))
    grad_first = by_ctx(after(own_grad[:, :half_width], own_inner))

    def prepare(ends, down_weight, out_weight):
        own_down = pick(down_weight.reshape(ctx_count, unit, model_width), 0)
        own_out = lax.dynamic_index_in_dim(
            out_weight.reshape(shard_heads, HEAD_DIM, model_width), head_slot, 0, keepdims=False
        )
        return own_down, own_out, turn_tables(ends, token_count)

    ends = jnp.cumsum(seq_lengths[0]).astype(jnp.int32)
    own_down, own_out, tables = beside(
        prepare, (ends, down_weight, out_weight), [inner_flow, vector_flow]
    )
    grad_second = by_ctx(after(own_grad[:, half_width:], own_down))
    packed = jnp.stack([piece.reshape(-1) for _, _, piece in vector_flow.result])
    packed = jnp.concatenate(
        [lax.dynamic_index_in_dim(packed, shard_index ^ i, 0) for i in range(shard_count)]
    )
    cuts = [0]
    for vector in vectors:
        cuts.append(cuts[-1] + vector.shape[0])
    gain_all, shift_all, qkv_bias_all, out_bias_all, up_bias_all, down_bias_all = [
        packed[:, start:stop].reshape(-1).astype(F32) for start, stop in zip(cuts, cuts[1:])
    ]
    own_qkv_bias = pick(qkv_bias_all.reshape(3, pairs, 2, ctx_count, HEAD_DIM), 3)
    own_qkv_bias = jnp.transpose(own_qkv_bias, (1, 0, 2, 3)).reshape(-1)
    own_up_bias = pick(up_bias_all.reshape(shard_count, ctx_count, unit), 1).reshape(-1)
    inner_bias = jnp.concatenate([own_up_bias, own_qkv_bias])
    while inner_flow.moves:
        own_down, own_out, inner_bias = beside(
            lambda *same: same, (own_down, own_out, inner_bias), [inner_flow]
        )
    inner = (shard_rows, inner_flow.result)
    down_flow = Flow(gather_steps(own_down, *both))
    out_flow = Flow(direct_steps(own_out))

    def enter(rows):
        return row_call(
            enter_kernel,
            where,
            [rows],
            [as_row(gain_all), as_row(shift_all), as_row(inner_bias)],
            [inner],
            [(model_width, BF16), (units, F32), (units, BF16), (3 * own_width, F32)],
            [],
            flops * (units + 3 * own_width),
        )

    normed, slope, active, linear = beside(enter, (all_tokens,), [down_flow, out_flow])
    attended, *kept = beside(
        lambda rows: attention_forward(block_place, ends, tables, rows), (linear,), [down_flow]
    )
    while down_flow.moves:
        attended = beside(lambda same: same, (attended,), [down_flow])
    down = (unit, down_flow.result)
    out = (HEAD_DIM, out_flow.result)
    if head_turns > 1:
        out_all = jnp.stack([piece for _, _, piece in out_flow.result])
        out_all = jnp.concatenate(
            [
                lax.dynamic_index_in_dim(
                    out_all, shard_index ^ (i * head_turns + turn_index), 0, keepdims=False
                )
                for i in range(own_heads)
            ]
        )
        out = (own_width, [(None, 0, out_all)])

    def down_terms(rows):
        return dot_tn(active, rows).astype(BF16).reshape(shard_count, unit, half_width)

    first_terms = down_terms(after(grad_first, attended))
    first_flow = Flow(scatter_steps(first_terms, *both))

    def leave(rows):
        return row_call(
            leave_kernel,
            where,
            [rows, active],
            [],
            [out, down],
            [(model_width, BF16)],
            [],
            flops * (units + own_width),
            split=True,
        )

    line_flow = Flow(line_steps(*beside(leave, (attended,), [first_flow])))
    grad_second = beside(lambda same: same, (grad_second,), [first_flow, line_flow])
    while first_flow.moves:
        grad_second = beside(lambda same: same, (grad_second,), [first_flow])
    second_terms = beside(down_terms, (grad_second,), [], late=[line_flow])
    second_flow = Flow(scatter_steps(second_terms, *both))

    def back(rows):
        return row_call(
            back_kernel,
            where,
            [grad_first, rows, slope],
            [],
            [down, out],
            [(units, BF16), (own_width, BF16)],
            [(1, units)],
            flops * (units + own_width),
        )

    grad_hidden, grad_att, hidden_sum = beside(
        back, (grad_second,), [second_flow], early=[line_flow]
    )
    up_terms = beside(
        lambda rows: dot_tn(normed, rows).astype(BF16),
        (grad_hidden,),
        [second_flow],
        late=[line_flow],
    )
    up_flow = Flow(scatter_steps(up_terms.reshape(shard_count, shard_rows, units), *both))
    grad_mixed = beside(
        lambda rows: attention_backward(block_place, ends, tables, kept, rows),
        (grad_att,),
        [up_flow],
        early=[line_flow],
    )

    def joint(rows):
        out_terms = [dot_tn(attended, piece).astype(BF16) for piece in (grad_first, grad_second)]
        return join_terms(
            dot_tn(normed, rows).astype(BF16), out_terms, shard_count, head_turns, turn_index
        )

    joint_terms = beside(joint, (grad_mixed,), [up_flow, line_flow])
    joint_flow = Flow(
        scatter_steps(joint_terms.reshape(shard_count, shard_rows, -1), *both)
    )

    def norm_back(rows):
        return row_call(
            norm_back_kernel,
            where,
            [all_tokens, rows, grad_hidden],
            [],
            [inner],
            [(model_width, BF16)],
            [(1, model_width), (1, model_width), (1, 3 * own_width)],
            flops * (units + 3 * own_width),
            split=True,
        )

    mine, other, gain_sum, shift_sum, mixed_sum = beside(norm_back, (grad_mixed,), [joint_flow])
    for flow in (second_flow, up_flow, line_flow):
        while flow.moves:
            mine = beside(lambda same: same, (mine,), [flow])

    def spread(value, count):
        value = value.reshape(count, 1, -1)
        whole = jnp.zeros((count, ctx_count, value.shape[2]), F32)
        return lax.dynamic_update_slice_in_dim(whole, value, ctx_index, 1).reshape(-1)

    grad_float = own_grad.astype(F32)
    mixed_sum = jnp.transpose(mixed_sum.reshape(pairs, 3, 2 * HEAD_DIM), (1, 0, 2))
    sums = (
        gain_sum.reshape(-1),
        shift_sum.reshape(-1),
        spread(mixed_sum, 3 * own_heads),
        jnp.sum(grad_float, axis=0),
        spread(hidden_sum, shard_count),
    )
    total_flow = Flow(total_steps(jnp.concatenate(sums)))
    norm_flow = Flow(line_steps(mine, other))
    beside(lambda: (), (), [norm_flow, total_flow, joint_flow])
    while joint_flow.moves:
        beside(lambda: (), (), [joint_flow])
    down_total = [by_ctx(flow.result) for flow in (first_flow, second_flow)]
    up_total = by_ctx(up_flow.result).reshape(ctx_count, shard_rows, -1)
    joint_total = by_ctx(joint_flow.result).reshape(ctx_count, shard_rows, -1)
    down_total = beside(side_by_side, tuple(down_total), [norm_flow, total_flow])
    while norm_flow.moves or total_flow.moves:
        beside(lambda: (), (), [flow for flow in (norm_flow, total_flow) if flow.moves])
    grad_normed = norm_flow.result

    inputs = own_tokens.astype(F32)
    output = (inputs + line_flow.result + (out_bias_all + down_bias_all)).astype(BF16)

    scaled, inv_std = standard(own_tokens)
    grad_scaled = grad_normed * gain_all
    grad_input = inv_std * (
        grad_scaled
        - jnp.mean(grad_scaled, axis=1, keepdims=True)
        - scaled * jnp.mean(grad_scaled * scaled, axis=1, keepdims=True)
    )
    input_grad = (grad_float + grad_input).astype(BF16)

    total = total_flow.result
    own_sums, start = [], 0
    for item in sums:
        size = item.shape[0] // shard_count
        own_sums.append(lax.dynamic_slice_in_dim(total, start + shard_index * size, size))
        start += item.shape[0]
    gain_total, shift_total, qkv_bias_total, bias_total, up_bias_total = own_sums

    out_turn = shard_index % head_turns
    up_dealt = deal_columns(up_total, unit, list(range(shard_count)), out_turn)[0]
    joint_total = after(joint_total, up_dealt)
    qkv_dealt, out_dealt = deal_columns(joint_total, HEAD_DIM, qkv_order, out_turn, with_out=True)
    return (
        output[None],
        input_grad[None],
        gain_total,
        shift_total,
        qkv_dealt,
        qkv_bias_total,
        out_dealt,
        bias_total,
        up_dealt,
        up_bias_total,
        down_total,
        bias_total,
    )


def solution(mesh):
    in_specs = (
        P("fsdp", "ctx", None),
        P(),
        P("fsdp", None),
        P("fsdp"),
        P("fsdp"),
        P("fsdp", None),
        P("fsdp"),
        P("fsdp", None),
        P("fsdp"),
        P("fsdp", None),
        P("fsdp"),
        P("fsdp", None),
        P("fsdp"),
        P("fsdp", "ctx", None),
    )
    out_specs = (
        P("fsdp", "ctx", None),
        P("fsdp", "ctx", None),
        P("fsdp"),
        P("fsdp"),
        P("fsdp", None),
        P("fsdp"),
        P("fsdp", None),
        P("fsdp"),
        P("fsdp", None),
        P("fsdp"),
        P("fsdp", None),
        P("fsdp"),
    )
    return jax.shard_map(shards, mesh=mesh, in_specs=in_specs, out_specs=out_specs, check_vma=False)
```

time: 987 us -> 672 us (0.68)
  waiting for transfers between devices: 386 us -> 201 us
  Pallas kernels: 57 us -> 195 us
  local copies, waits for them, and re-layouts: 198 us -> 65.1 us
  matrix products: 155 us -> 46.3 us
  other arithmetic: 77.9 us -> 57.5 us
    pallas_call x1 -> x11, Pallas kernels: 57 us -> 195 us  [the longest x4 96.9 us: row_call(): pl.pallas_call(body, out_shape=out_shape + [jax.ShapeDtypeStruct(shape, F...]
    dot_general x10 -> x0, matrix products: 117 us -> none  [the longest x6 64 us: dot_nt(): lax.dot_general(left, right, (((1,), (1,)), ((), ())), preferred_element_...]
    ppermute x41 -> x53, waiting for transfers between devices: 308 us -> 200 us  [beside(): lax.ppermute(value, axis, pairs)]
    all_gather x8 -> x7, waiting for transfers between devices: 76.9 us -> 0.03 us  [by_ctx(): return lax.all_gather(value, 'ctx', axis=0, tiled=True)]
    unnamed x81 -> x157, local copies, waits for them, and re-layouts: 83.1 us -> 32.6 us
    convert_element_type x3 -> x0, local copies, waits for them, and re-layouts: 49.6 us -> none  [deal(): return jnp.transpose(value, (1, 2, 0, 3)).reshape(rows, -1).astype(F32)]
    dynamic_update_slice x16 -> x0, local copies, waits for them, and re-layouts: 27.5 us -> none  [the longest x12 18.5 us: gather_rows(): whole = lax.dynamic_update_slice_in_dim(whole, piece, where * rows, 0)]
    convert_element_type x22, other arithmetic: 52.2 us -> 36.4 us  [the longest x6 26.3 us: line_steps(): down.astype(BF16)]
  transfers between devices with their start and end apart: 49 -> 60, of which waited for: 28 -> 16; matrix products, arithmetic and copies ran while one was open for 38% -> 21% of each run, Pallas kernels for 6% -> 28%
where the time goes in v2:
time: 672 us; the launch traced here: 663 us
  waiting for transfers between devices  201 us (30%)
  Pallas kernels  195 us (29%)
  starting transfers between devices  82.6 us (12%)
  local copies, waits for them, and re-layouts  65.1 us (10%)
  other arithmetic  57.5 us (9%)
  matrix products  46.3 us (7%)
  between operations  16 us (2%)
    ppermute x53, waiting for transfers between devices, beside(): lax.ppermute(value, axis, pairs)  200 us
    pallas_call x4, Pallas kernels, row_call(): pl.pallas_call(body, out_shape=out_shape + [jax.ShapeDtypeStruct(shape, F...  96.9 us
    ppermute x53, starting transfers between devices, beside(): lax.ppermute(value, axis, pairs)  82.1 us
    dot_general x6, matrix products, dot_tn(): lax.dot_general(left, right, (((0,), (0,)), ((), ())), preferred_element_...  46.3 us
    pallas_call x1, Pallas kernels, attention_forward(): pl.pallas_call(forward_kernel, out_shape=(jax.ShapeDtypeStruct((tokens, w...  34.1 us
    pallas_call x1, Pallas kernels, attention_backward(): pl.pallas_call(backward_kernel, out_shape=jax.ShapeDtypeStruct((tokens, 3...  33.1 us
    unnamed x157, local copies, waits for them, and re-layouts  32.6 us
    convert_element_type x6, other arithmetic, line_steps(): down.astype(BF16)  26.3 us
  transfers between devices with their start and end apart: 60, of which 16 were waited for; matrix products, arithmetic and copies ran while one was open for 21% of the time, Pallas kernels for 28%

profile of v2, /device:TPU:0, one launch (start us, length us, event | category | flops | bytes accessed | tf_op | source)
XLA Modules:
  0.0 663.3 jit_solution(14686091044322273006)
XLA Ops:
  8.0 3.4 copy-done.2
  11.4 2.8 copy-done.6
  19.2 3.0 fusion.53
  22.3 2.9 collective-permute-start
  27.2 2.9 collective-permute-start.4
  30.3 2.3 dynamic-slice_bitcast_fusion.4
  32.6 5.7 multiply_sine_fusion
  39.4 5.3 concatenate.31.cos_ref
  45.8 4.4 concatenate.32.sin_ref
  58.0 16.8 %collective-permute-done.5.refs_6_.refs_5_ = bf16[256,1792]{1,0:T(8,128)(2,1)} collective-permute-done((bf16[256,1792]{1,0:T(8,128)(2,1)}, bf16[256,1792]{1,0:T(8,128)(2,1)}, u32[]{:S(2)}, u32[]{:S(2)}) %collective-permute-start.5) | collective-permute-done | bytes 917536 | tf_op jit(solution)/shard_map/ppermute | solution.py:58
  74.8 17.1 %collective-permute-done.6.refs_7_.refs_6_ = bf16[256,1792]{1,0:T(8,128)(2,1)} collective-permute-done((bf16[256,1792]{1,0:T(8,128)(2,1)}, bf16[256,1792]{1,0:T(8,128)(2,1)}, u32[]{:S(2)}, u32[]{:S(2)}) %collective-permute-start.6) | collective-permute-done | bytes 917536 | tf_op jit(solution)/shard_map/ppermute | solution.py:58
  99.1 1.8 collective-permute-start.13
  100.9 31.1 %shard_map.230 = (bf16[2048,2048]{1,0:T(8,128)(2,1)}, f32[2048,1024]{1,0:T(8,128)}, bf16[2048,1024]{1,0:T(8,128)(2,1)}, f32[2048,768]{1,0:T(8,128)}) custom-call(s32[2]{0:T(128)} %pad_add_fusion.at, bf16[2048,2048]{1,0:T(8,128)(2,1)} %bitcast.291, f32[1,2048]{1,0:T(1,128)} %bitcast.286, f32[1,2048]{1,0:T(1,128)} %bitcast.287, f32[1,1792]{1,0:T(1,128)} %reshape.318.refs_3_, ...), custom_call_target="tpu_custom_call" | custom-call | flops 15032385536 | bytes 43015168 | tf_op jit(solution)/shard_map/pallas_call | solution.py:490
  136.3 34.1 %shard_map.231 = (bf16[2048,256]{1,0:T(8,128)(2,1)S(1)}, bf16[2048,768]{1,0:T(8,128)(2,1)}, f32[256,2048]{1,0:T(8,128)S(1)}, f32[4,2048]{1,0:T(4,128)S(1)}) custom-call(s32[128]{0:T(128)S(1)} %copy-done.9, s32[4]{0:T(128)S(1)} %bitcast.253, f32[2048,128]{1,0:T(8,128)S(1)} %concatenate.31.cos_ref, f32[2048,128]{1,0:T(8,128)S(1)} %copy-done.7, ...), custom_call_target="tpu_custom_call" | custom-call | flops 40000000000 | bytes 16000000 | tf_op jit(solution)/shard_map/pallas_call | solution.py:380
  173.5 8.1 %convolution_convert_fusion.3 = bf16[1024,1024]{1,0:T(8,128)(2,1)S(1)} fusion(bf16[2048,1024]{1,0:T(8,128)(2,1)} %get-tuple-element.242.refs_1_, bf16[2048,1024]{1,0:T(8,128)(2,1)} %all-gather.9.cloned.1.call-done.refs_0_), kind=kOutput, calls=%fused_computation.53 | convolution fusion | flops 4296015872 | bytes 10485760 | tf_op jit(solution)/shard_map/dot_general | solution.py:28
  181.9 5.8 collective-permute-start.18
  187.7 19.2 %shard_map.232 = (bf16[4,256,2048]{2,1,0:T(8,128)(2,1)}, bf16[4,256,2048]{2,1,0:T(8,128)(2,1)}) custom-call(s32[2]{0:T(128)} %pad_add_fusion.at, bf16[2048,256]{1,0:T(8,128)(2,1)} %copy-done.10, bf16[2048,1024]{1,0:T(8,128)(2,1)} %get-tuple-element.242.refs_1_, bf16[64,2048]{1,0:T(8,128)(2,1)} %copy-done.46, bf16[64,2048]{1,0:T(8,128)(2,1)} %copy-done.64, ...), custom_call_target="tpu_custom_call" | custom-call | flops 10737418240 | bytes 18874368 | tf_op jit(solution)/shard_map/pallas_call | solution.py:490
  209.0 2.1 collective-permute-start.20
  211.2 4.3 convolution_convert_fusion.5.refs_0_
  215.5 2.7 collective-permute-done.20
  220.5 4.6 fusion.29
  225.1 7.2 %convolution_convert_fusion.2 = bf16[1024,1024]{1,0:T(8,128)(2,1)S(1)} fusion(bf16[2048,1024]{1,0:T(8,128)(2,1)} %get-tuple-element.242.refs_1_, bf16[2048,1024]{1,0:T(8,128)(2,1)S(1)} %copy-done.56), kind=kOutput, calls=%fused_computation.52 | convolution fusion | flops 4296015872 | bytes 10485760 | tf_op jit(solution)/shard_map/dot_general | solution.py:28
  233.7 3.3 collective-permute-start.25
  237.7 19.3 %shard_map.233 = (bf16[2048,1024]{1,0:T(8,128)(2,1)}, bf16[2048,256]{1,0:T(8,128)(2,1)}, f32[1,1024]{1,0:T(1,128)}) custom-call(s32[2]{0:T(128)} %pad_add_fusion.at, bf16[2048,1024]{1,0:T(8,128)(2,1)} %all-gather.9.cloned.1.call-done.refs_0_, bf16[2048,1024]{1,0:T(8,128)(2,1)} %all-gather.11.cloned.1.call-done.refs_1_, ...), custom_call_target="tpu_custom_call" | custom-call | flops 10737418240 | bytes 27262976 | tf_op jit(solution)/shard_map/pallas_call | solution.py:490
  257.0 4.3 convolution_convert_fusion.4.refs_1_
  261.3 21.3 %collective-permute-done.25 = bf16[256,2048]{1,0:T(8,128)(2,1)S(1)} collective-permute-done((bf16[256,2048]{1,0:T(8,128)(2,1)}, bf16[256,2048]{1,0:T(8,128)(2,1)S(1)}, u32[]{:S(2)}, u32[]{:S(2)}) %collective-permute-start.25) | collective-permute-done | bytes 1048608 | tf_op jit(solution)/shard_map/ppermute | solution.py:58
  284.8 4.4 fusion.25
  290.9 1.8 collective-permute-start.28
  292.6 5.3 collective-permute-start.31
  299.6 11.8 %convolution_convert_fusion = bf16[2048,1024]{1,0:T(8,128)(2,1)S(1)} fusion(bf16[2048,2048]{1,0:T(8,128)(2,1)} %get-tuple-element.267, bf16[2048,1024]{1,0:T(8,128)(2,1)S(1)} %copy-done.68), kind=kOutput, calls=%fused_computation | convolution fusion | flops 8592031744 | bytes 16777216 | tf_op jit(solution)/shard_map/dot_general | solution.py:28
  318.8 33.1 %shard_map.234.refs_1_ = bf16[2048,768]{1,0:T(8,128)(2,1)} custom-call(s32[128]{0:T(128)S(1)} %copy-done.9, s32[4]{0:T(128)S(1)} %bitcast.254, f32[2048,128]{1,0:T(8,128)S(1)} %concatenate.31.cos_ref, f32[2048,128]{1,0:T(8,128)S(1)} %copy-done.8, bf16[2048,768]{1,0:T(8,128)(2,1)} %get-tuple-element.268.rows, f32[256,2048]{1,0:T(8,128)S(1)} %copy-done.14, ...), custom_call_target="tpu_custom_call" | custom-call | flops 40000000000 | bytes 16000000 | tf_op jit(solution)/shard_map/pallas_call | solution.py:405
  352.0 1.8 fusion.16
  354.6 1.8 fusion.15
  358.2 4.7 fusion.23
  363.5 5.9 collective-permute-start.34
  369.4 3.9 collective-permute-start.35
  374.5 10.6 %convolution_convert_fusion.1.left = bf16[2048,768]{1,0:T(8,128)(2,1)} fusion(bf16[2048,2048]{1,0:T(8,128)(2,1)} %get-tuple-element.267, bf16[2048,768]{1,0:T(8,128)(2,1)S(1)} %copy-done.69), kind=kOutput, calls=%fused_computation.1 | convolution fusion | flops 6444023808 | bytes 14680064 | tf_op jit(solution)/shard_map/dot_general | solution.py:28
  385.1 4.8 shard_map.235
  391.7 4.9 collective-permute-done.36
  400.6 2.7 fusion.49
  407.3 27.4 %shard_map.236 = (bf16[4,256,2048]{2,1,0:T(8,128)(2,1)}, bf16[4,256,2048]{2,1,0:T(8,128)(2,1)}, f32[1,2048]{1,0:T(1,128)}, f32[1,2048]{1,0:T(1,128)}, f32[1,768]{1,0:T(1,128)}) custom-call(s32[2]{0:T(128)} %pad_add_fusion.at, bf16[2048,2048]{1,0:T(8,128)(2,1)} %bitcast.292, bf16[2048,768]{1,0:T(8,128)(2,1)} %shard_map.234.refs_1_, ...), custom_call_target="tpu_custom_call" | custom-call | flops 15032385536 | bytes 31457280 | tf_op jit(solution)/shard_map/pallas_call | solution.py:490
  438.3 2.1 fusion.14
  440.9 1.8 copy-done.57
  445.1 5.1 collective-permute-done.40
  450.2 6.9 %collective-permute-done.41 = bf16[256,1024]{1,0:T(8,128)(2,1)S(1)} collective-permute-done((bf16[256,1024]{1,0:T(8,128)(2,1)S(1)}, bf16[256,1024]{1,0:T(8,128)(2,1)S(1)}, u32[]{:S(2)}, u32[]{:S(2)}) %collective-permute-start.41) | collective-permute-done | bytes 524320 | tf_op jit(solution)/shard_map/ppermute | solution.py:58
  459.0 4.4 fusion.31
  463.4 3.5 collective-permute-start.43
  467.7 10.2 %shard_map.237 = f32[2048,2048]{1,0:T(8,128)} custom-call(bf16[2048,1024]{1,0:T(8,128)(2,1)} %all-gather.13.cloned.1.call-done.refs_0_, bf16[2048,1024]{1,0:T(8,128)(2,1)} %all-gather.15.cloned.1.call-done.refs_1_), custom_call_target="tpu_custom_call" | custom-call | bytes 25165824 | tf_op jit(solution)/shard_map/pallas_call | solution.py:743
  477.9 21.9 %collective-permute-done.45 = f32[20480]{0:T(1024)S(1)} collective-permute-done((f32[20480]{0:T(1024)S(1)}, f32[20480]{0:T(1024)S(1)}, u32[]{:S(2)}, u32[]{:S(2)}) %collective-permute-start.45) | collective-permute-done | bytes 81952 | tf_op jit(solution)/shard_map/ppermute | solution.py:58
  499.8 4.2 fusion.18
  504.0 4.0 collective-permute-start.46
  508.8 5.1 collective-permute-start.48
  514.0 76.6 %collective-permute-done.48 = f32[20480]{0:T(1024)S(1)} collective-permute-done((f32[20480]{0:T(1024)S(1)}, f32[20480]{0:T(1024)S(1)}, u32[]{:S(2)}, u32[]{:S(2)}) %collective-permute-start.48) | collective-permute-done | bytes 81952 | tf_op jit(solution)/shard_map/ppermute | solution.py:58
  590.6 3.9 fusion.17
  594.6 2.5 collective-permute-start.49
  600.6 2.9 collective-permute-done.51
  603.6 14.1 %collective-permute-done.49 = bf16[256,2048]{1,0:T(8,128)(2,1)} collective-permute-done((bf16[256,2048]{1,0:T(8,128)(2,1)}, bf16[256,2048]{1,0:T(8,128)(2,1)}, u32[]{:S(2)}, u32[]{:S(2)}) %collective-permute-start.49) | collective-permute-done | bytes 1048608 | tf_op jit(solution)/shard_map/ppermute | solution.py:58
  617.7 4.9 collective-permute-done.50
  624.0 3.2 fusion.47
  627.3 5.0 fusion.33
  634.3 3.4 copy-done.3
  637.7 6.8 %shard_map.238 = f32[512,8192]{1,0:T(8,128)} custom-call(s32[1]{0:T(128)} %constant.283.clone.1.turn_ref, bf16[8,512,1024]{2,1,0:T(8,128)(2,1)S(1)} %bitcast.250), custom_call_target="tpu_custom_call" | custom-call | bytes 25165824 | tf_op jit(solution)/shard_map/pallas_call | solution.py:678
  644.5 3.4 copy-done.4
  647.9 7.5 %shard_map.239 = (f32[512,6144]{1,0:T(8,128)}, f32[512,2048]{1,0:T(8,128)}) custom-call(s32[1]{0:T(128)} %constant.283.clone.1.turn_ref, bf16[8,512,1024]{2,1,0:T(8,128)(2,1)S(1)} %bitcast.251), custom_call_target="tpu_custom_call" | custom-call | bytes 25165824 | tf_op jit(solution)/shard_map/pallas_call | solution.py:678
  (345 shorter events, 83.2 us)
Async XLA Ops:
  7.2 87.9 %all-gather.21.cloned.1.call-start = ((), (), s32[]{:S(2)}) async-start(), calls=%async_computation.6 | async-start | bytes 9437184 | tf_op jit(solution)/shard_map/all_gather | solution.py:798
  7.9 165.6 %all-gather.9.cloned.1.call-start = ((), (), s32[]{:S(2)}) async-start(), calls=%async_computation | async-start | bytes 4718592 | tf_op jit(solution)/shard_map/all_gather | solution.py:798
  17.9 191.0 %all-gather.11.cloned.1.call-start = ((), (), s32[]{:S(2)}) async-start(), calls=%async_computation.1 | async-start | bytes 4718592 | tf_op jit(solution)/shard_map/all_gather | solution.py:798
  22.3 27.9 %collective-permute-start = (bf16[256,1792]{1,0:T(8,128)(2,1)}, bf16[256,1792]{1,0:T(8,128)(2,1)}, u32[]{:S(2)}, u32[]{:S(2)}) collective-permute-start(bf16[256,1792]{1,0:T(8,128)(2,1)} %get-tuple-element.208.refs_4_.refs_3_), channel_id=1, source_target_pairs={{0,1},{1,0},{2,3},{3,2},{4,5},{5,4},{6,7},{7,6},{8,9},{9,8},{10,11... | collective-permute-start | bytes 2752520 | tf_op jit(solution)/shard_map/ppermute | solution.py:58
  25.2 25.0 %collective-permute-start.1 = (bf16[256,1792]{1,0:T(8,128)(2,1)}, bf16[256,1792]{1,0:T(8,128)(2,1)}, u32[]{:S(2)}, u32[]{:S(2)}) collective-permute-start(bf16[256,1792]{1,0:T(8,128)(2,1)} %get-tuple-element.210.refs_8_.refs_7_), channel_id=1, source_target_pairs={{0,2},{1,3},{2,0},{3,1},{4,6},{5,7},{6,4},{7,5},{8,10},{9,11},{10,... | collective-permute-start | bytes 2752520 | tf_op jit(solution)/shard_map/ppermute | solution.py:58
  26.7 23.5 %collective-permute-start.2 = (bf16[8,704]{1,0:T(8,128)(2,1)S(1)}, bf16[8,704]{1,0:T(8,128)(2,1)S(1)}, u32[]{:S(2)}, u32[]{:S(2)}) collective-permute-start(bf16[8,704]{1,0:T(8,128)(2,1)S(1)} %reshape.313), channel_id=1, source_target_pairs={{0,1},{1,0},{2,3},{3,2},{4,5},{5,4},{6,7},{7,6},{8,9},{9,8},{10,11... | collective-permute-start | bytes 33800 | tf_op jit(solution)/shard_map/ppermute | solution.py:58
  27.2 23.0 %collective-permute-start.3 = (bf16[8,704]{1,0:T(8,128)(2,1)S(1)}, bf16[8,704]{1,0:T(8,128)(2,1)S(1)}, u32[]{:S(2)}, u32[]{:S(2)}) collective-permute-start(bf16[8,704]{1,0:T(8,128)(2,1)S(1)} %reshape.313), channel_id=1, source_target_pairs={{0,2},{1,3},{2,0},{3,1},{4,6},{5,7},{6,4},{7,5},{8,10},{9,11},{10,... | collective-permute-start | bytes 33800 | tf_op jit(solution)/shard_map/ppermute | solution.py:58
  27.2 23.0 %collective-permute-start.4 = (bf16[8,704]{1,0:T(8,128)(2,1)S(1)}, bf16[8,704]{1,0:T(8,128)(2,1)S(1)}, u32[]{:S(2)}, u32[]{:S(2)}) collective-permute-start(bf16[8,704]{1,0:T(8,128)(2,1)S(1)} %reshape.313), channel_id=1, source_target_pairs={{0,3},{1,2},{2,1},{3,0},{4,7},{5,6},{6,5},{7,4},{8,11},{9,10},{10,... | collective-permute-start | bytes 33800 | tf_op jit(solution)/shard_map/ppermute | solution.py:58
  50.7 81.3 %copy-start.38 = (bf16[1,5632]{1,0:T(2,128)(2,1)}, bf16[1,5632]{1,0:T(2,128)(2,1)S(1)}, u32[]{:S(2)}) copy-start(bf16[1,5632]{1,0:T(2,128)(2,1)S(1)} %get-tuple-element.401) | copy-start | bytes 33796
  50.7 81.3 %copy-start.40 = (bf16[1,5632]{1,0:T(2,128)(2,1)}, bf16[1,5632]{1,0:T(2,128)(2,1)S(1)}, u32[]{:S(2)}) copy-start(bf16[1,5632]{1,0:T(2,128)(2,1)S(1)} %get-tuple-element.402) | copy-start | bytes 33796
  50.7 81.3 %copy-start.42 = (bf16[1,5632]{1,0:T(2,128)(2,1)}, bf16[1,5632]{1,0:T(2,128)(2,1)S(1)}, u32[]{:S(2)}) copy-start(bf16[1,5632]{1,0:T(2,128)(2,1)S(1)} %get-tuple-element.403) | copy-start | bytes 33796
  51.1 23.7 %collective-permute-start.5 = (bf16[256,1792]{1,0:T(8,128)(2,1)}, bf16[256,1792]{1,0:T(8,128)(2,1)}, u32[]{:S(2)}, u32[]{:S(2)}) collective-permute-start(bf16[256,1792]{1,0:T(8,128)(2,1)} %get-tuple-element.208.refs_4_.refs_3_), channel_id=1, source_target_pairs={{0,2},{1,3},{2,0},{3,1},{4,6},{5,7},{6,4},{7,5},{8,10},{9,11},{10,... | collective-permute-start | bytes 2752520 | tf_op jit(solution)/shard_map/ppermute | solution.py:58
  51.7 40.2 %collective-permute-start.6 = (bf16[256,1792]{1,0:T(8,128)(2,1)}, bf16[256,1792]{1,0:T(8,128)(2,1)}, u32[]{:S(2)}, u32[]{:S(2)}) collective-permute-start(bf16[256,1792]{1,0:T(8,128)(2,1)} %collective-permute-done.refs_5_.refs_4_), channel_id=1, source_target_pairs={{0,2},{1,3},{2,0},{3,1},{4,6},{5,7},{6,4},{7,5},{8,10},{9,11},{10,... | collective-permute-start | bytes 2752520 | tf_op jit(solution)/shard_map/ppermute | solution.py:58
  53.2 38.7 %collective-permute-start.7 = (bf16[256,1792]{1,0:T(8,128)(2,1)}, bf16[256,1792]{1,0:T(8,128)(2,1)}, u32[]{:S(2)}, u32[]{:S(2)}) collective-permute-start(bf16[256,1792]{1,0:T(8,128)(2,1)} %get-tuple-element.210.refs_8_.refs_7_), channel_id=1, source_target_pairs={{0,1},{1,0},{2,3},{3,2},{4,5},{5,4},{6,7},{7,6},{8,9},{9,8},{10,11... | collective-permute-start | bytes 2752520 | tf_op jit(solution)/shard_map/ppermute | solution.py:58
  53.8 39.6 %collective-permute-start.8 = (bf16[256,1792]{1,0:T(8,128)(2,1)}, bf16[256,1792]{1,0:T(8,128)(2,1)}, u32[]{:S(2)}, u32[]{:S(2)}) collective-permute-start(bf16[256,1792]{1,0:T(8,128)(2,1)} %collective-permute-done.1.refs_9_.refs_8_), channel_id=1, source_target_pairs={{0,1},{1,0},{2,3},{3,2},{4,5},{5,4},{6,7},{7,6},{8,9},{9,8},{10,11... | collective-permute-start | bytes 2752520 | tf_op jit(solution)/shard_map/ppermute | solution.py:58
  57.7 405.7 %all-gather.13.cloned.1.call-start = ((), (), s32[]{:S(2)}) async-start(), calls=%async_computation.2 | async-start | bytes 4718592 | tf_op jit(solution)/shard_map/all_gather | solution.py:798
  95.1 37.0 %collective-permute-start.9 = (bf16[128,2048]{1,0:T(8,128)(2,1)}, bf16[128,2048]{1,0:T(8,128)(2,1)S(1)}, u32[]{:S(2)}, u32[]{:S(2)}) collective-permute-start(bf16[128,2048]{1,0:T(8,128)(2,1)} %get-tuple-element.237.refs_6_.refs_3_), channel_id=1, source_target_pairs={{0,1},{1,0},{2,3},{3,2},{4,5},{5,4},{6,7},{7,6},{8,9},{9,8},{10,11... | collective-permute-start | bytes 1572872 | tf_op jit(solution)/shard_map/ppermute | solution.py:58
  95.9 36.2 %collective-permute-start.10 = (bf16[128,2048]{1,0:T(8,128)(2,1)}, bf16[128,2048]{1,0:T(8,128)(2,1)S(1)}, u32[]{:S(2)}, u32[]{:S(2)}) collective-permute-start(bf16[128,2048]{1,0:T(8,128)(2,1)} %get-tuple-element.239.refs_10_.refs_7_), channel_id=1, source_target_pairs={{0,2},{1,3},{2,0},{3,1},{4,6},{5,7},{6,4},{7,5},{8,10},{9,11},{10,... | collective-permute-start | bytes 1572872 | tf_op jit(solution)/shard_map/ppermute | solution.py:58
  97.4 34.6 %collective-permute-start.11 = (bf16[64,2048]{1,0:T(8,128)(2,1)S(1)}, bf16[64,2048]{1,0:T(8,128)(2,1)S(1)}, u32[]{:S(2)}, u32[]{:S(2)}) collective-permute-start(bf16[64,2048]{1,0:T(8,128)(2,1)S(1)} %dynamic-slice_bitcast_fusion.17.refs_2_.refs_11_), channel_id=1, source_target_pairs={{0,1},{1,0},{2,3},{3,2},{4,5},{5,4},{6,7},{7,6},{8,9},{9,8},{10,11... | collective-permute-start | bytes 786440 | tf_op jit(solution)/shard_map/ppermute | solution.py:58
  98.0 34.1 %collective-permute-start.12 = (bf16[64,2048]{1,0:T(8,128)(2,1)S(1)}, bf16[64,2048]{1,0:T(8,128)(2,1)S(1)}, u32[]{:S(2)}, u32[]{:S(2)}) collective-permute-start(bf16[64,2048]{1,0:T(8,128)(2,1)S(1)} %dynamic-slice_bitcast_fusion.17.refs_2_.refs_11_), channel_id=1, source_target_pairs={{0,2},{1,3},{2,0},{3,1},{4,6},{5,7},{6,4},{7,5},{8,10},{9,11},{10,... | collective-permute-start | bytes 786440 | tf_op jit(solution)/shard_map/ppermute | solution.py:58
  99.1 32.9 %collective-permute-start.13 = (bf16[64,2048]{1,0:T(8,128)(2,1)S(1)}, bf16[64,2048]{1,0:T(8,128)(2,1)S(1)}, u32[]{:S(2)}, u32[]{:S(2)}) collective-permute-start(bf16[64,2048]{1,0:T(8,128)(2,1)S(1)} %dynamic-slice_bitcast_fusion.17.refs_2_.refs_11_), channel_id=1, source_target_pairs={{0,3},{1,2},{2,1},{3,0},{4,7},{5,6},{6,5},{7,4},{8,11},{9,10},{10,... | collective-permute-start | bytes 786440 | tf_op jit(solution)/shard_map/ppermute | solution.py:58
  132.1 39.3 %collective-permute-start.14 = (bf16[128,2048]{1,0:T(8,128)(2,1)}, bf16[128,2048]{1,0:T(8,128)(2,1)S(1)}, u32[]{:S(2)}, u32[]{:S(2)}) collective-permute-start(bf16[128,2048]{1,0:T(8,128)(2,1)} %get-tuple-element.237.refs_6_.refs_3_), channel_id=1, source_target_pairs={{0,2},{1,3},{2,0},{3,1},{4,6},{5,7},{6,4},{7,5},{8,10},{9,11},{10,... | collective-permute-start | bytes 1572872 | tf_op jit(solution)/shard_map/ppermute | solution.py:58
  133.1 38.3 %collective-permute-start.15 = (bf16[128,2048]{1,0:T(8,128)(2,1)S(1)}, bf16[128,2048]{1,0:T(8,128)(2,1)S(1)}, u32[]{:S(2)}, u32[]{:S(2)}) collective-permute-start(bf16[128,2048]{1,0:T(8,128)(2,1)S(1)} %collective-permute-done.9.refs_7_.refs_4_), channel_id=1, source_target_pairs={{0,2},{1,3},{2,0},{3,1},{4,6},{5,7},{6,4},{7,5},{8,10},{9,11},{10,... | collective-permute-start | bytes 1572872 | tf_op jit(solution)/shard_map/ppermute | solution.py:58
  134.2 37.2 %collective-permute-start.16 = (bf16[128,2048]{1,0:T(8,128)(2,1)}, bf16[128,2048]{1,0:T(8,128)(2,1)S(1)}, u32[]{:S(2)}, u32[]{:S(2)}) collective-permute-start(bf16[128,2048]{1,0:T(8,128)(2,1)} %get-tuple-element.239.refs_10_.refs_7_), channel_id=1, source_target_pairs={{0,1},{1,0},{2,3},{3,2},{4,5},{5,4},{6,7},{7,6},{8,9},{9,8},{10,11... | collective-permute-start | bytes 1572872 | tf_op jit(solution)/shard_map/ppermute | solution.py:58
  135.1 36.3 %collective-permute-start.17 = (bf16[128,2048]{1,0:T(8,128)(2,1)S(1)}, bf16[128,2048]{1,0:T(8,128)(2,1)S(1)}, u32[]{:S(2)}, u32[]{:S(2)}) collective-permute-start(bf16[128,2048]{1,0:T(8,128)(2,1)S(1)} %collective-permute-done.10.refs_11_.refs_8_), channel_id=1, source_target_pairs={{0,1},{1,0},{2,3},{3,2},{4,5},{5,4},{6,7},{7,6},{8,9},{9,8},{10,11... | collective-permute-start | bytes 1572872 | tf_op jit(solution)/shard_map/ppermute | solution.py:58
  181.9 24.9 %collective-permute-start.18 = (bf16[2,128,1024]{2,1,0:T(8,128)(2,1)S(1)}, bf16[2,128,1024]{2,1,0:T(8,128)(2,1)S(1)}, u32[]{:S(2)}, u32[]{:S(2)}) collective-permute-start(bf16[2,128,1024]{2,1,0:T(8,128)(2,1)S(1)} %dynamic-slice_bitcast_fusion.12), channel_id=1, source_target_pairs={{0,1},{1,0},{2,3},{3,2},{4,5},{5,4},{6,7},{7,6},{8,9},{9,8},{10,11... | collective-permute-start | bytes 1572872 | tf_op jit(solution)/shard_map/ppermute | solution.py:58
  187.7 19.2 %collective-permute-start.19 = (bf16[2,128,1024]{2,1,0:T(8,128)(2,1)S(1)}, bf16[2,128,1024]{2,1,0:T(8,128)(2,1)S(1)}, u32[]{:S(2)}, u32[]{:S(2)}) collective-permute-start(bf16[2,128,1024]{2,1,0:T(8,128)(2,1)S(1)} %dynamic-slice_bitcast_fusion.11), channel_id=1, source_target_pairs={{0,2},{1,3},{2,0},{3,1},{4,6},{5,7},{6,4},{7,5},{8,10},{9,11},{10,... | collective-permute-start | bytes 1572872 | tf_op jit(solution)/shard_map/ppermute | solution.py:58
  208.9 10.5 %collective-permute-start.22 = (bf16[4,256,2048]{2,1,0:T(8,128)(2,1)}, bf16[4,256,2048]{2,1,0:T(8,128)(2,1)}, u32[]{:S(2)}, u32[]{:S(2)}) collective-permute-start(bf16[4,256,2048]{2,1,0:T(8,128)(2,1)} %get-tuple-element.265), channel_id=1, source_target_pairs={{0,4},{4,0},{8,12},{12,8},{16,20},{20,16},{24,28},{28,24},{1,5},{5... | collective-permute-start | bytes 12582920 | tf_op jit(solution)/shard_map/ppermute | solution.py:58
  209.0 9.1 %collective-permute-start.20 = (bf16[128,1024]{1,0:T(8,128)(2,1)}, bf16[128,1024]{1,0:T(8,128)(2,1)S(1)}, u32[]{:S(2)}, u32[]{:S(2)}) collective-permute-start(bf16[128,1024]{1,0:T(8,128)(2,1)} %dynamic-slice_bitcast_fusion.16), channel_id=1, source_target_pairs={{0,2},{1,3},{2,0},{3,1},{4,6},{5,7},{6,4},{7,5},{8,10},{9,11},{10,... | collective-permute-start | bytes 786440 | tf_op jit(solution)/shard_map/ppermute | solution.py:58
  211.1 8.3 %collective-permute-start.21 = (bf16[128,1024]{1,0:T(8,128)(2,1)S(1)}, bf16[128,1024]{1,0:T(8,128)(2,1)S(1)}, u32[]{:S(2)}, u32[]{:S(2)}) collective-permute-start(bf16[128,1024]{1,0:T(8,128)(2,1)S(1)} %dynamic-slice_bitcast_fusion.15), channel_id=1, source_target_pairs={{0,1},{1,0},{2,3},{3,2},{4,5},{5,4},{6,7},{7,6},{8,9},{9,8},{10,11... | collective-permute-start | bytes 786440 | tf_op jit(solution)/shard_map/ppermute | solution.py:58
  220.4 242.9 %all-gather.15.cloned.1.call-start = ((), (), s32[]{:S(2)}) async-start(), calls=%async_computation.3 | async-start | bytes 4718592 | tf_op jit(solution)/shard_map/all_gather | solution.py:798
  233.3 28.0 %collective-permute-start.23 = (bf16[2,128,1024]{2,1,0:T(8,128)(2,1)}, bf16[2,128,1024]{2,1,0:T(8,128)(2,1)S(1)}, u32[]{:S(2)}, u32[]{:S(2)}) collective-permute-start(bf16[2,128,1024]{2,1,0:T(8,128)(2,1)} %dynamic-slice_bitcast_fusion.10), channel_id=1, source_target_pairs={{0,1},{1,0},{2,3},{3,2},{4,5},{5,4},{6,7},{7,6},{8,9},{9,8},{10,11... | collective-permute-start | bytes 1572872 | tf_op jit(solution)/shard_map/ppermute | solution.py:58
  233.4 27.9 %collective-permute-start.24 = (bf16[2,128,1024]{2,1,0:T(8,128)(2,1)S(1)}, bf16[2,128,1024]{2,1,0:T(8,128)(2,1)S(1)}, u32[]{:S(2)}, u32[]{:S(2)}) collective-permute-start(bf16[2,128,1024]{2,1,0:T(8,128)(2,1)S(1)} %dynamic-slice_bitcast_fusion.9), channel_id=1, source_target_pairs={{0,2},{1,3},{2,0},{3,1},{4,6},{5,7},{6,4},{7,5},{8,10},{9,11},{10,... | collective-permute-start | bytes 1572872 | tf_op jit(solution)/shard_map/ppermute | solution.py:58
  233.7 48.9 %collective-permute-start.25 = (bf16[256,2048]{1,0:T(8,128)(2,1)}, bf16[256,2048]{1,0:T(8,128)(2,1)S(1)}, u32[]{:S(2)}, u32[]{:S(2)}) collective-permute-start(bf16[256,2048]{1,0:T(8,128)(2,1)} %get-tuple-element.280), channel_id=1, source_target_pairs={{0,8},{4,12},{1,9},{5,13},{2,10},{6,14},{3,11},{7,15}} | collective-permute-start | bytes 3145736 | tf_op jit(solution)/shard_map/ppermute | solution.py:58
  237.0 45.7 %collective-permute-start.26 = (bf16[256,2048]{1,0:T(8,128)(2,1)}, bf16[256,2048]{1,0:T(8,128)(2,1)S(1)}, u32[]{:S(2)}, u32[]{:S(2)}) collective-permute-start(bf16[256,2048]{1,0:T(8,128)(2,1)} %get-tuple-element.281), channel_id=1, source_target_pairs={{24,16},{28,20},{25,17},{29,21},{26,18},{30,22},{27,19},{31,23}} | collective-permute-start | bytes 3145736 | tf_op jit(solution)/shard_map/ppermute | solution.py:58
  289.3 22.1 %collective-permute-start.27 = (bf16[128,1024]{1,0:T(8,128)(2,1)S(1)}, bf16[128,1024]{1,0:T(8,128)(2,1)S(1)}, u32[]{:S(2)}, u32[]{:S(2)}) collective-permute-start(bf16[128,1024]{1,0:T(8,128)(2,1)S(1)} %dynamic-slice_bitcast_fusion.14), channel_id=1, source_target_pairs={{0,2},{1,3},{2,0},{3,1},{4,6},{5,7},{6,4},{7,5},{8,10},{9,11},{10,... | collective-permute-start | bytes 786440 | tf_op jit(solution)/shard_map/ppermute | solution.py:58
  290.9 20.5 %collective-permute-start.28 = (bf16[128,1024]{1,0:T(8,128)(2,1)S(1)}, bf16[128,1024]{1,0:T(8,128)(2,1)S(1)}, u32[]{:S(2)}, u32[]{:S(2)}) collective-permute-start(bf16[128,1024]{1,0:T(8,128)(2,1)S(1)} %dynamic-slice_bitcast_fusion.13), channel_id=1, source_target_pairs={{0,1},{1,0},{2,3},{3,2},{4,5},{5,4},{6,7},{7,6},{8,9},{9,8},{10,11... | collective-permute-start | bytes 786440 | tf_op jit(solution)/shard_map/ppermute | solution.py:58
  292.6 59.3 %collective-permute-start.31 = (bf16[256,2048]{1,0:T(8,128)(2,1)}, bf16[256,2048]{1,0:T(8,128)(2,1)}, u32[]{:S(2)}, u32[]{:S(2)}) collective-permute-start(bf16[256,2048]{1,0:T(8,128)(2,1)} %get-tuple-element.295), channel_id=1, source_target_pairs={{0,8},{4,12},{8,16},{12,20},{1,9},{5,13},{9,17},{13,21},{2,10},{6,... | collective-permute-start | bytes 3145736 | tf_op jit(solution)/shard_map/ppermute | solution.py:58
  297.9 54.0 %collective-permute-start.32 = (bf16[256,2048]{1,0:T(8,128)(2,1)}, bf16[256,2048]{1,0:T(8,128)(2,1)}, u32[]{:S(2)}, u32[]{:S(2)}) collective-permute-start(bf16[256,2048]{1,0:T(8,128)(2,1)} %get-tuple-element.296), channel_id=1, source_target_pairs={{16,8},{20,12},{24,16},{28,20},{17,9},{21,13},{25,17},{29,21},{18,... | collective-permute-start | bytes 3145736 | tf_op jit(solution)/shard_map/ppermute | solution.py:58
  314.6 37.3 %collective-permute-start.29 = (bf16[2,256,1024]{2,1,0:T(8,128)(2,1)}, bf16[2,256,1024]{2,1,0:T(8,128)(2,1)}, u32[]{:S(2)}, u32[]{:S(2)}) collective-permute-start(bf16[2,256,1024]{2,1,0:T(8,128)(2,1)} %dynamic-slice_bitcast_fusion.3), channel_id=1, source_target_pairs={{0,1},{1,0},{2,3},{3,2},{4,5},{5,4},{6,7},{7,6},{8,9},{9,8},{10,11... | collective-permute-start | bytes 3145736 | tf_op jit(solution)/shard_map/ppermute | solution.py:58
  314.9 37.1 %collective-permute-start.30 = (bf16[2,256,1024]{2,1,0:T(8,128)(2,1)}, bf16[2,256,1024]{2,1,0:T(8,128)(2,1)}, u32[]{:S(2)}, u32[]{:S(2)}) collective-permute-start(bf16[2,256,1024]{2,1,0:T(8,128)(2,1)} %dynamic-slice_bitcast_fusion.2), channel_id=1, source_target_pairs={{0,2},{1,3},{2,0},{3,1},{4,6},{5,7},{6,4},{7,5},{8,10},{9,11},{10,... | collective-permute-start | bytes 3145736 | tf_op jit(solution)/shard_map/ppermute | solution.py:58
  316.3 317.9 %all-gather.19.cloned.1.call-start = ((), (), s32[]{:S(2)}) async-start(), calls=%async_computation.5 | async-start | bytes 9437184 | tf_op jit(solution)/shard_map/all_gather | solution.py:798
  363.0 27.0 %collective-permute-start.33 = (bf16[256,1024]{1,0:T(8,128)(2,1)}, bf16[256,1024]{1,0:T(8,128)(2,1)}, u32[]{:S(2)}, u32[]{:S(2)}) collective-permute-start(bf16[256,1024]{1,0:T(8,128)(2,1)} %dynamic-slice_bitcast_fusion.8), channel_id=1, source_target_pairs={{0,2},{1,3},{2,0},{3,1},{4,6},{5,7},{6,4},{7,5},{8,10},{9,11},{10,... | collective-permute-start | bytes 1572872 | tf_op jit(solution)/shard_map/ppermute | solution.py:58
  363.5 26.5 %collective-permute-start.34 = (bf16[256,1024]{1,0:T(8,128)(2,1)}, bf16[256,1024]{1,0:T(8,128)(2,1)}, u32[]{:S(2)}, u32[]{:S(2)}) collective-permute-start(bf16[256,1024]{1,0:T(8,128)(2,1)} %dynamic-slice_bitcast_fusion.7), channel_id=1, source_target_pairs={{0,1},{1,0},{2,3},{3,2},{4,5},{5,4},{6,7},{7,6},{8,9},{9,8},{10,11... | collective-permute-start | bytes 1572872 | tf_op jit(solution)/shard_map/ppermute | solution.py:58
  369.4 22.3 %collective-permute-start.35 = (bf16[256,2048]{1,0:T(8,128)(2,1)}, bf16[256,2048]{1,0:T(8,128)(2,1)}, u32[]{:S(2)}, u32[]{:S(2)}) collective-permute-start(bf16[256,2048]{1,0:T(8,128)(2,1)} %get-tuple-element.305), channel_id=1, source_target_pairs={{0,8},{4,12},{8,16},{12,20},{16,24},{20,28},{1,9},{5,13},{9,17},{1... | collective-permute-start | bytes 3145736 | tf_op jit(solution)/shard_map/ppermute | solution.py:58
  373.2 23.4 %collective-permute-start.36 = (bf16[256,2048]{1,0:T(8,128)(2,1)S(1)}, bf16[256,2048]{1,0:T(8,128)(2,1)}, u32[]{:S(2)}, u32[]{:S(2)}) collective-permute-start(bf16[256,2048]{1,0:T(8,128)(2,1)S(1)} %get-tuple-element.306), channel_id=1, source_target_pairs={{8,0},{12,4},{16,8},{20,12},{24,16},{28,20},{9,1},{13,5},{17,9},{2... | collective-permute-start | bytes 3145736 | tf_op jit(solution)/shard_map/ppermute | solution.py:58
  400.2 244.2 %all-gather.17.cloned.1.call-start = ((), (), s32[]{:S(2)}) async-start(), calls=%async_computation.4 | async-start | bytes 9437184 | tf_op jit(solution)/shard_map/all_gather | solution.py:798
  405.3 29.4 %collective-permute-start.37 = (bf16[2,256,1024]{2,1,0:T(8,128)(2,1)S(1)}, bf16[2,256,1024]{2,1,0:T(8,128)(2,1)S(1)}, u32[]{:S(2)}, u32[]{:S(2)}) collective-permute-start(bf16[2,256,1024]{2,1,0:T(8,128)(2,1)S(1)} %dynamic-slice_bitcast_fusion.1), channel_id=1, source_target_pairs={{0,1},{1,0},{2,3},{3,2},{4,5},{5,4},{6,7},{7,6},{8,9},{9,8},{10,11... | collective-permute-start | bytes 3145736 | tf_op jit(solution)/shard_map/ppermute | solution.py:58
  405.5 29.2 %collective-permute-start.38 = (bf16[2,256,1024]{2,1,0:T(8,128)(2,1)S(1)}, bf16[2,256,1024]{2,1,0:T(8,128)(2,1)S(1)}, u32[]{:S(2)}, u32[]{:S(2)}) collective-permute-start(bf16[2,256,1024]{2,1,0:T(8,128)(2,1)S(1)} %dynamic-slice_bitcast_fusion), channel_id=1, source_target_pairs={{0,2},{1,3},{2,0},{3,1},{4,6},{5,7},{6,4},{7,5},{8,10},{9,11},{10,... | collective-permute-start | bytes 3145736 | tf_op jit(solution)/shard_map/ppermute | solution.py:58
  442.8 14.7 %collective-permute-start.39 = (bf16[4,256,2048]{2,1,0:T(8,128)(2,1)S(1)}, bf16[4,256,2048]{2,1,0:T(8,128)(2,1)}, u32[]{:S(2)}, u32[]{:S(2)}) collective-permute-start(bf16[4,256,2048]{2,1,0:T(8,128)(2,1)S(1)} %copy-done.57), channel_id=1, source_target_pairs={{0,4},{4,0},{8,12},{12,8},{16,20},{20,16},{24,28},{28,24},{1,5},{5... | collective-permute-start | bytes 12582920 | tf_op jit(solution)/shard_map/ppermute | solution.py:58
  442.8 14.3 %collective-permute-start.41 = (bf16[256,1024]{1,0:T(8,128)(2,1)S(1)}, bf16[256,1024]{1,0:T(8,128)(2,1)S(1)}, u32[]{:S(2)}, u32[]{:S(2)}) collective-permute-start(bf16[256,1024]{1,0:T(8,128)(2,1)S(1)} %dynamic-slice_bitcast_fusion.6), channel_id=1, source_target_pairs={{0,2},{1,3},{2,0},{3,1},{4,6},{5,7},{6,4},{7,5},{8,10},{9,11},{10,... | collective-permute-start | bytes 1572872 | tf_op jit(solution)/shard_map/ppermute | solution.py:58
  443.4 14.1 %collective-permute-start.42 = (bf16[256,1024]{1,0:T(8,128)(2,1)S(1)}, bf16[256,1024]{1,0:T(8,128)(2,1)S(1)}, u32[]{:S(2)}, u32[]{:S(2)}) collective-permute-start(bf16[256,1024]{1,0:T(8,128)(2,1)S(1)} %dynamic-slice_bitcast_fusion.5), channel_id=1, source_target_pairs={{0,1},{1,0},{2,3},{3,2},{4,5},{5,4},{6,7},{7,6},{8,9},{9,8},{10,11... | collective-permute-start | bytes 1572872 | tf_op jit(solution)/shard_map/ppermute | solution.py:58
  445.1 5.1 collective-permute-start.40
  463.4 36.4 %collective-permute-start.43 = (bf16[256,2048]{1,0:T(8,128)(2,1)}, bf16[256,2048]{1,0:T(8,128)(2,1)S(1)}, u32[]{:S(2)}, u32[]{:S(2)}) collective-permute-start(bf16[256,2048]{1,0:T(8,128)(2,1)} %get-tuple-element.338), channel_id=1, source_target_pairs={{0,8},{4,12},{1,9},{5,13},{2,10},{6,14},{3,11},{7,15}} | collective-permute-start | bytes 3145736 | tf_op jit(solution)/shard_map/ppermute | solution.py:58
  466.9 32.9 %collective-permute-start.44 = (bf16[256,2048]{1,0:T(8,128)(2,1)}, bf16[256,2048]{1,0:T(8,128)(2,1)S(1)}, u32[]{:S(2)}, u32[]{:S(2)}) collective-permute-start(bf16[256,2048]{1,0:T(8,128)(2,1)} %get-tuple-element.339), channel_id=1, source_target_pairs={{24,16},{28,20},{25,17},{29,21},{26,18},{30,22},{27,19},{31,23}} | collective-permute-start | bytes 3145736 | tf_op jit(solution)/shard_map/ppermute | solution.py:58
  467.6 32.1 %collective-permute-start.45 = (f32[20480]{0:T(1024)S(1)}, f32[20480]{0:T(1024)S(1)}, u32[]{:S(2)}, u32[]{:S(2)}) collective-permute-start(f32[20480]{0:T(1024)S(1)} %add.425), channel_id=1, source_target_pairs={{0,8},{4,12},{8,0},{12,4},{16,24},{20,28},{24,16},{28,20},{1,9},{5... | collective-permute-start | bytes 245768 | tf_op jit(solution)/shard_map/ppermute | solution.py:58
  499.8 90.8 %copy-start.16 = (bf16[4,256,2048]{2,1,0:T(8,128)(2,1)S(1)}, bf16[4,256,2048]{2,1,0:T(8,128)(2,1)}, u32[]{:S(2)}) copy-start(bf16[4,256,2048]{2,1,0:T(8,128)(2,1)} %get-tuple-element.318) | copy-start | bytes 12582916
  504.0 86.5 %collective-permute-start.46 = (bf16[256,2048]{1,0:T(8,128)(2,1)S(1)}, bf16[256,2048]{1,0:T(8,128)(2,1)S(1)}, u32[]{:S(2)}, u32[]{:S(2)}) collective-permute-start(bf16[256,2048]{1,0:T(8,128)(2,1)S(1)} %get-tuple-element.344), channel_id=1, source_target_pairs={{0,8},{4,12},{8,16},{12,20},{1,9},{5,13},{9,17},{13,21},{2,10},{6,... | collective-permute-start | bytes 3145736 | tf_op jit(solution)/shard_map/ppermute | solution.py:58
  508.1 82.5 %collective-permute-start.47 = (bf16[256,2048]{1,0:T(8,128)(2,1)S(1)}, bf16[256,2048]{1,0:T(8,128)(2,1)S(1)}, u32[]{:S(2)}, u32[]{:S(2)}) collective-permute-start(bf16[256,2048]{1,0:T(8,128)(2,1)S(1)} %get-tuple-element.345), channel_id=1, source_target_pairs={{16,8},{20,12},{24,16},{28,20},{17,9},{21,13},{25,17},{29,21},{18,... | collective-permute-start | bytes 3145736 | tf_op jit(solution)/shard_map/ppermute | solution.py:58
  508.8 81.8 %collective-permute-start.48 = (f32[20480]{0:T(1024)S(1)}, f32[20480]{0:T(1024)S(1)}, u32[]{:S(2)}, u32[]{:S(2)}) collective-permute-start(f32[20480]{0:T(1024)S(1)} %add.430), channel_id=1, source_target_pairs={{0,16},{4,20},{8,24},{12,28},{16,0},{20,4},{24,8},{28,12},{1,17},{... | collective-permute-start | bytes 245768 | tf_op jit(solution)/shard_map/ppermute | solution.py:58
  594.6 23.1 %collective-permute-start.49 = (bf16[256,2048]{1,0:T(8,128)(2,1)}, bf16[256,2048]{1,0:T(8,128)(2,1)}, u32[]{:S(2)}, u32[]{:S(2)}) collective-permute-start(bf16[256,2048]{1,0:T(8,128)(2,1)} %get-tuple-element.350), channel_id=1, source_target_pairs={{0,8},{4,12},{8,16},{12,20},{16,24},{20,28},{1,9},{5,13},{9,17},{1... | collective-permute-start | bytes 3145736 | tf_op jit(solution)/shard_map/ppermute | solution.py:58
  597.1 25.6 %collective-permute-start.50 = (bf16[256,2048]{1,0:T(8,128)(2,1)S(1)}, bf16[256,2048]{1,0:T(8,128)(2,1)}, u32[]{:S(2)}, u32[]{:S(2)}) collective-permute-start(bf16[256,2048]{1,0:T(8,128)(2,1)S(1)} %get-tuple-element.351), channel_id=1, source_target_pairs={{8,0},{12,4},{16,8},{20,12},{24,16},{28,20},{9,1},{13,5},{17,9},{2... | collective-permute-start | bytes 3145736 | tf_op jit(solution)/shard_map/ppermute | solution.py:58
  599.0 4.5 collective-permute-start.51
  622.6 9.7 %collective-permute-start.52 = (f32[20480]{0:T(1024)S(1)}, f32[20480]{0:T(1024)S(1)}, u32[]{:S(2)}, u32[]{:S(2)}) collective-permute-start(f32[20480]{0:T(1024)S(1)} %add.439), channel_id=1, source_target_pairs={{0,2},{1,3},{2,0},{3,1},{4,6},{5,7},{6,4},{7,5},{8,10},{9,11},{10,... | collective-permute-start | bytes 245768 | tf_op jit(solution)/shard_map/ppermute | solution.py:58
  (66 other events, 635.3 us)
Sparse Core Ops, SparseCore 0:
  9.6 84.7 all-gather.20
  96.0 45.6 all-gather.8
  143.3 45.8 all-gather.10
  220.5 63.7 all-gather.12
  316.5 48.1 all-gather.14
  400.4 83.6 all-gather.18
  486.3 112.5 all-gather.16

commit v3 on v2

v3 whole, which is shorter than its diff:
```python
import functools

import jax
import jax.numpy as jnp
from jax import lax
from jax.experimental import pallas as pl
from jax.experimental.pallas import tpu as pltpu
from jax.sharding import PartitionSpec as P

HEAD_DIM = 64
ROT = 32
BLK = 16
TILE = 256
ROWS = 512
LANES = 128
F32 = jnp.float32
BF16 = jnp.bfloat16


def dot_nn(left, right):
    return lax.dot_general(left, right, (((1,), (0,)), ((), ())), preferred_element_type=F32)


def dot_nt(left, right):
    return lax.dot_general(left, right, (((1,), (1,)), ((), ())), preferred_element_type=F32)


def dot_tn(left, right):
    return lax.dot_general(left, right, (((0,), (0,)), ((), ())), preferred_element_type=F32)


def bits_of(axis):
    return range(lax.axis_size(axis).bit_length() - 1)


def swaps(axis, mask):
    return axis, [(i, i ^ mask) for i in range(lax.axis_size(axis))]


class Flow:
    def __init__(self, steps):
        self.steps = steps
        self.result = None
        self.moves = next(steps)

    def arrive(self, values):
        try:
            self.moves = self.steps.send(values)
        except StopIteration as stop:
            self.moves, self.result = [], stop.value


def beside(work, inputs, flows, late=(), early=()):
    starting = [*flows, *late]
    sends = [[value for value, _, _ in flow.moves] for flow in starting]
    inputs, sends = lax.optimization_barrier((inputs, sends))
    for flow, values in zip(starting, sends):
        flow.moving = [
            lax.ppermute(value, axis, pairs) for value, (_, axis, pairs) in zip(values, flow.moves)
        ]
    outputs = work(*inputs)
    ending = [*flows, *early]
    outputs, arrived = lax.optimization_barrier((outputs, [flow.moving for flow in ending]))
    for flow, values in zip(ending, arrived):
        flow.arrive(values)
    return outputs


def gather_steps(own, *orders):
    share = own.shape[0] // len(orders)
    held = [[(0, own[i * share : (i + 1) * share])] for i in range(len(orders))]
    for step in range(len(orders[0])):
        moves = [
            (piece, *swaps("fsdp", 1 << order[step]))
            for pieces, order in zip(held, orders)
            for _, piece in pieces
        ]
        arrived = iter((yield moves))
        for i, order in enumerate(orders):
            held[i] = held[i] + [(mask ^ (1 << order[step]), next(arrived)) for mask, _ in held[i]]
    return [
        (mask, i * share, piece) for i, pieces in enumerate(held) for mask, piece in pieces
    ]


def direct_steps(own):
    masks = range(1, lax.axis_size("fsdp"))
    arrived = yield [(own, *swaps("fsdp", mask)) for mask in masks]
    return [(0, 0, own)] + [(mask, 0, piece) for mask, piece in zip(masks, arrived)]


def scatter_steps(parts, *orders, fold=0):
    index = lax.axis_index("fsdp")
    bits = len(orders[0])
    share = parts.shape[1] // len(orders)
    held = [
        parts[:, i * share : (i + 1) * share].reshape((2,) * bits + (share, parts.shape[2]))
        for i in range(len(orders))
    ]
    left = [list(range(bits))[::-1] for _ in orders]
    for step in range(bits):
        moves, keeps = [], []
        for i, order in enumerate(orders):
            axis = left[i].index(order[step])
            left[i].pop(axis)
            mine = (index >> order[step]) & 1
            send = lax.dynamic_index_in_dim(held[i], 1 - mine, axis, keepdims=False)
            keeps.append(lax.dynamic_index_in_dim(held[i], mine, axis, keepdims=False))
            moves.append((send, *swaps("fsdp", 1 << order[step])))
        arrived = yield moves
        held = [
            (keep.astype(F32) + got.astype(F32)).astype(BF16) for keep, got in zip(keeps, arrived)
        ]
    return jnp.concatenate(held, axis=fold)


def weave_steps(own, mine, other):
    count = lax.axis_size("ctx")
    line = count // 2
    place = lax.axis_index("ctx") // 2
    alike = own.shape == mine.shape[1:]
    forth = [(i, i + 2) for i in range(count - 2)]
    back = [(i, i - 2) for i in range(2, count)]
    ups, downs = [], []
    up, down, got = yield [
        (own, "ctx", forth), (own, "ctx", back), (other, *swaps("ctx", 1)),
    ]
    up_sum, down_sum = (up, down) if alike else (jnp.zeros_like(mine[0]),) * 2

    def block(target, added):
        target = jnp.clip(target, 0, line - 1)
        total = added.astype(F32)
        for half in (mine, got):
            total += lax.dynamic_index_in_dim(half, target, 0, keepdims=False).astype(F32)
        return total

    for step in range(2, line + 1):
        ups.append(up)
        downs.append(down)
        far = line + 1 - step
        up_sum = block(place + far, up_sum).astype(BF16)
        down_sum = block(place - far, down_sum).astype(BF16)
        if step == line:
            break
        if alike:
            up_sum = jnp.where(place >= step - 1, up, up_sum)
            down_sum = jnp.where(place <= line - step, down, down_sum)
            up_sum, down_sum = yield [(up_sum, "ctx", forth), (down_sum, "ctx", back)]
            up, down = up_sum, down_sum
        else:
            up, down, up_sum, down_sum = yield [
                (up, "ctx", [(i, j) for i, j in forth if i // 2 >= step - 1]),
                (down, "ctx", [(i, j) for i, j in back if i // 2 <= line - step]),
                (up_sum, "ctx", [(i, j) for i, j in forth if i // 2 < step - 1]),
                (down_sum, "ctx", [(i, j) for i, j in back if i // 2 > line - step]),
            ]

    def at_chip(chip):
        value = own
        for away in range(1, line):
            value = jnp.where(place == chip + away, ups[away - 1], value)
            value = jnp.where(place == chip - away, downs[away - 1], value)
        return value

    def swap_cores():
        blocks = jnp.stack([at_chip(chip) for chip in range(line)])
        (beside_blocks,) = yield [(blocks, *swaps("ctx", 1))]
        return blocks, beside_blocks

    def finish():
        last_up, last_down = yield [(up_sum, "ctx", forth), (down_sum, "ctx", back)]
        return block(place, last_up) + last_down.astype(F32)

    return Flow(swap_cores()), Flow(finish())


def total_steps(vector):
    for axis in ("ctx", "fsdp"):
        for bit in bits_of(axis):
            (got,) = yield [(vector, *swaps(axis, 1 << bit))]
            vector = vector + got
    return vector


def turn(values, cosine, sine):
    lane = lax.broadcasted_iota(jnp.int32, values.shape, 1) % HEAD_DIM
    half = ROT // 2
    partner = jnp.where(
        lane < half, pltpu.roll(values, LANES - half, 1), pltpu.roll(values, half, 1)
    )
    return values * cosine + partner * sine


def first_half(shape):
    return lax.broadcasted_iota(jnp.int32, shape, 1) < HEAD_DIM


def visible_range(ends_ref, step, tile):
    top = step * tile
    column = top + lax.broadcasted_iota(jnp.int32, (1, tile), 1)
    begin = jnp.zeros((1, tile), jnp.int32)
    first = jnp.int32(0)
    for sequence in range(ends_ref.shape[0]):
        end = ends_ref[sequence]
        begin = jnp.where(column >= end, jnp.maximum(begin, end), begin)
        first = jnp.where(top >= end, jnp.maximum(first, end), first)
    return column, begin, first // tile


def each_head(values, axis=1):
    half = lax.broadcasted_iota(jnp.int32, values.shape, axis) < HEAD_DIM
    zero = jnp.zeros_like(values)
    return [jnp.where(half, values, zero), jnp.where(half, zero, values)]


Q_LANES, K_LANES, V_LANES = (slice(i * LANES, (i + 1) * LANES) for i in range(3))
HEAD_ROWS = (slice(0, HEAD_DIM), slice(HEAD_DIM, LANES))


def each_block(place_ref, act):
    @pl.loop(0, place_ref.shape[0])
    def _(block):
        act(
            pl.ds(pl.multiple_of(block * BLK, BLK), BLK),
            pl.ds(pl.multiple_of(place_ref[block] * BLK, BLK), BLK),
        )


def part_lanes(pair, which):
    start = (3 * pair + which) * LANES
    return slice(start, start + LANES)


def forward_kernel(
    place_ref, ends_ref, lin_hbm, att_hbm, rows, summed_ref, lse_ref, values_t, att, sems
):
    tokens = rows.shape[0]
    tile = TILE
    pairs = rows.shape[1] // LANES // 3
    heads = 2 * pairs
    each_block(
        place_ref,
        lambda given, natural: pltpu.make_async_copy(
            lin_hbm.at[given], rows.at[natural], sems.at[0]
        ).start(),
    )
    pltpu.make_async_copy(lin_hbm, rows, sems.at[0]).wait()

    @pl.loop(0, tokens // tile)
    def _(step):
        part = pl.ds(pl.multiple_of(step * tile, tile), tile)
        for pair in range(pairs):
            lanes = slice(pair * LANES, (pair + 1) * LANES)
            values_t[lanes, part] = rows[part, part_lanes(pair, 2)].T

    @pl.loop(0, tokens // tile)
    def _(step):
        part = pl.ds(pl.multiple_of(step * tile, tile), tile)
        column, begin, low = visible_range(ends_ref, step, tile)
        queries = [
            query
            for pair in range(pairs)
            for query in each_head(rows[part, part_lanes(pair, 0)].T, 0)
        ]

        def combine(index, state):
            there = pl.ds(pl.multiple_of(index * tile, tile), tile)
            row = index * tile + lax.broadcasted_iota(jnp.int32, (tile, tile), 0)
            visible = (row <= column) & (row >= begin)
            result = []
            for head in range(heads):
                top, total, summed = state[head]
                key = rows[there, part_lanes(head // 2, 1)]
                scores = jnp.where(visible, dot_nn(key, queries[head]), -1e30)
                new_top = jnp.maximum(top, jnp.max(scores, axis=0, keepdims=True))
                weight = jnp.exp(scores - new_top)
                factor = jnp.exp(top - new_top)
                total = total * factor + jnp.sum(weight, axis=0, keepdims=True)
                here = slice(head * HEAD_DIM, (head + 1) * HEAD_DIM)
                summed = summed * factor + dot_nn(values_t[here, there], weight.astype(BF16))
                result.append((new_top, total, summed))
            return tuple(result)

        empty = (
            jnp.full((1, tile), -1e30, F32),
            jnp.zeros((1, tile), F32),
            jnp.zeros((HEAD_DIM, tile), F32),
        )
        state = lax.fori_loop(low, step + 1, combine, (empty,) * heads)
        for head in range(heads):
            top, total, summed = state[head]
            summed_ref[head * HEAD_DIM : (head + 1) * HEAD_DIM, part] = summed * (1.0 / total)
            lse_ref[head : head + 1, part] = top + jnp.log(total)
        for pair in range(pairs):
            lanes = slice(pair * LANES, (pair + 1) * LANES)
            att[part, lanes] = summed_ref[lanes, part].T.astype(BF16)

    each_block(
        place_ref,
        lambda given, natural: pltpu.make_async_copy(
            att.at[natural], att_hbm.at[given], sems.at[0]
        ).start(),
    )
    pltpu.make_async_copy(att, att_hbm, sems.at[0]).wait()


def backward_kernel(
    pair, place_ref, ends_ref, cos_ref, sin_ref, rows, summed_ref, lse_ref, grad_hbm, *refs
):
    mixed_hbm, grad, grad_t, keys_t, grad_k, grad_v, mixed, sems = refs[-8:]
    tokens = grad.shape[0]
    tile = TILE
    lanes = slice(pair * LANES, (pair + 1) * LANES)
    lanes3 = slice(3 * pair * LANES, 3 * (pair + 1) * LANES)
    each_block(
        place_ref,
        lambda given, natural: pltpu.make_async_copy(
            grad_hbm.at[given, lanes], grad.at[natural], sems.at[0]
        ).start(),
    )
    grad_k[...] = jnp.zeros_like(grad_k)
    grad_v[...] = jnp.zeros_like(grad_v)

    @pl.loop(0, tokens // tile)
    def _(step):
        part = pl.ds(pl.multiple_of(step * tile, tile), tile)
        keys_t[:, part] = rows[part, K_LANES].T

    pltpu.make_async_copy(grad_hbm.at[:, lanes], grad, sems.at[0]).wait()

    @pl.loop(0, tokens // tile)
    def _(step):
        part = pl.ds(pl.multiple_of(step * tile, tile), tile)
        column, begin, low = visible_range(ends_ref, step, tile)
        query, back = rows[part, Q_LANES], grad[part, :]
        back_t = back.T
        queries, queries_t = each_head(query), each_head(query.T, 0)
        backs, backs_t = each_head(back), each_head(back_t, 0)
        grad_t[...] = back_t.astype(F32)
        delta = [
            jnp.sum(summed_ref[here, part] * grad_t[here, :], axis=0, keepdims=True)
            for here in HEAD_ROWS
        ]
        lse = [lse_ref[2 * pair + head : 2 * pair + head + 1, part] for head in range(2)]

        def back_step(index, sums):
            there = pl.ds(pl.multiple_of(index * tile, tile), tile)
            row = index * tile + lax.broadcasted_iota(jnp.int32, (tile, tile), 0)
            visible = (row <= column) & (row >= begin)
            key, value = rows[there, K_LANES], rows[there, V_LANES]
            result, add_k, add_v = [], 0.0, 0.0
            for head in range(2):
                scores = jnp.where(visible, dot_nn(key, queries_t[head]), -1e30)
                weight = jnp.exp(scores - lse[head])
                grad_w = dot_nn(value, backs_t[head])
                grad_s = (weight * (grad_w - delta[head])).astype(BF16)
                add_k = add_k + dot_nn(grad_s, queries[head])
                add_v = add_v + dot_nn(weight.astype(BF16), backs[head])
                result.append(sums[head] + dot_nn(keys_t[HEAD_ROWS[head], there], grad_s))
            grad_k[there, :] += add_k
            grad_v[there, :] += add_v
            return tuple(result)

        sums = lax.fori_loop(low, step + 1, back_step, (jnp.zeros((HEAD_DIM, tile), F32),) * 2)
        grad_q = jnp.concatenate(sums, axis=0).T * HEAD_DIM ** (-0.5)
        mixed[part, Q_LANES] = turn(grad_q, cos_ref[part, :], -sin_ref[part, :]).astype(BF16)

    @pl.loop(0, tokens // tile)
    def _(step):
        part = pl.ds(pl.multiple_of(step * tile, tile), tile)
        turned = turn(grad_k[part, :], cos_ref[part, :], -sin_ref[part, :])
        mixed[part, K_LANES] = turned.astype(BF16)
        mixed[part, V_LANES] = grad_v[part, :].astype(BF16)

    each_block(
        place_ref,
        lambda given, natural: pltpu.make_async_copy(
            mixed.at[natural], mixed_hbm.at[given, lanes3], sems.at[0]
        ).start(),
    )
    pltpu.make_async_copy(mixed, mixed_hbm.at[:, lanes3], sems.at[0]).wait()


def turn_tables(position, ends):
    begin = jnp.max(jnp.where(position[:, None] >= ends[None, :], ends[None, :], 0), axis=1)
    within = (position - begin).astype(F32)
    half = ROT // 2
    lane = jnp.arange(LANES, dtype=jnp.int32) % HEAD_DIM
    frequency = 10000.0 ** (-(lane % half).astype(F32) * 2.0 / ROT)
    angles = within[:, None] * jnp.where(lane < ROT, frequency, 0.0)[None, :]
    return jnp.cos(angles), jnp.sin(angles) * jnp.where(lane < half, -1.0, 1.0)[None, :]


SMEM = pl.BlockSpec(memory_space=pltpu.SMEM)
VMEM = pl.BlockSpec(memory_space=pltpu.VMEM)
ANYWHERE = pl.BlockSpec(memory_space=pl.ANY)


def attention_forward(block_place, ends, linear):
    tokens, width3 = linear.shape
    width = width3 // 3
    return pl.pallas_call(
        forward_kernel,
        out_shape=(
            jax.ShapeDtypeStruct((tokens, width), BF16),
            jax.ShapeDtypeStruct((tokens, width3), BF16),
            jax.ShapeDtypeStruct((width, tokens), F32),
            jax.ShapeDtypeStruct((width // HEAD_DIM, tokens), F32),
        ),
        in_specs=[SMEM, SMEM, ANYWHERE],
        out_specs=(ANYWHERE, VMEM, VMEM, VMEM),
        scratch_shapes=[
            pltpu.VMEM((width, tokens), BF16),
            pltpu.VMEM((tokens, width), BF16),
            pltpu.SemaphoreType.DMA((1,)),
        ],
        compiler_params=pltpu.CompilerParams(vmem_limit_bytes=40 << 20),
        cost_estimate=pl.CostEstimate(
            flops=40 * 10**9, bytes_accessed=16 * 10**6, transcendentals=0
        ),
    )(block_place, ends, linear)


def attention_backward(pair, block_place, ends, tables, kept, grad_att, before):
    tokens, width = grad_att.shape
    return pl.pallas_call(
        functools.partial(backward_kernel, pair),
        out_shape=jax.ShapeDtypeStruct((tokens, 3 * width), BF16),
        grid=(1,),
        in_specs=[
            SMEM,
            SMEM,
            VMEM,
            VMEM,
            pl.BlockSpec((tokens, 3 * LANES), lambda i: (0, pair)),
            pl.BlockSpec((LANES, tokens), lambda i: (pair, 0)),
            VMEM,
        ]
        + [ANYWHERE] * (1 + len(before)),
        out_specs=ANYWHERE,
        input_output_aliases={8 + i: i for i in range(len(before))},
        scratch_shapes=[
            pltpu.VMEM((tokens, LANES), BF16),
            pltpu.VMEM((LANES, TILE), F32),
            pltpu.VMEM((LANES, tokens), BF16),
            pltpu.VMEM((tokens, LANES), F32),
            pltpu.VMEM((tokens, LANES), F32),
            pltpu.VMEM((tokens, 3 * LANES), BF16),
            pltpu.SemaphoreType.DMA((1,)),
        ],
        compiler_params=pltpu.CompilerParams(vmem_limit_bytes=40 << 20),
        cost_estimate=pl.CostEstimate(
            flops=20 * 10**9, bytes_accessed=8 * 10**6, transcendentals=0
        ),
    )(block_place, ends, *tables, *kept, grad_att, *before)


def row_call(kernel, where, rows, whole, assembled, outs, sums, flops, split=False):
    count = rows[0].shape[0]
    tiles = count // ROWS
    shards = lax.axis_size("fsdp")
    pieces = [piece for _, group in assembled for _, _, piece in group]
    height = sum(sum(piece.shape[0] for _, _, piece in group) for _, group in assembled)

    def body(at, *refs):
        inputs = refs[: len(rows) + len(whole)]
        sources = refs[len(inputs) : len(inputs) + len(pieces)]
        targets = refs[len(inputs) + len(pieces) : -2]
        buffer, sems = refs[-2:]

        @pl.when(pl.program_id(0) == 0)
        def _():
            copies, base = [], 0
            for shard_height, group in assembled:
                for mask, start, piece in group:
                    first = start if mask is None else (at[0] ^ mask) * shard_height + start
                    size = piece.shape[0]
                    target = buffer.at[pl.ds(pl.multiple_of(base + first, size), size)]
                    slot = len(copies)
                    copies.append(pltpu.make_async_copy(sources[slot], target, sems.at[slot]))
                base += sum(piece.shape[0] for _, _, piece in group)
            for copy in copies:
                copy.start()
            for copy in copies:
                copy.wait()

        if split:
            mine, other, *rest = targets

            def put(part, value):
                even = at[1] == 0
                half = value.shape[0] // 2
                first, second = value[:half], value[half:]
                mine[0, :, part] = jnp.where(even, first, second)
                other[0, :, part] = jnp.where(even, second, first)

            kernel(*inputs, buffer, put, *rest)
        else:
            kernel(*inputs, buffer, *targets)

    by_tile = lambda columns: pl.BlockSpec((ROWS, columns), lambda i, at: (i, 0))
    stay = lambda shape: pl.BlockSpec(shape, lambda i, at: (0, 0))
    moved = sum(item.size * item.dtype.itemsize for item in (*rows, *whole, *pieces))
    moved += sum(count * columns * jnp.dtype(kind).itemsize for columns, kind in outs)
    if split:
        ((columns, kind),) = outs
        out_shape = [jax.ShapeDtypeStruct((tiles, ROWS // 2, columns), kind)] * 2
        out_specs = [pl.BlockSpec((1, ROWS // 2, columns), lambda i, at: (i, 0, 0))] * 2
    else:
        out_shape = [jax.ShapeDtypeStruct((count, columns), kind) for columns, kind in outs]
        out_specs = [by_tile(columns) for columns, _ in outs]
    return pl.pallas_call(
        body,
        out_shape=out_shape + [jax.ShapeDtypeStruct(shape, F32) for shape in sums],
        grid_spec=pltpu.PrefetchScalarGridSpec(
            num_scalar_prefetch=1,
            grid=(tiles,),
            in_specs=[by_tile(item.shape[1]) for item in rows]
            + [stay(item.shape) for item in whole]
            + [ANYWHERE] * len(pieces),
            out_specs=out_specs + [stay(shape) for shape in sums],
            scratch_shapes=[
                pltpu.VMEM((height, pieces[0].shape[1]), BF16),
                pltpu.SemaphoreType.DMA((len(pieces),)),
            ],
        ),
        compiler_params=pltpu.CompilerParams(vmem_limit_bytes=56 << 20),
        cost_estimate=pl.CostEstimate(flops=flops, bytes_accessed=moved, transcendentals=0),
    )(where, *rows, *whole, *pieces)


def chunks_of(columns, size=256):
    return [slice(start, min(start + size, columns)) for start in range(0, columns, size)]


def standard(rows):
    values = rows.astype(F32)
    centred = values - jnp.mean(values, axis=1, keepdims=True)
    inv_std = lax.rsqrt(jnp.mean(centred * centred, axis=1, keepdims=True) + 1e-05)
    return centred * inv_std, inv_std


def enter_kernel(
    tokens, cosine, sine, gain, shift, bias, inner, normed_out, slope_out, active_out, linear_out
):
    for start in range(0, tokens.shape[0], 32):
        part = slice(start, start + 32)
        scaled, _ = standard(tokens[part, :])
        normed_out[part, :] = (scaled * gain[...] + shift[...]).astype(BF16)
    normed = normed_out[...]
    units = active_out.shape[1]
    for part in chunks_of(units):
        hidden = dot_nn(normed, inner[:, part]) + bias[:, part]
        square = hidden * hidden
        gate = 1.0 / (1.0 + jnp.exp(hidden * (-1.5957691216057308 - 0.07135481627260025 * square)))
        value = hidden * gate
        active_out[:, part] = value.astype(BF16)
        inner_slope = 1.5957691216057308 + 0.21406444881780073 * square
        slope_out[:, part] = (gate + (value - value * gate) * inner_slope).astype(BF16)
    for part in chunks_of(linear_out.shape[1], 3 * LANES):
        there = slice(units + part.start, units + part.stop)
        value = dot_nn(normed, inner[:, there]) + bias[:, there]
        query = turn(value[:, Q_LANES], cosine[...], sine[...]) * HEAD_DIM ** (-0.5)
        key = turn(value[:, K_LANES], cosine[...], sine[...])
        joined = jnp.concatenate([query, key, value[:, V_LANES]], axis=1)
        linear_out[:, part] = joined.astype(BF16)


def back_kernel(first, second, slope, weights, hidden_out, att_out, hidden_sum):
    @pl.when(pl.program_id(0) == 0)
    def _():
        hidden_sum[...] = jnp.zeros_like(hidden_sum)

    rows = jnp.concatenate([first[...], second[...]], axis=1)
    units = slope.shape[1]
    for part in chunks_of(units):
        grad = (dot_nt(rows, weights[part, :]) * slope[:, part]).astype(BF16)
        hidden_out[:, part] = grad
        hidden_sum[:, part] += jnp.sum(grad.astype(F32), axis=0, keepdims=True)
    for part in chunks_of(att_out.shape[1]):
        there = slice(units + part.start, units + part.stop)
        att_out[:, part] = dot_nt(rows, weights[there, :]).astype(BF16)


def leave_kernel(attended, active, weights, put):
    rows = jnp.concatenate([active[...], attended[...]], axis=1)
    for part in chunks_of(weights.shape[1], 512):
        put(part, dot_nn(rows, weights[:, part]).astype(BF16))


def norm_back_kernel(tokens, mixed, hidden, inner, put, gain_sum, shift_sum, mixed_sum):
    @pl.when(pl.program_id(0) == 0)
    def _():
        for total in (gain_sum, shift_sum, mixed_sum):
            total[...] = jnp.zeros_like(total)

    scaled, _ = standard(tokens[...])
    mixed_sum[...] += jnp.sum(mixed[...].astype(F32), axis=0, keepdims=True)
    rows = jnp.concatenate([hidden[...], mixed[...]], axis=1)
    for part in chunks_of(inner.shape[0], 512):
        grad = dot_nt(rows, inner[part, :])
        put(part, grad.astype(BF16))
        shift_sum[:, part] += jnp.sum(grad, axis=0, keepdims=True)
        gain_sum[:, part] += jnp.sum(grad * scaled[:, part], axis=0, keepdims=True)


def pick_kernel(plans, index_ref, *refs):
    *weights, target, tiles, sems = refs
    at = index_ref[0]
    count = plans[0][2]
    copies, late, slot, column = [], [], 0, 0
    for weight, (unit, order, _) in zip(weights, plans):
        if unit % LANES == 0:
            for place in order:
                first = pl.multiple_of((place * count + at) * unit, unit)
                copies.append(
                    (weight.at[:, pl.ds(first, unit)], target.at[:, column : column + unit])
                )
                column += unit
            continue
        for one, two in zip(order[::2], order[1::2]):
            for which, place in enumerate((one, two)):
                first = pl.multiple_of((place * count + at) // 2 * LANES, LANES)
                copies.append((weight.at[:, pl.ds(first, LANES)], tiles.at[slot, which]))
            late.append((slot, column))
            slot, column = slot + 1, column + LANES
    copies = [
        pltpu.make_async_copy(source, there, sems.at[i])
        for i, (source, there) in enumerate(copies)
    ]
    for copy in copies:
        copy.start()
    for copy in copies:
        copy.wait()
    for slot, column in late:
        first, second = tiles[slot, 0].astype(F32), tiles[slot, 1].astype(F32)
        odd = at % 2 == 1
        first = jnp.where(odd, pltpu.roll(first, HEAD_DIM, 1), first)
        second = jnp.where(odd, second, pltpu.roll(second, HEAD_DIM, 1))
        target[:, column : column + LANES] = jnp.where(
            first_half(first.shape), first, second
        ).astype(target.dtype)


def pick_columns(weights, units, orders, index, count):
    rows = weights[0].shape[0]
    width = sum(unit * len(order) for unit, order in zip(units, orders))
    narrow = [len(order) // 2 for unit, order in zip(units, orders) if unit % LANES]
    copies = sum(len(order) for order in orders)
    return pl.pallas_call(
        functools.partial(pick_kernel, [(unit, order, count) for unit, order in zip(units, orders)]),
        out_shape=jax.ShapeDtypeStruct((rows, width), weights[0].dtype),
        in_specs=[SMEM] + [ANYWHERE] * len(weights),
        out_specs=VMEM,
        scratch_shapes=[
            pltpu.VMEM((sum(narrow), 2, rows, LANES), weights[0].dtype),
            pltpu.SemaphoreType.DMA((copies,)),
        ],
        compiler_params=pltpu.CompilerParams(vmem_limit_bytes=32 << 20),
        cost_estimate=pl.CostEstimate(
            flops=0, bytes_accessed=4 * rows * width, transcendentals=0
        ),
    )(index.reshape(1), *weights)


def deal_kernel(unit, order, at_ref, mine, other, target, *rest):
    line = mine.shape[0]
    count = 2 * line
    even = at_ref[1] == 0

    def both_cores(chip, tile):
        one, two = mine[chip, :, tile], other[chip, :, tile]
        return jnp.where(even, one, two).astype(F32), jnp.where(even, two, one).astype(F32)

    for chip in range(line):
        for group, place in enumerate(order):
            start = (place * count + 2 * chip) * unit
            if unit % LANES == 0:
                values = both_cores(chip, slice(group * unit, (group + 1) * unit))
                for core, value in enumerate(values):
                    target[:, start + core * unit : start + (core + 1) * unit] = value
                continue
            first, second = both_cores(chip, slice(group // 2 * LANES, (group // 2 + 1) * LANES))
            if group % 2:
                first = pltpu.roll(first, HEAD_DIM, 1)
            else:
                second = pltpu.roll(second, HEAD_DIM, 1)
            target[:, start : start + LANES] = jnp.where(first_half(first.shape), first, second)
    for out in rest:
        chips = out.shape[0] // HEAD_DIM // 2
        tail = slice(len(order) * unit, mine.shape[2])
        for chip in range(chips):
            source = chip if chips == line else at_ref[0] * chips + chip
            for core, value in enumerate(both_cores(source, tail)):
                row = (2 * chip + core) * HEAD_DIM
                out[row : row + HEAD_DIM, :] = value


def deal_columns(mine, other, unit, order, where, with_out=False):
    line, rows, columns = mine.shape
    rows, columns = 2 * rows, columns // 2
    width = len(order) * unit
    step = HEAD_DIM
    steps = rows // step
    out_shape = [jax.ShapeDtypeStruct((rows, 2 * line * width), F32)]
    out_specs = [pl.BlockSpec((step, 2 * line * width), lambda i, at: (i, 0))]
    if with_out:
        out_shape.append(jax.ShapeDtypeStruct((rows, (columns - width) * (rows // step)), F32))
        out_specs.append(pl.BlockSpec((rows, columns - width), lambda i, at: (0, i)))
    return pl.pallas_call(
        functools.partial(deal_kernel, unit, order),
        out_shape=out_shape,
        grid_spec=pltpu.PrefetchScalarGridSpec(
            num_scalar_prefetch=1,
            grid=(rows // step,),
            in_specs=[
                pl.BlockSpec(
                    (line, step, columns),
                    lambda i, at: (0, i % (steps // 2), i // (steps // 2)),
                )
            ]
            * 2,
            out_specs=out_specs,
        ),
        compiler_params=pltpu.CompilerParams(vmem_limit_bytes=32 << 20),
        cost_estimate=pl.CostEstimate(
            flops=0, bytes_accessed=12 * rows * line * columns, transcendentals=0
        ),
    )(where, mine, other)


def join_kernel(turns, turn_ref, left, *refs):
    *pieces, target = refs
    width = left.shape[1]
    size = target.shape[1] - width
    target[:, :width] = left[...]
    keep = pl.program_id(0) % turns == turn_ref[0]
    for piece_index, piece in enumerate(pieces):
        for chunk in range(piece.shape[1] // size):
            value = piece[:, chunk * size : (chunk + 1) * size]
            if turns > 1:
                value = jnp.where(keep, value, jnp.zeros_like(value))
            row = (piece_index * (piece.shape[1] // size) + chunk) * HEAD_DIM
            target[row : row + HEAD_DIM, width:] = value


def join_terms(left, pieces, shards, turns, turn_index):
    rows = left.shape[0] // shards
    extra = sum(piece.shape[1] for piece in pieces) * HEAD_DIM // rows
    width = left.shape[1]
    return pl.pallas_call(
        functools.partial(join_kernel, turns),
        out_shape=jax.ShapeDtypeStruct((left.shape[0], width + extra), left.dtype),
        grid_spec=pltpu.PrefetchScalarGridSpec(
            num_scalar_prefetch=1,
            grid=(shards,),
            in_specs=[pl.BlockSpec((rows, width), lambda i, at: (i, 0))]
            + [
                pl.BlockSpec((HEAD_DIM, piece.shape[1]), lambda i, at: (i // turns, 0))
                for piece in pieces
            ],
            out_specs=pl.BlockSpec((rows, width + extra), lambda i, at: (i, 0)),
        ),
        cost_estimate=pl.CostEstimate(
            flops=0, bytes_accessed=4 * left.shape[0] * (width + extra), transcendentals=0
        ),
    )(turn_index.reshape(1), left, *pieces)


def side_kernel(*refs):
    *pieces, target = refs
    start = 0
    for piece in pieces:
        target[:, start : start + piece.shape[1]] = piece[...].astype(F32)
        start += piece.shape[1]


def side_by_side(*pieces):
    rows = pieces[0].shape[0]
    width = sum(piece.shape[1] for piece in pieces)
    return pl.pallas_call(
        side_kernel,
        out_shape=jax.ShapeDtypeStruct((rows, width), F32),
        grid=(rows // TILE,),
        in_specs=[pl.BlockSpec((TILE, piece.shape[1]), lambda i: (i, 0)) for piece in pieces],
        out_specs=pl.BlockSpec((TILE, width), lambda i: (i, 0)),
        cost_estimate=pl.CostEstimate(flops=0, bytes_accessed=6 * rows * width, transcendentals=0),
    )(*pieces)


def after(value, *others):
    return lax.optimization_barrier((value,) + others)[0]


def shards(
    tokens,
    block_place,
    seq_lengths,
    norm_gain,
    norm_bias,
    qkv_weight,
    qkv_bias,
    out_weight,
    out_bias,
    up_weight,
    up_bias,
    down_weight,
    down_bias,
    out_grad,
):
    ctx_count, ctx_index = lax.axis_size("ctx"), lax.axis_index("ctx")
    shard_count, shard_index = lax.axis_size("fsdp"), lax.axis_index("fsdp")
    own_tokens, own_grad = tokens[0], out_grad[0]
    own_rows, model_width = own_tokens.shape
    hidden_width = up_weight.shape[1]
    heads = model_width // HEAD_DIM
    own_heads = heads // ctx_count
    shard_heads = heads // shard_count
    unit = hidden_width // shard_count // ctx_count
    own_width = own_heads * HEAD_DIM
    head_turns = ctx_count // shard_heads
    low_first = list(bits_of("fsdp"))
    high_first = low_first[::-1]

    def pick(value, axis):
        return lax.dynamic_index_in_dim(value, ctx_index, axis, keepdims=False)

    half_width = model_width // 2
    pairs = own_heads // 2

    def section_order(slot):
        pair, rest = slot // 6, slot % 6
        return rest // 2 * own_heads + pair * 2 + rest % 2

    def by_ctx(value):
        return lax.all_gather(value, "ctx", axis=0, tiled=True)

    def as_row(value):
        return value.reshape(1, -1)

    token_count = ctx_count * own_rows
    units = shard_count * unit
    flops = 2 * token_count * model_width
    shard_rows = model_width // shard_count
    both = (low_first, high_first)
    qkv_order = [section_order(slot) for slot in range(3 * own_heads)]
    turn_index, head_slot = ctx_index // shard_heads, ctx_index % shard_heads
    where = jnp.stack([shard_index, ctx_index % 2]).astype(jnp.int32)

    all_tokens = by_ctx(own_tokens)
    own_inner = pick_columns(
        [up_weight, qkv_weight],
        [unit, HEAD_DIM],
        [list(range(shard_count)), qkv_order],
        ctx_index,
        ctx_count,
    )
    vectors = (norm_gain, norm_bias, qkv_bias, out_bias, up_bias, down_bias)
    inner_flow = Flow(gather_steps(own_inner, *both))
    vector_flow = Flow(direct_steps(jnp.concatenate(vectors).reshape(8, -1)))
    grad_first = by_ctx(after(own_grad[:, :half_width], own_inner))

    def prepare(down_weight, out_weight):
        own_down = pick(down_weight.reshape(ctx_count, unit, model_width), 0)
        own_out = lax.dynamic_index_in_dim(
            out_weight.reshape(shard_heads, HEAD_DIM, model_width), head_slot, 0, keepdims=False
        )
        return own_down, own_out

    def both_tables(ends, block_place):
        natural = jnp.arange(token_count, dtype=jnp.int32)
        given = (block_place[:, None] * BLK + jnp.arange(BLK, dtype=jnp.int32)).reshape(-1)
        return turn_tables(natural, ends), turn_tables(given, ends)

    ends = jnp.cumsum(seq_lengths[0]).astype(jnp.int32)
    own_down, own_out = beside(prepare, (down_weight, out_weight), [inner_flow, vector_flow])
    grad_second = by_ctx(after(own_grad[:, half_width:], own_down))
    natural_tables, given_tables = beside(both_tables, (ends, block_place), [inner_flow])
    while inner_flow.moves:
        own_down, own_out = beside(lambda *same: same, (own_down, own_out), [inner_flow])
    packed = jnp.stack([piece.reshape(-1) for _, _, piece in vector_flow.result])
    packed = jnp.concatenate(
        [lax.dynamic_index_in_dim(packed, shard_index ^ i, 0) for i in range(shard_count)]
    )
    cuts = [0]
    for vector in vectors:
        cuts.append(cuts[-1] + vector.shape[0])
    gain_all, shift_all, qkv_bias_all, out_bias_all, up_bias_all, down_bias_all = [
        packed[:, start:stop].reshape(-1).astype(F32) for start, stop in zip(cuts, cuts[1:])
    ]
    own_qkv_bias = pick(qkv_bias_all.reshape(3, pairs, 2, ctx_count, HEAD_DIM), 3)
    own_qkv_bias = jnp.transpose(own_qkv_bias, (1, 0, 2, 3)).reshape(-1)
    own_up_bias = pick(up_bias_all.reshape(shard_count, ctx_count, unit), 1).reshape(-1)
    inner_bias = jnp.concatenate([own_up_bias, own_qkv_bias])
    inner = (shard_rows, inner_flow.result)
    down_flow = Flow(direct_steps(own_down))
    out_flow = Flow(direct_steps(own_out))

    def enter(rows):
        return row_call(
            enter_kernel,
            where,
            [rows, *given_tables],
            [as_row(gain_all), as_row(shift_all), as_row(inner_bias)],
            [inner],
            [(model_width, BF16), (units, BF16), (units, BF16), (3 * own_width, BF16)],
            [],
            flops * (units + 3 * own_width),
        )

    normed, slope, active, linear = beside(enter, (all_tokens,), [down_flow])

    def down_terms(rows):
        return dot_tn(active, rows).astype(BF16).reshape(shard_count, unit, half_width)

    first_terms = down_terms(after(grad_first, active))
    first_flow = Flow(scatter_steps(first_terms, *both))
    attended, *kept = beside(
        lambda rows: attention_forward(block_place, ends, rows),
        (linear,),
        [first_flow, out_flow],
    )
    down = (unit, down_flow.result)
    out = (HEAD_DIM, out_flow.result)
    if head_turns > 1:
        out_all = jnp.stack([piece for _, _, piece in out_flow.result])
        out_all = jnp.concatenate(
            [
                lax.dynamic_index_in_dim(
                    out_all, shard_index ^ (i * head_turns + turn_index), 0, keepdims=False
                )
                for i in range(own_heads)
            ]
        )
        out = (own_width, [(None, 0, out_all)])
    second_terms = beside(down_terms, (after(grad_second, attended),), [first_flow])
    while first_flow.moves:
        second_terms = beside(lambda same: same, (second_terms,), [first_flow])
    second_flow = Flow(scatter_steps(second_terms, *both))

    def leave(rows):
        return row_call(
            leave_kernel,
            where,
            [rows, active],
            [],
            [down, out],
            [(model_width, BF16)],
            [],
            flops * (units + own_width),
            split=True,
        )

    def back(rows):
        return row_call(
            back_kernel,
            where,
            [grad_first, rows, slope],
            [],
            [down, out],
            [(units, BF16), (own_width, BF16)],
            [(1, units)],
            flops * (units + own_width),
        )

    grad_hidden, grad_att, hidden_sum = beside(
        back, (after(grad_second, first_flow.result),), [second_flow]
    )
    up_terms = beside(
        lambda rows: dot_tn(normed, rows).astype(BF16), (grad_hidden,), [second_flow]
    )
    while second_flow.moves:
        up_terms = beside(lambda same: same, (up_terms,), [second_flow])
    up_flow = Flow(scatter_steps(up_terms.reshape(shard_count, shard_rows, units), *both, fold=1))
    out_halves = beside(leave, (after(attended, second_flow.result),), [up_flow])
    down_total = tuple(by_ctx(flow.result) for flow in (first_flow, second_flow))
    grad_mixed, weave = (), None
    for pair in range(pairs):
        grad_mixed = (
            beside(
                lambda rows: attention_backward(
                    pair, block_place, ends, natural_tables, kept, rows, grad_mixed
                ),
                (after(grad_att, *out_halves, down_total[min(pair, 1)]),),
                [weave or up_flow],
            ),
        )
        while up_flow.moves and pair + 1 == pairs:
            out_halves = beside(lambda *same: same, tuple(out_halves), [up_flow])
        if not up_flow.moves and weave is None:
            weave = Flow(weave_steps(up_flow.result, *out_halves))
    (grad_mixed,) = grad_mixed

    def joint(rows):
        late = after(attended, rows)
        out_terms = [dot_tn(late, piece).astype(BF16) for piece in (grad_first, grad_second)]
        return join_terms(
            dot_tn(normed, rows).astype(BF16), out_terms, shard_count, head_turns, turn_index
        )

    joint_terms = beside(joint, (grad_mixed,), [weave])
    joint_flow = Flow(
        scatter_steps(joint_terms.reshape(shard_count, shard_rows, -1), *both, fold=1)
    )

    def norm_back(rows):
        return row_call(
            norm_back_kernel,
            where,
            [all_tokens, rows, grad_hidden],
            [],
            [inner],
            [(model_width, BF16)],
            [(1, model_width), (1, model_width), (1, 3 * own_width)],
            flops * (units + 3 * own_width),
            split=True,
        )

    mine, other, gain_sum, shift_sum, mixed_sum = beside(
        norm_back, (after(grad_mixed, joint_terms),), [joint_flow, weave]
    )

    def spread(value, count):
        value = value.reshape(count, 1, -1)
        whole = jnp.zeros((count, ctx_count, value.shape[2]), F32)
        return lax.dynamic_update_slice_in_dim(whole, value, ctx_index, 1).reshape(-1)

    grad_float = own_grad.astype(F32)
    mixed_sum = jnp.transpose(mixed_sum.reshape(pairs, 3, 2 * HEAD_DIM), (1, 0, 2))
    sums = (
        gain_sum.reshape(-1),
        shift_sum.reshape(-1),
        spread(mixed_sum, 3 * own_heads),
        jnp.sum(grad_float, axis=0),
        spread(hidden_sum, shard_count),
    )
    total_flow = Flow(total_steps(jnp.concatenate(sums)))
    at = jnp.stack([shard_index % head_turns, ctx_index % 2]).astype(jnp.int32)

    def nothing():
        return ()

    while weave.moves:
        beside(nothing, (), [weave])
    up_swap, out_finish = weave.result
    down_total = beside(side_by_side, down_total, [joint_flow, out_finish, up_swap])
    while joint_flow.moves:
        beside(nothing, (), [joint_flow])
    weave = Flow(weave_steps(joint_flow.result, mine, other))
    (up_dealt,) = beside(
        lambda *halves: deal_columns(*halves, unit, list(range(shard_count)), at),
        up_swap.result,
        [weave, total_flow],
    )
    while weave.moves:
        beside(nothing, (), [flow for flow in (weave, total_flow) if flow.moves])
    joint_swap, norm_finish = weave.result
    beside(
        nothing, (), [flow for flow in (joint_swap, total_flow) if flow.moves], late=[norm_finish]
    )
    qkv_dealt, out_dealt = beside(
        lambda *halves: deal_columns(*halves, HEAD_DIM, qkv_order, at, with_out=True),
        joint_swap.result,
        [flow for flow in (total_flow,) if flow.moves],
        early=[norm_finish],
    )
    out_sum, grad_normed = out_finish.result, norm_finish.result

    inputs = own_tokens.astype(F32)
    output = (inputs + out_sum + (out_bias_all + down_bias_all)).astype(BF16)

    scaled, inv_std = standard(own_tokens)
    grad_scaled = grad_normed * gain_all
    grad_input = inv_std * (
        grad_scaled
        - jnp.mean(grad_scaled, axis=1, keepdims=True)
        - scaled * jnp.mean(grad_scaled * scaled, axis=1, keepdims=True)
    )
    input_grad = (grad_float + grad_input).astype(BF16)

    while total_flow.moves:
        beside(nothing, (), [total_flow])
    total = total_flow.result
    own_sums, start = [], 0
    for item in sums:
        size = item.shape[0] // shard_count
        own_sums.append(lax.dynamic_slice_in_dim(total, start + shard_index * size, size))
        start += item.shape[0]
    gain_total, shift_total, qkv_bias_total, bias_total, up_bias_total = own_sums

    return (
        output[None],
        input_grad[None],
        gain_total,
        shift_total,
        qkv_dealt,
        qkv_bias_total,
        out_dealt,
        bias_total,
        up_dealt,
        up_bias_total,
        down_total,
        bias_total,
    )


def solution(mesh):
    in_specs = (
        P("fsdp", "ctx", None),
        P(),
        P("fsdp", None),
        P("fsdp"),
        P("fsdp"),
        P("fsdp", None),
        P("fsdp"),
        P("fsdp", None),
        P("fsdp"),
        P("fsdp", None),
        P("fsdp"),
        P("fsdp", None),
        P("fsdp"),
        P("fsdp", "ctx", None),
    )
    out_specs = (
        P("fsdp", "ctx", None),
        P("fsdp", "ctx", None),
        P("fsdp"),
        P("fsdp"),
        P("fsdp", None),
        P("fsdp"),
        P("fsdp", None),
        P("fsdp"),
        P("fsdp", None),
        P("fsdp"),
        P("fsdp", None),
        P("fsdp"),
    )
    return jax.shard_map(shards, mesh=mesh, in_specs=in_specs, out_specs=out_specs, check_vma=False)
```

time: 672 us -> 649 us (0.966)
  waiting for transfers between devices: 201 us -> 154 us
  Pallas kernels: 195 us -> 221 us
  other arithmetic: 57.5 us -> 66.8 us
    ppermute x53 -> x56, waiting for transfers between devices: 200 us -> 150 us  [beside(): lax.ppermute(value, axis, pairs)]
    convert_element_type x6 -> x2, other arithmetic: 26.3 us -> 6.35 us  [weave_steps(): down_sum = block(place - far, down_sum).astype(BF16)]
    select_n x0 -> x5, other arithmetic: none -> 12.9 us  [the longest x4 12.9 us: weave_steps(): down_sum = jnp.where(place <= line - step, down, down_sum)]
    another operation x1 -> x8, other arithmetic: 0.18 us -> 13 us  [the longest x6 12.8 us: swap_cores(): blocks = jnp.stack([at_chip(chip) for chip in range(line)])]
    pallas_call x1 -> x2, Pallas kernels: 33.1 us -> 45.3 us  [attention_backward(): pl.pallas_call(functools.partial(backward_kernel, pair), out_shape=jax.Sh...]
    concatenate x2 -> x0, local copies, waits for them, and re-layouts: 9.67 us -> none  [the longest x1 5.26 us: turn_tables(): cos_table = jnp.concatenate([cosine, cosine, ones] * 2, axis=1)]
    mul x0 -> x2, other arithmetic: none -> 8.82 us  [the longest x1 8.81 us: turn_tables(): jnp.sin(angles) * jnp.where(lane < half, -1.0, 1.0)[None, :]]
    pallas_call x2, Pallas kernels: 14.4 us -> 22.8 us  [deal_columns(): pl.pallas_call(functools.partial(deal_kernel, unit, order), out_shape=out...]
  transfers between devices with their start and end apart: 60 -> 61, of which waited for: 16 -> 23; matrix products, arithmetic and copies ran while one was open for 21% -> 13% of each run, Pallas kernels for 28% -> 34%
where the time goes in v3:
time: 649 us; the launch traced here: 642 us
  Pallas kernels  221 us (34%)
  waiting for transfers between devices  154 us (24%)
  starting transfers between devices  80.6 us (12%)
  other arithmetic  66.8 us (10%)
  local copies, waits for them, and re-layouts  58.8 us (9%)
  matrix products  44.8 us (7%)
  between operations  15.5 us (2%)
    ppermute x56, waiting for transfers between devices, beside(): lax.ppermute(value, axis, pairs)  150 us
    pallas_call x4, Pallas kernels, row_call(): pl.pallas_call(body, out_shape=out_shape + [jax.ShapeDtypeStruct(shape, F...  98.5 us
    ppermute x56, starting transfers between devices, beside(): lax.ppermute(value, axis, pairs)  80.2 us
    pallas_call x2, Pallas kernels, attention_backward(): pl.pallas_call(functools.partial(backward_kernel, pair), out_shape=jax.Sh...  45.3 us
    dot_general x6, matrix products, dot_tn(): lax.dot_general(left, right, (((0,), (0,)), ((), ())), preferred_element_...  44.8 us
    pallas_call x1, Pallas kernels, attention_forward(): pl.pallas_call(forward_kernel, out_shape=(jax.ShapeDtypeStruct((tokens, w...  38.4 us
    unnamed x195, local copies, waits for them, and re-layouts  33.4 us
    pallas_call x2, Pallas kernels, deal_columns(): pl.pallas_call(functools.partial(deal_kernel, unit, order), out_shape=out...  22.8 us
  transfers between devices with their start and end apart: 61, of which 23 were waited for; matrix products, arithmetic and copies ran while one was open for 13% of the time, Pallas kernels for 34%

profile of v3, /device:TPU:0, one launch (start us, length us, event | category | flops | bytes accessed | tf_op | source)
XLA Modules:
  0.0 641.8 jit_solution(11040802558474490989)
XLA Ops:
  8.0 3.4 copy-done.2
  11.4 2.8 copy-done.4
  19.0 3.0 fusion.67
  22.0 2.9 collective-permute-start
  27.0 2.9 collective-permute-start.4
  32.3 13.6 %collective-permute-done.2 = bf16[8,704]{1,0:T(8,128)(2,1)S(1)} collective-permute-done((bf16[8,704]{1,0:T(8,128)(2,1)S(1)}, bf16[8,704]{1,0:T(8,128)(2,1)S(1)}, u32[]{:S(2)}, u32[]{:S(2)}) %collective-permute-start.2) | collective-permute-done | bytes 11296 | tf_op jit(solution)/shard_map/ppermute | solution.py:59
  55.6 8.8 %fusion.41 = (f32[2048,128]{1,0:T(8,128)}, f32[2048,128]{1,0:T(8,128)}, f32[2048,128]{1,0:T(8,128)S(1)}, f32[2048,128]{1,0:T(8,128)}) fusion(f32[2048]{0:T(1024)S(1)} %get-tuple-element.459, f32[128]{0:T(128)S(1)} %get-tuple-element.457, f32[128]{0:T(128)S(1)} %get-tuple-element.458, f32[2048]{0:T(1024)S(1)} %get-tuple-element.460), kind=kLoop, calls=%fused_computation.89 | loop fusion | flops 1048576 | bytes 4211712 | tf_op jit(solution)/shard_map/mul | solution.py:391
  64.4 7.7 %collective-permute-done.5.refs_8_.refs_5_ = bf16[256,1792]{1,0:T(8,128)(2,1)} collective-permute-done((bf16[256,1792]{1,0:T(8,128)(2,1)}, bf16[256,1792]{1,0:T(8,128)(2,1)}, u32[]{:S(2)}, u32[]{:S(2)}) %collective-permute-start.5) | collective-permute-done | bytes 917536 | tf_op jit(solution)/shard_map/ppermute | solution.py:59
  72.1 17.4 %collective-permute-done.6.refs_9_.refs_6_ = bf16[256,1792]{1,0:T(8,128)(2,1)} collective-permute-done((bf16[256,1792]{1,0:T(8,128)(2,1)}, bf16[256,1792]{1,0:T(8,128)(2,1)}, u32[]{:S(2)}, u32[]{:S(2)}) %collective-permute-start.6) | collective-permute-done | bytes 917536 | tf_op jit(solution)/shard_map/ppermute | solution.py:59
  91.0 3.4 all-gather.15.cloned.1.call-done
  97.9 34.3 %shard_map.230 = (bf16[2048,2048]{1,0:T(8,128)(2,1)}, bf16[2048,1024]{1,0:T(8,128)(2,1)}, bf16[2048,1024]{1,0:T(8,128)(2,1)}, bf16[2048,768]{1,0:T(8,128)(2,1)}) custom-call(s32[2]{0:T(128)} %pad_add_fusion.at, bf16[2048,2048]{1,0:T(8,128)(2,1)} %bitcast.339, f32[2048,128]{1,0:T(8,128)} %get-tuple-element.224.refs_1_, ...), custom_call_target="tpu_custom_call" | custom-call | flops 15032385536 | bytes 37772288 | tf_op jit(solution)/shard_map/pallas_call | solution.py:512
  132.2 10.0 %collective-permute-done.10.refs_5_.refs_4_ = bf16[256,2048]{1,0:T(8,128)(2,1)S(1)} collective-permute-done((bf16[256,2048]{1,0:T(8,128)(2,1)S(1)}, bf16[256,2048]{1,0:T(8,128)(2,1)S(1)}, u32[]{:S(2)}, u32[]{:S(2)}) %collective-permute-start.10) | collective-permute-done | bytes 1048608 | tf_op jit(solution)/shard_map/ppermute | solution.py:59
  144.4 8.0 %convolution_convert_fusion.3 = bf16[1024,1024]{1,0:T(8,128)(2,1)S(1)} fusion(bf16[2048,1024]{1,0:T(8,128)(2,1)} %get-tuple-element.240.refs_1_, bf16[2048,1024]{1,0:T(8,128)(2,1)} %all-gather.7.cloned.1.call-done.refs_0_), kind=kOutput, calls=%fused_computation.73 | convolution fusion | flops 4296015872 | bytes 10485760 | tf_op jit(solution)/shard_map/dot_general | solution.py:29
  156.9 2.4 collective-permute-start.16
  159.3 38.4 %shard_map.231 = (bf16[2048,256]{1,0:T(8,128)(2,1)S(1)}, bf16[2048,768]{1,0:T(8,128)(2,1)S(1)}, f32[256,2048]{1,0:T(8,128)S(1)}, f32[4,2048]{1,0:T(4,128)S(1)}) custom-call(s32[128]{0:T(128)S(1)} %copy-done.7, s32[4]{0:T(128)S(1)} %bitcast.300, bf16[2048,768]{1,0:T(8,128)(2,1)S(1)} %copy-done.13), custom_call_target="tpu_custom_call" | custom-call | flops 40000000000 | bytes 16000000 | tf_op jit(solution)/shard_map/pallas_call | solution.py:402
  202.9 3.0 collective-permute-start.17
  205.9 9.4 %convolution_convert_fusion.2 = bf16[1024,1024]{1,0:T(8,128)(2,1)} fusion(bf16[2048,1024]{1,0:T(8,128)(2,1)} %get-tuple-element.240.refs_1_, bf16[2048,1024]{1,0:T(8,128)(2,1)} %all-gather.9.cloned.1.call-done.refs_1_), kind=kOutput, calls=%fused_computation.72 | convolution fusion | flops 4296015872 | bytes 10485760 | tf_op jit(solution)/shard_map/dot_general | solution.py:29
  218.2 2.1 collective-permute-start.19
  220.4 18.7 %shard_map.232 = (bf16[2048,1024]{1,0:T(8,128)(2,1)}, bf16[2048,256]{1,0:T(8,128)(2,1)}, f32[1,1024]{1,0:T(1,128)}) custom-call(s32[2]{0:T(128)} %pad_add_fusion.at, bf16[2048,1024]{1,0:T(8,128)(2,1)} %all-gather.7.cloned.1.call-done.refs_0_, bf16[2048,1024]{1,0:T(8,128)(2,1)} %all-gather.9.cloned.1.call-done.refs_1_, ...), custom_call_target="tpu_custom_call" | custom-call | flops 10737418240 | bytes 23068672 | tf_op jit(solution)/shard_map/pallas_call | solution.py:512
  241.9 12.8 %convolution_convert_fusion = bf16[2048,1024]{1,0:T(8,128)(2,1)} fusion(bf16[2048,2048]{1,0:T(8,128)(2,1)} %get-tuple-element.281, bf16[2048,1024]{1,0:T(8,128)(2,1)S(1)} %copy-done.88), kind=kOutput, calls=%fused_computation.2 | convolution fusion | flops 8592031744 | bytes 16777216 | tf_op jit(solution)/shard_map/dot_general | solution.py:29
  255.8 2.7 fusion.64
  262.5 17.6 %shard_map.233 = (bf16[4,256,2048]{2,1,0:T(8,128)(2,1)}, bf16[4,256,2048]{2,1,0:T(8,128)(2,1)}) custom-call(s32[2]{0:T(128)} %pad_add_fusion.at, bf16[2048,256]{1,0:T(8,128)(2,1)} %copy-done.8, bf16[2048,1024]{1,0:T(8,128)(2,1)} %get-tuple-element.240.refs_1_, bf16[256,2048]{1,0:T(8,128)(2,1)} %copy-done.56, bf16[256,2048]{1,0:T(8,128)(2,1)} %copy-done.83, ...), custom_call_target="tpu_custom_call" | custom-call | flops 10737418240 | bytes 18874368 | tf_op jit(solution)/shard_map/pallas_call | solution.py:512
  280.1 2.1 collective-permute-done.23
  295.9 22.7 %shard_map.234.refs_0_ = bf16[2048,768]{1,0:T(8,128)(2,1)S(1)} custom-call(s32[128]{0:T(128)S(1)} %copy-done.7, s32[4]{0:T(128)S(1)} %bitcast.301, f32[2048,128]{1,0:T(8,128)S(1)} %get-tuple-element.289.cos_ref, f32[2048,128]{1,0:T(8,128)S(1)} %copy-done.5, bf16[2048,768]{1,0:T(8,128)(2,1)S(1)} %copy-done.17, f32[256,2048]{1,0:T(8,128)S(1)} %get-tuple-element.292.summed_ref, ...), custom_call_target="tpu_custom_call" | custom-call | flops 20000000000 | bytes 8000000 | tf_op jit(solution)/shard_map/pallas_call | solution.py:426
  332.1 22.6 %shard_map.235.refs_1_ = bf16[2048,768]{1,0:T(8,128)(2,1)S(1)} custom-call(s32[128]{0:T(128)S(1)} %copy-done.7, s32[4]{0:T(128)S(1)} %bitcast.302, f32[2048,128]{1,0:T(8,128)S(1)} %get-tuple-element.289.cos_ref, f32[2048,128]{1,0:T(8,128)S(1)} %copy-done.6, bf16[2048,768]{1,0:T(8,128)(2,1)S(1)} %copy-done.18, ...), custom_call_target="tpu_custom_call", output_to_operand_aliasing={{}: (8, {})} | custom-call | flops 20000000000 | bytes 8000000 | tf_op jit(solution)/shard_map/pallas_call | solution.py:426
  354.8 5.9 fusion.33
  360.7 4.9 collective-permute-start.30
  366.9 10.4 %convolution_convert_fusion.1.left = bf16[2048,768]{1,0:T(8,128)(2,1)} fusion(bf16[2048,2048]{1,0:T(8,128)(2,1)} %get-tuple-element.281, bf16[2048,768]{1,0:T(8,128)(2,1)S(1)} %shard_map.235.refs_1_), kind=kOutput, calls=%fused_computation.3 | convolution fusion | flops 6444023808 | bytes 14680064 | tf_op jit(solution)/shard_map/dot_general | solution.py:29
  377.3 2.1 convolution_convert_fusion.4.refs_1_
  379.5 2.1 convolution_convert_fusion.5.refs_0_
  381.6 4.7 shard_map.236
  386.3 2.4 collective-permute-done.30
  388.6 4.1 collective-permute-done.31
  392.7 3.1 fusion.63
  397.9 2.3 copy-done.23
  400.2 4.3 fusion.35
  404.5 3.0 collective-permute-start.33
  407.5 3.5 collective-permute-start.34
  412.3 27.9 %shard_map.237 = (bf16[4,256,2048]{2,1,0:T(8,128)(2,1)}, bf16[4,256,2048]{2,1,0:T(8,128)(2,1)}, f32[1,2048]{1,0:T(1,128)}, f32[1,2048]{1,0:T(1,128)}, f32[1,768]{1,0:T(1,128)}) custom-call(s32[2]{0:T(128)} %pad_add_fusion.at, bf16[2048,2048]{1,0:T(8,128)(2,1)} %bitcast.340, bf16[2048,768]{1,0:T(8,128)(2,1)} %copy-done.12, ...), custom_call_target="tpu_custom_call" | custom-call | flops 15032385536 | bytes 31457280 | tf_op jit(solution)/shard_map/pallas_call | solution.py:512
  440.4 2.7 fusion.24
  447.7 3.0 select_bitcast_fusion.7
  452.4 3.8 fusion.22
  456.2 2.3 pad_maximum_fusion.mine
  458.5 5.6 collective-permute-start.38
  468.0 10.2 %shard_map.238 = f32[2048,2048]{1,0:T(8,128)} custom-call(bf16[2048,1024]{1,0:T(8,128)(2,1)} %all-gather.11.cloned.1.call-done.refs_0_, bf16[2048,1024]{1,0:T(8,128)(2,1)} %all-gather.13.cloned.1.call-done.refs_1_), custom_call_target="tpu_custom_call" | custom-call | bytes 25165824 | tf_op jit(solution)/shard_map/pallas_call | solution.py:781
  478.3 2.1 collective-permute-done.36
  480.7 5.8 collective-permute-done.38
  486.5 4.9 collective-permute-done.39
  497.9 11.1 %shard_map.239 = f32[512,8192]{1,0:T(8,128)} custom-call(s32[2]{0:T(128)S(1)} %pad_add_fusion.1.at_ref, bf16[4,256,2048]{2,1,0:T(8,128)(2,1)} %pad_maximum_fusion.mine, bf16[4,256,2048]{2,1,0:T(8,128)(2,1)} %collective-permute-done.40.other), custom_call_target="tpu_custom_call" | custom-call | bytes 25165824 | tf_op jit(solution)/shard_map/pallas_call | solution.py:710
  509.0 9.8 %collective-permute-done.41 = bf16[256,2048]{1,0:T(8,128)(2,1)S(1)} collective-permute-done((bf16[256,2048]{1,0:T(8,128)(2,1)S(1)}, bf16[256,2048]{1,0:T(8,128)(2,1)S(1)}, u32[]{:S(2)}, u32[]{:S(2)}) %collective-permute-start.41) | collective-permute-done | bytes 1048608 | tf_op jit(solution)/shard_map/ppermute | solution.py:59
  518.8 4.2 collective-permute-done.42
  527.7 2.7 collective-permute-start.47
  530.4 23.9 %collective-permute-done.47 = f32[20480]{0:T(1024)S(1)} collective-permute-done((f32[20480]{0:T(1024)S(1)}, f32[20480]{0:T(1024)S(1)}, u32[]{:S(2)}, u32[]{:S(2)}) %collective-permute-start.47) | collective-permute-done | bytes 81952 | tf_op jit(solution)/shard_map/ppermute | solution.py:59
  558.4 3.3 collective-permute-start.50
  561.7 25.0 %collective-permute-done.50 = f32[20480]{0:T(1024)S(1)} collective-permute-done((f32[20480]{0:T(1024)S(1)}, f32[20480]{0:T(1024)S(1)}, u32[]{:S(2)}, u32[]{:S(2)}) %collective-permute-start.50) | collective-permute-done | bytes 81952 | tf_op jit(solution)/shard_map/ppermute | solution.py:59
  586.7 2.6 fusion.15
  592.8 2.3 pad_maximum_fusion.1.mine
  599.0 2.1 collective-permute-start.52
  601.1 2.8 collective-permute-done.52
  604.1 11.7 %shard_map.240 = (f32[512,6144]{1,0:T(8,128)}, f32[512,2048]{1,0:T(8,128)}) custom-call(s32[2]{0:T(128)S(1)} %pad_add_fusion.1.at_ref, bf16[4,256,2048]{2,1,0:T(8,128)(2,1)} %pad_maximum_fusion.1.mine, bf16[4,256,2048]{2,1,0:T(8,128)(2,1)} %collective-permute-done.51.other), custom_call_target="tpu_custom_call" | custom-call | bytes 25165824 | tf_op jit(solution)/shard_map/pallas_call | solution.py:710
  615.8 4.3 collective-permute-done.54
  620.2 4.2 collective-permute-done.55
  626.3 3.0 fusion.61
  629.4 5.2 fusion.43
  (390 shorter events, 114.7 us)
Async XLA Ops:
  7.2 87.2 %all-gather.15.cloned.1.call-start = ((), (), s32[]{:S(2)}) async-start(), calls=%async_computation.4 | async-start | bytes 9437184 | tf_op jit(solution)/shard_map/all_gather | solution.py:836
  7.9 136.5 %all-gather.7.cloned.1.call-start = ((), (), s32[]{:S(2)}) async-start(), calls=%async_computation | async-start | bytes 4718592 | tf_op jit(solution)/shard_map/all_gather | solution.py:836
  17.9 185.0 %all-gather.9.cloned.1.call-start = ((), (), s32[]{:S(2)}) async-start(), calls=%async_computation.1 | async-start | bytes 4718592 | tf_op jit(solution)/shard_map/all_gather | solution.py:836
  22.0 25.5 %collective-permute-start = (bf16[256,1792]{1,0:T(8,128)(2,1)}, bf16[256,1792]{1,0:T(8,128)(2,1)}, u32[]{:S(2)}, u32[]{:S(2)}) collective-permute-start(bf16[256,1792]{1,0:T(8,128)(2,1)} %get-tuple-element.220.refs_6_.refs_3_), channel_id=1, source_target_pairs={{0,1},{1,0},{2,3},{3,2},{4,5},{5,4},{6,7},{7,6},{8,9},{9,8},{10,11... | collective-permute-start | bytes 2752520 | tf_op jit(solution)/shard_map/ppermute | solution.py:59
  24.9 22.6 %collective-permute-start.1 = (bf16[256,1792]{1,0:T(8,128)(2,1)}, bf16[256,1792]{1,0:T(8,128)(2,1)}, u32[]{:S(2)}, u32[]{:S(2)}) collective-permute-start(bf16[256,1792]{1,0:T(8,128)(2,1)} %get-tuple-element.222.refs_10_.refs_7_), channel_id=1, source_target_pairs={{0,2},{1,3},{2,0},{3,1},{4,6},{5,7},{6,4},{7,5},{8,10},{9,11},{10,... | collective-permute-start | bytes 2752520 | tf_op jit(solution)/shard_map/ppermute | solution.py:59
  26.5 19.5 %collective-permute-start.2 = (bf16[8,704]{1,0:T(8,128)(2,1)S(1)}, bf16[8,704]{1,0:T(8,128)(2,1)S(1)}, u32[]{:S(2)}, u32[]{:S(2)}) collective-permute-start(bf16[8,704]{1,0:T(8,128)(2,1)S(1)} %reshape.366), channel_id=1, source_target_pairs={{0,1},{1,0},{2,3},{3,2},{4,5},{5,4},{6,7},{7,6},{8,9},{9,8},{10,11... | collective-permute-start | bytes 33800 | tf_op jit(solution)/shard_map/ppermute | solution.py:59
  27.0 20.5 %collective-permute-start.3 = (bf16[8,704]{1,0:T(8,128)(2,1)S(1)}, bf16[8,704]{1,0:T(8,128)(2,1)S(1)}, u32[]{:S(2)}, u32[]{:S(2)}) collective-permute-start(bf16[8,704]{1,0:T(8,128)(2,1)S(1)} %reshape.366), channel_id=1, source_target_pairs={{0,2},{1,3},{2,0},{3,1},{4,6},{5,7},{6,4},{7,5},{8,10},{9,11},{10,... | collective-permute-start | bytes 33800 | tf_op jit(solution)/shard_map/ppermute | solution.py:59
  27.0 20.5 %collective-permute-start.4 = (bf16[8,704]{1,0:T(8,128)(2,1)S(1)}, bf16[8,704]{1,0:T(8,128)(2,1)S(1)}, u32[]{:S(2)}, u32[]{:S(2)}) collective-permute-start(bf16[8,704]{1,0:T(8,128)(2,1)S(1)} %reshape.366), channel_id=1, source_target_pairs={{0,3},{1,2},{2,1},{3,0},{4,7},{5,6},{6,5},{7,4},{8,11},{9,10},{10,... | collective-permute-start | bytes 33800 | tf_op jit(solution)/shard_map/ppermute | solution.py:59
  30.0 126.9 %copy-start.65 = (bf16[64,2048]{1,0:T(8,128)(2,1)}, bf16[64,2048]{1,0:T(8,128)(2,1)S(1)}, u32[]{:S(2)}) copy-start(bf16[64,2048]{1,0:T(8,128)(2,1)S(1)} %dynamic-slice_bitcast_fusion.17.refs_7_.refs_6_) | copy-start | bytes 786436
  31.4 66.0 %copy-start.56 = (bf16[256,2048]{1,0:T(8,128)(2,1)}, bf16[256,2048]{1,0:T(8,128)(2,1)S(1)}, u32[]{:S(2)}) copy-start(bf16[256,2048]{1,0:T(8,128)(2,1)S(1)} %dynamic-slice_bitcast_fusion.4.refs_3_.refs_2_) | copy-start | bytes 3145732
  48.4 23.7 %collective-permute-start.5 = (bf16[256,1792]{1,0:T(8,128)(2,1)}, bf16[256,1792]{1,0:T(8,128)(2,1)}, u32[]{:S(2)}, u32[]{:S(2)}) collective-permute-start(bf16[256,1792]{1,0:T(8,128)(2,1)} %get-tuple-element.220.refs_6_.refs_3_), channel_id=1, source_target_pairs={{0,2},{1,3},{2,0},{3,1},{4,6},{5,7},{6,4},{7,5},{8,10},{9,11},{10,... | collective-permute-start | bytes 2752520 | tf_op jit(solution)/shard_map/ppermute | solution.py:59
  50.0 39.5 %collective-permute-start.6 = (bf16[256,1792]{1,0:T(8,128)(2,1)}, bf16[256,1792]{1,0:T(8,128)(2,1)}, u32[]{:S(2)}, u32[]{:S(2)}) collective-permute-start(bf16[256,1792]{1,0:T(8,128)(2,1)} %collective-permute-done.refs_7_.refs_4_), channel_id=1, source_target_pairs={{0,2},{1,3},{2,0},{3,1},{4,6},{5,7},{6,4},{7,5},{8,10},{9,11},{10,... | collective-permute-start | bytes 2752520 | tf_op jit(solution)/shard_map/ppermute | solution.py:59
  50.5 39.0 %collective-permute-start.7 = (bf16[256,1792]{1,0:T(8,128)(2,1)}, bf16[256,1792]{1,0:T(8,128)(2,1)}, u32[]{:S(2)}, u32[]{:S(2)}) collective-permute-start(bf16[256,1792]{1,0:T(8,128)(2,1)} %get-tuple-element.222.refs_10_.refs_7_), channel_id=1, source_target_pairs={{0,1},{1,0},{2,3},{3,2},{4,5},{5,4},{6,7},{7,6},{8,9},{9,8},{10,11... | collective-permute-start | bytes 2752520 | tf_op jit(solution)/shard_map/ppermute | solution.py:59
  51.7 39.2 %collective-permute-start.8 = (bf16[256,1792]{1,0:T(8,128)(2,1)}, bf16[256,1792]{1,0:T(8,128)(2,1)}, u32[]{:S(2)}, u32[]{:S(2)}) collective-permute-start(bf16[256,1792]{1,0:T(8,128)(2,1)} %collective-permute-done.1.refs_11_.refs_8_), channel_id=1, source_target_pairs={{0,1},{1,0},{2,3},{3,2},{4,5},{5,4},{6,7},{7,6},{8,9},{9,8},{10,11... | collective-permute-start | bytes 2752520 | tf_op jit(solution)/shard_map/ppermute | solution.py:59
  55.2 234.2 %all-gather.11.cloned.1.call-start = ((), (), s32[]{:S(2)}) async-start(), calls=%async_computation.2 | async-start | bytes 4718592 | tf_op jit(solution)/shard_map/all_gather | solution.py:836
  94.4 47.8 %collective-permute-start.10 = (bf16[256,2048]{1,0:T(8,128)(2,1)S(1)}, bf16[256,2048]{1,0:T(8,128)(2,1)S(1)}, u32[]{:S(2)}, u32[]{:S(2)}) collective-permute-start(bf16[256,2048]{1,0:T(8,128)(2,1)S(1)} %dynamic-slice_bitcast_fusion.4.refs_3_.refs_2_), channel_id=1, source_target_pairs={{0,2},{1,3},{2,0},{3,1},{4,6},{5,7},{6,4},{7,5},{8,10},{9,11},{10,... | collective-permute-start | bytes 3145736 | tf_op jit(solution)/shard_map/ppermute | solution.py:59
  95.9 46.3 %collective-permute-start.11 = (bf16[256,2048]{1,0:T(8,128)(2,1)S(1)}, bf16[256,2048]{1,0:T(8,128)(2,1)S(1)}, u32[]{:S(2)}, u32[]{:S(2)}) collective-permute-start(bf16[256,2048]{1,0:T(8,128)(2,1)S(1)} %dynamic-slice_bitcast_fusion.4.refs_3_.refs_2_), channel_id=1, source_target_pairs={{0,3},{1,2},{2,1},{3,0},{4,7},{5,6},{6,5},{7,4},{8,11},{9,10},{10,... | collective-permute-start | bytes 3145736 | tf_op jit(solution)/shard_map/ppermute | solution.py:59
  97.4 46.0 %collective-permute-start.9 = (bf16[256,2048]{1,0:T(8,128)(2,1)S(1)}, bf16[256,2048]{1,0:T(8,128)(2,1)S(1)}, u32[]{:S(2)}, u32[]{:S(2)}) collective-permute-start(bf16[256,2048]{1,0:T(8,128)(2,1)S(1)} %dynamic-slice_bitcast_fusion.4.refs_3_.refs_2_), channel_id=1, source_target_pairs={{0,1},{1,0},{2,3},{3,2},{4,5},{5,4},{6,7},{7,6},{8,9},{9,8},{10,11... | collective-permute-start | bytes 3145736 | tf_op jit(solution)/shard_map/ppermute | solution.py:59
  152.8 47.6 %collective-permute-start.12 = (bf16[2,128,1024]{2,1,0:T(8,128)(2,1)S(1)}, bf16[2,128,1024]{2,1,0:T(8,128)(2,1)S(1)}, u32[]{:S(2)}, u32[]{:S(2)}) collective-permute-start(bf16[2,128,1024]{2,1,0:T(8,128)(2,1)S(1)} %dynamic-slice_bitcast_fusion.12), channel_id=1, source_target_pairs={{0,1},{1,0},{2,3},{3,2},{4,5},{5,4},{6,7},{7,6},{8,9},{9,8},{10,11... | collective-permute-start | bytes 1572872 | tf_op jit(solution)/shard_map/ppermute | solution.py:59
  154.3 46.0 %collective-permute-start.13 = (bf16[2,128,1024]{2,1,0:T(8,128)(2,1)S(1)}, bf16[2,128,1024]{2,1,0:T(8,128)(2,1)S(1)}, u32[]{:S(2)}, u32[]{:S(2)}) collective-permute-start(bf16[2,128,1024]{2,1,0:T(8,128)(2,1)S(1)} %dynamic-slice_bitcast_fusion.11), channel_id=1, source_target_pairs={{0,2},{1,3},{2,0},{3,1},{4,6},{5,7},{6,4},{7,5},{8,10},{9,11},{10,... | collective-permute-start | bytes 1572872 | tf_op jit(solution)/shard_map/ppermute | solution.py:59
  155.8 44.5 %collective-permute-start.14 = (bf16[64,2048]{1,0:T(8,128)(2,1)S(1)}, bf16[64,2048]{1,0:T(8,128)(2,1)S(1)}, u32[]{:S(2)}, u32[]{:S(2)}) collective-permute-start(bf16[64,2048]{1,0:T(8,128)(2,1)S(1)} %dynamic-slice_bitcast_fusion.17.refs_7_.refs_6_), channel_id=1, source_target_pairs={{0,1},{1,0},{2,3},{3,2},{4,5},{5,4},{6,7},{7,6},{8,9},{9,8},{10,11... | collective-permute-start | bytes 786440 | tf_op jit(solution)/shard_map/ppermute | solution.py:59
  156.4 44.0 %collective-permute-start.15 = (bf16[64,2048]{1,0:T(8,128)(2,1)S(1)}, bf16[64,2048]{1,0:T(8,128)(2,1)S(1)}, u32[]{:S(2)}, u32[]{:S(2)}) collective-permute-start(bf16[64,2048]{1,0:T(8,128)(2,1)S(1)} %dynamic-slice_bitcast_fusion.17.refs_7_.refs_6_), channel_id=1, source_target_pairs={{0,2},{1,3},{2,0},{3,1},{4,6},{5,7},{6,4},{7,5},{8,10},{9,11},{10,... | collective-permute-start | bytes 786440 | tf_op jit(solution)/shard_map/ppermute | solution.py:59
  156.9 43.4 %collective-permute-start.16 = (bf16[64,2048]{1,0:T(8,128)(2,1)S(1)}, bf16[64,2048]{1,0:T(8,128)(2,1)S(1)}, u32[]{:S(2)}, u32[]{:S(2)}) collective-permute-start(bf16[64,2048]{1,0:T(8,128)(2,1)S(1)} %dynamic-slice_bitcast_fusion.17.refs_7_.refs_6_), channel_id=1, source_target_pairs={{0,3},{1,2},{2,1},{3,0},{4,7},{5,6},{6,5},{7,4},{8,11},{9,10},{10,... | collective-permute-start | bytes 786440 | tf_op jit(solution)/shard_map/ppermute | solution.py:59
  202.9 12.4 %collective-permute-start.17 = (bf16[128,1024]{1,0:T(8,128)(2,1)}, bf16[128,1024]{1,0:T(8,128)(2,1)S(1)}, u32[]{:S(2)}, u32[]{:S(2)}) collective-permute-start(bf16[128,1024]{1,0:T(8,128)(2,1)} %dynamic-slice_bitcast_fusion.16), channel_id=1, source_target_pairs={{0,2},{1,3},{2,0},{3,1},{4,6},{5,7},{6,4},{7,5},{8,10},{9,11},{10,... | collective-permute-start | bytes 786440 | tf_op jit(solution)/shard_map/ppermute | solution.py:59
  205.9 9.4 %collective-permute-start.18 = (bf16[128,1024]{1,0:T(8,128)(2,1)S(1)}, bf16[128,1024]{1,0:T(8,128)(2,1)S(1)}, u32[]{:S(2)}, u32[]{:S(2)}) collective-permute-start(bf16[128,1024]{1,0:T(8,128)(2,1)S(1)} %dynamic-slice_bitcast_fusion.15), channel_id=1, source_target_pairs={{0,1},{1,0},{2,3},{3,2},{4,5},{5,4},{6,7},{7,6},{8,9},{9,8},{10,11... | collective-permute-start | bytes 786440 | tf_op jit(solution)/shard_map/ppermute | solution.py:59
  216.3 106.9 %all-gather.13.cloned.1.call-start = ((), (), s32[]{:S(2)}) async-start(), calls=%async_computation.3 | async-start | bytes 4718592 | tf_op jit(solution)/shard_map/all_gather | solution.py:836
  218.2 20.8 %collective-permute-start.19 = (bf16[2,128,1024]{2,1,0:T(8,128)(2,1)S(1)}, bf16[2,128,1024]{2,1,0:T(8,128)(2,1)S(1)}, u32[]{:S(2)}, u32[]{:S(2)}) collective-permute-start(bf16[2,128,1024]{2,1,0:T(8,128)(2,1)S(1)} %dynamic-slice_bitcast_fusion.10), channel_id=1, source_target_pairs={{0,1},{1,0},{2,3},{3,2},{4,5},{5,4},{6,7},{7,6},{8,9},{9,8},{10,11... | collective-permute-start | bytes 1572872 | tf_op jit(solution)/shard_map/ppermute | solution.py:59
  220.3 18.8 %collective-permute-start.20 = (bf16[2,128,1024]{2,1,0:T(8,128)(2,1)S(1)}, bf16[2,128,1024]{2,1,0:T(8,128)(2,1)S(1)}, u32[]{:S(2)}, u32[]{:S(2)}) collective-permute-start(bf16[2,128,1024]{2,1,0:T(8,128)(2,1)S(1)} %dynamic-slice_bitcast_fusion.9), channel_id=1, source_target_pairs={{0,2},{1,3},{2,0},{3,1},{4,6},{5,7},{6,4},{7,5},{8,10},{9,11},{10,... | collective-permute-start | bytes 1572872 | tf_op jit(solution)/shard_map/ppermute | solution.py:59
  239.6 15.1 %collective-permute-start.21 = (bf16[128,1024]{1,0:T(8,128)(2,1)S(1)}, bf16[128,1024]{1,0:T(8,128)(2,1)S(1)}, u32[]{:S(2)}, u32[]{:S(2)}) collective-permute-start(bf16[128,1024]{1,0:T(8,128)(2,1)S(1)} %dynamic-slice_bitcast_fusion.14), channel_id=1, source_target_pairs={{0,2},{1,3},{2,0},{3,1},{4,6},{5,7},{6,4},{7,5},{8,10},{9,11},{10,... | collective-permute-start | bytes 786440 | tf_op jit(solution)/shard_map/ppermute | solution.py:59
  241.6 13.2 %collective-permute-start.22 = (bf16[128,1024]{1,0:T(8,128)(2,1)S(1)}, bf16[128,1024]{1,0:T(8,128)(2,1)S(1)}, u32[]{:S(2)}, u32[]{:S(2)}) collective-permute-start(bf16[128,1024]{1,0:T(8,128)(2,1)S(1)} %dynamic-slice_bitcast_fusion.13), channel_id=1, source_target_pairs={{0,1},{1,0},{2,3},{3,2},{4,5},{5,4},{6,7},{7,6},{8,9},{9,8},{10,11... | collective-permute-start | bytes 786440 | tf_op jit(solution)/shard_map/ppermute | solution.py:59
  260.5 21.6 %collective-permute-start.23 = (bf16[2,256,1024]{2,1,0:T(8,128)(2,1)}, bf16[2,256,1024]{2,1,0:T(8,128)(2,1)}, u32[]{:S(2)}, u32[]{:S(2)}) collective-permute-start(bf16[2,256,1024]{2,1,0:T(8,128)(2,1)} %dynamic-slice_bitcast_fusion.3), channel_id=1, source_target_pairs={{0,1},{1,0},{2,3},{3,2},{4,5},{5,4},{6,7},{7,6},{8,9},{9,8},{10,11... | collective-permute-start | bytes 3145736 | tf_op jit(solution)/shard_map/ppermute | solution.py:59
  262.3 21.1 %collective-permute-start.24 = (bf16[2,256,1024]{2,1,0:T(8,128)(2,1)}, bf16[2,256,1024]{2,1,0:T(8,128)(2,1)}, u32[]{:S(2)}, u32[]{:S(2)}) collective-permute-start(bf16[2,256,1024]{2,1,0:T(8,128)(2,1)} %dynamic-slice_bitcast_fusion.2), channel_id=1, source_target_pairs={{0,2},{1,3},{2,0},{3,1},{4,6},{5,7},{6,4},{7,5},{8,10},{9,11},{10,... | collective-permute-start | bytes 3145736 | tf_op jit(solution)/shard_map/ppermute | solution.py:59
  289.4 30.9 %collective-permute-start.25 = (bf16[256,1024]{1,0:T(8,128)(2,1)}, bf16[256,1024]{1,0:T(8,128)(2,1)S(1)}, u32[]{:S(2)}, u32[]{:S(2)}) collective-permute-start(bf16[256,1024]{1,0:T(8,128)(2,1)} %dynamic-slice_bitcast_fusion.8), channel_id=1, source_target_pairs={{0,2},{1,3},{2,0},{3,1},{4,6},{5,7},{6,4},{7,5},{8,10},{9,11},{10,... | collective-permute-start | bytes 1572872 | tf_op jit(solution)/shard_map/ppermute | solution.py:59
  289.8 30.5 %collective-permute-start.26 = (bf16[256,1024]{1,0:T(8,128)(2,1)}, bf16[256,1024]{1,0:T(8,128)(2,1)S(1)}, u32[]{:S(2)}, u32[]{:S(2)}) collective-permute-start(bf16[256,1024]{1,0:T(8,128)(2,1)} %dynamic-slice_bitcast_fusion.7), channel_id=1, source_target_pairs={{0,1},{1,0},{2,3},{3,2},{4,5},{5,4},{6,7},{7,6},{8,9},{9,8},{10,11... | collective-permute-start | bytes 1572872 | tf_op jit(solution)/shard_map/ppermute | solution.py:59
  323.2 31.6 %collective-permute-start.29 = (bf16[4,256,2048]{2,1,0:T(8,128)(2,1)}, bf16[4,256,2048]{2,1,0:T(8,128)(2,1)}, u32[]{:S(2)}, u32[]{:S(2)}) collective-permute-start(bf16[4,256,2048]{2,1,0:T(8,128)(2,1)} %get-tuple-element.317), channel_id=1, source_target_pairs={{0,4},{4,0},{8,12},{12,8},{16,20},{20,16},{24,28},{28,24},{1,5},{5... | collective-permute-start | bytes 12582920 | tf_op jit(solution)/shard_map/ppermute | solution.py:59
  323.2 31.5 %collective-permute-start.27 = (bf16[256,2048]{1,0:T(8,128)(2,1)}, bf16[256,2048]{1,0:T(8,128)(2,1)S(1)}, u32[]{:S(2)}, u32[]{:S(2)}) collective-permute-start(bf16[256,2048]{1,0:T(8,128)(2,1)} %pad_maximum_fusion.2), channel_id=1, source_target_pairs={{0,8},{4,12},{8,16},{12,20},{16,24},{20,28},{1,9},{5,13},{9,17},{1... | collective-permute-start | bytes 3145736 | tf_op jit(solution)/shard_map/ppermute | solution.py:59
  324.6 30.2 %collective-permute-start.28 = (bf16[256,2048]{1,0:T(8,128)(2,1)}, bf16[256,2048]{1,0:T(8,128)(2,1)S(1)}, u32[]{:S(2)}, u32[]{:S(2)}) collective-permute-start(bf16[256,2048]{1,0:T(8,128)(2,1)} %pad_maximum_fusion.2), channel_id=1, source_target_pairs={{8,0},{12,4},{16,8},{20,12},{24,16},{28,20},{9,1},{13,5},{17,9},{2... | collective-permute-start | bytes 3145736 | tf_op jit(solution)/shard_map/ppermute | solution.py:59
  360.7 27.9 %collective-permute-start.30 = (bf16[256,2048]{1,0:T(8,128)(2,1)}, bf16[256,2048]{1,0:T(8,128)(2,1)S(1)}, u32[]{:S(2)}, u32[]{:S(2)}) collective-permute-start(bf16[256,2048]{1,0:T(8,128)(2,1)} %get-tuple-element.324), channel_id=1, source_target_pairs={{0,8},{4,12},{8,16},{12,20},{16,24},{20,28},{1,9},{5,13},{9,17},{1... | collective-permute-start | bytes 3145736 | tf_op jit(solution)/shard_map/ppermute | solution.py:59
  365.6 27.1 %collective-permute-start.31 = (bf16[256,2048]{1,0:T(8,128)(2,1)}, bf16[256,2048]{1,0:T(8,128)(2,1)S(1)}, u32[]{:S(2)}, u32[]{:S(2)}) collective-permute-start(bf16[256,2048]{1,0:T(8,128)(2,1)} %get-tuple-element.325), channel_id=1, source_target_pairs={{8,0},{12,4},{16,8},{20,12},{24,16},{28,20},{9,1},{13,5},{17,9},{2... | collective-permute-start | bytes 3145736 | tf_op jit(solution)/shard_map/ppermute | solution.py:59
  404.5 35.7 %collective-permute-start.32 = (bf16[2,256,1024]{2,1,0:T(8,128)(2,1)}, bf16[2,256,1024]{2,1,0:T(8,128)(2,1)}, u32[]{:S(2)}, u32[]{:S(2)}) collective-permute-start(bf16[2,256,1024]{2,1,0:T(8,128)(2,1)} %dynamic-slice_bitcast_fusion.1), channel_id=1, source_target_pairs={{0,1},{1,0},{2,3},{3,2},{4,5},{5,4},{6,7},{7,6},{8,9},{9,8},{10,11... | collective-permute-start | bytes 3145736 | tf_op jit(solution)/shard_map/ppermute | solution.py:59
  404.5 35.8 %collective-permute-start.33 = (bf16[2,256,1024]{2,1,0:T(8,128)(2,1)}, bf16[2,256,1024]{2,1,0:T(8,128)(2,1)}, u32[]{:S(2)}, u32[]{:S(2)}) collective-permute-start(bf16[2,256,1024]{2,1,0:T(8,128)(2,1)} %dynamic-slice_bitcast_fusion), channel_id=1, source_target_pairs={{0,2},{1,3},{2,0},{3,1},{4,6},{5,7},{6,4},{7,5},{8,10},{9,11},{10,... | collective-permute-start | bytes 3145736 | tf_op jit(solution)/shard_map/ppermute | solution.py:59
  407.5 32.8 %collective-permute-start.34 = (bf16[256,2048]{1,0:T(8,128)(2,1)}, bf16[256,2048]{1,0:T(8,128)(2,1)S(1)}, u32[]{:S(2)}, u32[]{:S(2)}) collective-permute-start(bf16[256,2048]{1,0:T(8,128)(2,1)} %get-tuple-element.338), channel_id=1, source_target_pairs={{0,8},{4,12},{8,16},{12,20},{16,24},{20,28},{1,9},{5,13},{9,17},{1... | collective-permute-start | bytes 3145736 | tf_op jit(solution)/shard_map/ppermute | solution.py:59
  411.0 29.3 %collective-permute-start.35 = (bf16[256,2048]{1,0:T(8,128)(2,1)}, bf16[256,2048]{1,0:T(8,128)(2,1)S(1)}, u32[]{:S(2)}, u32[]{:S(2)}) collective-permute-start(bf16[256,2048]{1,0:T(8,128)(2,1)} %get-tuple-element.339), channel_id=1, source_target_pairs={{8,0},{12,4},{16,8},{20,12},{24,16},{28,20},{9,1},{13,5},{17,9},{2... | collective-permute-start | bytes 3145736 | tf_op jit(solution)/shard_map/ppermute | solution.py:59
  458.5 32.9 %collective-permute-start.40 = (bf16[4,256,2048]{2,1,0:T(8,128)(2,1)}, bf16[4,256,2048]{2,1,0:T(8,128)(2,1)}, u32[]{:S(2)}, u32[]{:S(2)}) collective-permute-start(bf16[4,256,2048]{2,1,0:T(8,128)(2,1)} %pad_maximum_fusion.mine), channel_id=1, source_target_pairs={{0,4},{4,0},{8,12},{12,8},{16,20},{20,16},{24,28},{28,24},{1,5},{5... | collective-permute-start | bytes 12582920 | tf_op jit(solution)/shard_map/ppermute | solution.py:59
  458.5 28.0 %collective-permute-start.38 = (bf16[256,2048]{1,0:T(8,128)(2,1)}, bf16[256,2048]{1,0:T(8,128)(2,1)}, u32[]{:S(2)}, u32[]{:S(2)}) collective-permute-start(bf16[256,2048]{1,0:T(8,128)(2,1)} %get-tuple-element.348), channel_id=1, source_target_pairs={{0,8},{4,12},{8,16},{12,20},{16,24},{20,28},{1,9},{5,13},{9,17},{1... | collective-permute-start | bytes 3145736 | tf_op jit(solution)/shard_map/ppermute | solution.py:59
  464.1 27.3 %collective-permute-start.39 = (bf16[256,2048]{1,0:T(8,128)(2,1)S(1)}, bf16[256,2048]{1,0:T(8,128)(2,1)}, u32[]{:S(2)}, u32[]{:S(2)}) collective-permute-start(bf16[256,2048]{1,0:T(8,128)(2,1)S(1)} %get-tuple-element.349), channel_id=1, source_target_pairs={{8,0},{12,4},{16,8},{20,12},{24,16},{28,20},{9,1},{13,5},{17,9},{2... | collective-permute-start | bytes 3145736 | tf_op jit(solution)/shard_map/ppermute | solution.py:59
  465.9 14.4 %collective-permute-start.36 = (bf16[256,1024]{1,0:T(8,128)(2,1)}, bf16[256,1024]{1,0:T(8,128)(2,1)}, u32[]{:S(2)}, u32[]{:S(2)}) collective-permute-start(bf16[256,1024]{1,0:T(8,128)(2,1)} %dynamic-slice_bitcast_fusion.6), channel_id=1, source_target_pairs={{0,2},{1,3},{2,0},{3,1},{4,6},{5,7},{6,4},{7,5},{8,10},{9,11},{10,... | collective-permute-start | bytes 1572872 | tf_op jit(solution)/shard_map/ppermute | solution.py:59
  466.0 14.7 %collective-permute-start.37 = (bf16[256,1024]{1,0:T(8,128)(2,1)}, bf16[256,1024]{1,0:T(8,128)(2,1)}, u32[]{:S(2)}, u32[]{:S(2)}) collective-permute-start(bf16[256,1024]{1,0:T(8,128)(2,1)} %dynamic-slice_bitcast_fusion.5), channel_id=1, source_target_pairs={{0,1},{1,0},{2,3},{3,2},{4,5},{5,4},{6,7},{7,6},{8,9},{9,8},{10,11... | collective-permute-start | bytes 1572872 | tf_op jit(solution)/shard_map/ppermute | solution.py:59
  494.1 28.9 %collective-permute-start.43 = (bf16[4,256,2048]{2,1,0:T(8,128)(2,1)S(1)}, bf16[4,256,2048]{2,1,0:T(8,128)(2,1)S(1)}, u32[]{:S(2)}, u32[]{:S(2)}) collective-permute-start(bf16[4,256,2048]{2,1,0:T(8,128)(2,1)S(1)} %copy-done.80), channel_id=1, source_target_pairs={{0,4},{4,0},{8,12},{12,8},{16,20},{20,16},{24,28},{28,24},{1,5},{5... | collective-permute-start | bytes 12582920 | tf_op jit(solution)/shard_map/ppermute | solution.py:59
  494.2 24.6 %collective-permute-start.41 = (bf16[256,2048]{1,0:T(8,128)(2,1)S(1)}, bf16[256,2048]{1,0:T(8,128)(2,1)S(1)}, u32[]{:S(2)}, u32[]{:S(2)}) collective-permute-start(bf16[256,2048]{1,0:T(8,128)(2,1)S(1)} %pad_maximum_fusion.3), channel_id=1, source_target_pairs={{0,8},{4,12},{8,16},{12,20},{16,24},{20,28},{1,9},{5,13},{9,17},{1... | collective-permute-start | bytes 3145736 | tf_op jit(solution)/shard_map/ppermute | solution.py:59
  495.6 27.4 %collective-permute-start.42 = (bf16[256,2048]{1,0:T(8,128)(2,1)S(1)}, bf16[256,2048]{1,0:T(8,128)(2,1)S(1)}, u32[]{:S(2)}, u32[]{:S(2)}) collective-permute-start(bf16[256,2048]{1,0:T(8,128)(2,1)S(1)} %pad_maximum_fusion.3), channel_id=1, source_target_pairs={{8,0},{12,4},{16,8},{20,12},{24,16},{28,20},{9,1},{13,5},{17,9},{2... | collective-permute-start | bytes 3145736 | tf_op jit(solution)/shard_map/ppermute | solution.py:59
  497.3 11.7 %collective-permute-start.44 = (f32[20480]{0:T(1024)S(1)}, f32[20480]{0:T(1024)S(1)}, u32[]{:S(2)}, u32[]{:S(2)}) collective-permute-start(f32[20480]{0:T(1024)S(1)} %constant_dynamic-update-slice_fusion.2), channel_id=1, source_target_pairs={{0,4},{4,0},{8,12},{12,8},{16,20},{20,16},{24,28},{28,24},{1,5},{5... | collective-permute-start | bytes 245768 | tf_op jit(solution)/shard_map/ppermute | solution.py:59
  523.0 63.7 %copy-start.21 = (bf16[4,256,2048]{2,1,0:T(8,128)(2,1)}, bf16[4,256,2048]{2,1,0:T(8,128)(2,1)S(1)}, u32[]{:S(2)}) copy-start(bf16[4,256,2048]{2,1,0:T(8,128)(2,1)S(1)} %collective-permute-done.43) | copy-start | bytes 12582916
  524.4 29.8 %collective-permute-start.45 = (bf16[256,2048]{1,0:T(8,128)(2,1)S(1)}, bf16[256,2048]{1,0:T(8,128)(2,1)S(1)}, u32[]{:S(2)}, u32[]{:S(2)}) collective-permute-start(bf16[256,2048]{1,0:T(8,128)(2,1)S(1)} %get-tuple-element.372), channel_id=1, source_target_pairs={{0,8},{4,12},{8,16},{12,20},{16,24},{20,28},{1,9},{5,13},{9,17},{1... | collective-permute-start | bytes 3145736 | tf_op jit(solution)/shard_map/ppermute | solution.py:59
  526.4 27.9 %collective-permute-start.46 = (bf16[256,2048]{1,0:T(8,128)(2,1)S(1)}, bf16[256,2048]{1,0:T(8,128)(2,1)S(1)}, u32[]{:S(2)}, u32[]{:S(2)}) collective-permute-start(bf16[256,2048]{1,0:T(8,128)(2,1)S(1)} %get-tuple-element.373), channel_id=1, source_target_pairs={{8,0},{12,4},{16,8},{20,12},{24,16},{28,20},{9,1},{13,5},{17,9},{2... | collective-permute-start | bytes 3145736 | tf_op jit(solution)/shard_map/ppermute | solution.py:59
  527.7 26.6 %collective-permute-start.47 = (f32[20480]{0:T(1024)S(1)}, f32[20480]{0:T(1024)S(1)}, u32[]{:S(2)}, u32[]{:S(2)}) collective-permute-start(f32[20480]{0:T(1024)S(1)} %add.464), channel_id=1, source_target_pairs={{0,8},{4,12},{8,0},{12,4},{16,24},{20,28},{24,16},{28,20},{1,9},{5... | collective-permute-start | bytes 245768 | tf_op jit(solution)/shard_map/ppermute | solution.py:59
  555.6 31.1 %collective-permute-start.48 = (bf16[256,2048]{1,0:T(8,128)(2,1)S(1)}, bf16[256,2048]{1,0:T(8,128)(2,1)S(1)}, u32[]{:S(2)}, u32[]{:S(2)}) collective-permute-start(bf16[256,2048]{1,0:T(8,128)(2,1)S(1)} %get-tuple-element.378), channel_id=1, source_target_pairs={{0,8},{4,12},{8,16},{12,20},{16,24},{20,28},{1,9},{5,13},{9,17},{1... | collective-permute-start | bytes 3145736 | tf_op jit(solution)/shard_map/ppermute | solution.py:59
  557.1 29.6 %collective-permute-start.49 = (bf16[256,2048]{1,0:T(8,128)(2,1)S(1)}, bf16[256,2048]{1,0:T(8,128)(2,1)S(1)}, u32[]{:S(2)}, u32[]{:S(2)}) collective-permute-start(bf16[256,2048]{1,0:T(8,128)(2,1)S(1)} %get-tuple-element.379), channel_id=1, source_target_pairs={{8,0},{12,4},{16,8},{20,12},{24,16},{28,20},{9,1},{13,5},{17,9},{2... | collective-permute-start | bytes 3145736 | tf_op jit(solution)/shard_map/ppermute | solution.py:59
  558.4 28.3 %collective-permute-start.50 = (f32[20480]{0:T(1024)S(1)}, f32[20480]{0:T(1024)S(1)}, u32[]{:S(2)}, u32[]{:S(2)}) collective-permute-start(f32[20480]{0:T(1024)S(1)} %add.469), channel_id=1, source_target_pairs={{0,16},{4,20},{8,24},{12,28},{16,0},{20,4},{24,8},{28,12},{1,17},{... | collective-permute-start | bytes 245768 | tf_op jit(solution)/shard_map/ppermute | solution.py:59
  595.1 8.8 %collective-permute-start.51 = (bf16[4,256,2048]{2,1,0:T(8,128)(2,1)}, bf16[4,256,2048]{2,1,0:T(8,128)(2,1)}, u32[]{:S(2)}, u32[]{:S(2)}) collective-permute-start(bf16[4,256,2048]{2,1,0:T(8,128)(2,1)} %pad_maximum_fusion.1.mine), channel_id=1, source_target_pairs={{0,4},{4,0},{8,12},{12,8},{16,20},{20,16},{24,28},{28,24},{1,5},{5... | collective-permute-start | bytes 12582920 | tf_op jit(solution)/shard_map/ppermute | solution.py:59
  595.2 24.9 %collective-permute-start.54 = (bf16[256,2048]{1,0:T(8,128)(2,1)}, bf16[256,2048]{1,0:T(8,128)(2,1)S(1)}, u32[]{:S(2)}, u32[]{:S(2)}) collective-permute-start(bf16[256,2048]{1,0:T(8,128)(2,1)} %get-tuple-element.393), channel_id=1, source_target_pairs={{0,8},{4,12},{8,16},{12,20},{16,24},{20,28},{1,9},{5,13},{9,17},{1... | collective-permute-start | bytes 3145736 | tf_op jit(solution)/shard_map/ppermute | solution.py:59
  596.9 27.5 %collective-permute-start.55 = (bf16[256,2048]{1,0:T(8,128)(2,1)}, bf16[256,2048]{1,0:T(8,128)(2,1)}, u32[]{:S(2)}, u32[]{:S(2)}) collective-permute-start(bf16[256,2048]{1,0:T(8,128)(2,1)} %get-tuple-element.394), channel_id=1, source_target_pairs={{8,0},{12,4},{16,8},{20,12},{24,16},{28,20},{9,1},{13,5},{17,9},{2... | collective-permute-start | bytes 3145736 | tf_op jit(solution)/shard_map/ppermute | solution.py:59
  599.0 4.9 collective-permute-start.52
  603.9 20.4 %collective-permute-start.53 = (f32[20480]{0:T(1024)S(1)}, f32[20480]{0:T(1024)S(1)}, u32[]{:S(2)}, u32[]{:S(2)}) collective-permute-start(f32[20480]{0:T(1024)S(1)} %add.475), channel_id=1, source_target_pairs={{0,2},{1,3},{2,0},{3,1},{4,6},{5,7},{6,4},{7,5},{8,10},{9,11},{10,... | collective-permute-start | bytes 245768 | tf_op jit(solution)/shard_map/ppermute | solution.py:59
  (86 other events, 594.4 us)
Sparse Core Ops, SparseCore 0:
  9.6 84.7 all-gather.14
  96.0 45.6 all-gather.6
  143.3 45.8 all-gather.8
  216.5 45.2 all-gather.10
  263.2 45.8 all-gather.12

commit v4 on v3

--- a/solution.py
+++ b/solution.py
@@ -11,6 +11,7 @@
 ROT = 32
 BLK = 16
 TILE = 256
+WIDE = 512
 ROWS = 512
 LANES = 128
 F32 = jnp.float32
@@ -195,10 +196,10 @@
     return lax.broadcasted_iota(jnp.int32, shape, 1) < HEAD_DIM
 
 
-def visible_range(ends_ref, step, tile):
-    top = step * tile
-    column = top + lax.broadcasted_iota(jnp.int32, (1, tile), 1)
-    begin = jnp.zeros((1, tile), jnp.int32)
+def visible_range(ends_ref, step, wide, tile):
+    top = step * wide
+    column = top + lax.broadcasted_iota(jnp.int32, (1, wide), 1)
+    begin = jnp.zeros((1, wide), jnp.int32)
     first = jnp.int32(0)
     for sequence in range(ends_ref.shape[0]):
         end = ends_ref[sequence]
@@ -235,7 +236,7 @@
     place_ref, ends_ref, lin_hbm, att_hbm, rows, summed_ref, lse_ref, values_t, att, sems
 ):
     tokens = rows.shape[0]
-    tile = TILE
+    tile, wide = TILE, WIDE
     pairs = rows.shape[1] // LANES // 3
     heads = 2 * pairs
     each_block(
@@ -253,10 +254,10 @@
             lanes = slice(pair * LANES, (pair + 1) * LANES)
             values_t[lanes, part] = rows[part, part_lanes(pair, 2)].T
 
-    @pl.loop(0, tokens // tile)
+    @pl.loop(0, tokens // wide)
     def _(step):
-        part = pl.ds(pl.multiple_of(step * tile, tile), tile)
-        column, begin, low = visible_range(ends_ref, step, tile)
+        part = pl.ds(pl.multiple_of(step * wide, wide), wide)
+        column, begin, low = visible_range(ends_ref, step, wide, tile)
         queries = [
             query
             for pair in range(pairs)
@@ -265,7 +266,7 @@
 
         def combine(index, state):
             there = pl.ds(pl.multiple_of(index * tile, tile), tile)
-            row = index * tile + lax.broadcasted_iota(jnp.int32, (tile, tile), 0)
+            row = index * tile + lax.broadcasted_iota(jnp.int32, (tile, wide), 0)
             visible = (row <= column) & (row >= begin)
             result = []
             for head in range(heads):
@@ -282,11 +283,11 @@
             return tuple(result)
 
         empty = (
-            jnp.full((1, tile), -1e30, F32),
-            jnp.zeros((1, tile), F32),
-            jnp.zeros((HEAD_DIM, tile), F32),
+            jnp.full((1, wide), -1e30, F32),
+            jnp.zeros((1, wide), F32),
+            jnp.zeros((HEAD_DIM, wide), F32),
         )
-        state = lax.fori_loop(low, step + 1, combine, (empty,) * heads)
+        state = lax.fori_loop(low, (step + 1) * (wide // tile), combine, (empty,) * heads)
         for head in range(heads):
             top, total, summed = state[head]
             summed_ref[head * HEAD_DIM : (head + 1) * HEAD_DIM, part] = summed * (1.0 / total)
@@ -309,7 +310,7 @@
 ):
     mixed_hbm, grad, grad_t, keys_t, grad_k, grad_v, mixed, sems = refs[-8:]
     tokens = grad.shape[0]
-    tile = TILE
+    tile, wide = TILE, WIDE
     lanes = slice(pair * LANES, (pair + 1) * LANES)
     lanes3 = slice(3 * pair * LANES, 3 * (pair + 1) * LANES)
     each_block(
@@ -328,10 +329,10 @@
 
     pltpu.make_async_copy(grad_hbm.at[:, lanes], grad, sems.at[0]).wait()
 
-    @pl.loop(0, tokens // tile)
+    @pl.loop(0, tokens // wide)
     def _(step):
-        part = pl.ds(pl.multiple_of(step * tile, tile), tile)
-        column, begin, low = visible_range(ends_ref, step, tile)
+        part = pl.ds(pl.multiple_of(step * wide, wide), wide)
+        column, begin, low = visible_range(ends_ref, step, wide, tile)
         query, back = rows[part, Q_LANES], grad[part, :]
         back_t = back.T
         queries, queries_t = each_head(query), each_head(query.T, 0)
@@ -345,7 +346,7 @@
 
         def back_step(index, sums):
             there = pl.ds(pl.multiple_of(index * tile, tile), tile)
-            row = index * tile + lax.broadcasted_iota(jnp.int32, (tile, tile), 0)
+            row = index * tile + lax.broadcasted_iota(jnp.int32, (tile, wide), 0)
             visible = (row <= column) & (row >= begin)
             key, value = rows[there, K_LANES], rows[there, V_LANES]
             result, add_k, add_v = [], 0.0, 0.0
@@ -361,7 +362,7 @@
             grad_v[there, :] += add_v
             return tuple(result)
 
-        sums = lax.fori_loop(low, step + 1, back_step, (jnp.zeros((HEAD_DIM, tile), F32),) * 2)
+        sums = lax.fori_loop(low, (step + 1) * (wide // tile), back_step, (jnp.zeros((HEAD_DIM, wide), F32),) * 2)
         grad_q = jnp.concatenate(sums, axis=0).T * HEAD_DIM ** (-0.5)
         mixed[part, Q_LANES] = turn(grad_q, cos_ref[part, :], -sin_ref[part, :]).astype(BF16)
 
@@ -414,7 +415,7 @@
             pltpu.VMEM((tokens, width), BF16),
             pltpu.SemaphoreType.DMA((1,)),
         ],
-        compiler_params=pltpu.CompilerParams(vmem_limit_bytes=40 << 20),
+        compiler_params=pltpu.CompilerParams(vmem_limit_bytes=60 << 20),
         cost_estimate=pl.CostEstimate(
             flops=40 * 10**9, bytes_accessed=16 * 10**6, transcendentals=0
         ),
@@ -441,14 +442,14 @@
         input_output_aliases={8 + i: i for i in range(len(before))},
         scratch_shapes=[
             pltpu.VMEM((tokens, LANES), BF16),
-            pltpu.VMEM((LANES, TILE), F32),
+            pltpu.VMEM((LANES, WIDE), F32),
             pltpu.VMEM((LANES, tokens), BF16),
             pltpu.VMEM((tokens, LANES), F32),
             pltpu.VMEM((tokens, LANES), F32),
             pltpu.VMEM((tokens, 3 * LANES), BF16),
             pltpu.SemaphoreType.DMA((1,)),
         ],
-        compiler_params=pltpu.CompilerParams(vmem_limit_bytes=40 << 20),
+        compiler_params=pltpu.CompilerParams(vmem_limit_bytes=60 << 20),
         cost_estimate=pl.CostEstimate(
             flops=20 * 10**9, bytes_accessed=8 * 10**6, transcendentals=0
         ),
@@ -524,7 +525,7 @@
                 pltpu.SemaphoreType.DMA((len(pieces),)),
             ],
         ),
-        compiler_params=pltpu.CompilerParams(vmem_limit_bytes=56 << 20),
+        compiler_params=pltpu.CompilerParams(vmem_limit_bytes=60 << 20),
         cost_estimate=pl.CostEstimate(flops=flops, bytes_accessed=moved, transcendentals=0),
     )(where, *rows, *whole, *pieces)
 
@@ -1043,14 +1044,16 @@
     while weave.moves:
         beside(nothing, (), [weave])
     up_swap, out_finish = weave.result
-    down_total = beside(side_by_side, down_total, [joint_flow, out_finish, up_swap])
+    down_total = beside(side_by_side, down_total, [joint_flow, out_finish])
     while joint_flow.moves:
         beside(nothing, (), [joint_flow])
     weave = Flow(weave_steps(joint_flow.result, mine, other))
+    beside(nothing, (), [weave, total_flow])
+    beside(nothing, (), [flow for flow in (weave, total_flow, up_swap) if flow.moves])
     (up_dealt,) = beside(
         lambda *halves: deal_columns(*halves, unit, list(range(shard_count)), at),
         up_swap.result,
-        [weave, total_flow],
+        [flow for flow in (weave, total_flow) if flow.moves],
     )
     while weave.moves:
         beside(nothing, (), [flow for flow in (weave, total_flow) if flow.moves])

time: 649 us -> 626 us (0.965)
  local copies, waits for them, and re-layouts: 58.8 us -> 39 us
  Pallas kernels: 221 us -> 207 us
  other arithmetic: 66.8 us -> 74.1 us
    unnamed x195 -> x143, local copies, waits for them, and re-layouts: 33.4 us -> 14.8 us
    pallas_call x1, Pallas kernels: 38.4 us -> 28.7 us  [attention_forward(): pl.pallas_call(forward_kernel, out_shape=(jax.ShapeDtypeStruct((tokens, w...]
  transfers between devices with their start and end apart: 61 -> 61, of which waited for: 23 -> 25; matrix products, arithmetic and copies ran while one was open for 13% -> 14% of each run, Pallas kernels for 34% -> 33%
where the time goes in v4:
time: 626 us; the launch traced here: 621 us
  Pallas kernels  207 us (33%)
  waiting for transfers between devices  156 us (25%)
  starting transfers between devices  83.5 us (13%)
  other arithmetic  74.1 us (12%)
  matrix products  44.9 us (7%)
  local copies, waits for them, and re-layouts  39 us (6%)
  between operations  15.5 us (2%)
    ppermute x56, waiting for transfers between devices, beside(): lax.ppermute(value, axis, pairs)  151 us
    pallas_call x4, Pallas kernels, row_call(): pl.pallas_call(body, out_shape=out_shape + [jax.ShapeDtypeStruct(shape, F...  98.9 us
    ppermute x56, starting transfers between devices, beside(): lax.ppermute(value, axis, pairs)  83.1 us
    dot_general x6, matrix products, dot_tn(): lax.dot_general(left, right, (((0,), (0,)), ((), ())), preferred_element_...  44.9 us
    pallas_call x2, Pallas kernels, attention_backward(): pl.pallas_call(functools.partial(backward_kernel, pair), out_shape=jax.Sh...  44.2 us
    pallas_call x1, Pallas kernels, attention_forward(): pl.pallas_call(forward_kernel, out_shape=(jax.ShapeDtypeStruct((tokens, w...  28.7 us
    pallas_call x2, Pallas kernels, deal_columns(): pl.pallas_call(functools.partial(deal_kernel, unit, order), out_shape=out...  19.4 us
    select_n x4, other arithmetic, weave_steps(): down_sum = jnp.where(place <= line - step, down, down_sum)  16.2 us
  transfers between devices with their start and end apart: 61, of which 25 were waited for; matrix products, arithmetic and copies ran while one was open for 14% of the time, Pallas kernels for 33%

profile of v4, /device:TPU:0, one launch (start us, length us, event | category | flops | bytes accessed | tf_op | source)
XLA Modules:
  0.0 620.8 jit_solution(18072801016901010836)
XLA Ops:
  8.0 3.4 copy-done.2
  11.4 2.8 copy-done.4
  19.0 2.8 fusion.67
  21.8 2.9 collective-permute-start
  26.8 2.9 collective-permute-start.4
  32.1 13.6 %collective-permute-done.2 = bf16[8,704]{1,0:T(8,128)(2,1)S(1)} collective-permute-done((bf16[8,704]{1,0:T(8,128)(2,1)S(1)}, bf16[8,704]{1,0:T(8,128)(2,1)S(1)}, u32[]{:S(2)}, u32[]{:S(2)}) %collective-permute-start.2) | collective-permute-done | bytes 11296 | tf_op jit(solution)/shard_map/ppermute | solution.py:60
  55.1 8.9 %fusion.41 = (f32[2048,128]{1,0:T(8,128)}, f32[2048,128]{1,0:T(8,128)}, f32[2048,128]{1,0:T(8,128)}, f32[2048,128]{1,0:T(8,128)}) fusion(f32[2048]{0:T(1024)S(1)} %get-tuple-element.459, f32[128]{0:T(128)S(1)} %get-tuple-element.457, f32[128]{0:T(128)S(1)} %get-tuple-element.458, f32[2048]{0:T(1024)S(1)} %get-tuple-element.460), kind=kLoop, calls=%fused_computation.89 | loop fusion | flops 1048576 | bytes 4211712 | tf_op jit(solution)/shard_map/mul | solution.py:392
  64.0 7.6 %collective-permute-done.5.refs_8_.refs_5_ = bf16[256,1792]{1,0:T(8,128)(2,1)} collective-permute-done((bf16[256,1792]{1,0:T(8,128)(2,1)}, bf16[256,1792]{1,0:T(8,128)(2,1)}, u32[]{:S(2)}, u32[]{:S(2)}) %collective-permute-start.5) | collective-permute-done | bytes 917536 | tf_op jit(solution)/shard_map/ppermute | solution.py:60
  71.6 17.7 %collective-permute-done.6.refs_9_.refs_6_ = bf16[256,1792]{1,0:T(8,128)(2,1)} collective-permute-done((bf16[256,1792]{1,0:T(8,128)(2,1)}, bf16[256,1792]{1,0:T(8,128)(2,1)}, u32[]{:S(2)}, u32[]{:S(2)}) %collective-permute-start.6) | collective-permute-done | bytes 917536 | tf_op jit(solution)/shard_map/ppermute | solution.py:60
  90.6 3.9 all-gather.15.cloned.1.call-done
  97.9 34.3 %shard_map.230 = (bf16[2048,2048]{1,0:T(8,128)(2,1)}, bf16[2048,1024]{1,0:T(8,128)(2,1)}, bf16[2048,1024]{1,0:T(8,128)(2,1)}, bf16[2048,768]{1,0:T(8,128)(2,1)}) custom-call(s32[2]{0:T(128)} %pad_add_fusion.at, bf16[2048,2048]{1,0:T(8,128)(2,1)} %bitcast.339, f32[2048,128]{1,0:T(8,128)} %get-tuple-element.224.refs_1_, ...), custom_call_target="tpu_custom_call" | custom-call | flops 15032385536 | bytes 37772288 | tf_op jit(solution)/shard_map/pallas_call | solution.py:513
  132.2 10.0 %collective-permute-done.10.refs_5_.refs_4_ = bf16[256,2048]{1,0:T(8,128)(2,1)S(1)} collective-permute-done((bf16[256,2048]{1,0:T(8,128)(2,1)S(1)}, bf16[256,2048]{1,0:T(8,128)(2,1)S(1)}, u32[]{:S(2)}, u32[]{:S(2)}) %collective-permute-start.10) | collective-permute-done | bytes 1048608 | tf_op jit(solution)/shard_map/ppermute | solution.py:60
  143.5 8.0 %convolution_convert_fusion.3 = bf16[1024,1024]{1,0:T(8,128)(2,1)S(1)} fusion(bf16[2048,1024]{1,0:T(8,128)(2,1)} %get-tuple-element.240.refs_1_, bf16[2048,1024]{1,0:T(8,128)(2,1)} %all-gather.7.cloned.1.call-done.refs_0_), kind=kOutput, calls=%fused_computation.73 | convolution fusion | flops 4296015872 | bytes 10485760 | tf_op jit(solution)/shard_map/dot_general | solution.py:30
  156.8 2.4 collective-permute-start.16
  159.3 28.7 %shard_map.231 = (bf16[2048,256]{1,0:T(8,128)(2,1)}, bf16[2048,768]{1,0:T(8,128)(2,1)}, f32[256,2048]{1,0:T(8,128)}, f32[4,2048]{1,0:T(4,128)}) custom-call(s32[128]{0:T(128)} %place_ref.5, s32[4]{0:T(128)} %bitcast.336, bf16[2048,768]{1,0:T(8,128)(2,1)} %get-tuple-element.245.lin_hbm), custom_call_target="tpu_custom_call" | custom-call | flops 40000000000 | bytes 16000000 | tf_op jit(solution)/shard_map/pallas_call | solution.py:403
  189.2 4.4 collective-permute-start.17
  193.6 9.4 %convolution_convert_fusion.2 = bf16[1024,1024]{1,0:T(8,128)(2,1)} fusion(bf16[2048,1024]{1,0:T(8,128)(2,1)} %get-tuple-element.240.refs_1_, bf16[2048,1024]{1,0:T(8,128)(2,1)} %all-gather.9.cloned.1.call-done.refs_1_), kind=kOutput, calls=%fused_computation.72 | convolution fusion | flops 4296015872 | bytes 10485760 | tf_op jit(solution)/shard_map/dot_general | solution.py:30
  206.7 2.1 collective-permute-start.19
  208.9 18.9 %shard_map.232 = (bf16[2048,1024]{1,0:T(8,128)(2,1)}, bf16[2048,256]{1,0:T(8,128)(2,1)}, f32[1,1024]{1,0:T(1,128)}) custom-call(s32[2]{0:T(128)} %pad_add_fusion.at, bf16[2048,1024]{1,0:T(8,128)(2,1)} %all-gather.7.cloned.1.call-done.refs_0_, bf16[2048,1024]{1,0:T(8,128)(2,1)} %all-gather.9.cloned.1.call-done.refs_1_, ...), custom_call_target="tpu_custom_call" | custom-call | flops 10737418240 | bytes 23068672 | tf_op jit(solution)/shard_map/pallas_call | solution.py:513
  230.6 12.9 %convolution_convert_fusion = bf16[2048,1024]{1,0:T(8,128)(2,1)} fusion(bf16[2048,2048]{1,0:T(8,128)(2,1)} %get-tuple-element.281, bf16[2048,1024]{1,0:T(8,128)(2,1)S(1)} %copy-done.61), kind=kOutput, calls=%fused_computation.2 | convolution fusion | flops 8592031744 | bytes 16777216 | tf_op jit(solution)/shard_map/dot_general | solution.py:30
  244.4 2.7 fusion.64
  250.7 17.6 %shard_map.233 = (bf16[4,256,2048]{2,1,0:T(8,128)(2,1)}, bf16[4,256,2048]{2,1,0:T(8,128)(2,1)}) custom-call(s32[2]{0:T(128)} %pad_add_fusion.at, bf16[2048,256]{1,0:T(8,128)(2,1)} %get-tuple-element.323.refs_0_, bf16[2048,1024]{1,0:T(8,128)(2,1)} %get-tuple-element.240.refs_1_, bf16[256,2048]{1,0:T(8,128)(2,1)} %copy-done.29, ...), custom_call_target="tpu_custom_call" | custom-call | flops 10737418240 | bytes 18874368 | tf_op jit(solution)/shard_map/pallas_call | solution.py:513
  268.3 2.9 collective-permute-done.23
  279.1 22.2 %shard_map.234.refs_0_ = bf16[2048,768]{1,0:T(8,128)(2,1)} custom-call(s32[128]{0:T(128)} %place_ref.5, s32[4]{0:T(128)} %bitcast.337, f32[2048,128]{1,0:T(8,128)} %get-tuple-element.289.cos_ref, f32[2048,128]{1,0:T(8,128)} %get-tuple-element.290.sin_ref, bf16[2048,768]{1,0:T(8,128)(2,1)} %get-tuple-element.291.rows, ...), custom_call_target="tpu_custom_call" | custom-call | flops 20000000000 | bytes 8000000 | tf_op jit(solution)/shard_map/pallas_call | solution.py:427
  305.2 22.0 %shard_map.235.refs_1_ = bf16[2048,768]{1,0:T(8,128)(2,1)} custom-call(s32[128]{0:T(128)} %place_ref.5, s32[4]{0:T(128)} %bitcast.338, f32[2048,128]{1,0:T(8,128)} %get-tuple-element.289.cos_ref, f32[2048,128]{1,0:T(8,128)} %get-tuple-element.290.sin_ref, bf16[2048,768]{1,0:T(8,128)(2,1)} %get-tuple-element.291.rows, ...), custom_call_target="tpu_custom_call", output_to_operand_aliasing={{}: (8, {})} | custom-call | flops 20000000000 | bytes 8000000 | tf_op jit(solution)/shard_map/pallas_call | solution.py:427
  327.2 3.5 collective-permute-done.28
  330.8 5.0 fusion.33
  335.8 3.5 collective-permute-start.30
  340.6 10.5 %convolution_convert_fusion.1.left = bf16[2048,768]{1,0:T(8,128)(2,1)} fusion(bf16[2048,2048]{1,0:T(8,128)(2,1)} %get-tuple-element.281, bf16[2048,768]{1,0:T(8,128)(2,1)S(1)} %copy-done.62), kind=kOutput, calls=%fused_computation.3 | convolution fusion | flops 6444023808 | bytes 14680064 | tf_op jit(solution)/shard_map/dot_general | solution.py:30
  351.1 2.1 convolution_convert_fusion.4.refs_1_
  355.3 4.7 shard_map.236
  360.8 4.2 collective-permute-done.31
  365.0 2.7 fusion.63
  372.1 5.2 fusion.35
  377.2 5.5 collective-permute-start.33
  382.7 4.4 collective-permute-start.34
  388.4 28.2 %shard_map.237 = (bf16[4,256,2048]{2,1,0:T(8,128)(2,1)}, bf16[4,256,2048]{2,1,0:T(8,128)(2,1)}, f32[1,2048]{1,0:T(1,128)}, f32[1,2048]{1,0:T(1,128)}, f32[1,768]{1,0:T(1,128)}) custom-call(s32[2]{0:T(128)} %pad_add_fusion.at, bf16[2048,2048]{1,0:T(8,128)(2,1)} %bitcast.340, bf16[2048,768]{1,0:T(8,128)(2,1)} %shard_map.235.refs_1_, ...), custom_call_target="tpu_custom_call" | custom-call | flops 15032385536 | bytes 31457280 | tf_op jit(solution)/shard_map/pallas_call | solution.py:513
  416.7 2.1 fusion.24
  423.3 5.0 fusion.22
  428.3 5.5 collective-permute-start.38
  435.7 2.1 collective-permute-start.37
  437.8 10.2 %shard_map.238 = f32[2048,2048]{1,0:T(8,128)} custom-call(bf16[2048,1024]{1,0:T(8,128)(2,1)} %all-gather.11.cloned.1.call-done.refs_0_, bf16[2048,1024]{1,0:T(8,128)(2,1)} %all-gather.13.cloned.1.call-done.refs_1_), custom_call_target="tpu_custom_call" | custom-call | bytes 25165824 | tf_op jit(solution)/shard_map/pallas_call | solution.py:782
  448.1 5.0 collective-permute-done.38
  453.0 5.1 collective-permute-done.39
  462.1 4.0 select_bitcast_fusion.7
  469.0 3.6 select_bitcast_fusion.6
  474.0 16.9 %collective-permute-done.40 = bf16[256,2048]{1,0:T(8,128)(2,1)S(1)} collective-permute-done((bf16[256,2048]{1,0:T(8,128)(2,1)S(1)}, bf16[256,2048]{1,0:T(8,128)(2,1)S(1)}, u32[]{:S(2)}, u32[]{:S(2)}) %collective-permute-start.40) | collective-permute-done | bytes 1048608 | tf_op jit(solution)/shard_map/ppermute | solution.py:60
  490.8 4.2 collective-permute-done.41
  495.0 3.1 fusion.37
  498.2 2.1 collective-permute-start.44
  501.6 2.7 collective-permute-start.46
  504.3 24.9 %collective-permute-done.46 = f32[20480]{0:T(1024)S(1)} collective-permute-done((f32[20480]{0:T(1024)S(1)}, f32[20480]{0:T(1024)S(1)}, u32[]{:S(2)}, u32[]{:S(2)}) %collective-permute-start.46) | collective-permute-done | bytes 81952 | tf_op jit(solution)/shard_map/ppermute | solution.py:60
  529.3 2.9 fusion.39
  535.0 3.1 collective-permute-start.50
  538.2 7.4 %shard_map.239 = f32[512,8192]{1,0:T(8,128)} custom-call(s32[2]{0:T(128)S(1)} %pad_add_fusion.1.at_ref, bf16[4,256,2048]{2,1,0:T(8,128)(2,1)S(1)} %pad_maximum_fusion.mine, bf16[4,256,2048]{2,1,0:T(8,128)(2,1)S(1)} %collective-permute-done.47.other), custom_call_target="tpu_custom_call" | custom-call | bytes 25165824 | tf_op jit(solution)/shard_map/pallas_call | solution.py:711
  545.6 18.4 %collective-permute-done.50 = f32[20480]{0:T(1024)S(1)} collective-permute-done((f32[20480]{0:T(1024)S(1)}, f32[20480]{0:T(1024)S(1)}, u32[]{:S(2)}, u32[]{:S(2)}) %collective-permute-start.50) | collective-permute-done | bytes 81952 | tf_op jit(solution)/shard_map/ppermute | solution.py:60
  564.0 4.3 fusion.15
  571.7 2.3 pad_maximum_fusion.1.mine
  579.6 2.8 collective-permute-done.52
  582.8 12.0 %shard_map.240 = (f32[512,6144]{1,0:T(8,128)}, f32[512,2048]{1,0:T(8,128)}) custom-call(s32[2]{0:T(128)S(1)} %pad_add_fusion.1.at_ref, bf16[4,256,2048]{2,1,0:T(8,128)(2,1)} %pad_maximum_fusion.1.mine, bf16[4,256,2048]{2,1,0:T(8,128)(2,1)} %collective-permute-done.51.other), custom_call_target="tpu_custom_call" | custom-call | bytes 25165824 | tf_op jit(solution)/shard_map/pallas_call | solution.py:711
  594.7 4.3 collective-permute-done.54
  599.1 4.2 collective-permute-done.55
  605.2 3.1 fusion.61
  608.3 5.2 fusion.43
  (338 shorter events, 95.0 us)
Async XLA Ops:
  7.2 87.2 %all-gather.15.cloned.1.call-start = ((), (), s32[]{:S(2)}) async-start(), calls=%async_computation.4 | async-start | bytes 9437184 | tf_op jit(solution)/shard_map/all_gather | solution.py:837
  7.9 135.6 %all-gather.7.cloned.1.call-start = ((), (), s32[]{:S(2)}) async-start(), calls=%async_computation | async-start | bytes 4718592 | tf_op jit(solution)/shard_map/all_gather | solution.py:837
  17.9 171.3 %all-gather.9.cloned.1.call-start = ((), (), s32[]{:S(2)}) async-start(), calls=%async_computation.1 | async-start | bytes 4718592 | tf_op jit(solution)/shard_map/all_gather | solution.py:837
  21.8 33.0 %copy-start.31 = (bf16[256,1792]{1,0:T(8,128)(2,1)}, bf16[256,1792]{1,0:T(8,128)(2,1)S(1)}, u32[]{:S(2)}) copy-start(bf16[256,1792]{1,0:T(8,128)(2,1)S(1)} %get-tuple-element.222.refs_10_.refs_7_) | copy-start | bytes 2752516
  21.8 25.3 %collective-permute-start = (bf16[256,1792]{1,0:T(8,128)(2,1)}, bf16[256,1792]{1,0:T(8,128)(2,1)}, u32[]{:S(2)}, u32[]{:S(2)}) collective-permute-start(bf16[256,1792]{1,0:T(8,128)(2,1)} %get-tuple-element.220.refs_6_.refs_3_), channel_id=1, source_target_pairs={{0,1},{1,0},{2,3},{3,2},{4,5},{5,4},{6,7},{7,6},{8,9},{9,8},{10,11... | collective-permute-start | bytes 2752520 | tf_op jit(solution)/shard_map/ppermute | solution.py:60
  24.7 22.3 %collective-permute-start.1 = (bf16[256,1792]{1,0:T(8,128)(2,1)S(1)}, bf16[256,1792]{1,0:T(8,128)(2,1)}, u32[]{:S(2)}, u32[]{:S(2)}) collective-permute-start(bf16[256,1792]{1,0:T(8,128)(2,1)S(1)} %get-tuple-element.222.refs_10_.refs_7_), channel_id=1, source_target_pairs={{0,2},{1,3},{2,0},{3,1},{4,6},{5,7},{6,4},{7,5},{8,10},{9,11},{10,... | collective-permute-start | bytes 2752520 | tf_op jit(solution)/shard_map/ppermute | solution.py:60
  26.2 19.5 %collective-permute-start.2 = (bf16[8,704]{1,0:T(8,128)(2,1)S(1)}, bf16[8,704]{1,0:T(8,128)(2,1)S(1)}, u32[]{:S(2)}, u32[]{:S(2)}) collective-permute-start(bf16[8,704]{1,0:T(8,128)(2,1)S(1)} %reshape.366), channel_id=1, source_target_pairs={{0,1},{1,0},{2,3},{3,2},{4,5},{5,4},{6,7},{7,6},{8,9},{9,8},{10,11... | collective-permute-start | bytes 33800 | tf_op jit(solution)/shard_map/ppermute | solution.py:60
  26.8 20.2 %collective-permute-start.3 = (bf16[8,704]{1,0:T(8,128)(2,1)S(1)}, bf16[8,704]{1,0:T(8,128)(2,1)S(1)}, u32[]{:S(2)}, u32[]{:S(2)}) collective-permute-start(bf16[8,704]{1,0:T(8,128)(2,1)S(1)} %reshape.366), channel_id=1, source_target_pairs={{0,2},{1,3},{2,0},{3,1},{4,6},{5,7},{6,4},{7,5},{8,10},{9,11},{10,... | collective-permute-start | bytes 33800 | tf_op jit(solution)/shard_map/ppermute | solution.py:60
  26.8 20.2 %collective-permute-start.4 = (bf16[8,704]{1,0:T(8,128)(2,1)S(1)}, bf16[8,704]{1,0:T(8,128)(2,1)S(1)}, u32[]{:S(2)}, u32[]{:S(2)}) collective-permute-start(bf16[8,704]{1,0:T(8,128)(2,1)S(1)} %reshape.366), channel_id=1, source_target_pairs={{0,3},{1,2},{2,1},{3,0},{4,7},{5,6},{6,5},{7,4},{8,11},{9,10},{10,... | collective-permute-start | bytes 33800 | tf_op jit(solution)/shard_map/ppermute | solution.py:60
  29.8 127.1 %copy-start.40 = (bf16[64,2048]{1,0:T(8,128)(2,1)}, bf16[64,2048]{1,0:T(8,128)(2,1)S(1)}, u32[]{:S(2)}) copy-start(bf16[64,2048]{1,0:T(8,128)(2,1)S(1)} %dynamic-slice_bitcast_fusion.17.refs_7_.refs_6_) | copy-start | bytes 786436
  31.2 66.2 %copy-start.29 = (bf16[256,2048]{1,0:T(8,128)(2,1)}, bf16[256,2048]{1,0:T(8,128)(2,1)S(1)}, u32[]{:S(2)}) copy-start(bf16[256,2048]{1,0:T(8,128)(2,1)S(1)} %dynamic-slice_bitcast_fusion.4.refs_3_.refs_2_) | copy-start | bytes 3145732
  48.0 23.7 %collective-permute-start.5 = (bf16[256,1792]{1,0:T(8,128)(2,1)}, bf16[256,1792]{1,0:T(8,128)(2,1)}, u32[]{:S(2)}, u32[]{:S(2)}) collective-permute-start(bf16[256,1792]{1,0:T(8,128)(2,1)} %get-tuple-element.220.refs_6_.refs_3_), channel_id=1, source_target_pairs={{0,2},{1,3},{2,0},{3,1},{4,6},{5,7},{6,4},{7,5},{8,10},{9,11},{10,... | collective-permute-start | bytes 2752520 | tf_op jit(solution)/shard_map/ppermute | solution.py:60
  49.6 39.7 %collective-permute-start.6 = (bf16[256,1792]{1,0:T(8,128)(2,1)}, bf16[256,1792]{1,0:T(8,128)(2,1)}, u32[]{:S(2)}, u32[]{:S(2)}) collective-permute-start(bf16[256,1792]{1,0:T(8,128)(2,1)} %collective-permute-done.refs_7_.refs_4_), channel_id=1, source_target_pairs={{0,2},{1,3},{2,0},{3,1},{4,6},{5,7},{6,4},{7,5},{8,10},{9,11},{10,... | collective-permute-start | bytes 2752520 | tf_op jit(solution)/shard_map/ppermute | solution.py:60
  50.1 39.2 %collective-permute-start.7 = (bf16[256,1792]{1,0:T(8,128)(2,1)S(1)}, bf16[256,1792]{1,0:T(8,128)(2,1)}, u32[]{:S(2)}, u32[]{:S(2)}) collective-permute-start(bf16[256,1792]{1,0:T(8,128)(2,1)S(1)} %get-tuple-element.222.refs_10_.refs_7_), channel_id=1, source_target_pairs={{0,1},{1,0},{2,3},{3,2},{4,5},{5,4},{6,7},{7,6},{8,9},{9,8},{10,11... | collective-permute-start | bytes 2752520 | tf_op jit(solution)/shard_map/ppermute | solution.py:60
  51.5 39.1 %collective-permute-start.8 = (bf16[256,1792]{1,0:T(8,128)(2,1)}, bf16[256,1792]{1,0:T(8,128)(2,1)}, u32[]{:S(2)}, u32[]{:S(2)}) collective-permute-start(bf16[256,1792]{1,0:T(8,128)(2,1)} %collective-permute-done.1.refs_11_.refs_8_), channel_id=1, source_target_pairs={{0,1},{1,0},{2,3},{3,2},{4,5},{5,4},{6,7},{7,6},{8,9},{9,8},{10,11... | collective-permute-start | bytes 2752520 | tf_op jit(solution)/shard_map/ppermute | solution.py:60
  54.8 221.9 %all-gather.11.cloned.1.call-start = ((), (), s32[]{:S(2)}) async-start(), calls=%async_computation.2 | async-start | bytes 4718592 | tf_op jit(solution)/shard_map/all_gather | solution.py:837
  94.4 47.8 %collective-permute-start.10 = (bf16[256,2048]{1,0:T(8,128)(2,1)S(1)}, bf16[256,2048]{1,0:T(8,128)(2,1)S(1)}, u32[]{:S(2)}, u32[]{:S(2)}) collective-permute-start(bf16[256,2048]{1,0:T(8,128)(2,1)S(1)} %dynamic-slice_bitcast_fusion.4.refs_3_.refs_2_), channel_id=1, source_target_pairs={{0,2},{1,3},{2,0},{3,1},{4,6},{5,7},{6,4},{7,5},{8,10},{9,11},{10,... | collective-permute-start | bytes 3145736 | tf_op jit(solution)/shard_map/ppermute | solution.py:60
  95.9 46.3 %collective-permute-start.11 = (bf16[256,2048]{1,0:T(8,128)(2,1)S(1)}, bf16[256,2048]{1,0:T(8,128)(2,1)S(1)}, u32[]{:S(2)}, u32[]{:S(2)}) collective-permute-start(bf16[256,2048]{1,0:T(8,128)(2,1)S(1)} %dynamic-slice_bitcast_fusion.4.refs_3_.refs_2_), channel_id=1, source_target_pairs={{0,3},{1,2},{2,1},{3,0},{4,7},{5,6},{6,5},{7,4},{8,11},{9,10},{10,... | collective-permute-start | bytes 3145736 | tf_op jit(solution)/shard_map/ppermute | solution.py:60
  97.4 46.1 %collective-permute-start.9 = (bf16[256,2048]{1,0:T(8,128)(2,1)S(1)}, bf16[256,2048]{1,0:T(8,128)(2,1)}, u32[]{:S(2)}, u32[]{:S(2)}) collective-permute-start(bf16[256,2048]{1,0:T(8,128)(2,1)S(1)} %dynamic-slice_bitcast_fusion.4.refs_3_.refs_2_), channel_id=1, source_target_pairs={{0,1},{1,0},{2,3},{3,2},{4,5},{5,4},{6,7},{7,6},{8,9},{9,8},{10,11... | collective-permute-start | bytes 3145736 | tf_op jit(solution)/shard_map/ppermute | solution.py:60
  152.8 35.2 %collective-permute-start.12 = (bf16[2,128,1024]{2,1,0:T(8,128)(2,1)}, bf16[2,128,1024]{2,1,0:T(8,128)(2,1)S(1)}, u32[]{:S(2)}, u32[]{:S(2)}) collective-permute-start(bf16[2,128,1024]{2,1,0:T(8,128)(2,1)} %dynamic-slice_bitcast_fusion.12), channel_id=1, source_target_pairs={{0,1},{1,0},{2,3},{3,2},{4,5},{5,4},{6,7},{7,6},{8,9},{9,8},{10,11... | collective-permute-start | bytes 1572872 | tf_op jit(solution)/shard_map/ppermute | solution.py:60
  154.3 33.7 %collective-permute-start.13 = (bf16[2,128,1024]{2,1,0:T(8,128)(2,1)S(1)}, bf16[2,128,1024]{2,1,0:T(8,128)(2,1)S(1)}, u32[]{:S(2)}, u32[]{:S(2)}) collective-permute-start(bf16[2,128,1024]{2,1,0:T(8,128)(2,1)S(1)} %dynamic-slice_bitcast_fusion.11), channel_id=1, source_target_pairs={{0,2},{1,3},{2,0},{3,1},{4,6},{5,7},{6,4},{7,5},{8,10},{9,11},{10,... | collective-permute-start | bytes 1572872 | tf_op jit(solution)/shard_map/ppermute | solution.py:60
  155.8 32.2 %collective-permute-start.14 = (bf16[64,2048]{1,0:T(8,128)(2,1)S(1)}, bf16[64,2048]{1,0:T(8,128)(2,1)}, u32[]{:S(2)}, u32[]{:S(2)}) collective-permute-start(bf16[64,2048]{1,0:T(8,128)(2,1)S(1)} %dynamic-slice_bitcast_fusion.17.refs_7_.refs_6_), channel_id=1, source_target_pairs={{0,1},{1,0},{2,3},{3,2},{4,5},{5,4},{6,7},{7,6},{8,9},{9,8},{10,11... | collective-permute-start | bytes 786440 | tf_op jit(solution)/shard_map/ppermute | solution.py:60
  156.4 31.6 %collective-permute-start.15 = (bf16[64,2048]{1,0:T(8,128)(2,1)S(1)}, bf16[64,2048]{1,0:T(8,128)(2,1)}, u32[]{:S(2)}, u32[]{:S(2)}) collective-permute-start(bf16[64,2048]{1,0:T(8,128)(2,1)S(1)} %dynamic-slice_bitcast_fusion.17.refs_7_.refs_6_), channel_id=1, source_target_pairs={{0,2},{1,3},{2,0},{3,1},{4,6},{5,7},{6,4},{7,5},{8,10},{9,11},{10,... | collective-permute-start | bytes 786440 | tf_op jit(solution)/shard_map/ppermute | solution.py:60
  156.8 31.1 %collective-permute-start.16 = (bf16[64,2048]{1,0:T(8,128)(2,1)S(1)}, bf16[64,2048]{1,0:T(8,128)(2,1)}, u32[]{:S(2)}, u32[]{:S(2)}) collective-permute-start(bf16[64,2048]{1,0:T(8,128)(2,1)S(1)} %dynamic-slice_bitcast_fusion.17.refs_7_.refs_6_), channel_id=1, source_target_pairs={{0,3},{1,2},{2,1},{3,0},{4,7},{5,6},{6,5},{7,4},{8,11},{9,10},{10,... | collective-permute-start | bytes 786440 | tf_op jit(solution)/shard_map/ppermute | solution.py:60
  189.2 13.8 %collective-permute-start.17 = (bf16[128,1024]{1,0:T(8,128)(2,1)S(1)}, bf16[128,1024]{1,0:T(8,128)(2,1)S(1)}, u32[]{:S(2)}, u32[]{:S(2)}) collective-permute-start(bf16[128,1024]{1,0:T(8,128)(2,1)S(1)} %dynamic-slice_bitcast_fusion.16), channel_id=1, source_target_pairs={{0,2},{1,3},{2,0},{3,1},{4,6},{5,7},{6,4},{7,5},{8,10},{9,11},{10,... | collective-permute-start | bytes 786440 | tf_op jit(solution)/shard_map/ppermute | solution.py:60
  193.6 9.4 %collective-permute-start.18 = (bf16[128,1024]{1,0:T(8,128)(2,1)S(1)}, bf16[128,1024]{1,0:T(8,128)(2,1)S(1)}, u32[]{:S(2)}, u32[]{:S(2)}) collective-permute-start(bf16[128,1024]{1,0:T(8,128)(2,1)S(1)} %dynamic-slice_bitcast_fusion.15), channel_id=1, source_target_pairs={{0,1},{1,0},{2,3},{3,2},{4,5},{5,4},{6,7},{7,6},{8,9},{9,8},{10,11... | collective-permute-start | bytes 786440 | tf_op jit(solution)/shard_map/ppermute | solution.py:60
  204.0 97.9 %all-gather.13.cloned.1.call-start = ((), (), s32[]{:S(2)}) async-start(), calls=%async_computation.3 | async-start | bytes 4718592 | tf_op jit(solution)/shard_map/all_gather | solution.py:837
  206.7 21.1 %collective-permute-start.19 = (bf16[2,128,1024]{2,1,0:T(8,128)(2,1)}, bf16[2,128,1024]{2,1,0:T(8,128)(2,1)S(1)}, u32[]{:S(2)}, u32[]{:S(2)}) collective-permute-start(bf16[2,128,1024]{2,1,0:T(8,128)(2,1)} %dynamic-slice_bitcast_fusion.10), channel_id=1, source_target_pairs={{0,1},{1,0},{2,3},{3,2},{4,5},{5,4},{6,7},{7,6},{8,9},{9,8},{10,11... | collective-permute-start | bytes 1572872 | tf_op jit(solution)/shard_map/ppermute | solution.py:60
  208.8 19.0 %collective-permute-start.20 = (bf16[2,128,1024]{2,1,0:T(8,128)(2,1)S(1)}, bf16[2,128,1024]{2,1,0:T(8,128)(2,1)S(1)}, u32[]{:S(2)}, u32[]{:S(2)}) collective-permute-start(bf16[2,128,1024]{2,1,0:T(8,128)(2,1)S(1)} %dynamic-slice_bitcast_fusion.9), channel_id=1, source_target_pairs={{0,2},{1,3},{2,0},{3,1},{4,6},{5,7},{6,4},{7,5},{8,10},{9,11},{10,... | collective-permute-start | bytes 1572872 | tf_op jit(solution)/shard_map/ppermute | solution.py:60
  228.3 15.1 %collective-permute-start.21 = (bf16[128,1024]{1,0:T(8,128)(2,1)S(1)}, bf16[128,1024]{1,0:T(8,128)(2,1)S(1)}, u32[]{:S(2)}, u32[]{:S(2)}) collective-permute-start(bf16[128,1024]{1,0:T(8,128)(2,1)S(1)} %dynamic-slice_bitcast_fusion.14), channel_id=1, source_target_pairs={{0,2},{1,3},{2,0},{3,1},{4,6},{5,7},{6,4},{7,5},{8,10},{9,11},{10,... | collective-permute-start | bytes 786440 | tf_op jit(solution)/shard_map/ppermute | solution.py:60
  230.3 13.1 %collective-permute-start.22 = (bf16[128,1024]{1,0:T(8,128)(2,1)S(1)}, bf16[128,1024]{1,0:T(8,128)(2,1)S(1)}, u32[]{:S(2)}, u32[]{:S(2)}) collective-permute-start(bf16[128,1024]{1,0:T(8,128)(2,1)S(1)} %dynamic-slice_bitcast_fusion.13), channel_id=1, source_target_pairs={{0,1},{1,0},{2,3},{3,2},{4,5},{5,4},{6,7},{7,6},{8,9},{9,8},{10,11... | collective-permute-start | bytes 786440 | tf_op jit(solution)/shard_map/ppermute | solution.py:60
  248.8 22.4 %collective-permute-start.23 = (bf16[2,256,1024]{2,1,0:T(8,128)(2,1)}, bf16[2,256,1024]{2,1,0:T(8,128)(2,1)}, u32[]{:S(2)}, u32[]{:S(2)}) collective-permute-start(bf16[2,256,1024]{2,1,0:T(8,128)(2,1)} %dynamic-slice_bitcast_fusion.3), channel_id=1, source_target_pairs={{0,1},{1,0},{2,3},{3,2},{4,5},{5,4},{6,7},{7,6},{8,9},{9,8},{10,11... | collective-permute-start | bytes 3145736 | tf_op jit(solution)/shard_map/ppermute | solution.py:60
  250.7 21.4 %collective-permute-start.24 = (bf16[2,256,1024]{2,1,0:T(8,128)(2,1)S(1)}, bf16[2,256,1024]{2,1,0:T(8,128)(2,1)}, u32[]{:S(2)}, u32[]{:S(2)}) collective-permute-start(bf16[2,256,1024]{2,1,0:T(8,128)(2,1)S(1)} %dynamic-slice_bitcast_fusion.2), channel_id=1, source_target_pairs={{0,2},{1,3},{2,0},{3,1},{4,6},{5,7},{6,4},{7,5},{8,10},{9,11},{10,... | collective-permute-start | bytes 3145736 | tf_op jit(solution)/shard_map/ppermute | solution.py:60
  276.7 24.6 %collective-permute-start.25 = (bf16[256,1024]{1,0:T(8,128)(2,1)S(1)}, bf16[256,1024]{1,0:T(8,128)(2,1)S(1)}, u32[]{:S(2)}, u32[]{:S(2)}) collective-permute-start(bf16[256,1024]{1,0:T(8,128)(2,1)S(1)} %dynamic-slice_bitcast_fusion.8), channel_id=1, source_target_pairs={{0,2},{1,3},{2,0},{3,1},{4,6},{5,7},{6,4},{7,5},{8,10},{9,11},{10,... | collective-permute-start | bytes 1572872 | tf_op jit(solution)/shard_map/ppermute | solution.py:60
  277.5 23.8 %collective-permute-start.26 = (bf16[256,1024]{1,0:T(8,128)(2,1)}, bf16[256,1024]{1,0:T(8,128)(2,1)S(1)}, u32[]{:S(2)}, u32[]{:S(2)}) collective-permute-start(bf16[256,1024]{1,0:T(8,128)(2,1)} %dynamic-slice_bitcast_fusion.7), channel_id=1, source_target_pairs={{0,1},{1,0},{2,3},{3,2},{4,5},{5,4},{6,7},{7,6},{8,9},{9,8},{10,11... | collective-permute-start | bytes 1572872 | tf_op jit(solution)/shard_map/ppermute | solution.py:60
  301.9 28.9 %collective-permute-start.29 = (bf16[4,256,2048]{2,1,0:T(8,128)(2,1)}, bf16[4,256,2048]{2,1,0:T(8,128)(2,1)}, u32[]{:S(2)}, u32[]{:S(2)}) collective-permute-start(bf16[4,256,2048]{2,1,0:T(8,128)(2,1)} %get-tuple-element.317), channel_id=1, source_target_pairs={{0,4},{4,0},{8,12},{12,8},{16,20},{20,16},{24,28},{28,24},{1,5},{5... | collective-permute-start | bytes 12582920 | tf_op jit(solution)/shard_map/ppermute | solution.py:60
  302.6 24.7 %collective-permute-start.27 = (bf16[256,2048]{1,0:T(8,128)(2,1)S(1)}, bf16[256,2048]{1,0:T(8,128)(2,1)S(1)}, u32[]{:S(2)}, u32[]{:S(2)}) collective-permute-start(bf16[256,2048]{1,0:T(8,128)(2,1)S(1)} %pad_maximum_fusion.2), channel_id=1, source_target_pairs={{0,8},{4,12},{8,16},{12,20},{16,24},{20,28},{1,9},{5,13},{9,17},{1... | collective-permute-start | bytes 3145736 | tf_op jit(solution)/shard_map/ppermute | solution.py:60
  303.9 26.9 %collective-permute-start.28 = (bf16[256,2048]{1,0:T(8,128)(2,1)S(1)}, bf16[256,2048]{1,0:T(8,128)(2,1)S(1)}, u32[]{:S(2)}, u32[]{:S(2)}) collective-permute-start(bf16[256,2048]{1,0:T(8,128)(2,1)S(1)} %pad_maximum_fusion.2), channel_id=1, source_target_pairs={{8,0},{12,4},{16,8},{20,12},{24,16},{28,20},{9,1},{13,5},{17,9},{2... | collective-permute-start | bytes 3145736 | tf_op jit(solution)/shard_map/ppermute | solution.py:60
  335.8 25.0 %collective-permute-start.30 = (bf16[256,2048]{1,0:T(8,128)(2,1)}, bf16[256,2048]{1,0:T(8,128)(2,1)S(1)}, u32[]{:S(2)}, u32[]{:S(2)}) collective-permute-start(bf16[256,2048]{1,0:T(8,128)(2,1)} %get-tuple-element.324), channel_id=1, source_target_pairs={{0,8},{4,12},{8,16},{12,20},{16,24},{20,28},{1,9},{5,13},{9,17},{1... | collective-permute-start | bytes 3145736 | tf_op jit(solution)/shard_map/ppermute | solution.py:60
  339.3 25.7 %collective-permute-start.31 = (bf16[256,2048]{1,0:T(8,128)(2,1)}, bf16[256,2048]{1,0:T(8,128)(2,1)}, u32[]{:S(2)}, u32[]{:S(2)}) collective-permute-start(bf16[256,2048]{1,0:T(8,128)(2,1)} %get-tuple-element.325), channel_id=1, source_target_pairs={{8,0},{12,4},{16,8},{20,12},{24,16},{28,20},{9,1},{13,5},{17,9},{2... | collective-permute-start | bytes 3145736 | tf_op jit(solution)/shard_map/ppermute | solution.py:60
  377.2 39.4 %collective-permute-start.32 = (bf16[2,256,1024]{2,1,0:T(8,128)(2,1)}, bf16[2,256,1024]{2,1,0:T(8,128)(2,1)}, u32[]{:S(2)}, u32[]{:S(2)}) collective-permute-start(bf16[2,256,1024]{2,1,0:T(8,128)(2,1)} %dynamic-slice_bitcast_fusion.1), channel_id=1, source_target_pairs={{0,1},{1,0},{2,3},{3,2},{4,5},{5,4},{6,7},{7,6},{8,9},{9,8},{10,11... | collective-permute-start | bytes 3145736 | tf_op jit(solution)/shard_map/ppermute | solution.py:60
  377.2 39.4 %collective-permute-start.33 = (bf16[2,256,1024]{2,1,0:T(8,128)(2,1)}, bf16[2,256,1024]{2,1,0:T(8,128)(2,1)}, u32[]{:S(2)}, u32[]{:S(2)}) collective-permute-start(bf16[2,256,1024]{2,1,0:T(8,128)(2,1)} %dynamic-slice_bitcast_fusion), channel_id=1, source_target_pairs={{0,2},{1,3},{2,0},{3,1},{4,6},{5,7},{6,4},{7,5},{8,10},{9,11},{10,... | collective-permute-start | bytes 3145736 | tf_op jit(solution)/shard_map/ppermute | solution.py:60
  382.7 33.9 %collective-permute-start.34 = (bf16[256,2048]{1,0:T(8,128)(2,1)}, bf16[256,2048]{1,0:T(8,128)(2,1)}, u32[]{:S(2)}, u32[]{:S(2)}) collective-permute-start(bf16[256,2048]{1,0:T(8,128)(2,1)} %get-tuple-element.338), channel_id=1, source_target_pairs={{0,8},{4,12},{8,16},{12,20},{16,24},{20,28},{1,9},{5,13},{9,17},{1... | collective-permute-start | bytes 3145736 | tf_op jit(solution)/shard_map/ppermute | solution.py:60
  387.2 29.5 %collective-permute-start.35 = (bf16[256,2048]{1,0:T(8,128)(2,1)}, bf16[256,2048]{1,0:T(8,128)(2,1)}, u32[]{:S(2)}, u32[]{:S(2)}) collective-permute-start(bf16[256,2048]{1,0:T(8,128)(2,1)} %get-tuple-element.339), channel_id=1, source_target_pairs={{8,0},{12,4},{16,8},{20,12},{24,16},{28,20},{9,1},{13,5},{17,9},{2... | collective-permute-start | bytes 3145736 | tf_op jit(solution)/shard_map/ppermute | solution.py:60
  428.3 24.7 %collective-permute-start.38 = (bf16[256,2048]{1,0:T(8,128)(2,1)}, bf16[256,2048]{1,0:T(8,128)(2,1)}, u32[]{:S(2)}, u32[]{:S(2)}) collective-permute-start(bf16[256,2048]{1,0:T(8,128)(2,1)} %get-tuple-element.348), channel_id=1, source_target_pairs={{0,8},{4,12},{8,16},{12,20},{16,24},{20,28},{1,9},{5,13},{9,17},{1... | collective-permute-start | bytes 3145736 | tf_op jit(solution)/shard_map/ppermute | solution.py:60
  433.8 24.3 %collective-permute-start.39 = (bf16[256,2048]{1,0:T(8,128)(2,1)}, bf16[256,2048]{1,0:T(8,128)(2,1)}, u32[]{:S(2)}, u32[]{:S(2)}) collective-permute-start(bf16[256,2048]{1,0:T(8,128)(2,1)} %get-tuple-element.349), channel_id=1, source_target_pairs={{8,0},{12,4},{16,8},{20,12},{24,16},{28,20},{9,1},{13,5},{17,9},{2... | collective-permute-start | bytes 3145736 | tf_op jit(solution)/shard_map/ppermute | solution.py:60
  435.7 12.4 %collective-permute-start.36 = (bf16[256,1024]{1,0:T(8,128)(2,1)}, bf16[256,1024]{1,0:T(8,128)(2,1)}, u32[]{:S(2)}, u32[]{:S(2)}) collective-permute-start(bf16[256,1024]{1,0:T(8,128)(2,1)} %dynamic-slice_bitcast_fusion.6), channel_id=1, source_target_pairs={{0,2},{1,3},{2,0},{3,1},{4,6},{5,7},{6,4},{7,5},{8,10},{9,11},{10,... | collective-permute-start | bytes 1572872 | tf_op jit(solution)/shard_map/ppermute | solution.py:60
  435.7 12.3 %collective-permute-start.37 = (bf16[256,1024]{1,0:T(8,128)(2,1)}, bf16[256,1024]{1,0:T(8,128)(2,1)}, u32[]{:S(2)}, u32[]{:S(2)}) collective-permute-start(bf16[256,1024]{1,0:T(8,128)(2,1)} %dynamic-slice_bitcast_fusion.5), channel_id=1, source_target_pairs={{0,1},{1,0},{2,3},{3,2},{4,5},{5,4},{6,7},{7,6},{8,9},{9,8},{10,11... | collective-permute-start | bytes 1572872 | tf_op jit(solution)/shard_map/ppermute | solution.py:60
  462.1 32.9 %collective-permute-start.42 = (bf16[4,256,2048]{2,1,0:T(8,128)(2,1)}, bf16[4,256,2048]{2,1,0:T(8,128)(2,1)}, u32[]{:S(2)}, u32[]{:S(2)}) collective-permute-start(bf16[4,256,2048]{2,1,0:T(8,128)(2,1)} %get-tuple-element.361), channel_id=1, source_target_pairs={{0,4},{4,0},{8,12},{12,8},{16,20},{20,16},{24,28},{28,24},{1,5},{5... | collective-permute-start | bytes 12582920 | tf_op jit(solution)/shard_map/ppermute | solution.py:60
  466.2 24.6 %collective-permute-start.40 = (bf16[256,2048]{1,0:T(8,128)(2,1)S(1)}, bf16[256,2048]{1,0:T(8,128)(2,1)S(1)}, u32[]{:S(2)}, u32[]{:S(2)}) collective-permute-start(bf16[256,2048]{1,0:T(8,128)(2,1)S(1)} %copy-done.30), channel_id=1, source_target_pairs={{0,8},{4,12},{8,16},{12,20},{16,24},{20,28},{1,9},{5,13},{9,17},{1... | collective-permute-start | bytes 3145736 | tf_op jit(solution)/shard_map/ppermute | solution.py:60
  467.7 27.3 %collective-permute-start.41 = (bf16[256,2048]{1,0:T(8,128)(2,1)S(1)}, bf16[256,2048]{1,0:T(8,128)(2,1)S(1)}, u32[]{:S(2)}, u32[]{:S(2)}) collective-permute-start(bf16[256,2048]{1,0:T(8,128)(2,1)S(1)} %copy-done.30), channel_id=1, source_target_pairs={{8,0},{12,4},{16,8},{20,12},{24,16},{28,20},{9,1},{13,5},{17,9},{2... | collective-permute-start | bytes 3145736 | tf_op jit(solution)/shard_map/ppermute | solution.py:60
  472.6 1.3 collective-permute-start.43
  498.1 31.1 %collective-permute-start.47 = (bf16[4,256,2048]{2,1,0:T(8,128)(2,1)S(1)}, bf16[4,256,2048]{2,1,0:T(8,128)(2,1)S(1)}, u32[]{:S(2)}, u32[]{:S(2)}) collective-permute-start(bf16[4,256,2048]{2,1,0:T(8,128)(2,1)S(1)} %pad_maximum_fusion.mine), channel_id=1, source_target_pairs={{0,4},{4,0},{8,12},{12,8},{16,20},{20,16},{24,28},{28,24},{1,5},{5... | collective-permute-start | bytes 12582920 | tf_op jit(solution)/shard_map/ppermute | solution.py:60
  498.2 31.0 %collective-permute-start.44 = (bf16[256,2048]{1,0:T(8,128)(2,1)S(1)}, bf16[256,2048]{1,0:T(8,128)(2,1)S(1)}, u32[]{:S(2)}, u32[]{:S(2)}) collective-permute-start(bf16[256,2048]{1,0:T(8,128)(2,1)S(1)} %get-tuple-element.368), channel_id=1, source_target_pairs={{0,8},{4,12},{8,16},{12,20},{16,24},{20,28},{1,9},{5,13},{9,17},{1... | collective-permute-start | bytes 3145736 | tf_op jit(solution)/shard_map/ppermute | solution.py:60
  500.3 28.9 %collective-permute-start.45 = (bf16[256,2048]{1,0:T(8,128)(2,1)S(1)}, bf16[256,2048]{1,0:T(8,128)(2,1)S(1)}, u32[]{:S(2)}, u32[]{:S(2)}) collective-permute-start(bf16[256,2048]{1,0:T(8,128)(2,1)S(1)} %get-tuple-element.369), channel_id=1, source_target_pairs={{8,0},{12,4},{16,8},{20,12},{24,16},{28,20},{9,1},{13,5},{17,9},{2... | collective-permute-start | bytes 3145736 | tf_op jit(solution)/shard_map/ppermute | solution.py:60
  501.6 27.6 %collective-permute-start.46 = (f32[20480]{0:T(1024)S(1)}, f32[20480]{0:T(1024)S(1)}, u32[]{:S(2)}, u32[]{:S(2)}) collective-permute-start(f32[20480]{0:T(1024)S(1)} %add.464), channel_id=1, source_target_pairs={{0,8},{4,12},{8,0},{12,4},{16,24},{20,28},{24,16},{28,20},{1,9},{5... | collective-permute-start | bytes 245768 | tf_op jit(solution)/shard_map/ppermute | solution.py:60
  532.2 31.8 %collective-permute-start.48 = (bf16[256,2048]{1,0:T(8,128)(2,1)S(1)}, bf16[256,2048]{1,0:T(8,128)(2,1)S(1)}, u32[]{:S(2)}, u32[]{:S(2)}) collective-permute-start(bf16[256,2048]{1,0:T(8,128)(2,1)S(1)} %get-tuple-element.378), channel_id=1, source_target_pairs={{0,8},{4,12},{8,16},{12,20},{16,24},{20,28},{1,9},{5,13},{9,17},{1... | collective-permute-start | bytes 3145736 | tf_op jit(solution)/shard_map/ppermute | solution.py:60
  533.7 30.3 %collective-permute-start.49 = (bf16[256,2048]{1,0:T(8,128)(2,1)S(1)}, bf16[256,2048]{1,0:T(8,128)(2,1)S(1)}, u32[]{:S(2)}, u32[]{:S(2)}) collective-permute-start(bf16[256,2048]{1,0:T(8,128)(2,1)S(1)} %get-tuple-element.379), channel_id=1, source_target_pairs={{8,0},{12,4},{16,8},{20,12},{24,16},{28,20},{9,1},{13,5},{17,9},{2... | collective-permute-start | bytes 3145736 | tf_op jit(solution)/shard_map/ppermute | solution.py:60
  535.0 28.9 %collective-permute-start.50 = (f32[20480]{0:T(1024)S(1)}, f32[20480]{0:T(1024)S(1)}, u32[]{:S(2)}, u32[]{:S(2)}) collective-permute-start(f32[20480]{0:T(1024)S(1)} %add.469), channel_id=1, source_target_pairs={{0,16},{4,20},{8,24},{12,28},{16,0},{20,4},{24,8},{28,12},{1,17},{... | collective-permute-start | bytes 245768 | tf_op jit(solution)/shard_map/ppermute | solution.py:60
  574.0 8.3 %collective-permute-start.51 = (bf16[4,256,2048]{2,1,0:T(8,128)(2,1)}, bf16[4,256,2048]{2,1,0:T(8,128)(2,1)}, u32[]{:S(2)}, u32[]{:S(2)}) collective-permute-start(bf16[4,256,2048]{2,1,0:T(8,128)(2,1)} %pad_maximum_fusion.1.mine), channel_id=1, source_target_pairs={{0,4},{4,0},{8,12},{12,8},{16,20},{20,16},{24,28},{28,24},{1,5},{5... | collective-permute-start | bytes 12582920 | tf_op jit(solution)/shard_map/ppermute | solution.py:60
  574.1 25.0 %collective-permute-start.54 = (bf16[256,2048]{1,0:T(8,128)(2,1)}, bf16[256,2048]{1,0:T(8,128)(2,1)S(1)}, u32[]{:S(2)}, u32[]{:S(2)}) collective-permute-start(bf16[256,2048]{1,0:T(8,128)(2,1)} %get-tuple-element.393), channel_id=1, source_target_pairs={{0,8},{4,12},{8,16},{12,20},{16,24},{20,28},{1,9},{5,13},{9,17},{1... | collective-permute-start | bytes 3145736 | tf_op jit(solution)/shard_map/ppermute | solution.py:60
  575.8 27.5 %collective-permute-start.55 = (bf16[256,2048]{1,0:T(8,128)(2,1)}, bf16[256,2048]{1,0:T(8,128)(2,1)}, u32[]{:S(2)}, u32[]{:S(2)}) collective-permute-start(bf16[256,2048]{1,0:T(8,128)(2,1)} %get-tuple-element.394), channel_id=1, source_target_pairs={{8,0},{12,4},{16,8},{20,12},{24,16},{28,20},{9,1},{13,5},{17,9},{2... | collective-permute-start | bytes 3145736 | tf_op jit(solution)/shard_map/ppermute | solution.py:60
  577.7 4.6 collective-permute-start.52
  582.4 20.9 %collective-permute-start.53 = (f32[20480]{0:T(1024)S(1)}, f32[20480]{0:T(1024)S(1)}, u32[]{:S(2)}, u32[]{:S(2)}) collective-permute-start(f32[20480]{0:T(1024)S(1)} %add.475), channel_id=1, source_target_pairs={{0,2},{1,3},{2,0},{3,1},{4,6},{5,7},{6,4},{7,5},{8,10},{9,11},{10,... | collective-permute-start | bytes 245768 | tf_op jit(solution)/shard_map/ppermute | solution.py:60
  (60 other events, 515.2 us)
Sparse Core Ops, SparseCore 0:
  9.6 84.7 all-gather.14
  96.0 45.6 all-gather.6
  143.3 45.8 all-gather.8
  204.1 45.2 all-gather.10
  250.9 45.8 all-gather.12

commit v5 on v4

--- a/solution.py
+++ b/solution.py
@@ -115,25 +115,30 @@
     return jnp.concatenate(held, axis=fold)
 
 
-def weave_steps(own, mine, other):
+def swap_steps(value, kept=None):
+    (got,) = yield [(value, *swaps("ctx", 1))]
+    return value if kept is None else kept, got
+
+
+def add_pair(mine, got):
+    return (mine.astype(F32) + got.astype(F32)).astype(BF16)
+
+
+def weave_steps(own, held, shape):
     count = lax.axis_size("ctx")
     line = count // 2
     place = lax.axis_index("ctx") // 2
-    alike = own.shape == mine.shape[1:]
+    alike = own.shape == shape[1:]
     forth = [(i, i + 2) for i in range(count - 2)]
     back = [(i, i - 2) for i in range(2, count)]
     ups, downs = [], []
-    up, down, got = yield [
-        (own, "ctx", forth), (own, "ctx", back), (other, *swaps("ctx", 1)),
-    ]
-    up_sum, down_sum = (up, down) if alike else (jnp.zeros_like(mine[0]),) * 2
+    up, down = yield [(own, "ctx", forth), (own, "ctx", back)]
+    up_sum, down_sum = (up, down) if alike else (jnp.zeros(shape[1:], BF16),) * 2
 
     def block(target, added):
         target = jnp.clip(target, 0, line - 1)
-        total = added.astype(F32)
-        for half in (mine, got):
-            total += lax.dynamic_index_in_dim(half, target, 0, keepdims=False).astype(F32)
-        return total
+        part = lax.dynamic_index_in_dim(held[0], target, 0, keepdims=False)
+        return part.astype(F32) + added.astype(F32)
 
     for step in range(2, line + 1):
         ups.append(up)
@@ -156,23 +161,23 @@
                 (down_sum, "ctx", [(i, j) for i, j in back if i // 2 > line - step]),
             ]
 
-    def at_chip(chip):
-        value = own
-        for away in range(1, line):
-            value = jnp.where(place == chip + away, ups[away - 1], value)
-            value = jnp.where(place == chip - away, downs[away - 1], value)
-        return value
-
-    def swap_cores():
-        blocks = jnp.stack([at_chip(chip) for chip in range(line)])
-        (beside_blocks,) = yield [(blocks, *swaps("ctx", 1))]
-        return blocks, beside_blocks
-
     def finish():
         last_up, last_down = yield [(up_sum, "ctx", forth), (down_sum, "ctx", back)]
         return block(place, last_up) + last_down.astype(F32)
 
-    return Flow(swap_cores()), Flow(finish())
+    return (own, ups, downs), Flow(finish())
+
+
+def in_order(own, ups, downs):
+    place = lax.axis_index("ctx") // 2
+    blocks = []
+    for chip in range(len(ups) + 1):
+        value = own
+        for away, (up, down) in enumerate(zip(ups, downs), 1):
+            value = jnp.where(place == chip + away, up, value)
+            value = jnp.where(place == chip - away, down, value)
+        blocks.append(value)
+    return jnp.stack(blocks)
 
 
 def total_steps(vector):
@@ -974,22 +979,30 @@
         up_terms = beside(lambda same: same, (up_terms,), [second_flow])
     up_flow = Flow(scatter_steps(up_terms.reshape(shard_count, shard_rows, units), *both, fold=1))
     out_halves = beside(leave, (after(attended, second_flow.result),), [up_flow])
+    core_flow = Flow(swap_steps(out_halves[1], out_halves[0]))
+    held = []
     down_total = tuple(by_ctx(flow.result) for flow in (first_flow, second_flow))
     grad_mixed, weave = (), None
     for pair in range(pairs):
-        grad_mixed = (
-            beside(
-                lambda rows: attention_backward(
-                    pair, block_place, ends, natural_tables, kept, rows, grad_mixed
-                ),
-                (after(grad_att, *out_halves, down_total[min(pair, 1)]),),
-                [weave or up_flow],
-            ),
-        )
+
+        def backward(rows, *halves):
+            if halves:
+                held.append(add_pair(*halves))
+            result = attention_backward(
+                pair, block_place, ends, natural_tables, kept, rows, grad_mixed
+            )
+            return [result, *held]
+
+        rows = after(grad_att, *out_halves, down_total[min(pair, 1)])
+        halves = core_flow.result if weave else ()
+        flows = [weave] if weave else [flow for flow in (up_flow, core_flow) if flow.moves]
+        grad_mixed = (beside(backward, (rows, *halves), flows)[0],)
         while up_flow.moves and pair + 1 == pairs:
             out_halves = beside(lambda *same: same, tuple(out_halves), [up_flow])
         if not up_flow.moves and weave is None:
-            weave = Flow(weave_steps(up_flow.result, *out_halves))
+            weave = Flow(weave_steps(up_flow.result, held, out_halves[0].shape))
+    if not held:
+        held.append(add_pair(*core_flow.result))
     (grad_mixed,) = grad_mixed
 
     def joint(rows):
@@ -1043,12 +1056,22 @@
 
     while weave.moves:
         beside(nothing, (), [weave])
-    up_swap, out_finish = weave.result
-    down_total = beside(side_by_side, down_total, [joint_flow, out_finish])
+    up_blocks, out_finish = weave.result
+    core_flow = Flow(swap_steps(other, mine))
+    down_total = beside(side_by_side, down_total, [joint_flow, core_flow], late=[out_finish])
     while joint_flow.moves:
         beside(nothing, (), [joint_flow])
-    weave = Flow(weave_steps(joint_flow.result, mine, other))
-    beside(nothing, (), [weave, total_flow])
+    held = []
+    weave = Flow(weave_steps(joint_flow.result, held, mine.shape))
+
+    def order_and_add(blocks, halves):
+        held.append(add_pair(*halves))
+        return in_order(*blocks), held[0]
+
+    up_blocks, _ = beside(
+        order_and_add, (up_blocks, core_flow.result), [weave, total_flow], early=[out_finish]
+    )
+    up_swap = Flow(swap_steps(up_blocks))
     beside(nothing, (), [flow for flow in (weave, total_flow, up_swap) if flow.moves])
     (up_dealt,) = beside(
         lambda *halves: deal_columns(*halves, unit, list(range(shard_count)), at),
@@ -1057,7 +1080,8 @@
     )
     while weave.moves:
         beside(nothing, (), [flow for flow in (weave, total_flow) if flow.moves])
-    joint_swap, norm_finish = weave.result
+    joint_blocks, norm_finish = weave.result
+    joint_swap = Flow(swap_steps(in_order(*joint_blocks)))
     beside(
         nothing, (), [flow for flow in (joint_swap, total_flow) if flow.moves], late=[norm_finish]
     )

time: 626 us -> 611 us (0.976)
  waiting for transfers between devices: 156 us -> 145 us
  other arithmetic: 74.1 us -> 64.4 us
    ppermute x56, waiting for transfers between devices: 151 us -> 138 us  [beside(): lax.ppermute(value, axis, pairs)]
    select_n x4, other arithmetic: 16.2 us -> 5.99 us  [weave_steps(): down_sum = jnp.where(place <= line - step, down, down_sum)]
    convert_element_type x0 -> x2, other arithmetic: none -> 9.48 us  [add_pair(): return (mine.astype(F32) + got.astype(F32)).astype(BF16)]
    another operation x7 -> x6, other arithmetic: 14.2 us -> 8.84 us  [the longest x5 8.67 us: in_order(): return jnp.stack(blocks)]
    unnamed x143 -> x157, local copies, waits for them, and re-layouts: 14.8 us -> 20 us
  transfers between devices with their start and end apart: 61 -> 61, of which waited for: 25 -> 21; matrix products, arithmetic and copies ran while one was open for 14% -> 16% of each run, Pallas kernels for 33% -> 34%
where the time goes in v5:
time: 611 us; the launch traced here: 606 us
  Pallas kernels  204 us (33%)
  waiting for transfers between devices  145 us (24%)
  starting transfers between devices  87.5 us (14%)
  other arithmetic  64.4 us (11%)
  local copies, waits for them, and re-layouts  44.9 us (7%)
  matrix products  44.9 us (7%)
  between operations  15.5 us (3%)
    ppermute x56, waiting for transfers between devices, beside(): lax.ppermute(value, axis, pairs)  138 us
    pallas_call x4, Pallas kernels, row_call(): pl.pallas_call(body, out_shape=out_shape + [jax.ShapeDtypeStruct(shape, F...  98.9 us
    ppermute x56, starting transfers between devices, beside(): lax.ppermute(value, axis, pairs)  87.2 us
    dot_general x6, matrix products, dot_tn(): lax.dot_general(left, right, (((0,), (0,)), ((), ())), preferred_element_...  44.9 us
    pallas_call x2, Pallas kernels, attention_backward(): pl.pallas_call(functools.partial(backward_kernel, pair), out_shape=jax.Sh...  42.2 us
    pallas_call x1, Pallas kernels, attention_forward(): pl.pallas_call(forward_kernel, out_shape=(jax.ShapeDtypeStruct((tokens, w...  27.2 us
    unnamed x157, local copies, waits for them, and re-layouts  20 us
    pallas_call x2, Pallas kernels, deal_columns(): pl.pallas_call(functools.partial(deal_kernel, unit, order), out_shape=out...  19.4 us
  transfers between devices with their start and end apart: 61, of which 21 were waited for; matrix products, arithmetic and copies ran while one was open for 16% of the time, Pallas kernels for 34%

profile of v5, /device:TPU:0, one launch (start us, length us, event | category | flops | bytes accessed | tf_op | source)
XLA Modules:
  0.0 606.3 jit_solution(11481595977606440104)
XLA Ops:
  8.0 3.4 copy-done.2
  11.4 2.8 copy-done.4
  19.0 2.7 fusion.66
  21.7 2.9 collective-permute-start
  26.8 2.9 collective-permute-start.4
  32.1 13.5 %collective-permute-done.2 = bf16[8,704]{1,0:T(8,128)(2,1)S(1)} collective-permute-done((bf16[8,704]{1,0:T(8,128)(2,1)S(1)}, bf16[8,704]{1,0:T(8,128)(2,1)S(1)}, u32[]{:S(2)}, u32[]{:S(2)}) %collective-permute-start.2) | collective-permute-done | bytes 11296 | tf_op jit(solution)/shard_map/ppermute | solution.py:60
  55.1 8.9 %fusion.41 = (f32[2048,128]{1,0:T(8,128)}, f32[2048,128]{1,0:T(8,128)}, f32[2048,128]{1,0:T(8,128)}, f32[2048,128]{1,0:T(8,128)}) fusion(f32[2048]{0:T(1024)S(1)} %get-tuple-element.482, f32[128]{0:T(128)S(1)} %get-tuple-element.480, f32[128]{0:T(128)S(1)} %get-tuple-element.481, f32[2048]{0:T(1024)S(1)} %get-tuple-element.483), kind=kLoop, calls=%fused_computation.77 | loop fusion | flops 1048576 | bytes 4211712 | tf_op jit(solution)/shard_map/mul | solution.py:397
  64.0 7.6 %collective-permute-done.5.refs_8_.refs_5_ = bf16[256,1792]{1,0:T(8,128)(2,1)} collective-permute-done((bf16[256,1792]{1,0:T(8,128)(2,1)}, bf16[256,1792]{1,0:T(8,128)(2,1)}, u32[]{:S(2)}, u32[]{:S(2)}) %collective-permute-start.5) | collective-permute-done | bytes 917536 | tf_op jit(solution)/shard_map/ppermute | solution.py:60
  71.6 17.7 %collective-permute-done.6.refs_9_.refs_6_ = bf16[256,1792]{1,0:T(8,128)(2,1)} collective-permute-done((bf16[256,1792]{1,0:T(8,128)(2,1)}, bf16[256,1792]{1,0:T(8,128)(2,1)}, u32[]{:S(2)}, u32[]{:S(2)}) %collective-permute-start.6) | collective-permute-done | bytes 917536 | tf_op jit(solution)/shard_map/ppermute | solution.py:60
  90.5 3.9 all-gather.15.cloned.1.call-done
  97.9 34.2 %shard_map.230 = (bf16[2048,2048]{1,0:T(8,128)(2,1)}, bf16[2048,1024]{1,0:T(8,128)(2,1)}, bf16[2048,1024]{1,0:T(8,128)(2,1)}, bf16[2048,768]{1,0:T(8,128)(2,1)}) custom-call(s32[2]{0:T(128)} %pad_add_fusion.at, bf16[2048,2048]{1,0:T(8,128)(2,1)} %bitcast.302, f32[2048,128]{1,0:T(8,128)} %get-tuple-element.238.refs_1_, ...), custom_call_target="tpu_custom_call" | custom-call | flops 15032385536 | bytes 37772288 | tf_op jit(solution)/shard_map/pallas_call | solution.py:518
  132.2 10.0 %collective-permute-done.10.refs_5_.refs_4_ = bf16[256,2048]{1,0:T(8,128)(2,1)S(1)} collective-permute-done((bf16[256,2048]{1,0:T(8,128)(2,1)S(1)}, bf16[256,2048]{1,0:T(8,128)(2,1)S(1)}, u32[]{:S(2)}, u32[]{:S(2)}) %collective-permute-start.10) | collective-permute-done | bytes 1048608 | tf_op jit(solution)/shard_map/ppermute | solution.py:60
  143.5 8.0 %convolution_convert_fusion.3 = bf16[1024,1024]{1,0:T(8,128)(2,1)S(1)} fusion(bf16[2048,1024]{1,0:T(8,128)(2,1)} %get-tuple-element.254.refs_1_, bf16[2048,1024]{1,0:T(8,128)(2,1)} %all-gather.7.cloned.1.call-done.refs_0_), kind=kOutput, calls=%fused_computation.61 | convolution fusion | flops 4296015872 | bytes 10485760 | tf_op jit(solution)/shard_map/dot_general | solution.py:30
  156.9 2.4 collective-permute-start.16
  159.3 27.2 %shard_map.231 = (bf16[2048,256]{1,0:T(8,128)(2,1)}, bf16[2048,768]{1,0:T(8,128)(2,1)}, f32[256,2048]{1,0:T(8,128)}, f32[4,2048]{1,0:T(4,128)}) custom-call(s32[128]{0:T(128)} %place_ref.5, s32[4]{0:T(128)} %bitcast.299, bf16[2048,768]{1,0:T(8,128)(2,1)} %get-tuple-element.258.lin_hbm), custom_call_target="tpu_custom_call" | custom-call | flops 40000000000 | bytes 16000000 | tf_op jit(solution)/shard_map/pallas_call | solution.py:408
  187.0 2.3 all-gather.9.cloned.1.call-done.refs_1_
  192.2 9.4 %convolution_convert_fusion.2 = bf16[1024,1024]{1,0:T(8,128)(2,1)} fusion(bf16[2048,1024]{1,0:T(8,128)(2,1)} %get-tuple-element.254.refs_1_, bf16[2048,1024]{1,0:T(8,128)(2,1)} %all-gather.9.cloned.1.call-done.refs_1_), kind=kOutput, calls=%fused_computation.60 | convolution fusion | flops 4296015872 | bytes 10485760 | tf_op jit(solution)/shard_map/dot_general | solution.py:30
  207.4 18.9 %shard_map.232 = (bf16[2048,1024]{1,0:T(8,128)(2,1)}, bf16[2048,256]{1,0:T(8,128)(2,1)}, f32[1,1024]{1,0:T(1,128)}) custom-call(s32[2]{0:T(128)} %pad_add_fusion.at, bf16[2048,1024]{1,0:T(8,128)(2,1)} %all-gather.7.cloned.1.call-done.refs_0_, bf16[2048,1024]{1,0:T(8,128)(2,1)} %all-gather.9.cloned.1.call-done.refs_1_, ...), custom_call_target="tpu_custom_call" | custom-call | flops 10737418240 | bytes 23068672 | tf_op jit(solution)/shard_map/pallas_call | solution.py:518
  229.1 12.9 %convolution_convert_fusion = bf16[2048,1024]{1,0:T(8,128)(2,1)} fusion(bf16[2048,2048]{1,0:T(8,128)(2,1)} %get-tuple-element.294, bf16[2048,1024]{1,0:T(8,128)(2,1)S(1)} %copy-done.68), kind=kOutput, calls=%fused_computation.4 | convolution fusion | flops 8592031744 | bytes 16777216 | tf_op jit(solution)/shard_map/dot_general | solution.py:30
  242.9 2.7 fusion.63
  249.2 17.6 %shard_map.233 = (bf16[4,256,2048]{2,1,0:T(8,128)(2,1)}, bf16[4,256,2048]{2,1,0:T(8,128)(2,1)}) custom-call(s32[2]{0:T(128)} %pad_add_fusion.at, bf16[2048,256]{1,0:T(8,128)(2,1)} %get-tuple-element.337.refs_0_, bf16[2048,1024]{1,0:T(8,128)(2,1)} %get-tuple-element.254.refs_1_, bf16[256,2048]{1,0:T(8,128)(2,1)} %copy-done.35, ...), custom_call_target="tpu_custom_call" | custom-call | flops 10737418240 | bytes 18874368 | tf_op jit(solution)/shard_map/pallas_call | solution.py:518
  266.8 4.5 collective-permute-done.23
  271.6 2.0 fusion.30
  279.9 21.2 %shard_map.234.refs_0_ = bf16[2048,768]{1,0:T(8,128)(2,1)} custom-call(s32[128]{0:T(128)} %place_ref.5, s32[4]{0:T(128)} %bitcast.300, f32[2048,128]{1,0:T(8,128)} %get-tuple-element.312.cos_ref, f32[2048,128]{1,0:T(8,128)} %get-tuple-element.313.sin_ref, bf16[2048,768]{1,0:T(8,128)(2,1)} %get-tuple-element.314.rows, ...), custom_call_target="tpu_custom_call" | custom-call | flops 20000000000 | bytes 8000000 | tf_op jit(solution)/shard_map/pallas_call | solution.py:432
  306.5 21.0 %shard_map.235.refs_1_ = bf16[2048,768]{1,0:T(8,128)(2,1)} custom-call(s32[128]{0:T(128)} %place_ref.5, s32[4]{0:T(128)} %bitcast.301, f32[2048,128]{1,0:T(8,128)} %get-tuple-element.312.cos_ref, f32[2048,128]{1,0:T(8,128)} %get-tuple-element.313.sin_ref, bf16[2048,768]{1,0:T(8,128)(2,1)} %get-tuple-element.314.rows, ...), custom_call_target="tpu_custom_call", output_to_operand_aliasing={{}: (8, {})} | custom-call | flops 20000000000 | bytes 8000000 | tf_op jit(solution)/shard_map/pallas_call | solution.py:432
  327.5 5.4 add_convert_fusion.1
  332.9 2.2 fusion.33
  336.7 4.9 collective-permute-start.30
  342.9 10.5 %convolution_convert_fusion.1.left = bf16[2048,768]{1,0:T(8,128)(2,1)} fusion(bf16[2048,2048]{1,0:T(8,128)(2,1)} %get-tuple-element.294, bf16[2048,768]{1,0:T(8,128)(2,1)S(1)} %copy-done.69), kind=kOutput, calls=%fused_computation.5 | convolution fusion | flops 6444023808 | bytes 14680064 | tf_op jit(solution)/shard_map/dot_general | solution.py:30
  353.4 2.1 convolution_convert_fusion.4.refs_1_
  355.6 2.1 convolution_convert_fusion.5.refs_0_
  357.7 4.7 shard_map.236
  363.8 4.1 collective-permute-done.31
  368.9 2.8 fusion.62
  375.4 2.1 fusion.35
  377.5 7.8 %collective-permute-start.32 = (bf16[2,256,1024]{2,1,0:T(8,128)(2,1)}, bf16[2,256,1024]{2,1,0:T(8,128)(2,1)}, u32[]{:S(2)}, u32[]{:S(2)}) collective-permute-start(bf16[2,256,1024]{2,1,0:T(8,128)(2,1)} %dynamic-slice_bitcast_fusion.1), channel_id=1, source_target_pairs={{0,1},{1,0},{2,3},{3,2},{4,5},{5,4},{6,7},{7,6},{8,9},{9,8},{10,11... | collective-permute-start | bytes 3145736 | tf_op jit(solution)/shard_map/ppermute | solution.py:60
  385.3 3.5 collective-permute-start.34
  390.1 28.1 %shard_map.237 = (bf16[4,256,2048]{2,1,0:T(8,128)(2,1)}, bf16[4,256,2048]{2,1,0:T(8,128)(2,1)}, f32[1,2048]{1,0:T(1,128)}, f32[1,2048]{1,0:T(1,128)}, f32[1,768]{1,0:T(1,128)}) custom-call(s32[2]{0:T(128)} %pad_add_fusion.at, bf16[2048,2048]{1,0:T(8,128)(2,1)} %bitcast.303, bf16[2048,768]{1,0:T(8,128)(2,1)} %shard_map.235.refs_1_, ...), custom_call_target="tpu_custom_call" | custom-call | flops 15032385536 | bytes 31457280 | tf_op jit(solution)/shard_map/pallas_call | solution.py:518
  419.2 1.9 fusion.23
  422.0 1.8 fusion.24
  425.6 3.4 fusion.21
  429.6 2.1 collective-permute-start.36
  431.7 5.5 collective-permute-start.42
  438.5 10.2 %shard_map.238 = f32[2048,2048]{1,0:T(8,128)} custom-call(bf16[2048,1024]{1,0:T(8,128)(2,1)} %all-gather.13.cloned.1.call-done.refs_0_, bf16[2048,1024]{1,0:T(8,128)(2,1)} %all-gather.11.cloned.1.call-done.refs_1_), custom_call_target="tpu_custom_call" | custom-call | bytes 25165824 | tf_op jit(solution)/shard_map/pallas_call | solution.py:787
  452.5 4.6 collective-permute-start.39
  458.5 2.3 select_bitcast_fusion.7
  461.3 4.1 add_convert_fusion
  466.1 15.6 %collective-permute-done.39 = bf16[256,2048]{1,0:T(8,128)(2,1)S(1)} collective-permute-done((bf16[256,2048]{1,0:T(8,128)(2,1)S(1)}, bf16[256,2048]{1,0:T(8,128)(2,1)S(1)}, u32[]{:S(2)}, u32[]{:S(2)}) %collective-permute-start.39) | collective-permute-done | bytes 1048608 | tf_op jit(solution)/shard_map/ppermute | solution.py:60
  481.7 5.1 collective-permute-done.40
  490.7 2.7 collective-permute-start.46
  493.4 24.9 %collective-permute-done.46 = f32[20480]{0:T(1024)S(1)} collective-permute-done((f32[20480]{0:T(1024)S(1)}, f32[20480]{0:T(1024)S(1)}, u32[]{:S(2)}, u32[]{:S(2)}) %collective-permute-start.46) | collective-permute-done | bytes 81952 | tf_op jit(solution)/shard_map/ppermute | solution.py:60
  522.0 3.5 collective-permute-start.50
  525.5 7.4 %shard_map.239 = f32[512,8192]{1,0:T(8,128)} custom-call(s32[2]{0:T(128)S(1)} %pad_add_fusion.1.at_ref, bf16[4,256,2048]{2,1,0:T(8,128)(2,1)S(1)} %pad_maximum_fusion.mine, bf16[4,256,2048]{2,1,0:T(8,128)(2,1)S(1)} %collective-permute-done.47.other), custom_call_target="tpu_custom_call" | custom-call | bytes 25165824 | tf_op jit(solution)/shard_map/pallas_call | solution.py:716
  533.0 18.4 %collective-permute-done.50 = f32[20480]{0:T(1024)S(1)} collective-permute-done((f32[20480]{0:T(1024)S(1)}, f32[20480]{0:T(1024)S(1)}, u32[]{:S(2)}, u32[]{:S(2)}) %collective-permute-start.50) | collective-permute-done | bytes 81952 | tf_op jit(solution)/shard_map/ppermute | solution.py:60
  551.4 2.1 fusion.13
  555.2 1.7 select_bitcast_fusion.2
  557.0 2.3 pad_maximum_fusion.1.mine
  563.0 1.8 collective-permute-start.52
  564.8 2.8 collective-permute-done.52
  568.3 12.0 %shard_map.240 = (f32[512,6144]{1,0:T(8,128)}, f32[512,2048]{1,0:T(8,128)}) custom-call(s32[2]{0:T(128)S(1)} %pad_add_fusion.1.at_ref, bf16[4,256,2048]{2,1,0:T(8,128)(2,1)} %pad_maximum_fusion.1.mine, bf16[4,256,2048]{2,1,0:T(8,128)(2,1)} %collective-permute-done.51.other), custom_call_target="tpu_custom_call" | custom-call | bytes 25165824 | tf_op jit(solution)/shard_map/pallas_call | solution.py:716
  580.3 4.0 collective-permute-done.54
  584.3 4.2 collective-permute-done.55
  590.5 2.2 fusion.56
  592.8 6.2 %fusion.43 = (bf16[1,256,2048]{2,1,0:T(8,128)(2,1)}, bf16[1,256,2048]{2,1,0:T(8,128)(2,1)}) fusion(bf16[1,256,2048]{2,1,0:T(8,128)(2,1)S(1)} %copy-done.10, f32[256]{0:T(256)S(1)} %broadcast_multiply_fusion, f32[256]{0:T(256)S(1)} %broadcast_multiply_fusion.1, f32[256]{0:T(256)S(1)} %add_rsqrt_fusion, f32[256]{0:T(256)S(1)} %broadcast_multiply_fusion.2, ...), kind=kLoop, calls=%fused_computation.79 | loop fusion | flops 12582912 | bytes 10506244 | tf_op jit(solution)/shard_map/broadcast_in_dim | solution.py:1120
  (353 shorter events, 97.0 us)
Async XLA Ops:
  7.2 87.2 %all-gather.15.cloned.1.call-start = ((), (), s32[]{:S(2)}) async-start(), calls=%async_computation.4 | async-start | bytes 9437184 | tf_op jit(solution)/shard_map/all_gather | solution.py:842
  7.9 135.6 %all-gather.7.cloned.1.call-start = ((), (), s32[]{:S(2)}) async-start(), calls=%async_computation | async-start | bytes 4718592 | tf_op jit(solution)/shard_map/all_gather | solution.py:842
  17.8 171.4 %all-gather.9.cloned.1.call-start = ((), (), s32[]{:S(2)}) async-start(), calls=%async_computation.1 | async-start | bytes 4718592 | tf_op jit(solution)/shard_map/all_gather | solution.py:842
  21.7 25.3 %collective-permute-start = (bf16[256,1792]{1,0:T(8,128)(2,1)}, bf16[256,1792]{1,0:T(8,128)(2,1)}, u32[]{:S(2)}, u32[]{:S(2)}) collective-permute-start(bf16[256,1792]{1,0:T(8,128)(2,1)} %get-tuple-element.234.refs_6_.refs_3_), channel_id=1, source_target_pairs={{0,1},{1,0},{2,3},{3,2},{4,5},{5,4},{6,7},{7,6},{8,9},{9,8},{10,11... | collective-permute-start | bytes 2752520 | tf_op jit(solution)/shard_map/ppermute | solution.py:60
  24.7 22.4 %collective-permute-start.1 = (bf16[256,1792]{1,0:T(8,128)(2,1)S(1)}, bf16[256,1792]{1,0:T(8,128)(2,1)}, u32[]{:S(2)}, u32[]{:S(2)}) collective-permute-start(bf16[256,1792]{1,0:T(8,128)(2,1)S(1)} %get-tuple-element.236.refs_10_.refs_7_), channel_id=1, source_target_pairs={{0,2},{1,3},{2,0},{3,1},{4,6},{5,7},{6,4},{7,5},{8,10},{9,11},{10,... | collective-permute-start | bytes 2752520 | tf_op jit(solution)/shard_map/ppermute | solution.py:60
  26.2 19.4 %collective-permute-start.2 = (bf16[8,704]{1,0:T(8,128)(2,1)S(1)}, bf16[8,704]{1,0:T(8,128)(2,1)S(1)}, u32[]{:S(2)}, u32[]{:S(2)}) collective-permute-start(bf16[8,704]{1,0:T(8,128)(2,1)S(1)} %reshape.338), channel_id=1, source_target_pairs={{0,1},{1,0},{2,3},{3,2},{4,5},{5,4},{6,7},{7,6},{8,9},{9,8},{10,11... | collective-permute-start | bytes 33800 | tf_op jit(solution)/shard_map/ppermute | solution.py:60
  26.7 20.2 %collective-permute-start.3 = (bf16[8,704]{1,0:T(8,128)(2,1)S(1)}, bf16[8,704]{1,0:T(8,128)(2,1)S(1)}, u32[]{:S(2)}, u32[]{:S(2)}) collective-permute-start(bf16[8,704]{1,0:T(8,128)(2,1)S(1)} %reshape.338), channel_id=1, source_target_pairs={{0,2},{1,3},{2,0},{3,1},{4,6},{5,7},{6,4},{7,5},{8,10},{9,11},{10,... | collective-permute-start | bytes 33800 | tf_op jit(solution)/shard_map/ppermute | solution.py:60
  26.8 20.2 %collective-permute-start.4 = (bf16[8,704]{1,0:T(8,128)(2,1)S(1)}, bf16[8,704]{1,0:T(8,128)(2,1)S(1)}, u32[]{:S(2)}, u32[]{:S(2)}) collective-permute-start(bf16[8,704]{1,0:T(8,128)(2,1)S(1)} %reshape.338), channel_id=1, source_target_pairs={{0,3},{1,2},{2,1},{3,0},{4,7},{5,6},{6,5},{7,4},{8,11},{9,10},{10,... | collective-permute-start | bytes 33800 | tf_op jit(solution)/shard_map/ppermute | solution.py:60
  29.7 127.1 %copy-start.47 = (bf16[64,2048]{1,0:T(8,128)(2,1)}, bf16[64,2048]{1,0:T(8,128)(2,1)S(1)}, u32[]{:S(2)}) copy-start(bf16[64,2048]{1,0:T(8,128)(2,1)S(1)} %dynamic-slice_bitcast_fusion.17.refs_7_.refs_6_) | copy-start | bytes 786436
  31.2 66.2 %copy-start.35 = (bf16[256,2048]{1,0:T(8,128)(2,1)}, bf16[256,2048]{1,0:T(8,128)(2,1)S(1)}, u32[]{:S(2)}) copy-start(bf16[256,2048]{1,0:T(8,128)(2,1)S(1)} %dynamic-slice_bitcast_fusion.4.refs_3_.refs_2_) | copy-start | bytes 3145732
  47.9 23.7 %collective-permute-start.5 = (bf16[256,1792]{1,0:T(8,128)(2,1)}, bf16[256,1792]{1,0:T(8,128)(2,1)}, u32[]{:S(2)}, u32[]{:S(2)}) collective-permute-start(bf16[256,1792]{1,0:T(8,128)(2,1)} %get-tuple-element.234.refs_6_.refs_3_), channel_id=1, source_target_pairs={{0,2},{1,3},{2,0},{3,1},{4,6},{5,7},{6,4},{7,5},{8,10},{9,11},{10,... | collective-permute-start | bytes 2752520 | tf_op jit(solution)/shard_map/ppermute | solution.py:60
  49.5 39.7 %collective-permute-start.6 = (bf16[256,1792]{1,0:T(8,128)(2,1)}, bf16[256,1792]{1,0:T(8,128)(2,1)}, u32[]{:S(2)}, u32[]{:S(2)}) collective-permute-start(bf16[256,1792]{1,0:T(8,128)(2,1)} %collective-permute-done.refs_7_.refs_4_), channel_id=1, source_target_pairs={{0,2},{1,3},{2,0},{3,1},{4,6},{5,7},{6,4},{7,5},{8,10},{9,11},{10,... | collective-permute-start | bytes 2752520 | tf_op jit(solution)/shard_map/ppermute | solution.py:60
  50.0 39.2 %collective-permute-start.7 = (bf16[256,1792]{1,0:T(8,128)(2,1)S(1)}, bf16[256,1792]{1,0:T(8,128)(2,1)}, u32[]{:S(2)}, u32[]{:S(2)}) collective-permute-start(bf16[256,1792]{1,0:T(8,128)(2,1)S(1)} %get-tuple-element.236.refs_10_.refs_7_), channel_id=1, source_target_pairs={{0,1},{1,0},{2,3},{3,2},{4,5},{5,4},{6,7},{7,6},{8,9},{9,8},{10,11... | collective-permute-start | bytes 2752520 | tf_op jit(solution)/shard_map/ppermute | solution.py:60
  51.5 39.0 %collective-permute-start.8 = (bf16[256,1792]{1,0:T(8,128)(2,1)}, bf16[256,1792]{1,0:T(8,128)(2,1)}, u32[]{:S(2)}, u32[]{:S(2)}) collective-permute-start(bf16[256,1792]{1,0:T(8,128)(2,1)} %collective-permute-done.1.refs_11_.refs_8_), channel_id=1, source_target_pairs={{0,1},{1,0},{2,3},{3,2},{4,5},{5,4},{6,7},{7,6},{8,9},{9,8},{10,11... | collective-permute-start | bytes 2752520 | tf_op jit(solution)/shard_map/ppermute | solution.py:60
  54.7 223.2 %all-gather.13.cloned.1.call-start = ((), (), s32[]{:S(2)}) async-start(), calls=%async_computation.3 | async-start | bytes 4718592 | tf_op jit(solution)/shard_map/all_gather | solution.py:842
  94.4 47.8 %collective-permute-start.10 = (bf16[256,2048]{1,0:T(8,128)(2,1)S(1)}, bf16[256,2048]{1,0:T(8,128)(2,1)S(1)}, u32[]{:S(2)}, u32[]{:S(2)}) collective-permute-start(bf16[256,2048]{1,0:T(8,128)(2,1)S(1)} %dynamic-slice_bitcast_fusion.4.refs_3_.refs_2_), channel_id=1, source_target_pairs={{0,2},{1,3},{2,0},{3,1},{4,6},{5,7},{6,4},{7,5},{8,10},{9,11},{10,... | collective-permute-start | bytes 3145736 | tf_op jit(solution)/shard_map/ppermute | solution.py:60
  95.9 46.3 %collective-permute-start.11 = (bf16[256,2048]{1,0:T(8,128)(2,1)S(1)}, bf16[256,2048]{1,0:T(8,128)(2,1)S(1)}, u32[]{:S(2)}, u32[]{:S(2)}) collective-permute-start(bf16[256,2048]{1,0:T(8,128)(2,1)S(1)} %dynamic-slice_bitcast_fusion.4.refs_3_.refs_2_), channel_id=1, source_target_pairs={{0,3},{1,2},{2,1},{3,0},{4,7},{5,6},{6,5},{7,4},{8,11},{9,10},{10,... | collective-permute-start | bytes 3145736 | tf_op jit(solution)/shard_map/ppermute | solution.py:60
  97.4 46.1 %collective-permute-start.9 = (bf16[256,2048]{1,0:T(8,128)(2,1)S(1)}, bf16[256,2048]{1,0:T(8,128)(2,1)}, u32[]{:S(2)}, u32[]{:S(2)}) collective-permute-start(bf16[256,2048]{1,0:T(8,128)(2,1)S(1)} %dynamic-slice_bitcast_fusion.4.refs_3_.refs_2_), channel_id=1, source_target_pairs={{0,1},{1,0},{2,3},{3,2},{4,5},{5,4},{6,7},{7,6},{8,9},{9,8},{10,11... | collective-permute-start | bytes 3145736 | tf_op jit(solution)/shard_map/ppermute | solution.py:60
  152.8 33.7 %collective-permute-start.12 = (bf16[2,128,1024]{2,1,0:T(8,128)(2,1)}, bf16[2,128,1024]{2,1,0:T(8,128)(2,1)S(1)}, u32[]{:S(2)}, u32[]{:S(2)}) collective-permute-start(bf16[2,128,1024]{2,1,0:T(8,128)(2,1)} %dynamic-slice_bitcast_fusion.12), channel_id=1, source_target_pairs={{0,1},{1,0},{2,3},{3,2},{4,5},{5,4},{6,7},{7,6},{8,9},{9,8},{10,11... | collective-permute-start | bytes 1572872 | tf_op jit(solution)/shard_map/ppermute | solution.py:60
  154.3 32.2 %collective-permute-start.13 = (bf16[2,128,1024]{2,1,0:T(8,128)(2,1)S(1)}, bf16[2,128,1024]{2,1,0:T(8,128)(2,1)S(1)}, u32[]{:S(2)}, u32[]{:S(2)}) collective-permute-start(bf16[2,128,1024]{2,1,0:T(8,128)(2,1)S(1)} %dynamic-slice_bitcast_fusion.11), channel_id=1, source_target_pairs={{0,2},{1,3},{2,0},{3,1},{4,6},{5,7},{6,4},{7,5},{8,10},{9,11},{10,... | collective-permute-start | bytes 1572872 | tf_op jit(solution)/shard_map/ppermute | solution.py:60
  155.8 30.7 %collective-permute-start.14 = (bf16[64,2048]{1,0:T(8,128)(2,1)S(1)}, bf16[64,2048]{1,0:T(8,128)(2,1)}, u32[]{:S(2)}, u32[]{:S(2)}) collective-permute-start(bf16[64,2048]{1,0:T(8,128)(2,1)S(1)} %dynamic-slice_bitcast_fusion.17.refs_7_.refs_6_), channel_id=1, source_target_pairs={{0,1},{1,0},{2,3},{3,2},{4,5},{5,4},{6,7},{7,6},{8,9},{9,8},{10,11... | collective-permute-start | bytes 786440 | tf_op jit(solution)/shard_map/ppermute | solution.py:60
  156.3 30.1 %collective-permute-start.15 = (bf16[64,2048]{1,0:T(8,128)(2,1)S(1)}, bf16[64,2048]{1,0:T(8,128)(2,1)}, u32[]{:S(2)}, u32[]{:S(2)}) collective-permute-start(bf16[64,2048]{1,0:T(8,128)(2,1)S(1)} %dynamic-slice_bitcast_fusion.17.refs_7_.refs_6_), channel_id=1, source_target_pairs={{0,2},{1,3},{2,0},{3,1},{4,6},{5,7},{6,4},{7,5},{8,10},{9,11},{10,... | collective-permute-start | bytes 786440 | tf_op jit(solution)/shard_map/ppermute | solution.py:60
  156.9 29.6 %collective-permute-start.16 = (bf16[64,2048]{1,0:T(8,128)(2,1)S(1)}, bf16[64,2048]{1,0:T(8,128)(2,1)}, u32[]{:S(2)}, u32[]{:S(2)}) collective-permute-start(bf16[64,2048]{1,0:T(8,128)(2,1)S(1)} %dynamic-slice_bitcast_fusion.17.refs_7_.refs_6_), channel_id=1, source_target_pairs={{0,3},{1,2},{2,1},{3,0},{4,7},{5,6},{6,5},{7,4},{8,11},{9,10},{10,... | collective-permute-start | bytes 786440 | tf_op jit(solution)/shard_map/ppermute | solution.py:60
  189.2 12.4 %collective-permute-start.17 = (bf16[128,1024]{1,0:T(8,128)(2,1)S(1)}, bf16[128,1024]{1,0:T(8,128)(2,1)S(1)}, u32[]{:S(2)}, u32[]{:S(2)}) collective-permute-start(bf16[128,1024]{1,0:T(8,128)(2,1)S(1)} %dynamic-slice_bitcast_fusion.16), channel_id=1, source_target_pairs={{0,2},{1,3},{2,0},{3,1},{4,6},{5,7},{6,4},{7,5},{8,10},{9,11},{10,... | collective-permute-start | bytes 786440 | tf_op jit(solution)/shard_map/ppermute | solution.py:60
  190.7 10.9 %collective-permute-start.18 = (bf16[128,1024]{1,0:T(8,128)(2,1)S(1)}, bf16[128,1024]{1,0:T(8,128)(2,1)S(1)}, u32[]{:S(2)}, u32[]{:S(2)}) collective-permute-start(bf16[128,1024]{1,0:T(8,128)(2,1)S(1)} %dynamic-slice_bitcast_fusion.15), channel_id=1, source_target_pairs={{0,1},{1,0},{2,3},{3,2},{4,5},{5,4},{6,7},{7,6},{8,9},{9,8},{10,11... | collective-permute-start | bytes 786440 | tf_op jit(solution)/shard_map/ppermute | solution.py:60
  202.6 98.5 %all-gather.11.cloned.1.call-start = ((), (), s32[]{:S(2)}) async-start(), calls=%async_computation.2 | async-start | bytes 4718592 | tf_op jit(solution)/shard_map/all_gather | solution.py:842
  205.3 21.0 %collective-permute-start.19 = (bf16[2,128,1024]{2,1,0:T(8,128)(2,1)}, bf16[2,128,1024]{2,1,0:T(8,128)(2,1)S(1)}, u32[]{:S(2)}, u32[]{:S(2)}) collective-permute-start(bf16[2,128,1024]{2,1,0:T(8,128)(2,1)} %dynamic-slice_bitcast_fusion.10), channel_id=1, source_target_pairs={{0,1},{1,0},{2,3},{3,2},{4,5},{5,4},{6,7},{7,6},{8,9},{9,8},{10,11... | collective-permute-start | bytes 1572872 | tf_op jit(solution)/shard_map/ppermute | solution.py:60
  205.8 20.5 %collective-permute-start.20 = (bf16[2,128,1024]{2,1,0:T(8,128)(2,1)S(1)}, bf16[2,128,1024]{2,1,0:T(8,128)(2,1)S(1)}, u32[]{:S(2)}, u32[]{:S(2)}) collective-permute-start(bf16[2,128,1024]{2,1,0:T(8,128)(2,1)S(1)} %dynamic-slice_bitcast_fusion.9), channel_id=1, source_target_pairs={{0,2},{1,3},{2,0},{3,1},{4,6},{5,7},{6,4},{7,5},{8,10},{9,11},{10,... | collective-permute-start | bytes 1572872 | tf_op jit(solution)/shard_map/ppermute | solution.py:60
  226.8 15.1 %collective-permute-start.21 = (bf16[128,1024]{1,0:T(8,128)(2,1)S(1)}, bf16[128,1024]{1,0:T(8,128)(2,1)S(1)}, u32[]{:S(2)}, u32[]{:S(2)}) collective-permute-start(bf16[128,1024]{1,0:T(8,128)(2,1)S(1)} %dynamic-slice_bitcast_fusion.14), channel_id=1, source_target_pairs={{0,2},{1,3},{2,0},{3,1},{4,6},{5,7},{6,4},{7,5},{8,10},{9,11},{10,... | collective-permute-start | bytes 786440 | tf_op jit(solution)/shard_map/ppermute | solution.py:60
  227.6 14.4 %collective-permute-start.22 = (bf16[128,1024]{1,0:T(8,128)(2,1)S(1)}, bf16[128,1024]{1,0:T(8,128)(2,1)S(1)}, u32[]{:S(2)}, u32[]{:S(2)}) collective-permute-start(bf16[128,1024]{1,0:T(8,128)(2,1)S(1)} %dynamic-slice_bitcast_fusion.13), channel_id=1, source_target_pairs={{0,1},{1,0},{2,3},{3,2},{4,5},{5,4},{6,7},{7,6},{8,9},{9,8},{10,11... | collective-permute-start | bytes 786440 | tf_op jit(solution)/shard_map/ppermute | solution.py:60
  247.3 24.0 %collective-permute-start.23 = (bf16[2,256,1024]{2,1,0:T(8,128)(2,1)}, bf16[2,256,1024]{2,1,0:T(8,128)(2,1)}, u32[]{:S(2)}, u32[]{:S(2)}) collective-permute-start(bf16[2,256,1024]{2,1,0:T(8,128)(2,1)} %dynamic-slice_bitcast_fusion.3), channel_id=1, source_target_pairs={{0,1},{1,0},{2,3},{3,2},{4,5},{5,4},{6,7},{7,6},{8,9},{9,8},{10,11... | collective-permute-start | bytes 3145736 | tf_op jit(solution)/shard_map/ppermute | solution.py:60
  248.8 22.8 %collective-permute-start.24 = (bf16[2,256,1024]{2,1,0:T(8,128)(2,1)S(1)}, bf16[2,256,1024]{2,1,0:T(8,128)(2,1)}, u32[]{:S(2)}, u32[]{:S(2)}) collective-permute-start(bf16[2,256,1024]{2,1,0:T(8,128)(2,1)S(1)} %dynamic-slice_bitcast_fusion.2), channel_id=1, source_target_pairs={{0,2},{1,3},{2,0},{3,1},{4,6},{5,7},{6,4},{7,5},{8,10},{9,11},{10,... | collective-permute-start | bytes 3145736 | tf_op jit(solution)/shard_map/ppermute | solution.py:60
  277.9 24.1 %collective-permute-start.27 = (bf16[4,256,2048]{2,1,0:T(8,128)(2,1)}, bf16[4,256,2048]{2,1,0:T(8,128)(2,1)}, u32[]{:S(2)}, u32[]{:S(2)}) collective-permute-start(bf16[4,256,2048]{2,1,0:T(8,128)(2,1)} %get-tuple-element.323), channel_id=1, source_target_pairs={{0,4},{4,0},{8,12},{12,8},{16,20},{20,16},{24,28},{28,24},{1,5},{5... | collective-permute-start | bytes 12582920 | tf_op jit(solution)/shard_map/ppermute | solution.py:60
  277.9 23.2 %collective-permute-start.25 = (bf16[256,1024]{1,0:T(8,128)(2,1)}, bf16[256,1024]{1,0:T(8,128)(2,1)S(1)}, u32[]{:S(2)}, u32[]{:S(2)}) collective-permute-start(bf16[256,1024]{1,0:T(8,128)(2,1)} %dynamic-slice_bitcast_fusion.8), channel_id=1, source_target_pairs={{0,2},{1,3},{2,0},{3,1},{4,6},{5,7},{6,4},{7,5},{8,10},{9,11},{10,... | collective-permute-start | bytes 1572872 | tf_op jit(solution)/shard_map/ppermute | solution.py:60
  279.4 21.8 %collective-permute-start.26 = (bf16[256,1024]{1,0:T(8,128)(2,1)}, bf16[256,1024]{1,0:T(8,128)(2,1)S(1)}, u32[]{:S(2)}, u32[]{:S(2)}) collective-permute-start(bf16[256,1024]{1,0:T(8,128)(2,1)} %dynamic-slice_bitcast_fusion.7), channel_id=1, source_target_pairs={{0,1},{1,0},{2,3},{3,2},{4,5},{5,4},{6,7},{7,6},{8,9},{9,8},{10,11... | collective-permute-start | bytes 1572872 | tf_op jit(solution)/shard_map/ppermute | solution.py:60
  303.5 29.4 %collective-permute-start.28 = (bf16[256,2048]{1,0:T(8,128)(2,1)S(1)}, bf16[256,2048]{1,0:T(8,128)(2,1)S(1)}, u32[]{:S(2)}, u32[]{:S(2)}) collective-permute-start(bf16[256,2048]{1,0:T(8,128)(2,1)S(1)} %pad_maximum_fusion.2), channel_id=1, source_target_pairs={{0,8},{4,12},{8,16},{12,20},{16,24},{20,28},{1,9},{5,13},{9,17},{1... | collective-permute-start | bytes 3145736 | tf_op jit(solution)/shard_map/ppermute | solution.py:60
  305.2 27.7 %collective-permute-start.29 = (bf16[256,2048]{1,0:T(8,128)(2,1)S(1)}, bf16[256,2048]{1,0:T(8,128)(2,1)S(1)}, u32[]{:S(2)}, u32[]{:S(2)}) collective-permute-start(bf16[256,2048]{1,0:T(8,128)(2,1)S(1)} %pad_maximum_fusion.2), channel_id=1, source_target_pairs={{8,0},{12,4},{16,8},{20,12},{24,16},{28,20},{9,1},{13,5},{17,9},{2... | collective-permute-start | bytes 3145736 | tf_op jit(solution)/shard_map/ppermute | solution.py:60
  336.7 27.1 %collective-permute-start.30 = (bf16[256,2048]{1,0:T(8,128)(2,1)}, bf16[256,2048]{1,0:T(8,128)(2,1)S(1)}, u32[]{:S(2)}, u32[]{:S(2)}) collective-permute-start(bf16[256,2048]{1,0:T(8,128)(2,1)} %get-tuple-element.338), channel_id=1, source_target_pairs={{0,8},{4,12},{8,16},{12,20},{16,24},{20,28},{1,9},{5,13},{9,17},{1... | collective-permute-start | bytes 3145736 | tf_op jit(solution)/shard_map/ppermute | solution.py:60
  341.6 26.3 %collective-permute-start.31 = (bf16[256,2048]{1,0:T(8,128)(2,1)}, bf16[256,2048]{1,0:T(8,128)(2,1)S(1)}, u32[]{:S(2)}, u32[]{:S(2)}) collective-permute-start(bf16[256,2048]{1,0:T(8,128)(2,1)} %get-tuple-element.339), channel_id=1, source_target_pairs={{8,0},{12,4},{16,8},{20,12},{24,16},{28,20},{9,1},{13,5},{17,9},{2... | collective-permute-start | bytes 3145736 | tf_op jit(solution)/shard_map/ppermute | solution.py:60
  377.5 40.7 %collective-permute-start.32 = (bf16[2,256,1024]{2,1,0:T(8,128)(2,1)}, bf16[2,256,1024]{2,1,0:T(8,128)(2,1)}, u32[]{:S(2)}, u32[]{:S(2)}) collective-permute-start(bf16[2,256,1024]{2,1,0:T(8,128)(2,1)} %dynamic-slice_bitcast_fusion.1), channel_id=1, source_target_pairs={{0,1},{1,0},{2,3},{3,2},{4,5},{5,4},{6,7},{7,6},{8,9},{9,8},{10,11... | collective-permute-start | bytes 3145736 | tf_op jit(solution)/shard_map/ppermute | solution.py:60
  385.3 33.0 %collective-permute-start.33 = (bf16[2,256,1024]{2,1,0:T(8,128)(2,1)}, bf16[2,256,1024]{2,1,0:T(8,128)(2,1)}, u32[]{:S(2)}, u32[]{:S(2)}) collective-permute-start(bf16[2,256,1024]{2,1,0:T(8,128)(2,1)} %dynamic-slice_bitcast_fusion), channel_id=1, source_target_pairs={{0,2},{1,3},{2,0},{3,1},{4,6},{5,7},{6,4},{7,5},{8,10},{9,11},{10,... | collective-permute-start | bytes 3145736 | tf_op jit(solution)/shard_map/ppermute | solution.py:60
  385.3 33.0 %collective-permute-start.34 = (bf16[256,2048]{1,0:T(8,128)(2,1)}, bf16[256,2048]{1,0:T(8,128)(2,1)S(1)}, u32[]{:S(2)}, u32[]{:S(2)}) collective-permute-start(bf16[256,2048]{1,0:T(8,128)(2,1)} %get-tuple-element.352), channel_id=1, source_target_pairs={{0,8},{4,12},{8,16},{12,20},{16,24},{20,28},{1,9},{5,13},{9,17},{1... | collective-permute-start | bytes 3145736 | tf_op jit(solution)/shard_map/ppermute | solution.py:60
  388.8 29.5 %collective-permute-start.35 = (bf16[256,2048]{1,0:T(8,128)(2,1)}, bf16[256,2048]{1,0:T(8,128)(2,1)}, u32[]{:S(2)}, u32[]{:S(2)}) collective-permute-start(bf16[256,2048]{1,0:T(8,128)(2,1)} %get-tuple-element.353), channel_id=1, source_target_pairs={{8,0},{12,4},{16,8},{20,12},{24,16},{28,20},{9,1},{13,5},{17,9},{2... | collective-permute-start | bytes 3145736 | tf_op jit(solution)/shard_map/ppermute | solution.py:60
  429.1 20.5 %collective-permute-start.38 = (bf16[4,256,2048]{2,1,0:T(8,128)(2,1)}, bf16[4,256,2048]{2,1,0:T(8,128)(2,1)}, u32[]{:S(2)}, u32[]{:S(2)}) collective-permute-start(bf16[4,256,2048]{2,1,0:T(8,128)(2,1)} %get-tuple-element.364), channel_id=1, source_target_pairs={{0,4},{4,0},{8,12},{12,8},{16,20},{20,16},{24,28},{28,24},{1,5},{5... | collective-permute-start | bytes 12582920 | tf_op jit(solution)/shard_map/ppermute | solution.py:60
  429.6 19.1 %collective-permute-start.36 = (bf16[256,1024]{1,0:T(8,128)(2,1)}, bf16[256,1024]{1,0:T(8,128)(2,1)S(1)}, u32[]{:S(2)}, u32[]{:S(2)}) collective-permute-start(bf16[256,1024]{1,0:T(8,128)(2,1)} %dynamic-slice_bitcast_fusion.6), channel_id=1, source_target_pairs={{0,2},{1,3},{2,0},{3,1},{4,6},{5,7},{6,4},{7,5},{8,10},{9,11},{10,... | collective-permute-start | bytes 1572872 | tf_op jit(solution)/shard_map/ppermute | solution.py:60
  431.7 17.1 %collective-permute-start.37 = (bf16[256,1024]{1,0:T(8,128)(2,1)}, bf16[256,1024]{1,0:T(8,128)(2,1)}, u32[]{:S(2)}, u32[]{:S(2)}) collective-permute-start(bf16[256,1024]{1,0:T(8,128)(2,1)} %dynamic-slice_bitcast_fusion.5), channel_id=1, source_target_pairs={{0,1},{1,0},{2,3},{3,2},{4,5},{5,4},{6,7},{7,6},{8,9},{9,8},{10,11... | collective-permute-start | bytes 1572872 | tf_op jit(solution)/shard_map/ppermute | solution.py:60
  431.7 34.3 %collective-permute-start.42 = (bf16[256,2048]{1,0:T(8,128)(2,1)}, bf16[256,2048]{1,0:T(8,128)(2,1)}, u32[]{:S(2)}, u32[]{:S(2)}) collective-permute-start(bf16[256,2048]{1,0:T(8,128)(2,1)} %get-tuple-element.384), channel_id=1, source_target_pairs={{0,8},{4,12},{8,16},{12,20},{16,24},{20,28},{1,9},{5,13},{9,17},{1... | collective-permute-start | bytes 3145736 | tf_op jit(solution)/shard_map/ppermute | solution.py:60
  437.2 28.8 %collective-permute-start.43 = (bf16[256,2048]{1,0:T(8,128)(2,1)}, bf16[256,2048]{1,0:T(8,128)(2,1)}, u32[]{:S(2)}, u32[]{:S(2)}) collective-permute-start(bf16[256,2048]{1,0:T(8,128)(2,1)} %get-tuple-element.385), channel_id=1, source_target_pairs={{8,0},{12,4},{16,8},{20,12},{24,16},{28,20},{9,1},{13,5},{17,9},{2... | collective-permute-start | bytes 3145736 | tf_op jit(solution)/shard_map/ppermute | solution.py:60
  452.5 29.2 %collective-permute-start.39 = (bf16[256,2048]{1,0:T(8,128)(2,1)S(1)}, bf16[256,2048]{1,0:T(8,128)(2,1)S(1)}, u32[]{:S(2)}, u32[]{:S(2)}) collective-permute-start(bf16[256,2048]{1,0:T(8,128)(2,1)S(1)} %pad_maximum_fusion.3), channel_id=1, source_target_pairs={{0,8},{4,12},{8,16},{12,20},{16,24},{20,28},{1,9},{5,13},{9,17},{1... | collective-permute-start | bytes 3145736 | tf_op jit(solution)/shard_map/ppermute | solution.py:60
  457.1 29.7 %collective-permute-start.40 = (bf16[256,2048]{1,0:T(8,128)(2,1)S(1)}, bf16[256,2048]{1,0:T(8,128)(2,1)S(1)}, u32[]{:S(2)}, u32[]{:S(2)}) collective-permute-start(bf16[256,2048]{1,0:T(8,128)(2,1)S(1)} %pad_maximum_fusion.3), channel_id=1, source_target_pairs={{8,0},{12,4},{16,8},{20,12},{24,16},{28,20},{9,1},{13,5},{17,9},{2... | collective-permute-start | bytes 3145736 | tf_op jit(solution)/shard_map/ppermute | solution.py:60
  458.4 7.7 %collective-permute-start.41 = (f32[20480]{0:T(1024)S(1)}, f32[20480]{0:T(1024)S(1)}, u32[]{:S(2)}, u32[]{:S(2)}) collective-permute-start(f32[20480]{0:T(1024)S(1)} %constant_dynamic-update-slice_fusion.2), channel_id=1, source_target_pairs={{0,4},{4,0},{8,12},{12,8},{16,20},{20,16},{24,28},{28,24},{1,5},{5... | collective-permute-start | bytes 245768 | tf_op jit(solution)/shard_map/ppermute | solution.py:60
  465.4 85.9 %copy-start.5 = (bf16[4,256,2048]{2,1,0:T(8,128)(2,1)}, bf16[4,256,2048]{2,1,0:T(8,128)(2,1)S(1)}, u32[]{:S(2)}) copy-start(bf16[4,256,2048]{2,1,0:T(8,128)(2,1)S(1)} %add_convert_fusion) | copy-start | bytes 12582916
  487.6 30.7 %collective-permute-start.47 = (bf16[4,256,2048]{2,1,0:T(8,128)(2,1)S(1)}, bf16[4,256,2048]{2,1,0:T(8,128)(2,1)S(1)}, u32[]{:S(2)}, u32[]{:S(2)}) collective-permute-start(bf16[4,256,2048]{2,1,0:T(8,128)(2,1)S(1)} %pad_maximum_fusion.mine), channel_id=1, source_target_pairs={{0,4},{4,0},{8,12},{12,8},{16,20},{20,16},{24,28},{28,24},{1,5},{5... | collective-permute-start | bytes 12582920 | tf_op jit(solution)/shard_map/ppermute | solution.py:60
  487.7 30.6 %collective-permute-start.44 = (bf16[256,2048]{1,0:T(8,128)(2,1)S(1)}, bf16[256,2048]{1,0:T(8,128)(2,1)S(1)}, u32[]{:S(2)}, u32[]{:S(2)}) collective-permute-start(bf16[256,2048]{1,0:T(8,128)(2,1)S(1)} %get-tuple-element.392), channel_id=1, source_target_pairs={{0,8},{4,12},{8,16},{12,20},{16,24},{20,28},{1,9},{5,13},{9,17},{1... | collective-permute-start | bytes 3145736 | tf_op jit(solution)/shard_map/ppermute | solution.py:60
  489.2 29.0 %collective-permute-start.45 = (bf16[256,2048]{1,0:T(8,128)(2,1)S(1)}, bf16[256,2048]{1,0:T(8,128)(2,1)S(1)}, u32[]{:S(2)}, u32[]{:S(2)}) collective-permute-start(bf16[256,2048]{1,0:T(8,128)(2,1)S(1)} %get-tuple-element.393), channel_id=1, source_target_pairs={{8,0},{12,4},{16,8},{20,12},{24,16},{28,20},{9,1},{13,5},{17,9},{2... | collective-permute-start | bytes 3145736 | tf_op jit(solution)/shard_map/ppermute | solution.py:60
  490.7 27.6 %collective-permute-start.46 = (f32[20480]{0:T(1024)S(1)}, f32[20480]{0:T(1024)S(1)}, u32[]{:S(2)}, u32[]{:S(2)}) collective-permute-start(f32[20480]{0:T(1024)S(1)} %add.407), channel_id=1, source_target_pairs={{0,8},{4,12},{8,0},{12,4},{16,24},{20,28},{24,16},{28,20},{1,9},{5... | collective-permute-start | bytes 245768 | tf_op jit(solution)/shard_map/ppermute | solution.py:60
  519.2 32.2 %collective-permute-start.48 = (bf16[256,2048]{1,0:T(8,128)(2,1)S(1)}, bf16[256,2048]{1,0:T(8,128)(2,1)S(1)}, u32[]{:S(2)}, u32[]{:S(2)}) collective-permute-start(bf16[256,2048]{1,0:T(8,128)(2,1)S(1)} %get-tuple-element.402), channel_id=1, source_target_pairs={{0,8},{4,12},{8,16},{12,20},{16,24},{20,28},{1,9},{5,13},{9,17},{1... | collective-permute-start | bytes 3145736 | tf_op jit(solution)/shard_map/ppermute | solution.py:60
  520.7 30.7 %collective-permute-start.49 = (bf16[256,2048]{1,0:T(8,128)(2,1)S(1)}, bf16[256,2048]{1,0:T(8,128)(2,1)S(1)}, u32[]{:S(2)}, u32[]{:S(2)}) collective-permute-start(bf16[256,2048]{1,0:T(8,128)(2,1)S(1)} %get-tuple-element.403), channel_id=1, source_target_pairs={{8,0},{12,4},{16,8},{20,12},{24,16},{28,20},{9,1},{13,5},{17,9},{2... | collective-permute-start | bytes 3145736 | tf_op jit(solution)/shard_map/ppermute | solution.py:60
  522.0 29.4 %collective-permute-start.50 = (f32[20480]{0:T(1024)S(1)}, f32[20480]{0:T(1024)S(1)}, u32[]{:S(2)}, u32[]{:S(2)}) collective-permute-start(f32[20480]{0:T(1024)S(1)} %add.410), channel_id=1, source_target_pairs={{0,16},{4,20},{8,24},{12,28},{16,0},{20,4},{24,8},{28,12},{1,17},{... | collective-permute-start | bytes 245768 | tf_op jit(solution)/shard_map/ppermute | solution.py:60
  559.3 8.3 %collective-permute-start.51 = (bf16[4,256,2048]{2,1,0:T(8,128)(2,1)}, bf16[4,256,2048]{2,1,0:T(8,128)(2,1)}, u32[]{:S(2)}, u32[]{:S(2)}) collective-permute-start(bf16[4,256,2048]{2,1,0:T(8,128)(2,1)} %pad_maximum_fusion.1.mine), channel_id=1, source_target_pairs={{0,4},{4,0},{8,12},{12,8},{16,20},{20,16},{24,28},{28,24},{1,5},{5... | collective-permute-start | bytes 12582920 | tf_op jit(solution)/shard_map/ppermute | solution.py:60
  559.4 24.9 %collective-permute-start.54 = (bf16[256,2048]{1,0:T(8,128)(2,1)}, bf16[256,2048]{1,0:T(8,128)(2,1)S(1)}, u32[]{:S(2)}, u32[]{:S(2)}) collective-permute-start(bf16[256,2048]{1,0:T(8,128)(2,1)} %get-tuple-element.417), channel_id=1, source_target_pairs={{0,8},{4,12},{8,16},{12,20},{16,24},{20,28},{1,9},{5,13},{9,17},{1... | collective-permute-start | bytes 3145736 | tf_op jit(solution)/shard_map/ppermute | solution.py:60
  561.0 27.5 %collective-permute-start.55 = (bf16[256,2048]{1,0:T(8,128)(2,1)}, bf16[256,2048]{1,0:T(8,128)(2,1)}, u32[]{:S(2)}, u32[]{:S(2)}) collective-permute-start(bf16[256,2048]{1,0:T(8,128)(2,1)} %get-tuple-element.418), channel_id=1, source_target_pairs={{8,0},{12,4},{16,8},{20,12},{24,16},{28,20},{9,1},{13,5},{17,9},{2... | collective-permute-start | bytes 3145736 | tf_op jit(solution)/shard_map/ppermute | solution.py:60
  563.0 4.6 collective-permute-start.52
  567.6 20.9 %collective-permute-start.53 = (f32[20480]{0:T(1024)S(1)}, f32[20480]{0:T(1024)S(1)}, u32[]{:S(2)}, u32[]{:S(2)}) collective-permute-start(f32[20480]{0:T(1024)S(1)} %add.414), channel_id=1, source_target_pairs={{0,2},{1,3},{2,0},{3,1},{4,6},{5,7},{6,4},{7,5},{8,10},{9,11},{10,... | collective-permute-start | bytes 245768 | tf_op jit(solution)/shard_map/ppermute | solution.py:60
  (67 other events, 574.9 us)
Sparse Core Ops, SparseCore 0:
  9.6 84.7 all-gather.14
  96.0 45.6 all-gather.6
  143.3 45.8 all-gather.8
  202.7 45.1 all-gather.12
  249.4 45.8 all-gather.10

commit v6 on v5

--- a/solution.py
+++ b/solution.py
@@ -10,7 +10,7 @@
 HEAD_DIM = 64
 ROT = 32
 BLK = 16
-TILE = 256
+TILE = 512
 WIDE = 512
 ROWS = 512
 LANES = 128
@@ -1031,7 +1031,7 @@
         )
 
     mine, other, gain_sum, shift_sum, mixed_sum = beside(
-        norm_back, (after(grad_mixed, joint_terms),), [joint_flow, weave]
+        norm_back, (after(grad_mixed, joint_terms),), [weave, joint_flow]
     )
 
     def spread(value, count):
@@ -1081,10 +1081,11 @@
     while weave.moves:
         beside(nothing, (), [flow for flow in (weave, total_flow) if flow.moves])
     joint_blocks, norm_finish = weave.result
-    joint_swap = Flow(swap_steps(in_order(*joint_blocks)))
-    beside(
-        nothing, (), [flow for flow in (joint_swap, total_flow) if flow.moves], late=[norm_finish]
-    )
+    joint_blocks = beside(
+        in_order, joint_blocks, [flow for flow in (total_flow,) if flow.moves], late=[norm_finish]
+    )
+    joint_swap = Flow(swap_steps(joint_blocks))
+    beside(nothing, (), [flow for flow in (joint_swap, total_flow) if flow.moves])
     qkv_dealt, out_dealt = beside(
         lambda *halves: deal_columns(*halves, HEAD_DIM, qkv_order, at, with_out=True),
         joint_swap.result,

time: 611 us -> 601 us (0.984)
  starting transfers between devices: 87.5 us -> 81 us
    ppermute x56, starting transfers between devices: 87.2 us -> 80.6 us  [beside(): lax.ppermute(value, axis, pairs)]
    unnamed x157 -> x155, local copies, waits for them, and re-layouts: 20 us -> 19.2 us
  transfers between devices with their start and end apart: 61 -> 61, of which waited for: 21 -> 23; matrix products, arithmetic and copies ran while one was open for 16% -> 17% of each run, Pallas kernels for 34% -> 34%
where the time goes in v6:
time: 601 us; the launch traced here: 598 us
  Pallas kernels  204 us (34%)
  waiting for transfers between devices  149 us (25%)
  starting transfers between devices  81 us (13%)
  other arithmetic  59.6 us (10%)
  matrix products  45 us (7%)
  local copies, waits for them, and re-layouts  44.1 us (7%)
  between operations  15.8 us (3%)
    ppermute x56, waiting for transfers between devices, beside(): lax.ppermute(value, axis, pairs)  143 us
    pallas_call x4, Pallas kernels, row_call(): pl.pallas_call(body, out_shape=out_shape + [jax.ShapeDtypeStruct(shape, F...  98.7 us
    ppermute x56, starting transfers between devices, beside(): lax.ppermute(value, axis, pairs)  80.6 us
    dot_general x6, matrix products, dot_tn(): lax.dot_general(left, right, (((0,), (0,)), ((), ())), preferred_element_...  45 us
    pallas_call x2, Pallas kernels, attention_backward(): pl.pallas_call(functools.partial(backward_kernel, pair), out_shape=jax.Sh...  42.8 us
    pallas_call x1, Pallas kernels, attention_forward(): pl.pallas_call(forward_kernel, out_shape=(jax.ShapeDtypeStruct((tokens, w...  27.6 us
    pallas_call x2, Pallas kernels, deal_columns(): pl.pallas_call(functools.partial(deal_kernel, unit, order), out_shape=out...  19.4 us
    unnamed x155, local copies, waits for them, and re-layouts  19.2 us
  transfers between devices with their start and end apart: 61, of which 23 were waited for; matrix products, arithmetic and copies ran while one was open for 17% of the time, Pallas kernels for 34%

profile of v6, /device:TPU:0, one launch (start us, length us, event | category | flops | bytes accessed | tf_op | source)
XLA Modules:
  0.0 598.4 jit_solution(13840858825463519220)
XLA Ops:
  8.0 3.4 copy-done.2
  11.4 2.8 copy-done.4
  19.0 2.7 fusion.66
  21.7 2.9 collective-permute-start
  26.7 2.9 collective-permute-start.4
  32.1 13.6 %collective-permute-done.2 = bf16[8,704]{1,0:T(8,128)(2,1)S(1)} collective-permute-done((bf16[8,704]{1,0:T(8,128)(2,1)S(1)}, bf16[8,704]{1,0:T(8,128)(2,1)S(1)}, u32[]{:S(2)}, u32[]{:S(2)}) %collective-permute-start.2) | collective-permute-done | bytes 11296 | tf_op jit(solution)/shard_map/ppermute | solution.py:60
  55.1 8.9 %fusion.41 = (f32[2048,128]{1,0:T(8,128)}, f32[2048,128]{1,0:T(8,128)}, f32[2048,128]{1,0:T(8,128)}, f32[2048,128]{1,0:T(8,128)}) fusion(f32[2048]{0:T(1024)S(1)} %get-tuple-element.498, f32[128]{0:T(128)S(1)} %get-tuple-element.496, f32[128]{0:T(128)S(1)} %get-tuple-element.497, f32[2048]{0:T(1024)S(1)} %get-tuple-element.499), kind=kLoop, calls=%fused_computation.77 | loop fusion | flops 1048576 | bytes 4211712 | tf_op jit(solution)/shard_map/mul | solution.py:397
  64.0 7.6 %collective-permute-done.5.refs_8_.refs_5_ = bf16[256,1792]{1,0:T(8,128)(2,1)} collective-permute-done((bf16[256,1792]{1,0:T(8,128)(2,1)}, bf16[256,1792]{1,0:T(8,128)(2,1)}, u32[]{:S(2)}, u32[]{:S(2)}) %collective-permute-start.5) | collective-permute-done | bytes 917536 | tf_op jit(solution)/shard_map/ppermute | solution.py:60
  71.6 17.6 %collective-permute-done.6.refs_9_.refs_6_ = bf16[256,1792]{1,0:T(8,128)(2,1)} collective-permute-done((bf16[256,1792]{1,0:T(8,128)(2,1)}, bf16[256,1792]{1,0:T(8,128)(2,1)}, u32[]{:S(2)}, u32[]{:S(2)}) %collective-permute-start.6) | collective-permute-done | bytes 917536 | tf_op jit(solution)/shard_map/ppermute | solution.py:60
  90.5 3.9 all-gather.15.cloned.1.call-done
  97.9 34.2 %shard_map.230 = (bf16[2048,2048]{1,0:T(8,128)(2,1)}, bf16[2048,1024]{1,0:T(8,128)(2,1)}, bf16[2048,1024]{1,0:T(8,128)(2,1)}, bf16[2048,768]{1,0:T(8,128)(2,1)}) custom-call(s32[2]{0:T(128)} %pad_add_fusion.at, bf16[2048,2048]{1,0:T(8,128)(2,1)} %bitcast.302, f32[2048,128]{1,0:T(8,128)} %get-tuple-element.246.refs_1_, ...), custom_call_target="tpu_custom_call" | custom-call | flops 15032385536 | bytes 37772288 | tf_op jit(solution)/shard_map/pallas_call | solution.py:518
  132.2 10.0 %collective-permute-done.10.refs_5_.refs_4_ = bf16[256,2048]{1,0:T(8,128)(2,1)S(1)} collective-permute-done((bf16[256,2048]{1,0:T(8,128)(2,1)S(1)}, bf16[256,2048]{1,0:T(8,128)(2,1)S(1)}, u32[]{:S(2)}, u32[]{:S(2)}) %collective-permute-start.10) | collective-permute-done | bytes 1048608 | tf_op jit(solution)/shard_map/ppermute | solution.py:60
  143.5 8.0 %convolution_convert_fusion.3 = bf16[1024,1024]{1,0:T(8,128)(2,1)S(1)} fusion(bf16[2048,1024]{1,0:T(8,128)(2,1)} %get-tuple-element.262.refs_1_, bf16[2048,1024]{1,0:T(8,128)(2,1)} %all-gather.7.cloned.1.call-done.refs_0_), kind=kOutput, calls=%fused_computation.61 | convolution fusion | flops 4296015872 | bytes 10485760 | tf_op jit(solution)/shard_map/dot_general | solution.py:30
  156.8 2.4 collective-permute-start.16
  159.3 27.6 %shard_map.231 = (bf16[2048,256]{1,0:T(8,128)(2,1)}, bf16[2048,768]{1,0:T(8,128)(2,1)}, f32[256,2048]{1,0:T(8,128)}, f32[4,2048]{1,0:T(4,128)}) custom-call(s32[128]{0:T(128)} %place_ref.5, s32[4]{0:T(128)} %bitcast.299, bf16[2048,768]{1,0:T(8,128)(2,1)} %get-tuple-element.266.lin_hbm), custom_call_target="tpu_custom_call" | custom-call | flops 40000000000 | bytes 16000000 | tf_op jit(solution)/shard_map/pallas_call | solution.py:408
  187.4 1.9 all-gather.9.cloned.1.call-done.refs_1_
  192.2 9.4 %convolution_convert_fusion.2 = bf16[1024,1024]{1,0:T(8,128)(2,1)} fusion(bf16[2048,1024]{1,0:T(8,128)(2,1)} %get-tuple-element.262.refs_1_, bf16[2048,1024]{1,0:T(8,128)(2,1)} %all-gather.9.cloned.1.call-done.refs_1_), kind=kOutput, calls=%fused_computation.60 | convolution fusion | flops 4296015872 | bytes 10485760 | tf_op jit(solution)/shard_map/dot_general | solution.py:30
  206.4 18.9 %shard_map.232 = (bf16[2048,1024]{1,0:T(8,128)(2,1)}, bf16[2048,256]{1,0:T(8,128)(2,1)}, f32[1,1024]{1,0:T(1,128)}) custom-call(s32[2]{0:T(128)} %pad_add_fusion.at, bf16[2048,1024]{1,0:T(8,128)(2,1)} %all-gather.7.cloned.1.call-done.refs_0_, bf16[2048,1024]{1,0:T(8,128)(2,1)} %all-gather.9.cloned.1.call-done.refs_1_, ...), custom_call_target="tpu_custom_call" | custom-call | flops 10737418240 | bytes 23068672 | tf_op jit(solution)/shard_map/pallas_call | solution.py:518
  228.9 12.9 %convolution_convert_fusion = bf16[2048,1024]{1,0:T(8,128)(2,1)} fusion(bf16[2048,2048]{1,0:T(8,128)(2,1)} %get-tuple-element.302, bf16[2048,1024]{1,0:T(8,128)(2,1)S(1)} %copy-done.67), kind=kOutput, calls=%fused_computation.4 | convolution fusion | flops 8592031744 | bytes 16777216 | tf_op jit(solution)/shard_map/dot_general | solution.py:30
  242.9 2.7 fusion.63
  248.8 17.6 %shard_map.233 = (bf16[4,256,2048]{2,1,0:T(8,128)(2,1)}, bf16[4,256,2048]{2,1,0:T(8,128)(2,1)}) custom-call(s32[2]{0:T(128)} %pad_add_fusion.at, bf16[2048,256]{1,0:T(8,128)(2,1)} %get-tuple-element.345.refs_0_, bf16[2048,1024]{1,0:T(8,128)(2,1)} %get-tuple-element.262.refs_1_, bf16[256,2048]{1,0:T(8,128)(2,1)} %copy-done.35, ...), custom_call_target="tpu_custom_call" | custom-call | flops 10737418240 | bytes 18874368 | tf_op jit(solution)/shard_map/pallas_call | solution.py:518
  266.4 4.9 collective-permute-done.23
  271.4 2.0 fusion.30
  279.8 21.5 %shard_map.234.refs_0_ = bf16[2048,768]{1,0:T(8,128)(2,1)} custom-call(s32[128]{0:T(128)} %place_ref.5, s32[4]{0:T(128)} %bitcast.300, f32[2048,128]{1,0:T(8,128)} %get-tuple-element.320.cos_ref, f32[2048,128]{1,0:T(8,128)} %get-tuple-element.321.sin_ref, bf16[2048,768]{1,0:T(8,128)(2,1)} %get-tuple-element.322.rows, ...), custom_call_target="tpu_custom_call" | custom-call | flops 20000000000 | bytes 8000000 | tf_op jit(solution)/shard_map/pallas_call | solution.py:432
  303.7 2.2 collective-permute-start.28
  307.2 21.3 %shard_map.235.refs_1_ = bf16[2048,768]{1,0:T(8,128)(2,1)} custom-call(s32[128]{0:T(128)} %place_ref.5, s32[4]{0:T(128)} %bitcast.301, f32[2048,128]{1,0:T(8,128)} %get-tuple-element.320.cos_ref, f32[2048,128]{1,0:T(8,128)} %get-tuple-element.321.sin_ref, bf16[2048,768]{1,0:T(8,128)(2,1)} %get-tuple-element.322.rows, ...), custom_call_target="tpu_custom_call", output_to_operand_aliasing={{}: (8, {})} | custom-call | flops 20000000000 | bytes 8000000 | tf_op jit(solution)/shard_map/pallas_call | solution.py:432
  328.5 5.4 add_convert_fusion.1
  334.0 2.2 fusion.33
  337.8 4.9 collective-permute-start.30
  343.9 10.5 %convolution_convert_fusion.1.left = bf16[2048,768]{1,0:T(8,128)(2,1)} fusion(bf16[2048,2048]{1,0:T(8,128)(2,1)} %get-tuple-element.302, bf16[2048,768]{1,0:T(8,128)(2,1)S(1)} %copy-done.68), kind=kOutput, calls=%fused_computation.5 | convolution fusion | flops 6444023808 | bytes 14680064 | tf_op jit(solution)/shard_map/dot_general | solution.py:30
  354.5 2.1 convolution_convert_fusion.4.refs_1_
  356.7 2.1 convolution_convert_fusion.5.refs_0_
  358.7 4.7 shard_map.236
  364.9 4.1 collective-permute-done.31
  370.0 2.8 fusion.62
  376.5 2.2 fusion.35
  378.7 3.4 collective-permute-start.32
  383.5 27.9 %shard_map.237 = (bf16[4,256,2048]{2,1,0:T(8,128)(2,1)}, bf16[4,256,2048]{2,1,0:T(8,128)(2,1)}, f32[1,2048]{1,0:T(1,128)}, f32[1,2048]{1,0:T(1,128)}, f32[1,768]{1,0:T(1,128)}) custom-call(s32[2]{0:T(128)} %pad_add_fusion.at, bf16[2048,2048]{1,0:T(8,128)(2,1)} %bitcast.303, bf16[2048,768]{1,0:T(8,128)(2,1)} %shard_map.235.refs_1_, ...), custom_call_target="tpu_custom_call" | custom-call | flops 15032385536 | bytes 31457280 | tf_op jit(solution)/shard_map/pallas_call | solution.py:518
  412.5 1.9 fusion.23
  415.3 1.8 fusion.24
  418.9 3.5 fusion.21
  422.9 2.1 collective-permute-start.36
  425.0 1.9 collective-permute-start.37
  426.9 5.6 collective-permute-start.42
  433.8 9.4 %shard_map.238 = f32[2048,2048]{1,0:T(8,128)} custom-call(bf16[2048,1024]{1,0:T(8,128)(2,1)} %all-gather.13.cloned.1.call-done.refs_0_, bf16[2048,1024]{1,0:T(8,128)(2,1)} %all-gather.11.cloned.1.call-done.refs_1_), custom_call_target="tpu_custom_call" | custom-call | bytes 25165824 | tf_op jit(solution)/shard_map/pallas_call | solution.py:787
  443.8 4.9 collective-permute-start.39
  450.1 2.3 select_bitcast_fusion.7
  452.9 4.1 add_convert_fusion
  457.6 3.1 collective-permute-done.43
  460.7 15.9 %collective-permute-done.39 = bf16[256,2048]{1,0:T(8,128)(2,1)S(1)} collective-permute-done((bf16[256,2048]{1,0:T(8,128)(2,1)S(1)}, bf16[256,2048]{1,0:T(8,128)(2,1)S(1)}, u32[]{:S(2)}, u32[]{:S(2)}) %collective-permute-start.39) | collective-permute-done | bytes 1048608 | tf_op jit(solution)/shard_map/ppermute | solution.py:60
  476.7 5.1 collective-permute-done.40
  485.9 2.7 collective-permute-start.46
  488.6 24.7 %collective-permute-done.46 = f32[20480]{0:T(1024)S(1)} collective-permute-done((f32[20480]{0:T(1024)S(1)}, f32[20480]{0:T(1024)S(1)}, u32[]{:S(2)}, u32[]{:S(2)}) %collective-permute-start.46) | collective-permute-done | bytes 81952 | tf_op jit(solution)/shard_map/ppermute | solution.py:60
  516.9 3.7 collective-permute-start.50
  520.7 7.4 %shard_map.239 = f32[512,8192]{1,0:T(8,128)} custom-call(s32[2]{0:T(128)S(1)} %pad_add_fusion.1.at_ref, bf16[4,256,2048]{2,1,0:T(8,128)(2,1)S(1)} %pad_maximum_fusion.mine, bf16[4,256,2048]{2,1,0:T(8,128)(2,1)S(1)} %collective-permute-done.47.other), custom_call_target="tpu_custom_call" | custom-call | bytes 25165824 | tf_op jit(solution)/shard_map/pallas_call | solution.py:716
  528.2 18.4 %collective-permute-done.50 = f32[20480]{0:T(1024)S(1)} collective-permute-done((f32[20480]{0:T(1024)S(1)}, f32[20480]{0:T(1024)S(1)}, u32[]{:S(2)}, u32[]{:S(2)}) %collective-permute-start.50) | collective-permute-done | bytes 81952 | tf_op jit(solution)/shard_map/ppermute | solution.py:60
  546.6 2.1 fusion.13
  549.9 2.3 pad_maximum_fusion.1.mine
  557.4 4.1 collective-permute-done.53
  563.5 12.0 %shard_map.240 = (f32[512,6144]{1,0:T(8,128)}, f32[512,2048]{1,0:T(8,128)}) custom-call(s32[2]{0:T(128)S(1)} %pad_add_fusion.1.at_ref, bf16[4,256,2048]{2,1,0:T(8,128)(2,1)} %pad_maximum_fusion.1.mine, bf16[4,256,2048]{2,1,0:T(8,128)(2,1)} %collective-permute-done.52.other), custom_call_target="tpu_custom_call" | custom-call | bytes 25165824 | tf_op jit(solution)/shard_map/pallas_call | solution.py:716
  575.5 2.7 collective-permute-done.54
  578.2 4.2 collective-permute-done.55
  582.4 2.2 fusion.56
  584.7 6.2 %fusion.43 = (bf16[1,256,2048]{2,1,0:T(8,128)(2,1)}, bf16[1,256,2048]{2,1,0:T(8,128)(2,1)}) fusion(bf16[1,256,2048]{2,1,0:T(8,128)(2,1)S(1)} %copy-done.10, f32[256]{0:T(256)S(1)} %broadcast_multiply_fusion, f32[256]{0:T(256)S(1)} %broadcast_multiply_fusion.1, f32[256]{0:T(256)S(1)} %add_rsqrt_fusion, f32[256]{0:T(256)S(1)} %broadcast_multiply_fusion.2, ...), kind=kLoop, calls=%fused_computation.79 | loop fusion | flops 12582912 | bytes 10506244 | tf_op jit(solution)/shard_map/broadcast_in_dim | solution.py:1121
  (350 shorter events, 92.3 us)
Async XLA Ops:
  7.2 87.2 %all-gather.15.cloned.1.call-start = ((), (), s32[]{:S(2)}) async-start(), calls=%async_computation.4 | async-start | bytes 9437184 | tf_op jit(solution)/shard_map/all_gather | solution.py:842
  7.9 135.6 %all-gather.7.cloned.1.call-start = ((), (), s32[]{:S(2)}) async-start(), calls=%async_computation | async-start | bytes 4718592 | tf_op jit(solution)/shard_map/all_gather | solution.py:842
  17.8 171.4 %all-gather.9.cloned.1.call-start = ((), (), s32[]{:S(2)}) async-start(), calls=%async_computation.1 | async-start | bytes 4718592 | tf_op jit(solution)/shard_map/all_gather | solution.py:842
  21.7 25.3 %collective-permute-start = (bf16[256,1792]{1,0:T(8,128)(2,1)}, bf16[256,1792]{1,0:T(8,128)(2,1)}, u32[]{:S(2)}, u32[]{:S(2)}) collective-permute-start(bf16[256,1792]{1,0:T(8,128)(2,1)} %get-tuple-element.242.refs_6_.refs_3_), channel_id=1, source_target_pairs={{0,1},{1,0},{2,3},{3,2},{4,5},{5,4},{6,7},{7,6},{8,9},{9,8},{10,11... | collective-permute-start | bytes 2752520 | tf_op jit(solution)/shard_map/ppermute | solution.py:60
  24.6 22.4 %collective-permute-start.1 = (bf16[256,1792]{1,0:T(8,128)(2,1)S(1)}, bf16[256,1792]{1,0:T(8,128)(2,1)}, u32[]{:S(2)}, u32[]{:S(2)}) collective-permute-start(bf16[256,1792]{1,0:T(8,128)(2,1)S(1)} %get-tuple-element.244.refs_10_.refs_7_), channel_id=1, source_target_pairs={{0,2},{1,3},{2,0},{3,1},{4,6},{5,7},{6,4},{7,5},{8,10},{9,11},{10,... | collective-permute-start | bytes 2752520 | tf_op jit(solution)/shard_map/ppermute | solution.py:60
  26.2 19.5 %collective-permute-start.2 = (bf16[8,704]{1,0:T(8,128)(2,1)S(1)}, bf16[8,704]{1,0:T(8,128)(2,1)S(1)}, u32[]{:S(2)}, u32[]{:S(2)}) collective-permute-start(bf16[8,704]{1,0:T(8,128)(2,1)S(1)} %reshape.338), channel_id=1, source_target_pairs={{0,1},{1,0},{2,3},{3,2},{4,5},{5,4},{6,7},{7,6},{8,9},{9,8},{10,11... | collective-permute-start | bytes 33800 | tf_op jit(solution)/shard_map/ppermute | solution.py:60
  26.7 20.2 %collective-permute-start.3 = (bf16[8,704]{1,0:T(8,128)(2,1)S(1)}, bf16[8,704]{1,0:T(8,128)(2,1)S(1)}, u32[]{:S(2)}, u32[]{:S(2)}) collective-permute-start(bf16[8,704]{1,0:T(8,128)(2,1)S(1)} %reshape.338), channel_id=1, source_target_pairs={{0,2},{1,3},{2,0},{3,1},{4,6},{5,7},{6,4},{7,5},{8,10},{9,11},{10,... | collective-permute-start | bytes 33800 | tf_op jit(solution)/shard_map/ppermute | solution.py:60
  26.7 20.3 %collective-permute-start.4 = (bf16[8,704]{1,0:T(8,128)(2,1)S(1)}, bf16[8,704]{1,0:T(8,128)(2,1)S(1)}, u32[]{:S(2)}, u32[]{:S(2)}) collective-permute-start(bf16[8,704]{1,0:T(8,128)(2,1)S(1)} %reshape.338), channel_id=1, source_target_pairs={{0,3},{1,2},{2,1},{3,0},{4,7},{5,6},{6,5},{7,4},{8,11},{9,10},{10,... | collective-permute-start | bytes 33800 | tf_op jit(solution)/shard_map/ppermute | solution.py:60
  29.7 127.1 %copy-start.46 = (bf16[64,2048]{1,0:T(8,128)(2,1)}, bf16[64,2048]{1,0:T(8,128)(2,1)S(1)}, u32[]{:S(2)}) copy-start(bf16[64,2048]{1,0:T(8,128)(2,1)S(1)} %dynamic-slice_bitcast_fusion.17.refs_7_.refs_6_) | copy-start | bytes 786436
  31.1 66.3 %copy-start.35 = (bf16[256,2048]{1,0:T(8,128)(2,1)}, bf16[256,2048]{1,0:T(8,128)(2,1)S(1)}, u32[]{:S(2)}) copy-start(bf16[256,2048]{1,0:T(8,128)(2,1)S(1)} %dynamic-slice_bitcast_fusion.4.refs_3_.refs_2_) | copy-start | bytes 3145732
  47.9 23.7 %collective-permute-start.5 = (bf16[256,1792]{1,0:T(8,128)(2,1)}, bf16[256,1792]{1,0:T(8,128)(2,1)}, u32[]{:S(2)}, u32[]{:S(2)}) collective-permute-start(bf16[256,1792]{1,0:T(8,128)(2,1)} %get-tuple-element.242.refs_6_.refs_3_), channel_id=1, source_target_pairs={{0,2},{1,3},{2,0},{3,1},{4,6},{5,7},{6,4},{7,5},{8,10},{9,11},{10,... | collective-permute-start | bytes 2752520 | tf_op jit(solution)/shard_map/ppermute | solution.py:60
  49.5 39.7 %collective-permute-start.6 = (bf16[256,1792]{1,0:T(8,128)(2,1)}, bf16[256,1792]{1,0:T(8,128)(2,1)}, u32[]{:S(2)}, u32[]{:S(2)}) collective-permute-start(bf16[256,1792]{1,0:T(8,128)(2,1)} %collective-permute-done.refs_7_.refs_4_), channel_id=1, source_target_pairs={{0,2},{1,3},{2,0},{3,1},{4,6},{5,7},{6,4},{7,5},{8,10},{9,11},{10,... | collective-permute-start | bytes 2752520 | tf_op jit(solution)/shard_map/ppermute | solution.py:60
  50.0 39.2 %collective-permute-start.7 = (bf16[256,1792]{1,0:T(8,128)(2,1)S(1)}, bf16[256,1792]{1,0:T(8,128)(2,1)}, u32[]{:S(2)}, u32[]{:S(2)}) collective-permute-start(bf16[256,1792]{1,0:T(8,128)(2,1)S(1)} %get-tuple-element.244.refs_10_.refs_7_), channel_id=1, source_target_pairs={{0,1},{1,0},{2,3},{3,2},{4,5},{5,4},{6,7},{7,6},{8,9},{9,8},{10,11... | collective-permute-start | bytes 2752520 | tf_op jit(solution)/shard_map/ppermute | solution.py:60
  51.4 39.0 %collective-permute-start.8 = (bf16[256,1792]{1,0:T(8,128)(2,1)}, bf16[256,1792]{1,0:T(8,128)(2,1)}, u32[]{:S(2)}, u32[]{:S(2)}) collective-permute-start(bf16[256,1792]{1,0:T(8,128)(2,1)} %collective-permute-done.1.refs_11_.refs_8_), channel_id=1, source_target_pairs={{0,1},{1,0},{2,3},{3,2},{4,5},{5,4},{6,7},{7,6},{8,9},{9,8},{10,11... | collective-permute-start | bytes 2752520 | tf_op jit(solution)/shard_map/ppermute | solution.py:60
  54.7 223.0 %all-gather.13.cloned.1.call-start = ((), (), s32[]{:S(2)}) async-start(), calls=%async_computation.3 | async-start | bytes 4718592 | tf_op jit(solution)/shard_map/all_gather | solution.py:842
  94.4 47.8 %collective-permute-start.10 = (bf16[256,2048]{1,0:T(8,128)(2,1)S(1)}, bf16[256,2048]{1,0:T(8,128)(2,1)S(1)}, u32[]{:S(2)}, u32[]{:S(2)}) collective-permute-start(bf16[256,2048]{1,0:T(8,128)(2,1)S(1)} %dynamic-slice_bitcast_fusion.4.refs_3_.refs_2_), channel_id=1, source_target_pairs={{0,2},{1,3},{2,0},{3,1},{4,6},{5,7},{6,4},{7,5},{8,10},{9,11},{10,... | collective-permute-start | bytes 3145736 | tf_op jit(solution)/shard_map/ppermute | solution.py:60
  95.9 46.3 %collective-permute-start.11 = (bf16[256,2048]{1,0:T(8,128)(2,1)S(1)}, bf16[256,2048]{1,0:T(8,128)(2,1)S(1)}, u32[]{:S(2)}, u32[]{:S(2)}) collective-permute-start(bf16[256,2048]{1,0:T(8,128)(2,1)S(1)} %dynamic-slice_bitcast_fusion.4.refs_3_.refs_2_), channel_id=1, source_target_pairs={{0,3},{1,2},{2,1},{3,0},{4,7},{5,6},{6,5},{7,4},{8,11},{9,10},{10,... | collective-permute-start | bytes 3145736 | tf_op jit(solution)/shard_map/ppermute | solution.py:60
  97.4 46.1 %collective-permute-start.9 = (bf16[256,2048]{1,0:T(8,128)(2,1)S(1)}, bf16[256,2048]{1,0:T(8,128)(2,1)}, u32[]{:S(2)}, u32[]{:S(2)}) collective-permute-start(bf16[256,2048]{1,0:T(8,128)(2,1)S(1)} %dynamic-slice_bitcast_fusion.4.refs_3_.refs_2_), channel_id=1, source_target_pairs={{0,1},{1,0},{2,3},{3,2},{4,5},{5,4},{6,7},{7,6},{8,9},{9,8},{10,11... | collective-permute-start | bytes 3145736 | tf_op jit(solution)/shard_map/ppermute | solution.py:60
  152.8 34.1 %collective-permute-start.12 = (bf16[2,128,1024]{2,1,0:T(8,128)(2,1)}, bf16[2,128,1024]{2,1,0:T(8,128)(2,1)S(1)}, u32[]{:S(2)}, u32[]{:S(2)}) collective-permute-start(bf16[2,128,1024]{2,1,0:T(8,128)(2,1)} %dynamic-slice_bitcast_fusion.12), channel_id=1, source_target_pairs={{0,1},{1,0},{2,3},{3,2},{4,5},{5,4},{6,7},{7,6},{8,9},{9,8},{10,11... | collective-permute-start | bytes 1572872 | tf_op jit(solution)/shard_map/ppermute | solution.py:60
  154.3 32.6 %collective-permute-start.13 = (bf16[2,128,1024]{2,1,0:T(8,128)(2,1)S(1)}, bf16[2,128,1024]{2,1,0:T(8,128)(2,1)S(1)}, u32[]{:S(2)}, u32[]{:S(2)}) collective-permute-start(bf16[2,128,1024]{2,1,0:T(8,128)(2,1)S(1)} %dynamic-slice_bitcast_fusion.11), channel_id=1, source_target_pairs={{0,2},{1,3},{2,0},{3,1},{4,6},{5,7},{6,4},{7,5},{8,10},{9,11},{10,... | collective-permute-start | bytes 1572872 | tf_op jit(solution)/shard_map/ppermute | solution.py:60
  155.8 31.1 %collective-permute-start.14 = (bf16[64,2048]{1,0:T(8,128)(2,1)S(1)}, bf16[64,2048]{1,0:T(8,128)(2,1)}, u32[]{:S(2)}, u32[]{:S(2)}) collective-permute-start(bf16[64,2048]{1,0:T(8,128)(2,1)S(1)} %dynamic-slice_bitcast_fusion.17.refs_7_.refs_6_), channel_id=1, source_target_pairs={{0,1},{1,0},{2,3},{3,2},{4,5},{5,4},{6,7},{7,6},{8,9},{9,8},{10,11... | collective-permute-start | bytes 786440 | tf_op jit(solution)/shard_map/ppermute | solution.py:60
  156.3 30.5 %collective-permute-start.15 = (bf16[64,2048]{1,0:T(8,128)(2,1)S(1)}, bf16[64,2048]{1,0:T(8,128)(2,1)}, u32[]{:S(2)}, u32[]{:S(2)}) collective-permute-start(bf16[64,2048]{1,0:T(8,128)(2,1)S(1)} %dynamic-slice_bitcast_fusion.17.refs_7_.refs_6_), channel_id=1, source_target_pairs={{0,2},{1,3},{2,0},{3,1},{4,6},{5,7},{6,4},{7,5},{8,10},{9,11},{10,... | collective-permute-start | bytes 786440 | tf_op jit(solution)/shard_map/ppermute | solution.py:60
  156.8 30.0 %collective-permute-start.16 = (bf16[64,2048]{1,0:T(8,128)(2,1)S(1)}, bf16[64,2048]{1,0:T(8,128)(2,1)}, u32[]{:S(2)}, u32[]{:S(2)}) collective-permute-start(bf16[64,2048]{1,0:T(8,128)(2,1)S(1)} %dynamic-slice_bitcast_fusion.17.refs_7_.refs_6_), channel_id=1, source_target_pairs={{0,3},{1,2},{2,1},{3,0},{4,7},{5,6},{6,5},{7,4},{8,11},{9,10},{10,... | collective-permute-start | bytes 786440 | tf_op jit(solution)/shard_map/ppermute | solution.py:60
  189.2 12.3 %collective-permute-start.17 = (bf16[128,1024]{1,0:T(8,128)(2,1)S(1)}, bf16[128,1024]{1,0:T(8,128)(2,1)S(1)}, u32[]{:S(2)}, u32[]{:S(2)}) collective-permute-start(bf16[128,1024]{1,0:T(8,128)(2,1)S(1)} %dynamic-slice_bitcast_fusion.16), channel_id=1, source_target_pairs={{0,2},{1,3},{2,0},{3,1},{4,6},{5,7},{6,4},{7,5},{8,10},{9,11},{10,... | collective-permute-start | bytes 786440 | tf_op jit(solution)/shard_map/ppermute | solution.py:60
  190.7 10.8 %collective-permute-start.18 = (bf16[128,1024]{1,0:T(8,128)(2,1)S(1)}, bf16[128,1024]{1,0:T(8,128)(2,1)S(1)}, u32[]{:S(2)}, u32[]{:S(2)}) collective-permute-start(bf16[128,1024]{1,0:T(8,128)(2,1)S(1)} %dynamic-slice_bitcast_fusion.15), channel_id=1, source_target_pairs={{0,1},{1,0},{2,3},{3,2},{4,5},{5,4},{6,7},{7,6},{8,9},{9,8},{10,11... | collective-permute-start | bytes 786440 | tf_op jit(solution)/shard_map/ppermute | solution.py:60
  202.5 98.8 %all-gather.11.cloned.1.call-start = ((), (), s32[]{:S(2)}) async-start(), calls=%async_computation.2 | async-start | bytes 4718592 | tf_op jit(solution)/shard_map/all_gather | solution.py:842
  205.2 20.1 %collective-permute-start.19 = (bf16[2,128,1024]{2,1,0:T(8,128)(2,1)}, bf16[2,128,1024]{2,1,0:T(8,128)(2,1)S(1)}, u32[]{:S(2)}, u32[]{:S(2)}) collective-permute-start(bf16[2,128,1024]{2,1,0:T(8,128)(2,1)} %dynamic-slice_bitcast_fusion.10), channel_id=1, source_target_pairs={{0,1},{1,0},{2,3},{3,2},{4,5},{5,4},{6,7},{7,6},{8,9},{9,8},{10,11... | collective-permute-start | bytes 1572872 | tf_op jit(solution)/shard_map/ppermute | solution.py:60
  205.8 19.4 %collective-permute-start.20 = (bf16[2,128,1024]{2,1,0:T(8,128)(2,1)S(1)}, bf16[2,128,1024]{2,1,0:T(8,128)(2,1)S(1)}, u32[]{:S(2)}, u32[]{:S(2)}) collective-permute-start(bf16[2,128,1024]{2,1,0:T(8,128)(2,1)S(1)} %dynamic-slice_bitcast_fusion.9), channel_id=1, source_target_pairs={{0,2},{1,3},{2,0},{3,1},{4,6},{5,7},{6,4},{7,5},{8,10},{9,11},{10,... | collective-permute-start | bytes 1572872 | tf_op jit(solution)/shard_map/ppermute | solution.py:60
  225.8 16.1 %collective-permute-start.21 = (bf16[128,1024]{1,0:T(8,128)(2,1)S(1)}, bf16[128,1024]{1,0:T(8,128)(2,1)S(1)}, u32[]{:S(2)}, u32[]{:S(2)}) collective-permute-start(bf16[128,1024]{1,0:T(8,128)(2,1)S(1)} %dynamic-slice_bitcast_fusion.14), channel_id=1, source_target_pairs={{0,2},{1,3},{2,0},{3,1},{4,6},{5,7},{6,4},{7,5},{8,10},{9,11},{10,... | collective-permute-start | bytes 786440 | tf_op jit(solution)/shard_map/ppermute | solution.py:60
  227.5 14.4 %collective-permute-start.22 = (bf16[128,1024]{1,0:T(8,128)(2,1)S(1)}, bf16[128,1024]{1,0:T(8,128)(2,1)S(1)}, u32[]{:S(2)}, u32[]{:S(2)}) collective-permute-start(bf16[128,1024]{1,0:T(8,128)(2,1)S(1)} %dynamic-slice_bitcast_fusion.13), channel_id=1, source_target_pairs={{0,1},{1,0},{2,3},{3,2},{4,5},{5,4},{6,7},{7,6},{8,9},{9,8},{10,11... | collective-permute-start | bytes 786440 | tf_op jit(solution)/shard_map/ppermute | solution.py:60
  247.3 24.0 %collective-permute-start.23 = (bf16[2,256,1024]{2,1,0:T(8,128)(2,1)}, bf16[2,256,1024]{2,1,0:T(8,128)(2,1)}, u32[]{:S(2)}, u32[]{:S(2)}) collective-permute-start(bf16[2,256,1024]{2,1,0:T(8,128)(2,1)} %dynamic-slice_bitcast_fusion.3), channel_id=1, source_target_pairs={{0,1},{1,0},{2,3},{3,2},{4,5},{5,4},{6,7},{7,6},{8,9},{9,8},{10,11... | collective-permute-start | bytes 3145736 | tf_op jit(solution)/shard_map/ppermute | solution.py:60
  247.8 23.7 %collective-permute-start.24 = (bf16[2,256,1024]{2,1,0:T(8,128)(2,1)S(1)}, bf16[2,256,1024]{2,1,0:T(8,128)(2,1)}, u32[]{:S(2)}, u32[]{:S(2)}) collective-permute-start(bf16[2,256,1024]{2,1,0:T(8,128)(2,1)S(1)} %dynamic-slice_bitcast_fusion.2), channel_id=1, source_target_pairs={{0,2},{1,3},{2,0},{3,1},{4,6},{5,7},{6,4},{7,5},{8,10},{9,11},{10,... | collective-permute-start | bytes 3145736 | tf_op jit(solution)/shard_map/ppermute | solution.py:60
  277.7 24.4 %collective-permute-start.27 = (bf16[4,256,2048]{2,1,0:T(8,128)(2,1)}, bf16[4,256,2048]{2,1,0:T(8,128)(2,1)}, u32[]{:S(2)}, u32[]{:S(2)}) collective-permute-start(bf16[4,256,2048]{2,1,0:T(8,128)(2,1)} %get-tuple-element.331), channel_id=1, source_target_pairs={{0,4},{4,0},{8,12},{12,8},{16,20},{20,16},{24,28},{28,24},{1,5},{5... | collective-permute-start | bytes 12582920 | tf_op jit(solution)/shard_map/ppermute | solution.py:60
  277.7 23.6 %collective-permute-start.25 = (bf16[256,1024]{1,0:T(8,128)(2,1)}, bf16[256,1024]{1,0:T(8,128)(2,1)S(1)}, u32[]{:S(2)}, u32[]{:S(2)}) collective-permute-start(bf16[256,1024]{1,0:T(8,128)(2,1)} %dynamic-slice_bitcast_fusion.8), channel_id=1, source_target_pairs={{0,2},{1,3},{2,0},{3,1},{4,6},{5,7},{6,4},{7,5},{8,10},{9,11},{10,... | collective-permute-start | bytes 1572872 | tf_op jit(solution)/shard_map/ppermute | solution.py:60
  279.2 22.1 %collective-permute-start.26 = (bf16[256,1024]{1,0:T(8,128)(2,1)}, bf16[256,1024]{1,0:T(8,128)(2,1)S(1)}, u32[]{:S(2)}, u32[]{:S(2)}) collective-permute-start(bf16[256,1024]{1,0:T(8,128)(2,1)} %dynamic-slice_bitcast_fusion.7), channel_id=1, source_target_pairs={{0,1},{1,0},{2,3},{3,2},{4,5},{5,4},{6,7},{7,6},{8,9},{9,8},{10,11... | collective-permute-start | bytes 1572872 | tf_op jit(solution)/shard_map/ppermute | solution.py:60
  303.7 30.3 %collective-permute-start.28 = (bf16[256,2048]{1,0:T(8,128)(2,1)S(1)}, bf16[256,2048]{1,0:T(8,128)(2,1)S(1)}, u32[]{:S(2)}, u32[]{:S(2)}) collective-permute-start(bf16[256,2048]{1,0:T(8,128)(2,1)S(1)} %pad_maximum_fusion.2), channel_id=1, source_target_pairs={{0,8},{4,12},{8,16},{12,20},{16,24},{20,28},{1,9},{5,13},{9,17},{1... | collective-permute-start | bytes 3145736 | tf_op jit(solution)/shard_map/ppermute | solution.py:60
  305.9 28.1 %collective-permute-start.29 = (bf16[256,2048]{1,0:T(8,128)(2,1)S(1)}, bf16[256,2048]{1,0:T(8,128)(2,1)S(1)}, u32[]{:S(2)}, u32[]{:S(2)}) collective-permute-start(bf16[256,2048]{1,0:T(8,128)(2,1)S(1)} %pad_maximum_fusion.2), channel_id=1, source_target_pairs={{8,0},{12,4},{16,8},{20,12},{24,16},{28,20},{9,1},{13,5},{17,9},{2... | collective-permute-start | bytes 3145736 | tf_op jit(solution)/shard_map/ppermute | solution.py:60
  337.8 27.1 %collective-permute-start.30 = (bf16[256,2048]{1,0:T(8,128)(2,1)}, bf16[256,2048]{1,0:T(8,128)(2,1)S(1)}, u32[]{:S(2)}, u32[]{:S(2)}) collective-permute-start(bf16[256,2048]{1,0:T(8,128)(2,1)} %get-tuple-element.346), channel_id=1, source_target_pairs={{0,8},{4,12},{8,16},{12,20},{16,24},{20,28},{1,9},{5,13},{9,17},{1... | collective-permute-start | bytes 3145736 | tf_op jit(solution)/shard_map/ppermute | solution.py:60
  342.6 26.3 %collective-permute-start.31 = (bf16[256,2048]{1,0:T(8,128)(2,1)}, bf16[256,2048]{1,0:T(8,128)(2,1)S(1)}, u32[]{:S(2)}, u32[]{:S(2)}) collective-permute-start(bf16[256,2048]{1,0:T(8,128)(2,1)} %get-tuple-element.347), channel_id=1, source_target_pairs={{8,0},{12,4},{16,8},{20,12},{24,16},{28,20},{9,1},{13,5},{17,9},{2... | collective-permute-start | bytes 3145736 | tf_op jit(solution)/shard_map/ppermute | solution.py:60
  378.7 32.8 %collective-permute-start.32 = (bf16[256,2048]{1,0:T(8,128)(2,1)}, bf16[256,2048]{1,0:T(8,128)(2,1)S(1)}, u32[]{:S(2)}, u32[]{:S(2)}) collective-permute-start(bf16[256,2048]{1,0:T(8,128)(2,1)} %get-tuple-element.358), channel_id=1, source_target_pairs={{0,8},{4,12},{8,16},{12,20},{16,24},{20,28},{1,9},{5,13},{9,17},{1... | collective-permute-start | bytes 3145736 | tf_op jit(solution)/shard_map/ppermute | solution.py:60
  382.1 29.4 %collective-permute-start.33 = (bf16[256,2048]{1,0:T(8,128)(2,1)}, bf16[256,2048]{1,0:T(8,128)(2,1)}, u32[]{:S(2)}, u32[]{:S(2)}) collective-permute-start(bf16[256,2048]{1,0:T(8,128)(2,1)} %get-tuple-element.359), channel_id=1, source_target_pairs={{8,0},{12,4},{16,8},{20,12},{24,16},{28,20},{9,1},{13,5},{17,9},{2... | collective-permute-start | bytes 3145736 | tf_op jit(solution)/shard_map/ppermute | solution.py:60
  383.4 28.1 %collective-permute-start.34 = (bf16[2,256,1024]{2,1,0:T(8,128)(2,1)}, bf16[2,256,1024]{2,1,0:T(8,128)(2,1)}, u32[]{:S(2)}, u32[]{:S(2)}) collective-permute-start(bf16[2,256,1024]{2,1,0:T(8,128)(2,1)} %dynamic-slice_bitcast_fusion.1), channel_id=1, source_target_pairs={{0,1},{1,0},{2,3},{3,2},{4,5},{5,4},{6,7},{7,6},{8,9},{9,8},{10,11... | collective-permute-start | bytes 3145736 | tf_op jit(solution)/shard_map/ppermute | solution.py:60
  383.5 28.1 %collective-permute-start.35 = (bf16[2,256,1024]{2,1,0:T(8,128)(2,1)}, bf16[2,256,1024]{2,1,0:T(8,128)(2,1)}, u32[]{:S(2)}, u32[]{:S(2)}) collective-permute-start(bf16[2,256,1024]{2,1,0:T(8,128)(2,1)} %dynamic-slice_bitcast_fusion), channel_id=1, source_target_pairs={{0,2},{1,3},{2,0},{3,1},{4,6},{5,7},{6,4},{7,5},{8,10},{9,11},{10,... | collective-permute-start | bytes 3145736 | tf_op jit(solution)/shard_map/ppermute | solution.py:60
  422.4 20.8 %collective-permute-start.38 = (bf16[4,256,2048]{2,1,0:T(8,128)(2,1)}, bf16[4,256,2048]{2,1,0:T(8,128)(2,1)}, u32[]{:S(2)}, u32[]{:S(2)}) collective-permute-start(bf16[4,256,2048]{2,1,0:T(8,128)(2,1)} %get-tuple-element.372), channel_id=1, source_target_pairs={{0,4},{4,0},{8,12},{12,8},{16,20},{20,16},{24,28},{28,24},{1,5},{5... | collective-permute-start | bytes 12582920 | tf_op jit(solution)/shard_map/ppermute | solution.py:60
  422.9 20.2 %collective-permute-start.36 = (bf16[256,1024]{1,0:T(8,128)(2,1)}, bf16[256,1024]{1,0:T(8,128)(2,1)S(1)}, u32[]{:S(2)}, u32[]{:S(2)}) collective-permute-start(bf16[256,1024]{1,0:T(8,128)(2,1)} %dynamic-slice_bitcast_fusion.6), channel_id=1, source_target_pairs={{0,2},{1,3},{2,0},{3,1},{4,6},{5,7},{6,4},{7,5},{8,10},{9,11},{10,... | collective-permute-start | bytes 1572872 | tf_op jit(solution)/shard_map/ppermute | solution.py:60
  425.0 18.2 %collective-permute-start.37 = (bf16[256,1024]{1,0:T(8,128)(2,1)}, bf16[256,1024]{1,0:T(8,128)(2,1)S(1)}, u32[]{:S(2)}, u32[]{:S(2)}) collective-permute-start(bf16[256,1024]{1,0:T(8,128)(2,1)} %dynamic-slice_bitcast_fusion.5), channel_id=1, source_target_pairs={{0,1},{1,0},{2,3},{3,2},{4,5},{5,4},{6,7},{7,6},{8,9},{9,8},{10,11... | collective-permute-start | bytes 1572872 | tf_op jit(solution)/shard_map/ppermute | solution.py:60
  426.9 30.7 %collective-permute-start.42 = (bf16[256,2048]{1,0:T(8,128)(2,1)}, bf16[256,2048]{1,0:T(8,128)(2,1)}, u32[]{:S(2)}, u32[]{:S(2)}) collective-permute-start(bf16[256,2048]{1,0:T(8,128)(2,1)} %get-tuple-element.392), channel_id=1, source_target_pairs={{0,8},{4,12},{8,16},{12,20},{16,24},{20,28},{1,9},{5,13},{9,17},{1... | collective-permute-start | bytes 3145736 | tf_op jit(solution)/shard_map/ppermute | solution.py:60
  432.5 28.3 %collective-permute-start.43 = (bf16[256,2048]{1,0:T(8,128)(2,1)}, bf16[256,2048]{1,0:T(8,128)(2,1)}, u32[]{:S(2)}, u32[]{:S(2)}) collective-permute-start(bf16[256,2048]{1,0:T(8,128)(2,1)} %get-tuple-element.393), channel_id=1, source_target_pairs={{8,0},{12,4},{16,8},{20,12},{24,16},{28,20},{9,1},{13,5},{17,9},{2... | collective-permute-start | bytes 3145736 | tf_op jit(solution)/shard_map/ppermute | solution.py:60
  443.8 32.9 %collective-permute-start.39 = (bf16[256,2048]{1,0:T(8,128)(2,1)S(1)}, bf16[256,2048]{1,0:T(8,128)(2,1)S(1)}, u32[]{:S(2)}, u32[]{:S(2)}) collective-permute-start(bf16[256,2048]{1,0:T(8,128)(2,1)S(1)} %pad_maximum_fusion.3), channel_id=1, source_target_pairs={{0,8},{4,12},{8,16},{12,20},{16,24},{20,28},{1,9},{5,13},{9,17},{1... | collective-permute-start | bytes 3145736 | tf_op jit(solution)/shard_map/ppermute | solution.py:60
  448.7 33.1 %collective-permute-start.40 = (bf16[256,2048]{1,0:T(8,128)(2,1)S(1)}, bf16[256,2048]{1,0:T(8,128)(2,1)S(1)}, u32[]{:S(2)}, u32[]{:S(2)}) collective-permute-start(bf16[256,2048]{1,0:T(8,128)(2,1)S(1)} %pad_maximum_fusion.3), channel_id=1, source_target_pairs={{8,0},{12,4},{16,8},{20,12},{24,16},{28,20},{9,1},{13,5},{17,9},{2... | collective-permute-start | bytes 3145736 | tf_op jit(solution)/shard_map/ppermute | solution.py:60
  450.0 10.8 %collective-permute-start.41 = (f32[20480]{0:T(1024)S(1)}, f32[20480]{0:T(1024)S(1)}, u32[]{:S(2)}, u32[]{:S(2)}) collective-permute-start(f32[20480]{0:T(1024)S(1)} %constant_dynamic-update-slice_fusion.2), channel_id=1, source_target_pairs={{0,4},{4,0},{8,12},{12,8},{16,20},{20,16},{24,28},{28,24},{1,5},{5... | collective-permute-start | bytes 245768 | tf_op jit(solution)/shard_map/ppermute | solution.py:60
  457.0 89.6 %copy-start.5 = (bf16[4,256,2048]{2,1,0:T(8,128)(2,1)}, bf16[4,256,2048]{2,1,0:T(8,128)(2,1)S(1)}, u32[]{:S(2)}) copy-start(bf16[4,256,2048]{2,1,0:T(8,128)(2,1)S(1)} %add_convert_fusion) | copy-start | bytes 12582916
  482.6 30.7 %collective-permute-start.47 = (bf16[4,256,2048]{2,1,0:T(8,128)(2,1)S(1)}, bf16[4,256,2048]{2,1,0:T(8,128)(2,1)S(1)}, u32[]{:S(2)}, u32[]{:S(2)}) collective-permute-start(bf16[4,256,2048]{2,1,0:T(8,128)(2,1)S(1)} %pad_maximum_fusion.mine), channel_id=1, source_target_pairs={{0,4},{4,0},{8,12},{12,8},{16,20},{20,16},{24,28},{28,24},{1,5},{5... | collective-permute-start | bytes 12582920 | tf_op jit(solution)/shard_map/ppermute | solution.py:60
  482.7 30.6 %collective-permute-start.44 = (bf16[256,2048]{1,0:T(8,128)(2,1)S(1)}, bf16[256,2048]{1,0:T(8,128)(2,1)S(1)}, u32[]{:S(2)}, u32[]{:S(2)}) collective-permute-start(bf16[256,2048]{1,0:T(8,128)(2,1)S(1)} %get-tuple-element.400), channel_id=1, source_target_pairs={{0,8},{4,12},{8,16},{12,20},{16,24},{20,28},{1,9},{5,13},{9,17},{1... | collective-permute-start | bytes 3145736 | tf_op jit(solution)/shard_map/ppermute | solution.py:60
  484.3 28.9 %collective-permute-start.45 = (bf16[256,2048]{1,0:T(8,128)(2,1)S(1)}, bf16[256,2048]{1,0:T(8,128)(2,1)S(1)}, u32[]{:S(2)}, u32[]{:S(2)}) collective-permute-start(bf16[256,2048]{1,0:T(8,128)(2,1)S(1)} %get-tuple-element.401), channel_id=1, source_target_pairs={{8,0},{12,4},{16,8},{20,12},{24,16},{28,20},{9,1},{13,5},{17,9},{2... | collective-permute-start | bytes 3145736 | tf_op jit(solution)/shard_map/ppermute | solution.py:60
  485.9 27.4 %collective-permute-start.46 = (f32[20480]{0:T(1024)S(1)}, f32[20480]{0:T(1024)S(1)}, u32[]{:S(2)}, u32[]{:S(2)}) collective-permute-start(f32[20480]{0:T(1024)S(1)} %add.407), channel_id=1, source_target_pairs={{0,8},{4,12},{8,0},{12,4},{16,24},{20,28},{24,16},{28,20},{1,9},{5... | collective-permute-start | bytes 245768 | tf_op jit(solution)/shard_map/ppermute | solution.py:60
  514.1 32.4 %collective-permute-start.48 = (bf16[256,2048]{1,0:T(8,128)(2,1)S(1)}, bf16[256,2048]{1,0:T(8,128)(2,1)S(1)}, u32[]{:S(2)}, u32[]{:S(2)}) collective-permute-start(bf16[256,2048]{1,0:T(8,128)(2,1)S(1)} %get-tuple-element.410), channel_id=1, source_target_pairs={{0,8},{4,12},{8,16},{12,20},{16,24},{20,28},{1,9},{5,13},{9,17},{1... | collective-permute-start | bytes 3145736 | tf_op jit(solution)/shard_map/ppermute | solution.py:60
  515.6 30.9 %collective-permute-start.49 = (bf16[256,2048]{1,0:T(8,128)(2,1)S(1)}, bf16[256,2048]{1,0:T(8,128)(2,1)S(1)}, u32[]{:S(2)}, u32[]{:S(2)}) collective-permute-start(bf16[256,2048]{1,0:T(8,128)(2,1)S(1)} %get-tuple-element.411), channel_id=1, source_target_pairs={{8,0},{12,4},{16,8},{20,12},{24,16},{28,20},{9,1},{13,5},{17,9},{2... | collective-permute-start | bytes 3145736 | tf_op jit(solution)/shard_map/ppermute | solution.py:60
  516.9 29.6 %collective-permute-start.50 = (f32[20480]{0:T(1024)S(1)}, f32[20480]{0:T(1024)S(1)}, u32[]{:S(2)}, u32[]{:S(2)}) collective-permute-start(f32[20480]{0:T(1024)S(1)} %add.410), channel_id=1, source_target_pairs={{0,16},{4,20},{8,24},{12,28},{16,0},{20,4},{24,8},{28,12},{1,17},{... | collective-permute-start | bytes 245768 | tf_op jit(solution)/shard_map/ppermute | solution.py:60
  548.7 4.4 collective-permute-start.51
  553.2 8.4 %collective-permute-start.52 = (bf16[4,256,2048]{2,1,0:T(8,128)(2,1)}, bf16[4,256,2048]{2,1,0:T(8,128)(2,1)}, u32[]{:S(2)}, u32[]{:S(2)}) collective-permute-start(bf16[4,256,2048]{2,1,0:T(8,128)(2,1)} %pad_maximum_fusion.1.mine), channel_id=1, source_target_pairs={{0,4},{4,0},{8,12},{12,8},{16,20},{20,16},{24,28},{28,24},{1,5},{5... | collective-permute-start | bytes 12582920 | tf_op jit(solution)/shard_map/ppermute | solution.py:60
  553.3 25.0 %collective-permute-start.54 = (bf16[256,2048]{1,0:T(8,128)(2,1)}, bf16[256,2048]{1,0:T(8,128)(2,1)S(1)}, u32[]{:S(2)}, u32[]{:S(2)}) collective-permute-start(bf16[256,2048]{1,0:T(8,128)(2,1)} %get-tuple-element.433), channel_id=1, source_target_pairs={{0,8},{4,12},{8,16},{12,20},{16,24},{20,28},{1,9},{5,13},{9,17},{1... | collective-permute-start | bytes 3145736 | tf_op jit(solution)/shard_map/ppermute | solution.py:60
  554.9 27.5 %collective-permute-start.55 = (bf16[256,2048]{1,0:T(8,128)(2,1)}, bf16[256,2048]{1,0:T(8,128)(2,1)}, u32[]{:S(2)}, u32[]{:S(2)}) collective-permute-start(bf16[256,2048]{1,0:T(8,128)(2,1)} %get-tuple-element.434), channel_id=1, source_target_pairs={{8,0},{12,4},{16,8},{20,12},{24,16},{28,20},{9,1},{13,5},{17,9},{2... | collective-permute-start | bytes 3145736 | tf_op jit(solution)/shard_map/ppermute | solution.py:60
  556.9 4.6 collective-permute-start.53
  (66 other events, 570.7 us)
Sparse Core Ops, SparseCore 0:
  9.6 84.7 all-gather.14
  96.0 45.6 all-gather.6
  143.3 45.8 all-gather.8
  202.7 43.9 all-gather.12
  248.1 45.9 all-gather.10

commit v7 on v6

--- a/solution.py
+++ b/solution.py
@@ -1072,7 +1072,14 @@
         order_and_add, (up_blocks, core_flow.result), [weave, total_flow], early=[out_finish]
     )
     up_swap = Flow(swap_steps(up_blocks))
-    beside(nothing, (), [flow for flow in (weave, total_flow, up_swap) if flow.moves])
+    output, scaled, inv_std = beside(
+        lambda rows, sums, bias: (
+            (rows.astype(F32) + sums + bias).astype(BF16),
+            *standard(rows),
+        ),
+        (own_tokens, out_finish.result, out_bias_all + down_bias_all),
+        [flow for flow in (weave, total_flow, up_swap) if flow.moves],
+    )
     (up_dealt,) = beside(
         lambda *halves: deal_columns(*halves, unit, list(range(shard_count)), at),
         up_swap.result,
@@ -1092,12 +1099,8 @@
         [flow for flow in (total_flow,) if flow.moves],
         early=[norm_finish],
     )
-    out_sum, grad_normed = out_finish.result, norm_finish.result
-
-    inputs = own_tokens.astype(F32)
-    output = (inputs + out_sum + (out_bias_all + down_bias_all)).astype(BF16)
-
-    scaled, inv_std = standard(own_tokens)
+    grad_normed = norm_finish.result
+
     grad_scaled = grad_normed * gain_all
     grad_input = inv_std * (
         grad_scaled

time: 601 us -> 603 us (level)
  Pallas kernels: 204 us -> 193 us
  starting transfers between devices: 81 us -> 87.6 us
    ppermute x56, starting transfers between devices: 80.6 us -> 87.2 us  [beside(): lax.ppermute(value, axis, pairs)]
    pallas_call x2, Pallas kernels: 42.8 us -> 36.3 us  [attention_backward(): pl.pallas_call(functools.partial(backward_kernel, pair), out_shape=jax.Sh...]
  transfers between devices with their start and end apart: 61 -> 61, of which waited for: 23 -> 23; matrix products, arithmetic and copies ran while one was open for 17% -> 17% of each run, Pallas kernels for 34% -> 32%
where the time goes in v7:
time: 603 us; the launch traced here: 597 us
  Pallas kernels  193 us (32%)
  waiting for transfers between devices  149 us (25%)
  starting transfers between devices  87.6 us (15%)
  other arithmetic  64.9 us (11%)
  matrix products  45.3 us (8%)
  local copies, waits for them, and re-layouts  41.6 us (7%)
  between operations  15.8 us (3%)
    ppermute x56, waiting for transfers between devices, beside(): lax.ppermute(value, axis, pairs)  138 us
    pallas_call x4, Pallas kernels, row_call(): pl.pallas_call(body, out_shape=out_shape + [jax.ShapeDtypeStruct(shape, F...  98.7 us
    ppermute x56, starting transfers between devices, beside(): lax.ppermute(value, axis, pairs)  87.2 us
    dot_general x6, matrix products, dot_tn(): lax.dot_general(left, right, (((0,), (0,)), ((), ())), preferred_element_...  45.3 us
    pallas_call x2, Pallas kernels, attention_backward(): pl.pallas_call(functools.partial(backward_kernel, pair), out_shape=jax.Sh...  36.3 us
    pallas_call x1, Pallas kernels, attention_forward(): pl.pallas_call(forward_kernel, out_shape=(jax.ShapeDtypeStruct((tokens, w...  22.8 us
    pallas_call x2, Pallas kernels, deal_columns(): pl.pallas_call(functools.partial(deal_kernel, unit, order), out_shape=out...  19.7 us
    unnamed x155, local copies, waits for them, and re-layouts  16.4 us
  transfers between devices with their start and end apart: 61, of which 23 were waited for; matrix products, arithmetic and copies ran while one was open for 17% of the time, Pallas kernels for 32%

profile of v7, /device:TPU:0, one launch (start us, length us, event | category | flops | bytes accessed | tf_op | source)
XLA Modules:
  0.0 597.4 jit_solution(5647460486572045978)
XLA Ops:
  8.0 3.4 copy-done.2
  11.4 2.8 copy-done.4
  19.0 2.7 fusion.58
  21.8 2.9 collective-permute-start
  26.8 2.9 collective-permute-start.4
  32.1 13.6 %collective-permute-done.2 = bf16[8,704]{1,0:T(8,128)(2,1)S(1)} collective-permute-done((bf16[8,704]{1,0:T(8,128)(2,1)S(1)}, bf16[8,704]{1,0:T(8,128)(2,1)S(1)}, u32[]{:S(2)}, u32[]{:S(2)}) %collective-permute-start.2) | collective-permute-done | bytes 11296 | tf_op jit(solution)/shard_map/ppermute | solution.py:60
  55.1 8.9 %fusion.34 = (f32[2048,128]{1,0:T(8,128)}, f32[2048,128]{1,0:T(8,128)}, f32[2048,128]{1,0:T(8,128)}, f32[2048,128]{1,0:T(8,128)}) fusion(f32[2048]{0:T(1024)S(1)} %get-tuple-element.510, f32[128]{0:T(128)S(1)} %get-tuple-element.508, f32[128]{0:T(128)S(1)} %get-tuple-element.509, f32[2048]{0:T(1024)S(1)} %get-tuple-element.511), kind=kLoop, calls=%fused_computation.72 | loop fusion | flops 1048576 | bytes 4211712 | tf_op jit(solution)/shard_map/mul | solution.py:397
  64.0 7.6 %collective-permute-done.5.refs_8_.refs_5_ = bf16[256,1792]{1,0:T(8,128)(2,1)} collective-permute-done((bf16[256,1792]{1,0:T(8,128)(2,1)}, bf16[256,1792]{1,0:T(8,128)(2,1)}, u32[]{:S(2)}, u32[]{:S(2)}) %collective-permute-start.5) | collective-permute-done | bytes 917536 | tf_op jit(solution)/shard_map/ppermute | solution.py:60
  71.6 17.6 %collective-permute-done.6.refs_9_.refs_6_ = bf16[256,1792]{1,0:T(8,128)(2,1)} collective-permute-done((bf16[256,1792]{1,0:T(8,128)(2,1)}, bf16[256,1792]{1,0:T(8,128)(2,1)}, u32[]{:S(2)}, u32[]{:S(2)}) %collective-permute-start.6) | collective-permute-done | bytes 917536 | tf_op jit(solution)/shard_map/ppermute | solution.py:60
  90.5 3.9 all-gather.15.cloned.1.call-done
  97.9 34.2 %shard_map.230 = (bf16[2048,2048]{1,0:T(8,128)(2,1)}, bf16[2048,1024]{1,0:T(8,128)(2,1)}, bf16[2048,1024]{1,0:T(8,128)(2,1)}, bf16[2048,768]{1,0:T(8,128)(2,1)}) custom-call(s32[2]{0:T(128)} %pad_add_fusion.at, bf16[2048,2048]{1,0:T(8,128)(2,1)} %bitcast.274, f32[2048,128]{1,0:T(8,128)} %get-tuple-element.252.refs_1_, ...), custom_call_target="tpu_custom_call" | custom-call | flops 15032385536 | bytes 37772288 | tf_op jit(solution)/shard_map/pallas_call | solution.py:518
  132.2 10.0 %collective-permute-done.10.refs_5_.refs_4_ = bf16[256,2048]{1,0:T(8,128)(2,1)S(1)} collective-permute-done((bf16[256,2048]{1,0:T(8,128)(2,1)S(1)}, bf16[256,2048]{1,0:T(8,128)(2,1)S(1)}, u32[]{:S(2)}, u32[]{:S(2)}) %collective-permute-start.10) | collective-permute-done | bytes 1048608 | tf_op jit(solution)/shard_map/ppermute | solution.py:60
  143.5 8.0 %convolution_convert_fusion.3 = bf16[1024,1024]{1,0:T(8,128)(2,1)S(1)} fusion(bf16[2048,1024]{1,0:T(8,128)(2,1)} %get-tuple-element.268.refs_1_, bf16[2048,1024]{1,0:T(8,128)(2,1)} %all-gather.7.cloned.1.call-done.refs_0_), kind=kOutput, calls=%fused_computation.56 | convolution fusion | flops 4296015872 | bytes 10485760 | tf_op jit(solution)/shard_map/dot_general | solution.py:30
  156.8 2.4 collective-permute-start.16
  159.3 22.8 %shard_map.231 = (bf16[2048,256]{1,0:T(8,128)(2,1)}, bf16[2048,768]{1,0:T(8,128)(2,1)}, f32[256,2048]{1,0:T(8,128)}, f32[4,2048]{1,0:T(4,128)}) custom-call(s32[128]{0:T(128)} %place_ref.5, s32[4]{0:T(128)} %bitcast.271, bf16[2048,768]{1,0:T(8,128)(2,1)} %get-tuple-element.272.lin_hbm), custom_call_target="tpu_custom_call" | custom-call | flops 40000000000 | bytes 16000000 | tf_op jit(solution)/shard_map/pallas_call | solution.py:408
  182.6 6.6 %all-gather.9.cloned.1.call-done.refs_1_ = bf16[2048,1024]{1,0:T(8,128)(2,1)} async-done(((bf16[256,1024]{1,0:T(8,128)(2,1)}), bf16[2048,1024]{1,0:T(8,128)(2,1)}) %all-gather.9.cloned.1.call-update) | async-done | bytes 4194320 | tf_op jit(solution)/shard_map/all_gather | solution.py:842
  192.2 9.4 %convolution_convert_fusion.2 = bf16[1024,1024]{1,0:T(8,128)(2,1)} fusion(bf16[2048,1024]{1,0:T(8,128)(2,1)} %get-tuple-element.268.refs_1_, bf16[2048,1024]{1,0:T(8,128)(2,1)} %all-gather.9.cloned.1.call-done.refs_1_), kind=kOutput, calls=%fused_computation.55 | convolution fusion | flops 4296015872 | bytes 10485760 | tf_op jit(solution)/shard_map/dot_general | solution.py:30
  206.4 18.9 %shard_map.232 = (bf16[2048,1024]{1,0:T(8,128)(2,1)}, bf16[2048,256]{1,0:T(8,128)(2,1)}, f32[1,1024]{1,0:T(1,128)}) custom-call(s32[2]{0:T(128)} %pad_add_fusion.at, bf16[2048,1024]{1,0:T(8,128)(2,1)} %all-gather.7.cloned.1.call-done.refs_0_, bf16[2048,1024]{1,0:T(8,128)(2,1)} %all-gather.9.cloned.1.call-done.refs_1_, ...), custom_call_target="tpu_custom_call" | custom-call | flops 10737418240 | bytes 23068672 | tf_op jit(solution)/shard_map/pallas_call | solution.py:518
  228.9 12.9 %convolution_convert_fusion = bf16[2048,1024]{1,0:T(8,128)(2,1)} fusion(bf16[2048,2048]{1,0:T(8,128)(2,1)} %get-tuple-element.308, bf16[2048,1024]{1,0:T(8,128)(2,1)S(1)} %copy-done.67), kind=kOutput, calls=%fused_computation.4 | convolution fusion | flops 8592031744 | bytes 16777216 | tf_op jit(solution)/shard_map/dot_general | solution.py:30
  242.9 2.7 fusion.55
  248.8 17.6 %shard_map.233 = (bf16[4,256,2048]{2,1,0:T(8,128)(2,1)}, bf16[4,256,2048]{2,1,0:T(8,128)(2,1)}) custom-call(s32[2]{0:T(128)} %pad_add_fusion.at, bf16[2048,256]{1,0:T(8,128)(2,1)} %get-tuple-element.351.refs_0_, bf16[2048,1024]{1,0:T(8,128)(2,1)} %get-tuple-element.268.refs_1_, bf16[256,2048]{1,0:T(8,128)(2,1)} %copy-done.35, ...), custom_call_target="tpu_custom_call" | custom-call | flops 10737418240 | bytes 18874368 | tf_op jit(solution)/shard_map/pallas_call | solution.py:518
  266.4 4.9 collective-permute-done.23
  271.4 2.0 fusion.23
  279.8 18.2 %shard_map.234.refs_0_ = bf16[2048,768]{1,0:T(8,128)(2,1)} custom-call(s32[128]{0:T(128)} %place_ref.5, s32[4]{0:T(128)} %bitcast.272, f32[2048,128]{1,0:T(8,128)} %get-tuple-element.326.cos_ref, f32[2048,128]{1,0:T(8,128)} %get-tuple-element.327.sin_ref, bf16[2048,768]{1,0:T(8,128)(2,1)} %get-tuple-element.328.rows, ...), custom_call_target="tpu_custom_call" | custom-call | flops 20000000000 | bytes 8000000 | tf_op jit(solution)/shard_map/pallas_call | solution.py:432
  300.4 2.2 collective-permute-start.28
  303.9 18.1 %shard_map.235.refs_1_ = bf16[2048,768]{1,0:T(8,128)(2,1)} custom-call(s32[128]{0:T(128)} %place_ref.5, s32[4]{0:T(128)} %bitcast.273, f32[2048,128]{1,0:T(8,128)} %get-tuple-element.326.cos_ref, f32[2048,128]{1,0:T(8,128)} %get-tuple-element.327.sin_ref, bf16[2048,768]{1,0:T(8,128)(2,1)} %get-tuple-element.328.rows, ...), custom_call_target="tpu_custom_call", output_to_operand_aliasing={{}: (8, {})} | custom-call | flops 20000000000 | bytes 8000000 | tf_op jit(solution)/shard_map/pallas_call | solution.py:432
  322.0 5.4 add_convert_fusion.1
  327.4 1.9 collective-permute-done.29
  329.3 2.1 fusion.26
  331.4 4.6 collective-permute-start.30
  337.4 10.8 %convolution_convert_fusion.1.left = bf16[2048,768]{1,0:T(8,128)(2,1)} fusion(bf16[2048,2048]{1,0:T(8,128)(2,1)} %get-tuple-element.308, bf16[2048,768]{1,0:T(8,128)(2,1)S(1)} %copy-done.68), kind=kOutput, calls=%fused_computation.5 | convolution fusion | flops 6444023808 | bytes 14680064 | tf_op jit(solution)/shard_map/dot_general | solution.py:30
  348.2 2.1 convolution_convert_fusion.4.refs_1_
  350.4 2.1 convolution_convert_fusion.5.refs_0_
  352.5 4.7 shard_map.236
  358.3 4.1 collective-permute-done.31
  363.4 2.8 fusion.54
  369.9 2.2 fusion.28
  372.1 3.4 collective-permute-start.32
  378.2 7.2 %collective-permute-start.35 = (bf16[2,256,1024]{2,1,0:T(8,128)(2,1)}, bf16[2,256,1024]{2,1,0:T(8,128)(2,1)}, u32[]{:S(2)}, u32[]{:S(2)}) collective-permute-start(bf16[2,256,1024]{2,1,0:T(8,128)(2,1)} %dynamic-slice_bitcast_fusion), channel_id=1, source_target_pairs={{0,2},{1,3},{2,0},{3,1},{4,6},{5,7},{6,4},{7,5},{8,10},{9,11},{10,... | collective-permute-start | bytes 3145736 | tf_op jit(solution)/shard_map/ppermute | solution.py:60
  385.3 28.0 %shard_map.237 = (bf16[4,256,2048]{2,1,0:T(8,128)(2,1)}, bf16[4,256,2048]{2,1,0:T(8,128)(2,1)}, f32[1,2048]{1,0:T(1,128)}, f32[1,2048]{1,0:T(1,128)}, f32[1,768]{1,0:T(1,128)}) custom-call(s32[2]{0:T(128)} %pad_add_fusion.at, bf16[2048,2048]{1,0:T(8,128)(2,1)} %bitcast.275, bf16[2048,768]{1,0:T(8,128)(2,1)} %shard_map.235.refs_1_, ...), custom_call_target="tpu_custom_call" | custom-call | flops 15032385536 | bytes 31457280 | tf_op jit(solution)/shard_map/pallas_call | solution.py:518
  413.4 2.3 fusion.16
  420.3 3.8 fusion.14
  425.0 5.7 collective-permute-start.42
  431.9 9.4 %shard_map.238 = f32[2048,2048]{1,0:T(8,128)} custom-call(bf16[2048,1024]{1,0:T(8,128)(2,1)} %all-gather.13.cloned.1.call-done.refs_0_, bf16[2048,1024]{1,0:T(8,128)(2,1)} %all-gather.11.cloned.1.call-done.refs_1_), custom_call_target="tpu_custom_call" | custom-call | bytes 25165824 | tf_op jit(solution)/shard_map/pallas_call | solution.py:787
  444.3 4.6 collective-permute-start.39
  450.3 2.8 select_bitcast_fusion.7
  453.5 4.1 add_convert_fusion
  458.8 16.5 %collective-permute-done.39 = bf16[256,2048]{1,0:T(8,128)(2,1)S(1)} collective-permute-done((bf16[256,2048]{1,0:T(8,128)(2,1)S(1)}, bf16[256,2048]{1,0:T(8,128)(2,1)S(1)}, u32[]{:S(2)}, u32[]{:S(2)}) %collective-permute-start.39) | collective-permute-done | bytes 1048608 | tf_op jit(solution)/shard_map/ppermute | solution.py:60
  475.4 5.1 collective-permute-done.40
  481.5 2.5 fusion.22
  487.2 2.7 collective-permute-start.46
  490.4 2.2 fusion
  492.6 22.1 %collective-permute-done.46 = f32[20480]{0:T(1024)S(1)} collective-permute-done((f32[20480]{0:T(1024)S(1)}, f32[20480]{0:T(1024)S(1)}, u32[]{:S(2)}, u32[]{:S(2)}) %collective-permute-start.46) | collective-permute-done | bytes 81952 | tf_op jit(solution)/shard_map/ppermute | solution.py:60
  518.4 3.6 collective-permute-start.50
  522.1 7.4 %shard_map.239 = f32[512,8192]{1,0:T(8,128)} custom-call(s32[2]{0:T(128)S(1)} %pad_add_fusion.1.at_ref, bf16[4,256,2048]{2,1,0:T(8,128)(2,1)S(1)} %pad_maximum_fusion.mine, bf16[4,256,2048]{2,1,0:T(8,128)(2,1)S(1)} %collective-permute-done.47.other), custom_call_target="tpu_custom_call" | custom-call | bytes 25165824 | tf_op jit(solution)/shard_map/pallas_call | solution.py:716
  529.5 18.4 %collective-permute-done.50 = f32[20480]{0:T(1024)S(1)} collective-permute-done((f32[20480]{0:T(1024)S(1)}, f32[20480]{0:T(1024)S(1)}, u32[]{:S(2)}, u32[]{:S(2)}) %collective-permute-start.50) | collective-permute-done | bytes 81952 | tf_op jit(solution)/shard_map/ppermute | solution.py:60
  547.9 2.1 fusion.6
  552.6 2.3 pad_maximum_fusion.1.mine
  559.7 2.9 collective-permute-done.53
  564.5 12.3 %shard_map.240 = (f32[512,6144]{1,0:T(8,128)}, f32[512,2048]{1,0:T(8,128)}) custom-call(s32[2]{0:T(128)S(1)} %pad_add_fusion.1.at_ref, bf16[4,256,2048]{2,1,0:T(8,128)(2,1)} %pad_maximum_fusion.1.mine, bf16[4,256,2048]{2,1,0:T(8,128)(2,1)} %collective-permute-done.52.other), custom_call_target="tpu_custom_call" | custom-call | bytes 25165824 | tf_op jit(solution)/shard_map/pallas_call | solution.py:716
  576.8 3.1 collective-permute-done.54
  579.9 4.2 collective-permute-done.55
  584.1 2.0 fusion.48
  586.2 3.6 fusion.35
  (352 shorter events, 97.5 us)
Async XLA Ops:
  7.2 87.2 %all-gather.15.cloned.1.call-start = ((), (), s32[]{:S(2)}) async-start(), calls=%async_computation.4 | async-start | bytes 9437184 | tf_op jit(solution)/shard_map/all_gather | solution.py:842
  7.9 135.6 %all-gather.7.cloned.1.call-start = ((), (), s32[]{:S(2)}) async-start(), calls=%async_computation | async-start | bytes 4718592 | tf_op jit(solution)/shard_map/all_gather | solution.py:842
  17.9 171.4 %all-gather.9.cloned.1.call-start = ((), (), s32[]{:S(2)}) async-start(), calls=%async_computation.1 | async-start | bytes 4718592 | tf_op jit(solution)/shard_map/all_gather | solution.py:842
  21.8 25.3 %collective-permute-start = (bf16[256,1792]{1,0:T(8,128)(2,1)}, bf16[256,1792]{1,0:T(8,128)(2,1)}, u32[]{:S(2)}, u32[]{:S(2)}) collective-permute-start(bf16[256,1792]{1,0:T(8,128)(2,1)} %get-tuple-element.248.refs_6_.refs_3_), channel_id=1, source_target_pairs={{0,1},{1,0},{2,3},{3,2},{4,5},{5,4},{6,7},{7,6},{8,9},{9,8},{10,11... | collective-permute-start | bytes 2752520 | tf_op jit(solution)/shard_map/ppermute | solution.py:60
  24.7 22.4 %collective-permute-start.1 = (bf16[256,1792]{1,0:T(8,128)(2,1)S(1)}, bf16[256,1792]{1,0:T(8,128)(2,1)}, u32[]{:S(2)}, u32[]{:S(2)}) collective-permute-start(bf16[256,1792]{1,0:T(8,128)(2,1)S(1)} %get-tuple-element.250.refs_10_.refs_7_), channel_id=1, source_target_pairs={{0,2},{1,3},{2,0},{3,1},{4,6},{5,7},{6,4},{7,5},{8,10},{9,11},{10,... | collective-permute-start | bytes 2752520 | tf_op jit(solution)/shard_map/ppermute | solution.py:60
  26.2 19.5 %collective-permute-start.2 = (bf16[8,704]{1,0:T(8,128)(2,1)S(1)}, bf16[8,704]{1,0:T(8,128)(2,1)S(1)}, u32[]{:S(2)}, u32[]{:S(2)}) collective-permute-start(bf16[8,704]{1,0:T(8,128)(2,1)S(1)} %reshape.341), channel_id=1, source_target_pairs={{0,1},{1,0},{2,3},{3,2},{4,5},{5,4},{6,7},{7,6},{8,9},{9,8},{10,11... | collective-permute-start | bytes 33800 | tf_op jit(solution)/shard_map/ppermute | solution.py:60
  26.7 20.2 %collective-permute-start.3 = (bf16[8,704]{1,0:T(8,128)(2,1)S(1)}, bf16[8,704]{1,0:T(8,128)(2,1)S(1)}, u32[]{:S(2)}, u32[]{:S(2)}) collective-permute-start(bf16[8,704]{1,0:T(8,128)(2,1)S(1)} %reshape.341), channel_id=1, source_target_pairs={{0,2},{1,3},{2,0},{3,1},{4,6},{5,7},{6,4},{7,5},{8,10},{9,11},{10,... | collective-permute-start | bytes 33800 | tf_op jit(solution)/shard_map/ppermute | solution.py:60
  26.8 20.2 %collective-permute-start.4 = (bf16[8,704]{1,0:T(8,128)(2,1)S(1)}, bf16[8,704]{1,0:T(8,128)(2,1)S(1)}, u32[]{:S(2)}, u32[]{:S(2)}) collective-permute-start(bf16[8,704]{1,0:T(8,128)(2,1)S(1)} %reshape.341), channel_id=1, source_target_pairs={{0,3},{1,2},{2,1},{3,0},{4,7},{5,6},{6,5},{7,4},{8,11},{9,10},{10,... | collective-permute-start | bytes 33800 | tf_op jit(solution)/shard_map/ppermute | solution.py:60
  29.7 127.1 %copy-start.46 = (bf16[64,2048]{1,0:T(8,128)(2,1)}, bf16[64,2048]{1,0:T(8,128)(2,1)S(1)}, u32[]{:S(2)}) copy-start(bf16[64,2048]{1,0:T(8,128)(2,1)S(1)} %dynamic-slice_bitcast_fusion.17.refs_7_.refs_6_) | copy-start | bytes 786436
  31.2 66.2 %copy-start.35 = (bf16[256,2048]{1,0:T(8,128)(2,1)}, bf16[256,2048]{1,0:T(8,128)(2,1)S(1)}, u32[]{:S(2)}) copy-start(bf16[256,2048]{1,0:T(8,128)(2,1)S(1)} %dynamic-slice_bitcast_fusion.4.refs_3_.refs_2_) | copy-start | bytes 3145732
  47.9 23.7 %collective-permute-start.5 = (bf16[256,1792]{1,0:T(8,128)(2,1)}, bf16[256,1792]{1,0:T(8,128)(2,1)}, u32[]{:S(2)}, u32[]{:S(2)}) collective-permute-start(bf16[256,1792]{1,0:T(8,128)(2,1)} %get-tuple-element.248.refs_6_.refs_3_), channel_id=1, source_target_pairs={{0,2},{1,3},{2,0},{3,1},{4,6},{5,7},{6,4},{7,5},{8,10},{9,11},{10,... | collective-permute-start | bytes 2752520 | tf_op jit(solution)/shard_map/ppermute | solution.py:60
  49.5 39.7 %collective-permute-start.6 = (bf16[256,1792]{1,0:T(8,128)(2,1)}, bf16[256,1792]{1,0:T(8,128)(2,1)}, u32[]{:S(2)}, u32[]{:S(2)}) collective-permute-start(bf16[256,1792]{1,0:T(8,128)(2,1)} %collective-permute-done.refs_7_.refs_4_), channel_id=1, source_target_pairs={{0,2},{1,3},{2,0},{3,1},{4,6},{5,7},{6,4},{7,5},{8,10},{9,11},{10,... | collective-permute-start | bytes 2752520 | tf_op jit(solution)/shard_map/ppermute | solution.py:60
  50.0 39.2 %collective-permute-start.7 = (bf16[256,1792]{1,0:T(8,128)(2,1)S(1)}, bf16[256,1792]{1,0:T(8,128)(2,1)}, u32[]{:S(2)}, u32[]{:S(2)}) collective-permute-start(bf16[256,1792]{1,0:T(8,128)(2,1)S(1)} %get-tuple-element.250.refs_10_.refs_7_), channel_id=1, source_target_pairs={{0,1},{1,0},{2,3},{3,2},{4,5},{5,4},{6,7},{7,6},{8,9},{9,8},{10,11... | collective-permute-start | bytes 2752520 | tf_op jit(solution)/shard_map/ppermute | solution.py:60
  51.5 39.0 %collective-permute-start.8 = (bf16[256,1792]{1,0:T(8,128)(2,1)}, bf16[256,1792]{1,0:T(8,128)(2,1)}, u32[]{:S(2)}, u32[]{:S(2)}) collective-permute-start(bf16[256,1792]{1,0:T(8,128)(2,1)} %collective-permute-done.1.refs_11_.refs_8_), channel_id=1, source_target_pairs={{0,1},{1,0},{2,3},{3,2},{4,5},{5,4},{6,7},{7,6},{8,9},{9,8},{10,11... | collective-permute-start | bytes 2752520 | tf_op jit(solution)/shard_map/ppermute | solution.py:60
  54.7 223.0 %all-gather.13.cloned.1.call-start = ((), (), s32[]{:S(2)}) async-start(), calls=%async_computation.3 | async-start | bytes 4718592 | tf_op jit(solution)/shard_map/all_gather | solution.py:842
  94.4 47.8 %collective-permute-start.10 = (bf16[256,2048]{1,0:T(8,128)(2,1)S(1)}, bf16[256,2048]{1,0:T(8,128)(2,1)S(1)}, u32[]{:S(2)}, u32[]{:S(2)}) collective-permute-start(bf16[256,2048]{1,0:T(8,128)(2,1)S(1)} %dynamic-slice_bitcast_fusion.4.refs_3_.refs_2_), channel_id=1, source_target_pairs={{0,2},{1,3},{2,0},{3,1},{4,6},{5,7},{6,4},{7,5},{8,10},{9,11},{10,... | collective-permute-start | bytes 3145736 | tf_op jit(solution)/shard_map/ppermute | solution.py:60
  95.9 46.3 %collective-permute-start.11 = (bf16[256,2048]{1,0:T(8,128)(2,1)S(1)}, bf16[256,2048]{1,0:T(8,128)(2,1)S(1)}, u32[]{:S(2)}, u32[]{:S(2)}) collective-permute-start(bf16[256,2048]{1,0:T(8,128)(2,1)S(1)} %dynamic-slice_bitcast_fusion.4.refs_3_.refs_2_), channel_id=1, source_target_pairs={{0,3},{1,2},{2,1},{3,0},{4,7},{5,6},{6,5},{7,4},{8,11},{9,10},{10,... | collective-permute-start | bytes 3145736 | tf_op jit(solution)/shard_map/ppermute | solution.py:60
  97.4 46.1 %collective-permute-start.9 = (bf16[256,2048]{1,0:T(8,128)(2,1)S(1)}, bf16[256,2048]{1,0:T(8,128)(2,1)}, u32[]{:S(2)}, u32[]{:S(2)}) collective-permute-start(bf16[256,2048]{1,0:T(8,128)(2,1)S(1)} %dynamic-slice_bitcast_fusion.4.refs_3_.refs_2_), channel_id=1, source_target_pairs={{0,1},{1,0},{2,3},{3,2},{4,5},{5,4},{6,7},{7,6},{8,9},{9,8},{10,11... | collective-permute-start | bytes 3145736 | tf_op jit(solution)/shard_map/ppermute | solution.py:60
  152.8 29.4 %collective-permute-start.12 = (bf16[2,128,1024]{2,1,0:T(8,128)(2,1)}, bf16[2,128,1024]{2,1,0:T(8,128)(2,1)S(1)}, u32[]{:S(2)}, u32[]{:S(2)}) collective-permute-start(bf16[2,128,1024]{2,1,0:T(8,128)(2,1)} %dynamic-slice_bitcast_fusion.12), channel_id=1, source_target_pairs={{0,1},{1,0},{2,3},{3,2},{4,5},{5,4},{6,7},{7,6},{8,9},{9,8},{10,11... | collective-permute-start | bytes 1572872 | tf_op jit(solution)/shard_map/ppermute | solution.py:60
  154.3 27.9 %collective-permute-start.13 = (bf16[2,128,1024]{2,1,0:T(8,128)(2,1)S(1)}, bf16[2,128,1024]{2,1,0:T(8,128)(2,1)S(1)}, u32[]{:S(2)}, u32[]{:S(2)}) collective-permute-start(bf16[2,128,1024]{2,1,0:T(8,128)(2,1)S(1)} %dynamic-slice_bitcast_fusion.11), channel_id=1, source_target_pairs={{0,2},{1,3},{2,0},{3,1},{4,6},{5,7},{6,4},{7,5},{8,10},{9,11},{10,... | collective-permute-start | bytes 1572872 | tf_op jit(solution)/shard_map/ppermute | solution.py:60
  155.8 26.3 %collective-permute-start.14 = (bf16[64,2048]{1,0:T(8,128)(2,1)S(1)}, bf16[64,2048]{1,0:T(8,128)(2,1)}, u32[]{:S(2)}, u32[]{:S(2)}) collective-permute-start(bf16[64,2048]{1,0:T(8,128)(2,1)S(1)} %dynamic-slice_bitcast_fusion.17.refs_7_.refs_6_), channel_id=1, source_target_pairs={{0,1},{1,0},{2,3},{3,2},{4,5},{5,4},{6,7},{7,6},{8,9},{9,8},{10,11... | collective-permute-start | bytes 786440 | tf_op jit(solution)/shard_map/ppermute | solution.py:60
  156.3 25.8 %collective-permute-start.15 = (bf16[64,2048]{1,0:T(8,128)(2,1)S(1)}, bf16[64,2048]{1,0:T(8,128)(2,1)}, u32[]{:S(2)}, u32[]{:S(2)}) collective-permute-start(bf16[64,2048]{1,0:T(8,128)(2,1)S(1)} %dynamic-slice_bitcast_fusion.17.refs_7_.refs_6_), channel_id=1, source_target_pairs={{0,2},{1,3},{2,0},{3,1},{4,6},{5,7},{6,4},{7,5},{8,10},{9,11},{10,... | collective-permute-start | bytes 786440 | tf_op jit(solution)/shard_map/ppermute | solution.py:60
  156.8 25.3 %collective-permute-start.16 = (bf16[64,2048]{1,0:T(8,128)(2,1)S(1)}, bf16[64,2048]{1,0:T(8,128)(2,1)}, u32[]{:S(2)}, u32[]{:S(2)}) collective-permute-start(bf16[64,2048]{1,0:T(8,128)(2,1)S(1)} %dynamic-slice_bitcast_fusion.17.refs_7_.refs_6_), channel_id=1, source_target_pairs={{0,3},{1,2},{2,1},{3,0},{4,7},{5,6},{6,5},{7,4},{8,11},{9,10},{10,... | collective-permute-start | bytes 786440 | tf_op jit(solution)/shard_map/ppermute | solution.py:60
  189.2 12.3 %collective-permute-start.17 = (bf16[128,1024]{1,0:T(8,128)(2,1)S(1)}, bf16[128,1024]{1,0:T(8,128)(2,1)S(1)}, u32[]{:S(2)}, u32[]{:S(2)}) collective-permute-start(bf16[128,1024]{1,0:T(8,128)(2,1)S(1)} %dynamic-slice_bitcast_fusion.16), channel_id=1, source_target_pairs={{0,2},{1,3},{2,0},{3,1},{4,6},{5,7},{6,4},{7,5},{8,10},{9,11},{10,... | collective-permute-start | bytes 786440 | tf_op jit(solution)/shard_map/ppermute | solution.py:60
  190.7 10.8 %collective-permute-start.18 = (bf16[128,1024]{1,0:T(8,128)(2,1)S(1)}, bf16[128,1024]{1,0:T(8,128)(2,1)S(1)}, u32[]{:S(2)}, u32[]{:S(2)}) collective-permute-start(bf16[128,1024]{1,0:T(8,128)(2,1)S(1)} %dynamic-slice_bitcast_fusion.15), channel_id=1, source_target_pairs={{0,1},{1,0},{2,3},{3,2},{4,5},{5,4},{6,7},{7,6},{8,9},{9,8},{10,11... | collective-permute-start | bytes 786440 | tf_op jit(solution)/shard_map/ppermute | solution.py:60
  202.5 95.5 %all-gather.11.cloned.1.call-start = ((), (), s32[]{:S(2)}) async-start(), calls=%async_computation.2 | async-start | bytes 4718592 | tf_op jit(solution)/shard_map/all_gather | solution.py:842
  205.2 20.1 %collective-permute-start.19 = (bf16[2,128,1024]{2,1,0:T(8,128)(2,1)}, bf16[2,128,1024]{2,1,0:T(8,128)(2,1)S(1)}, u32[]{:S(2)}, u32[]{:S(2)}) collective-permute-start(bf16[2,128,1024]{2,1,0:T(8,128)(2,1)} %dynamic-slice_bitcast_fusion.10), channel_id=1, source_target_pairs={{0,1},{1,0},{2,3},{3,2},{4,5},{5,4},{6,7},{7,6},{8,9},{9,8},{10,11... | collective-permute-start | bytes 1572872 | tf_op jit(solution)/shard_map/ppermute | solution.py:60
  205.8 19.4 %collective-permute-start.20 = (bf16[2,128,1024]{2,1,0:T(8,128)(2,1)S(1)}, bf16[2,128,1024]{2,1,0:T(8,128)(2,1)S(1)}, u32[]{:S(2)}, u32[]{:S(2)}) collective-permute-start(bf16[2,128,1024]{2,1,0:T(8,128)(2,1)S(1)} %dynamic-slice_bitcast_fusion.9), channel_id=1, source_target_pairs={{0,2},{1,3},{2,0},{3,1},{4,6},{5,7},{6,4},{7,5},{8,10},{9,11},{10,... | collective-permute-start | bytes 1572872 | tf_op jit(solution)/shard_map/ppermute | solution.py:60
  225.8 16.1 %collective-permute-start.21 = (bf16[128,1024]{1,0:T(8,128)(2,1)S(1)}, bf16[128,1024]{1,0:T(8,128)(2,1)S(1)}, u32[]{:S(2)}, u32[]{:S(2)}) collective-permute-start(bf16[128,1024]{1,0:T(8,128)(2,1)S(1)} %dynamic-slice_bitcast_fusion.14), channel_id=1, source_target_pairs={{0,2},{1,3},{2,0},{3,1},{4,6},{5,7},{6,4},{7,5},{8,10},{9,11},{10,... | collective-permute-start | bytes 786440 | tf_op jit(solution)/shard_map/ppermute | solution.py:60
  227.5 14.4 %collective-permute-start.22 = (bf16[128,1024]{1,0:T(8,128)(2,1)S(1)}, bf16[128,1024]{1,0:T(8,128)(2,1)S(1)}, u32[]{:S(2)}, u32[]{:S(2)}) collective-permute-start(bf16[128,1024]{1,0:T(8,128)(2,1)S(1)} %dynamic-slice_bitcast_fusion.13), channel_id=1, source_target_pairs={{0,1},{1,0},{2,3},{3,2},{4,5},{5,4},{6,7},{7,6},{8,9},{9,8},{10,11... | collective-permute-start | bytes 786440 | tf_op jit(solution)/shard_map/ppermute | solution.py:60
  247.3 24.0 %collective-permute-start.23 = (bf16[2,256,1024]{2,1,0:T(8,128)(2,1)}, bf16[2,256,1024]{2,1,0:T(8,128)(2,1)}, u32[]{:S(2)}, u32[]{:S(2)}) collective-permute-start(bf16[2,256,1024]{2,1,0:T(8,128)(2,1)} %dynamic-slice_bitcast_fusion.3), channel_id=1, source_target_pairs={{0,1},{1,0},{2,3},{3,2},{4,5},{5,4},{6,7},{7,6},{8,9},{9,8},{10,11... | collective-permute-start | bytes 3145736 | tf_op jit(solution)/shard_map/ppermute | solution.py:60
  247.8 23.7 %collective-permute-start.24 = (bf16[2,256,1024]{2,1,0:T(8,128)(2,1)S(1)}, bf16[2,256,1024]{2,1,0:T(8,128)(2,1)}, u32[]{:S(2)}, u32[]{:S(2)}) collective-permute-start(bf16[2,256,1024]{2,1,0:T(8,128)(2,1)S(1)} %dynamic-slice_bitcast_fusion.2), channel_id=1, source_target_pairs={{0,2},{1,3},{2,0},{3,1},{4,6},{5,7},{6,4},{7,5},{8,10},{9,11},{10,... | collective-permute-start | bytes 3145736 | tf_op jit(solution)/shard_map/ppermute | solution.py:60
  277.7 21.2 %collective-permute-start.27 = (bf16[4,256,2048]{2,1,0:T(8,128)(2,1)}, bf16[4,256,2048]{2,1,0:T(8,128)(2,1)}, u32[]{:S(2)}, u32[]{:S(2)}) collective-permute-start(bf16[4,256,2048]{2,1,0:T(8,128)(2,1)} %get-tuple-element.337), channel_id=1, source_target_pairs={{0,4},{4,0},{8,12},{12,8},{16,20},{20,16},{24,28},{28,24},{1,5},{5... | collective-permute-start | bytes 12582920 | tf_op jit(solution)/shard_map/ppermute | solution.py:60
  277.7 20.3 %collective-permute-start.25 = (bf16[256,1024]{1,0:T(8,128)(2,1)}, bf16[256,1024]{1,0:T(8,128)(2,1)S(1)}, u32[]{:S(2)}, u32[]{:S(2)}) collective-permute-start(bf16[256,1024]{1,0:T(8,128)(2,1)} %dynamic-slice_bitcast_fusion.8), channel_id=1, source_target_pairs={{0,2},{1,3},{2,0},{3,1},{4,6},{5,7},{6,4},{7,5},{8,10},{9,11},{10,... | collective-permute-start | bytes 1572872 | tf_op jit(solution)/shard_map/ppermute | solution.py:60
  279.2 18.9 %collective-permute-start.26 = (bf16[256,1024]{1,0:T(8,128)(2,1)}, bf16[256,1024]{1,0:T(8,128)(2,1)S(1)}, u32[]{:S(2)}, u32[]{:S(2)}) collective-permute-start(bf16[256,1024]{1,0:T(8,128)(2,1)} %dynamic-slice_bitcast_fusion.7), channel_id=1, source_target_pairs={{0,1},{1,0},{2,3},{3,2},{4,5},{5,4},{6,7},{7,6},{8,9},{9,8},{10,11... | collective-permute-start | bytes 1572872 | tf_op jit(solution)/shard_map/ppermute | solution.py:60
  300.4 27.0 %collective-permute-start.28 = (bf16[256,2048]{1,0:T(8,128)(2,1)S(1)}, bf16[256,2048]{1,0:T(8,128)(2,1)S(1)}, u32[]{:S(2)}, u32[]{:S(2)}) collective-permute-start(bf16[256,2048]{1,0:T(8,128)(2,1)S(1)} %pad_maximum_fusion.2), channel_id=1, source_target_pairs={{0,8},{4,12},{8,16},{12,20},{16,24},{20,28},{1,9},{5,13},{9,17},{1... | collective-permute-start | bytes 3145736 | tf_op jit(solution)/shard_map/ppermute | solution.py:60
  302.6 26.7 %collective-permute-start.29 = (bf16[256,2048]{1,0:T(8,128)(2,1)S(1)}, bf16[256,2048]{1,0:T(8,128)(2,1)S(1)}, u32[]{:S(2)}, u32[]{:S(2)}) collective-permute-start(bf16[256,2048]{1,0:T(8,128)(2,1)S(1)} %pad_maximum_fusion.2), channel_id=1, source_target_pairs={{8,0},{12,4},{16,8},{20,12},{24,16},{28,20},{9,1},{13,5},{17,9},{2... | collective-permute-start | bytes 3145736 | tf_op jit(solution)/shard_map/ppermute | solution.py:60
  331.4 26.9 %collective-permute-start.30 = (bf16[256,2048]{1,0:T(8,128)(2,1)}, bf16[256,2048]{1,0:T(8,128)(2,1)S(1)}, u32[]{:S(2)}, u32[]{:S(2)}) collective-permute-start(bf16[256,2048]{1,0:T(8,128)(2,1)} %get-tuple-element.352), channel_id=1, source_target_pairs={{0,8},{4,12},{8,16},{12,20},{16,24},{20,28},{1,9},{5,13},{9,17},{1... | collective-permute-start | bytes 3145736 | tf_op jit(solution)/shard_map/ppermute | solution.py:60
  336.1 26.3 %collective-permute-start.31 = (bf16[256,2048]{1,0:T(8,128)(2,1)}, bf16[256,2048]{1,0:T(8,128)(2,1)S(1)}, u32[]{:S(2)}, u32[]{:S(2)}) collective-permute-start(bf16[256,2048]{1,0:T(8,128)(2,1)} %get-tuple-element.353), channel_id=1, source_target_pairs={{8,0},{12,4},{16,8},{20,12},{24,16},{28,20},{9,1},{13,5},{17,9},{2... | collective-permute-start | bytes 3145736 | tf_op jit(solution)/shard_map/ppermute | solution.py:60
  372.1 41.3 %collective-permute-start.32 = (bf16[256,2048]{1,0:T(8,128)(2,1)}, bf16[256,2048]{1,0:T(8,128)(2,1)S(1)}, u32[]{:S(2)}, u32[]{:S(2)}) collective-permute-start(bf16[256,2048]{1,0:T(8,128)(2,1)} %get-tuple-element.364), channel_id=1, source_target_pairs={{0,8},{4,12},{8,16},{12,20},{16,24},{20,28},{1,9},{5,13},{9,17},{1... | collective-permute-start | bytes 3145736 | tf_op jit(solution)/shard_map/ppermute | solution.py:60
  375.4 37.9 %collective-permute-start.33 = (bf16[256,2048]{1,0:T(8,128)(2,1)}, bf16[256,2048]{1,0:T(8,128)(2,1)}, u32[]{:S(2)}, u32[]{:S(2)}) collective-permute-start(bf16[256,2048]{1,0:T(8,128)(2,1)} %get-tuple-element.365), channel_id=1, source_target_pairs={{8,0},{12,4},{16,8},{20,12},{24,16},{28,20},{9,1},{13,5},{17,9},{2... | collective-permute-start | bytes 3145736 | tf_op jit(solution)/shard_map/ppermute | solution.py:60
  376.7 36.6 %collective-permute-start.34 = (bf16[2,256,1024]{2,1,0:T(8,128)(2,1)}, bf16[2,256,1024]{2,1,0:T(8,128)(2,1)}, u32[]{:S(2)}, u32[]{:S(2)}) collective-permute-start(bf16[2,256,1024]{2,1,0:T(8,128)(2,1)} %dynamic-slice_bitcast_fusion.1), channel_id=1, source_target_pairs={{0,1},{1,0},{2,3},{3,2},{4,5},{5,4},{6,7},{7,6},{8,9},{9,8},{10,11... | collective-permute-start | bytes 3145736 | tf_op jit(solution)/shard_map/ppermute | solution.py:60
  378.2 35.2 %collective-permute-start.35 = (bf16[2,256,1024]{2,1,0:T(8,128)(2,1)}, bf16[2,256,1024]{2,1,0:T(8,128)(2,1)}, u32[]{:S(2)}, u32[]{:S(2)}) collective-permute-start(bf16[2,256,1024]{2,1,0:T(8,128)(2,1)} %dynamic-slice_bitcast_fusion), channel_id=1, source_target_pairs={{0,2},{1,3},{2,0},{3,1},{4,6},{5,7},{6,4},{7,5},{8,10},{9,11},{10,... | collective-permute-start | bytes 3145736 | tf_op jit(solution)/shard_map/ppermute | solution.py:60
  424.1 17.3 %collective-permute-start.38 = (bf16[4,256,2048]{2,1,0:T(8,128)(2,1)}, bf16[4,256,2048]{2,1,0:T(8,128)(2,1)}, u32[]{:S(2)}, u32[]{:S(2)}) collective-permute-start(bf16[4,256,2048]{2,1,0:T(8,128)(2,1)} %get-tuple-element.378), channel_id=1, source_target_pairs={{0,4},{4,0},{8,12},{12,8},{16,20},{20,16},{24,28},{28,24},{1,5},{5... | collective-permute-start | bytes 12582920 | tf_op jit(solution)/shard_map/ppermute | solution.py:60
  424.7 16.6 %collective-permute-start.36 = (bf16[256,1024]{1,0:T(8,128)(2,1)}, bf16[256,1024]{1,0:T(8,128)(2,1)}, u32[]{:S(2)}, u32[]{:S(2)}) collective-permute-start(bf16[256,1024]{1,0:T(8,128)(2,1)} %dynamic-slice_bitcast_fusion.6), channel_id=1, source_target_pairs={{0,2},{1,3},{2,0},{3,1},{4,6},{5,7},{6,4},{7,5},{8,10},{9,11},{10,... | collective-permute-start | bytes 1572872 | tf_op jit(solution)/shard_map/ppermute | solution.py:60
  424.8 16.6 %collective-permute-start.37 = (bf16[256,1024]{1,0:T(8,128)(2,1)}, bf16[256,1024]{1,0:T(8,128)(2,1)}, u32[]{:S(2)}, u32[]{:S(2)}) collective-permute-start(bf16[256,1024]{1,0:T(8,128)(2,1)} %dynamic-slice_bitcast_fusion.5), channel_id=1, source_target_pairs={{0,1},{1,0},{2,3},{3,2},{4,5},{5,4},{6,7},{7,6},{8,9},{9,8},{10,11... | collective-permute-start | bytes 1572872 | tf_op jit(solution)/shard_map/ppermute | solution.py:60
  425.0 33.2 %collective-permute-start.42 = (bf16[256,2048]{1,0:T(8,128)(2,1)}, bf16[256,2048]{1,0:T(8,128)(2,1)}, u32[]{:S(2)}, u32[]{:S(2)}) collective-permute-start(bf16[256,2048]{1,0:T(8,128)(2,1)} %get-tuple-element.398), channel_id=1, source_target_pairs={{0,8},{4,12},{8,16},{12,20},{16,24},{20,28},{1,9},{5,13},{9,17},{1... | collective-permute-start | bytes 3145736 | tf_op jit(solution)/shard_map/ppermute | solution.py:60
  430.6 28.2 %collective-permute-start.43 = (bf16[256,2048]{1,0:T(8,128)(2,1)}, bf16[256,2048]{1,0:T(8,128)(2,1)}, u32[]{:S(2)}, u32[]{:S(2)}) collective-permute-start(bf16[256,2048]{1,0:T(8,128)(2,1)} %get-tuple-element.399), channel_id=1, source_target_pairs={{8,0},{12,4},{16,8},{20,12},{24,16},{28,20},{9,1},{13,5},{17,9},{2... | collective-permute-start | bytes 3145736 | tf_op jit(solution)/shard_map/ppermute | solution.py:60
  444.3 31.1 %collective-permute-start.39 = (bf16[256,2048]{1,0:T(8,128)(2,1)S(1)}, bf16[256,2048]{1,0:T(8,128)(2,1)S(1)}, u32[]{:S(2)}, u32[]{:S(2)}) collective-permute-start(bf16[256,2048]{1,0:T(8,128)(2,1)S(1)} %pad_maximum_fusion.3), channel_id=1, source_target_pairs={{0,8},{4,12},{8,16},{12,20},{16,24},{20,28},{1,9},{5,13},{9,17},{1... | collective-permute-start | bytes 3145736 | tf_op jit(solution)/shard_map/ppermute | solution.py:60
  448.9 31.5 %collective-permute-start.40 = (bf16[256,2048]{1,0:T(8,128)(2,1)S(1)}, bf16[256,2048]{1,0:T(8,128)(2,1)S(1)}, u32[]{:S(2)}, u32[]{:S(2)}) collective-permute-start(bf16[256,2048]{1,0:T(8,128)(2,1)S(1)} %pad_maximum_fusion.3), channel_id=1, source_target_pairs={{8,0},{12,4},{16,8},{20,12},{24,16},{28,20},{9,1},{13,5},{17,9},{2... | collective-permute-start | bytes 3145736 | tf_op jit(solution)/shard_map/ppermute | solution.py:60
  450.2 8.6 %collective-permute-start.41 = (f32[20480]{0:T(1024)S(1)}, f32[20480]{0:T(1024)S(1)}, u32[]{:S(2)}, u32[]{:S(2)}) collective-permute-start(f32[20480]{0:T(1024)S(1)} %constant_dynamic-update-slice_fusion.2), channel_id=1, source_target_pairs={{0,4},{4,0},{8,12},{12,8},{16,20},{20,16},{24,28},{28,24},{1,5},{5... | collective-permute-start | bytes 245768 | tf_op jit(solution)/shard_map/ppermute | solution.py:60
  457.6 90.4 %copy-start.5 = (bf16[4,256,2048]{2,1,0:T(8,128)(2,1)}, bf16[4,256,2048]{2,1,0:T(8,128)(2,1)S(1)}, u32[]{:S(2)}) copy-start(bf16[4,256,2048]{2,1,0:T(8,128)(2,1)S(1)} %add_convert_fusion) | copy-start | bytes 12582916
  483.9 30.7 %collective-permute-start.47 = (bf16[4,256,2048]{2,1,0:T(8,128)(2,1)S(1)}, bf16[4,256,2048]{2,1,0:T(8,128)(2,1)S(1)}, u32[]{:S(2)}, u32[]{:S(2)}) collective-permute-start(bf16[4,256,2048]{2,1,0:T(8,128)(2,1)S(1)} %pad_maximum_fusion.mine), channel_id=1, source_target_pairs={{0,4},{4,0},{8,12},{12,8},{16,20},{20,16},{24,28},{28,24},{1,5},{5... | collective-permute-start | bytes 12582920 | tf_op jit(solution)/shard_map/ppermute | solution.py:60
  484.0 30.6 %collective-permute-start.44 = (bf16[256,2048]{1,0:T(8,128)(2,1)S(1)}, bf16[256,2048]{1,0:T(8,128)(2,1)S(1)}, u32[]{:S(2)}, u32[]{:S(2)}) collective-permute-start(bf16[256,2048]{1,0:T(8,128)(2,1)S(1)} %get-tuple-element.409), channel_id=1, source_target_pairs={{0,8},{4,12},{8,16},{12,20},{16,24},{20,28},{1,9},{5,13},{9,17},{1... | collective-permute-start | bytes 3145736 | tf_op jit(solution)/shard_map/ppermute | solution.py:60
  485.7 28.9 %collective-permute-start.45 = (bf16[256,2048]{1,0:T(8,128)(2,1)S(1)}, bf16[256,2048]{1,0:T(8,128)(2,1)S(1)}, u32[]{:S(2)}, u32[]{:S(2)}) collective-permute-start(bf16[256,2048]{1,0:T(8,128)(2,1)S(1)} %get-tuple-element.410), channel_id=1, source_target_pairs={{8,0},{12,4},{16,8},{20,12},{24,16},{28,20},{9,1},{13,5},{17,9},{2... | collective-permute-start | bytes 3145736 | tf_op jit(solution)/shard_map/ppermute | solution.py:60
  487.2 27.4 %collective-permute-start.46 = (f32[20480]{0:T(1024)S(1)}, f32[20480]{0:T(1024)S(1)}, u32[]{:S(2)}, u32[]{:S(2)}) collective-permute-start(f32[20480]{0:T(1024)S(1)} %add.403), channel_id=1, source_target_pairs={{0,8},{4,12},{8,0},{12,4},{16,24},{20,28},{24,16},{28,20},{1,9},{5... | collective-permute-start | bytes 245768 | tf_op jit(solution)/shard_map/ppermute | solution.py:60
  515.5 32.4 %collective-permute-start.48 = (bf16[256,2048]{1,0:T(8,128)(2,1)S(1)}, bf16[256,2048]{1,0:T(8,128)(2,1)S(1)}, u32[]{:S(2)}, u32[]{:S(2)}) collective-permute-start(bf16[256,2048]{1,0:T(8,128)(2,1)S(1)} %get-tuple-element.421), channel_id=1, source_target_pairs={{0,8},{4,12},{8,16},{12,20},{16,24},{20,28},{1,9},{5,13},{9,17},{1... | collective-permute-start | bytes 3145736 | tf_op jit(solution)/shard_map/ppermute | solution.py:60
  517.1 30.8 %collective-permute-start.49 = (bf16[256,2048]{1,0:T(8,128)(2,1)S(1)}, bf16[256,2048]{1,0:T(8,128)(2,1)S(1)}, u32[]{:S(2)}, u32[]{:S(2)}) collective-permute-start(bf16[256,2048]{1,0:T(8,128)(2,1)S(1)} %get-tuple-element.422), channel_id=1, source_target_pairs={{8,0},{12,4},{16,8},{20,12},{24,16},{28,20},{9,1},{13,5},{17,9},{2... | collective-permute-start | bytes 3145736 | tf_op jit(solution)/shard_map/ppermute | solution.py:60
  518.4 29.5 %collective-permute-start.50 = (f32[20480]{0:T(1024)S(1)}, f32[20480]{0:T(1024)S(1)}, u32[]{:S(2)}, u32[]{:S(2)}) collective-permute-start(f32[20480]{0:T(1024)S(1)} %add.411), channel_id=1, source_target_pairs={{0,16},{4,20},{8,24},{12,28},{16,0},{20,4},{24,8},{28,12},{1,17},{... | collective-permute-start | bytes 245768 | tf_op jit(solution)/shard_map/ppermute | solution.py:60
  550.1 4.8 collective-permute-start.51
  554.9 7.7 %collective-permute-start.52 = (bf16[4,256,2048]{2,1,0:T(8,128)(2,1)}, bf16[4,256,2048]{2,1,0:T(8,128)(2,1)}, u32[]{:S(2)}, u32[]{:S(2)}) collective-permute-start(bf16[4,256,2048]{2,1,0:T(8,128)(2,1)} %pad_maximum_fusion.1.mine), channel_id=1, source_target_pairs={{0,4},{4,0},{8,12},{12,8},{16,20},{20,16},{24,28},{28,24},{1,5},{5... | collective-permute-start | bytes 12582920 | tf_op jit(solution)/shard_map/ppermute | solution.py:60
  555.0 25.0 %collective-permute-start.54 = (bf16[256,2048]{1,0:T(8,128)(2,1)}, bf16[256,2048]{1,0:T(8,128)(2,1)S(1)}, u32[]{:S(2)}, u32[]{:S(2)}) collective-permute-start(bf16[256,2048]{1,0:T(8,128)(2,1)} %get-tuple-element.444), channel_id=1, source_target_pairs={{0,8},{4,12},{8,16},{12,20},{16,24},{20,28},{1,9},{5,13},{9,17},{1... | collective-permute-start | bytes 3145736 | tf_op jit(solution)/shard_map/ppermute | solution.py:60
  556.6 27.5 %collective-permute-start.55 = (bf16[256,2048]{1,0:T(8,128)(2,1)}, bf16[256,2048]{1,0:T(8,128)(2,1)}, u32[]{:S(2)}, u32[]{:S(2)}) collective-permute-start(bf16[256,2048]{1,0:T(8,128)(2,1)} %get-tuple-element.445), channel_id=1, source_target_pairs={{8,0},{12,4},{16,8},{20,12},{24,16},{28,20},{9,1},{13,5},{17,9},{2... | collective-permute-start | bytes 3145736 | tf_op jit(solution)/shard_map/ppermute | solution.py:60
  557.9 4.6 collective-permute-start.53
  (66 other events, 565.5 us)
Sparse Core Ops, SparseCore 0:
  9.6 84.7 all-gather.14
  96.0 45.6 all-gather.6
  143.3 45.8 all-gather.8
  202.7 43.9 all-gather.12
  248.1 45.9 all-gather.10
